TPU v7x, 32 devices: a whole 2x2x4 slice. The times are simulated.
32 devices in a mesh: groups: 2 (over y), expert: 4 (over z), blk: 2 (over x), tensor: 2 (over core).
Axes of the slice: x: 2, y: 2, z: 4, core: 2. Of those that a mesh axis runs over, the one named last changes fastest.
Arguments:
- tokens: bfloat16 [2048, 1024], P(('groups', 'expert', 'blk')), parts along dimension 0, may hold values from -6 to 6
- cotangent: bfloat16 [2048, 1024], P(('groups', 'expert', 'blk')), parts along dimension 0, may hold values from -6 to 6
- probs: bfloat16 [2048, 6], P(('groups', 'expert', 'blk')), parts along dimension 0, may hold values from 0.049804688 to 0.59765625
- experts: int32 [2048, 6], P(('groups', 'expert', 'blk')), parts along dimension 0, may hold values from 0 to 63, all different within a row; in each aligned block of 128 rows (0 to 127, 128 to 255, ...) at most 16 rows name the same one
- w_gate: bfloat16 [128, 1024, 352], P(('expert', 'blk'), None, 'tensor'), may hold values from -0.1875 to 0.1875
- w_up: bfloat16 [128, 1024, 352], P(('expert', 'blk'), None, 'tensor'), may hold values from -0.1875 to 0.1875
- w_down: bfloat16 [128, 352, 1024], P(('expert', 'blk'), 'tensor'), may hold values from -0.21875 to 0.21875
Outputs:
- grad_tokens: bfloat16 [2048, 1024], P(('groups', 'expert', 'blk')), parts along dimension 0
- grad_probs: float32 [2048, 6], P(('groups', 'expert', 'blk')), parts along dimension 0
- grad_gate: bfloat16 [256, 1024, 352], P(('groups', 'expert', 'blk'), None, 'tensor'), parts along dimension 0
- grad_up: bfloat16 [256, 1024, 352], P(('groups', 'expert', 'blk'), None, 'tensor'), parts along dimension 0
- grad_down: bfloat16 [256, 352, 1024], P(('groups', 'expert', 'blk'), 'tensor'), parts along dimension 0
There are 2 independent parts, one for each index of `groups`. A program takes and returns all parts, laid end to end along the dimension named above; an argument that names none is the same for every part. Nothing has to cross between parts.
Inputs may be any that keep to these rules, and one draw needn't show every extreme that they name: Each row names 6 different experts. Within the rows of one device no expert is named more than 16 times; in every draw some expert is named exactly 16 times by one device's rows.
All inputs are finite; a program needn't handle non-finite values.
Results may differ from a plain program's by a relative error of at most 0.0065.
Values may be sent and summed in bfloat16 or wider, within the bound.
No kernel may reach another device: no remote copies, remote signals or barrier semaphores. Data moves between devices by JAX's collectives and lax.ppermute only.
A program may use at most 192 MiB of HBM per device.

v0:
```python
import jax
import jax.numpy as jnp
from jax import lax
from jax.sharding import PartitionSpec as P

MOST = 16


row_block = 128


def expert_block(x_blk, dy_blk, prob_blk, gate_part, up_part, down_part):
    last_dims = (((1,), (1,)), ((), ()))
    gate_value = jnp.dot(x_blk, gate_part, preferred_element_type=jnp.float32)
    up_value = jnp.dot(x_blk, up_part, preferred_element_type=jnp.float32)
    sigmoid_value = jax.nn.sigmoid(gate_value)
    active = gate_value * sigmoid_value
    hidden = active * up_value
    gate_scale = prob_blk[:, None]
    gated_hidden = (gate_scale * hidden).astype(jnp.bfloat16)
    raw_grad = lax.dot_general(dy_blk, down_part, last_dims, preferred_element_type=jnp.float32)
    prob_part = jnp.sum(hidden * raw_grad, axis=1)
    grad_hidden = gate_scale * raw_grad
    grad_gate = (
        grad_hidden * up_value * sigmoid_value * (1.0 + gate_value * (1.0 - sigmoid_value))
    ).astype(jnp.bfloat16)
    grad_up = (grad_hidden * active).astype(jnp.bfloat16)
    input_part = (
        lax.dot_general(grad_gate, gate_part, last_dims, preferred_element_type=jnp.float32)
        + lax.dot_general(grad_up, up_part, last_dims, preferred_element_type=jnp.float32)
    ).astype(jnp.bfloat16)
    return (input_part, prob_part, grad_gate, grad_up, gated_hidden)


def per_device(tokens, cotangent, probs, experts, w_gate, w_up, w_down):
    tok_rows, features = tokens.shape
    top_count = experts.shape[1]
    cycle_length = lax.axis_size("blk")
    expert_length = lax.axis_size("expert")
    positions = expert_length * cycle_length
    local_halves = w_gate.shape[0]
    expert_total = local_halves * positions // 2
    per_half = MOST
    capacity = local_halves * per_half
    slot_total = positions * capacity
    flat_experts = experts.reshape(-1)
    assign_total = flat_experts.shape[0]
    one_hot = (flat_experts[:, None] == jnp.arange(expert_total, dtype=jnp.int32)[None, :]).astype(
        jnp.int32
    )
    earlier = jnp.sum((jnp.cumsum(one_hot, axis=0) - one_hot) * one_hot, axis=1)
    half_ids = 2 * flat_experts[:, None] + jnp.arange(2, dtype=jnp.int32)[None, :]
    home_pos = half_ids // local_halves
    local_ids = half_ids % local_halves
    rank_both = jnp.broadcast_to(earlier[:, None], half_ids.shape)
    target_slot = local_ids * per_half + rank_both
    target = (home_pos * capacity + target_slot).reshape(-1)
    entry_total = 2 * assign_total
    slot_table = (
        jnp.full((slot_total,), entry_total, jnp.int32)
        .at[target]
        .set(jnp.arange(entry_total, dtype=jnp.int32))
    )
    assign_of_slot = slot_table // 2
    token_of_slot = assign_of_slot // top_count
    pad_rows = jnp.zeros((1, features), jnp.bfloat16)
    send_x = jnp.concatenate([tokens, pad_rows])[token_of_slot].reshape(
        positions, capacity, features
    )
    send_dy = jnp.concatenate([cotangent, pad_rows])[token_of_slot].reshape(
        positions, capacity, features
    )
    send_prob = jnp.concatenate([probs.reshape(-1), jnp.zeros((1,), jnp.bfloat16)])[
        assign_of_slot
    ].reshape(positions, capacity)
    got_x, got_dy, got_prob = (
        lax.all_to_all(send_x, ("expert", "blk"), split_axis=0, concat_axis=0, tiled=True),
        lax.all_to_all(send_dy, ("expert", "blk"), split_axis=0, concat_axis=0, tiled=True),
        lax.all_to_all(send_prob, ("expert", "blk"), split_axis=0, concat_axis=0, tiled=True),
    )
    stack_gate, stack_up, stack_down = (w_gate, w_up, w_down)
    groups = capacity // per_half
    slot_ids = jnp.arange(slot_total, dtype=jnp.int32)
    group_of = slot_ids % capacity // per_half
    filled = got_prob.reshape(-1) != 0
    group_hot = (group_of[:, None] == jnp.arange(groups, dtype=jnp.int32)[None, :]).astype(
        jnp.int32
    )
    member = group_hot * filled[:, None].astype(jnp.int32)
    group_sizes = jnp.sum(member, axis=0)
    group_blocks = (group_sizes + row_block - 1) // row_block
    block_ends = jnp.cumsum(group_blocks)
    block_begins = block_ends - group_blocks
    within = jnp.sum((jnp.cumsum(member, axis=0) - member) * member, axis=1)
    row_total = row_block * (slot_total // row_block + groups + 1)
    begin_of = jnp.sum(group_hot * block_begins[None, :], axis=1)
    row_place = jnp.where(filled, begin_of * row_block + within, row_total)
    source_of = (
        jnp.full((row_total,), slot_total, jnp.int32).at[row_place].set(slot_ids, mode="drop")
    )
    rows_x = jnp.concatenate([got_x.reshape(slot_total, features), pad_rows])[source_of]
    rows_dy = jnp.concatenate([got_dy.reshape(slot_total, features), pad_rows])[source_of]
    rows_prob = jnp.concatenate([got_prob.reshape(-1), jnp.zeros((1,), jnp.bfloat16)])[
        source_of
    ].astype(jnp.float32)
    quarter = stack_gate.shape[2]

    def run_block(block_index, carry):
        input_rows, prob_rows, gate_rows, up_rows, gated_rows = carry
        group_index = jnp.sum((block_ends <= block_index).astype(jnp.int32))
        row_start = block_index * row_block
        x_blk = lax.dynamic_slice_in_dim(rows_x, row_start, row_block, 0)
        dy_blk = lax.dynamic_slice_in_dim(rows_dy, row_start, row_block, 0)
        prob_blk = lax.dynamic_slice_in_dim(rows_prob, row_start, row_block, 0)
        pieces = expert_block(
            x_blk,
            dy_blk,
            prob_blk,
            lax.dynamic_index_in_dim(stack_gate, group_index, 0, False),
            lax.dynamic_index_in_dim(stack_up, group_index, 0, False),
            lax.dynamic_index_in_dim(stack_down, group_index, 0, False),
        )
        input_part, prob_part, grad_gate, grad_up, gated_hidden = pieces
        input_rows = lax.dynamic_update_slice_in_dim(input_rows, input_part, row_start, 0)
        prob_rows = lax.dynamic_update_slice_in_dim(prob_rows, prob_part, row_start, 0)
        gate_rows = lax.dynamic_update_slice_in_dim(gate_rows, grad_gate, row_start, 0)
        up_rows = lax.dynamic_update_slice_in_dim(up_rows, grad_up, row_start, 0)
        gated_rows = lax.dynamic_update_slice_in_dim(gated_rows, gated_hidden, row_start, 0)
        return (input_rows, prob_rows, gate_rows, up_rows, gated_rows)

    initial = (
        jnp.zeros((row_total + 1, features), jnp.bfloat16),
        jnp.zeros((row_total + 1,), jnp.float32),
        jnp.zeros((row_total, quarter), jnp.bfloat16),
        jnp.zeros((row_total, quarter), jnp.bfloat16),
        jnp.zeros((row_total, quarter), jnp.bfloat16),
    )
    input_rows, prob_rows, gate_rows, up_rows, gated_rows = lax.fori_loop(
        0, block_ends[-1], run_block, initial
    )
    window = row_block * ((positions * per_half + row_block - 1) // row_block)
    lead_dims = (((0,), (0,)), ((), ()))
    window_ids = jnp.arange(window, dtype=jnp.int32)

    def group_weights(group_index, accs):
        acc_gate, acc_up, acc_down = accs
        begin = block_begins[group_index] * row_block
        start = jnp.minimum(begin, row_total - window)
        offset = begin - start
        keep = ((window_ids >= offset) & (window_ids < offset + group_sizes[group_index]))[:, None]
        x_win = lax.dynamic_slice_in_dim(rows_x, start, window, 0)
        dy_win = lax.dynamic_slice_in_dim(rows_dy, start, window, 0)
        zero_rows = jnp.zeros((window, quarter), jnp.bfloat16)
        gate_win = jnp.where(keep, lax.dynamic_slice_in_dim(gate_rows, start, window, 0), zero_rows)
        up_win = jnp.where(keep, lax.dynamic_slice_in_dim(up_rows, start, window, 0), zero_rows)
        gated_win = jnp.where(
            keep, lax.dynamic_slice_in_dim(gated_rows, start, window, 0), zero_rows
        )
        weight_gate = lax.dot_general(
            x_win, gate_win, lead_dims, preferred_element_type=jnp.float32
        )
        weight_up = lax.dot_general(x_win, up_win, lead_dims, preferred_element_type=jnp.float32)
        weight_down = lax.dot_general(
            gated_win, dy_win, lead_dims, preferred_element_type=jnp.float32
        )
        acc_gate = lax.dynamic_update_index_in_dim(acc_gate, weight_gate, group_index, 0)
        acc_up = lax.dynamic_update_index_in_dim(acc_up, weight_up, group_index, 0)
        acc_down = lax.dynamic_update_index_in_dim(acc_down, weight_down, group_index, 0)
        return (acc_gate, acc_up, acc_down)

    weight_init = (
        jnp.zeros((groups, features, quarter), jnp.float32),
        jnp.zeros((groups, features, quarter), jnp.float32),
        jnp.zeros((groups, quarter, features), jnp.float32),
    )
    acc_gate, acc_up, acc_down = lax.fori_loop(0, groups, group_weights, weight_init)
    slot_input = input_rows[row_place].reshape(positions, capacity, features)
    slot_prob = prob_rows[row_place].astype(jnp.bfloat16).reshape(positions, capacity)
    back_input, back_prob = (
        lax.all_to_all(slot_input, ("expert", "blk"), split_axis=0, concat_axis=0, tiled=True),
        lax.all_to_all(slot_prob, ("expert", "blk"), split_axis=0, concat_axis=0, tiled=True),
    )
    picked = back_input.reshape(slot_total, features)[target].reshape(
        tok_rows, top_count, 2, features
    )
    picked = picked.astype(jnp.float32)
    pair_input = (picked[:, :, 0] + picked[:, :, 1]).astype(jnp.bfloat16)
    input_local = jnp.sum(lax.optimization_barrier(pair_input).astype(jnp.float32), axis=1)
    picked_prob = back_prob.reshape(-1)[target].reshape(tok_rows, top_count, 2).astype(jnp.float32)
    pair_prob = (picked_prob[:, :, 0] + picked_prob[:, :, 1]).astype(jnp.bfloat16)
    prob_local = lax.optimization_barrier(pair_prob).astype(jnp.float32)
    input_sum, prob_sum = lax.psum((input_local, prob_local), "tensor")
    total_gate, total_up, total_down = (acc_gate, acc_up, acc_down)
    return (
        input_sum.astype(jnp.bfloat16),
        prob_sum,
        total_gate.astype(jnp.bfloat16),
        total_up.astype(jnp.bfloat16),
        total_down.astype(jnp.bfloat16),
    )


def solution(mesh):
    return jax.shard_map(
        per_device,
        mesh=mesh,
        in_specs=(
            P(("groups", "expert", "blk"), None),
            P(("groups", "expert", "blk"), None),
            P(("groups", "expert", "blk"), None),
            P(("groups", "expert", "blk"), None),
            P(("expert", "blk"), None, "tensor"),
            P(("expert", "blk"), None, "tensor"),
            P(("expert", "blk"), "tensor", None),
        ),
        out_specs=(
            P(("groups", "expert", "blk"), None),
            P(("groups", "expert", "blk"), None),
            P(("groups", "expert", "blk"), None, "tensor"),
            P(("groups", "expert", "blk"), None, "tensor"),
            P(("groups", "expert", "blk"), "tensor", None),
        ),
        check_vma=False,
    )
```

profile of v0, /device:TPU:0, one launch (start us, length us, event | category | flops | bytes accessed | tf_op | source)
XLA Modules:
  0.0 748.9 jit_solution(9256096414976842783)
XLA Ops:
  5.9 6.2 scatter_custom_fusion
  12.2 13.1 %gather_fusion = bf16[2048]{0:T(1024)(128)(2,1)S(1)} fusion(bf16[769]{0:T(1024)(128)(2,1)S(1)} %pad_maximum_fusion.1, s32[2048]{0:T(1024)S(1)} %get-tuple-element.488), kind=kCustom, calls=%fused_computation | custom fusion | bytes 16384 | tf_op jit(solution)/shard_map/gather | solution.py:73
  27.1 7.3 all-to-all-start
  34.3 9.6 %gather_fusion.2 = bf16[2048,1024]{1,0:T(8,128)(2,1)} fusion(bf16[129,1024]{1,0:T(8,128)(2,1)S(1)} %concatenate.20, s32[2048]{0:T(1024)S(1)} %get-tuple-element.487), kind=kCustom, calls=%fused_computation.2 | custom fusion | bytes 8396800 | tf_op jit(solution)/shard_map/gather | solution.py:70
  44.0 6.1 all-to-all-start.1
  50.1 9.6 %gather_fusion.4 = bf16[2048,1024]{1,0:T(8,128)(2,1)} fusion(bf16[129,1024]{1,0:T(8,128)(2,1)S(1)} %concatenate.22, s32[2048]{0:T(1024)S(1)} %get-tuple-element.487), kind=kCustom, calls=%fused_computation.4 | custom fusion | bytes 8396800 | tf_op jit(solution)/shard_map/gather | solution.py:67
  59.7 83.1 %all-to-all-done.1 = bf16[8,256,1024]{2,1,0:T(8,128)(2,1)} async-done(((bf16[8,256,1024]{2,1,0:T(8,128)(2,1)}), bf16[8,256,1024]{2,1,0:T(8,128)(2,1)}, u32[]{:S(2)}, u32[]{:S(2)}) %all-to-all-start.1) | async-done | bytes 4194336 | tf_op jit(solution)/shard_map/all_to_all | solution.py:78
  142.8 4.5 all-to-all-start.2
  147.5 4.5 reduce-window.21
  153.9 8.3 %scatter_custom_fusion.1 = s32[4224]{0:T(1024)S(1)} fusion(s32[2048]{0:T(1024)S(1)} %bitcast.130, s32[2048]{0:T(1024)S(1)} %iota.57, s32[]{:T(128)} %constant.209.clone.1), kind=kCustom, calls=%fused_computation.128 | custom fusion | bytes 16900 | tf_op jit(solution)/shard_map/scatter | solution.py:99
  162.2 25.1 %gather_fusion.1 = bf16[4224]{0:T(1024)(128)(2,1)S(1)} fusion(bf16[2049]{0:T(1024)(128)(2,1)S(1)} %pad_maximum_fusion, s32[5120]{0:T(1024)S(1)} %pad_clamp_fusion), kind=kCustom, calls=%fused_computation.1 | custom fusion | bytes 33792 | tf_op jit(solution)/shard_map/gather | solution.py:103
  187.9 4.6 concatenate.21
  192.6 22.3 %gather_fusion.3 = bf16[4224,1024]{1,0:T(8,128)(2,1)} fusion(bf16[2049,1024]{1,0:T(8,128)(2,1)} %concatenate.21, s32[5120]{0:T(1024)S(1)} %pad_clamp_fusion), kind=kCustom, calls=%fused_computation.3 | custom fusion | bytes 17318400 | tf_op jit(solution)/shard_map/gather | solution.py:102
  214.8 25.1 %all-to-all-done.2 = bf16[8,256,1024]{2,1,0:T(8,128)(2,1)} async-done(((bf16[8,256,1024]{2,1,0:T(8,128)(2,1)}), bf16[8,256,1024]{2,1,0:T(8,128)(2,1)}, u32[]{:S(2)}, u32[]{:S(2)}) %all-to-all-start.2) | async-done | bytes 4194336 | tf_op jit(solution)/shard_map/all_to_all | solution.py:77
  239.9 4.6 concatenate.23
  244.6 22.3 %gather_fusion.5 = bf16[4224,1024]{1,0:T(8,128)(2,1)} fusion(bf16[2049,1024]{1,0:T(8,128)(2,1)} %concatenate.23, s32[5120]{0:T(1024)S(1)} %pad_clamp_fusion), kind=kCustom, calls=%fused_computation.5 | custom fusion | bytes 17318400 | tf_op jit(solution)/shard_map/gather | solution.py:101
  266.9 4.4 broadcast_in_dim.103
  272.7 226.8 %while.37 = (s32[]{:T(128)}, bf16[4225,1024]{1,0:T(8,128)(2,1)}, bf16[4225]{0:T(1024)(128)(2,1)S(1)}, bf16[4224,176]{0,1:T(8,128)(2,1)S(1)}, bf16[4224,176]{0,1:...) while((s32[]{:T(128)}, bf16[4225,1024]{1,0:T(8,128)(2,1)}, ...), condition=%wide.region_14.15_spmd, body=%wide.region_11.14_spmd.sunk | while | flops 231489472 | bytes 5464210 | solution.py:138
  283.9 2.8 dynamic_update_slice.57
  298.0 2.7 dynamic_update_slice.57
  312.1 2.7 dynamic_update_slice.57
  326.3 2.7 dynamic_update_slice.57
  340.4 2.7 dynamic_update_slice.57
  354.5 2.7 dynamic_update_slice.57
  368.7 2.7 dynamic_update_slice.57
  382.8 2.7 dynamic_update_slice.57
  397.0 2.7 dynamic_update_slice.57
  411.1 2.7 dynamic_update_slice.57
  425.2 2.7 dynamic_update_slice.57
  439.4 2.7 dynamic_update_slice.57
  453.5 2.8 dynamic_update_slice.57
  467.6 2.7 dynamic_update_slice.57
  481.8 2.7 dynamic_update_slice.57
  495.9 2.7 dynamic_update_slice.57
  499.5 13.1 %gather_fusion.8 = bf16[2048]{0:T(1024)(128)(2,1)S(1)} fusion(bf16[4225]{0:T(1024)(128)(2,1)S(1)} %get-tuple-element.287, s32[2048]{0:T(1024)S(1)} %broadcast_clamp_fusion), kind=kCustom, calls=%fused_computation.8 | custom fusion | bytes 16384 | tf_op jit(solution)/shard_map/gather | solution.py:178
  513.9 3.6 all-to-all-start.4
  517.6 15.6 %gather_fusion.6 = bf16[2048,1024]{1,0:T(8,128)(2,1)} fusion(bf16[4225,1024]{1,0:T(8,128)(2,1)} %get-tuple-element.286, s32[2048]{0:T(1024)S(1)} %broadcast_clamp_fusion), kind=kCustom, calls=%fused_computation.6 | custom fusion | bytes 8396800 | tf_op jit(solution)/shard_map/gather | solution.py:177
  533.2 6.0 all-to-all-start.3
  539.2 162.0 %while.38 = (s32[]{:T(128)}, bf16[16,1024,176]{1,2,0:T(8,128)(2,1)}, bf16[16,1024,176]{1,2,0:T(8,128)(2,1)}, bf16[16,176,1024]{2,1,0:T(8,128)(2,1)}, s32[16]{0:T...) while((s32[]{:T(128)}, ...), condition=%wide.region_19.20_spmd.clone.clone, body=%wide.region_18.19_spmd.clone.clone.sunk | while | flops 138480000 | bytes 3625775 | solution.py:176
  541.9 2.1 fusion.129
  545.1 2.1 fusion.130
  552.0 2.1 fusion.129
  555.2 2.1 fusion.130
  562.2 2.1 fusion.129
  565.3 2.1 fusion.130
  572.3 2.1 fusion.129
  585.6 2.1 fusion.130
  592.5 2.1 fusion.129
  595.7 2.1 fusion.130
  602.6 2.1 fusion.129
  612.8 2.1 fusion.129
  615.9 2.1 fusion.130
  633.0 2.1 fusion.129
  636.2 2.1 fusion.130
  643.1 2.1 fusion.129
  646.3 2.1 fusion.130
  663.4 2.1 fusion.129
  666.6 2.1 fusion.130
  701.2 9.5 %gather_fusion.9 = bf16[1536]{0:T(1024)(128)(2,1)S(1)} fusion(bf16[2048]{0:T(1024)(128)(2,1)S(1)} %bitcast.114, s32[2048]{0:T(1024)S(1)} %pad_clamp_fusion.1), kind=kCustom, calls=%fused_computation.9 | custom fusion | bytes 12288 | tf_op jit(solution)/shard_map/gather | solution.py:189
  711.5 9.8 %gather_fusion.7 = bf16[1536,1024]{1,0:T(8,128)(2,1)S(1)} fusion(bf16[2048,1024]{1,0:T(8,128)(2,1)} %bitcast.17, s32[2048]{0:T(1024)S(1)} %pad_clamp_fusion.1), kind=kCustom, calls=%fused_computation.7 | custom fusion | bytes 6297600 | tf_op jit(solution)/shard_map/gather | solution.py:183
  721.3 5.7 reshape.433
  727.0 12.7 %fusion.84 = (f32[128,6,1,1024]{3,2,1,0:T(1,128)S(1)}, f32[128,6,1,1024]{3,2,1,0:T(1,128)}) fusion(f32[128,6,2,1024]{3,2,1,0:T(2,128)} %reshape.433), kind=kLoop, calls=%fused_computation.182 | loop fusion | bytes 12582912 | tf_op jit(solution)/shard_map/slice | solution.py:187
  739.7 3.6 fusion.50
  743.6 5.4 all-reduce.6
  (381 shorter events, 255.4 us)
Async XLA Ops:
  0.6 33.7 %copy-start = (bf16[128,1024]{1,0:T(8,128)(2,1)S(1)}, bf16[128,1024]{1,0:T(8,128)(2,1)}, u32[]{:S(2)}) copy-start(bf16[128,1024]{1,0:T(8,128)(2,1)} %param.12) | copy-start | bytes 786436
  27.1 16.9 %all-to-all-start = ((bf16[8,2,128]{2,1,0:T(2,128)(2,1)}), bf16[8,2,128]{2,1,0:T(2,128)(2,1)S(1)}, u32[]{:S(2)}, u32[]{:S(2)}) async-start(bf16[8,2,128]{2,1,0:T(2,128)(2,1)} %reshape.547), calls=%async_computation | async-start | bytes 8192 | tf_op jit(solution)/shard_map/all_to_all | solution.py:79
  44.0 6.1 copy-start.1
  44.0 98.8 %all-to-all-start.1 = ((bf16[8,256,1024]{2,1,0:T(8,128)(2,1)}), bf16[8,256,1024]{2,1,0:T(8,128)(2,1)}, u32[]{:S(2)}, u32[]{:S(2)}) async-start(bf16[8,256,1024]{2,1,0:T(8,128)(2,1)} %bitcast.117), calls=%async_computation.1 | async-start | bytes 8388608 | tf_op jit(solution)/shard_map/all_to_all | solution.py:78
  142.8 97.1 %all-to-all-start.2 = ((bf16[8,256,1024]{2,1,0:T(8,128)(2,1)}), bf16[8,256,1024]{2,1,0:T(8,128)(2,1)}, u32[]{:S(2)}, u32[]{:S(2)}) async-start(bf16[8,256,1024]{2,1,0:T(8,128)(2,1)} %bitcast.116), calls=%async_computation.2 | async-start | bytes 8388608 | tf_op jit(solution)/shard_map/all_to_all | solution.py:77
  513.9 19.3 %all-to-all-start.4 = ((bf16[8,2,128]{2,1,0:T(2,128)(2,1)}), bf16[8,2,128]{2,1,0:T(2,128)(2,1)S(1)}, u32[]{:S(2)}, u32[]{:S(2)}) async-start(bf16[8,2,128]{2,1,0:T(2,128)(2,1)} %reshape.549), calls=%async_computation.4 | async-start | bytes 8192 | tf_op jit(solution)/shard_map/all_to_all | solution.py:181
  533.2 178.3 %all-to-all-start.3 = ((bf16[8,256,1024]{2,1,0:T(8,128)(2,1)}), bf16[8,256,1024]{2,1,0:T(8,128)(2,1)}, u32[]{:S(2)}, u32[]{:S(2)}) async-start(bf16[8,256,1024]{2,1,0:T(8,128)(2,1)} %bitcast.115), calls=%async_computation.3 | async-start | bytes 8388608 | tf_op jit(solution)/shard_map/all_to_all | solution.py:180
where the time goes:
time: 756 us; the launch traced here: 749 us
  local copies, waits for them, and re-layouts  306 us (40%)
  matrix products  213 us (28%)
  waiting for transfers between devices  108 us (14%)
  loops' own time  63.6 us (8%)
  starting transfers between devices  27.5 us (4%)
  other arithmetic  24.6 us (3%)
    all_to_all x1, waiting for transfers between devices, per_device(): lax.all_to_all(send_dy, ('expert', 'blk'), split_axis=0, concat_axis=0, t...  83.1 us
    dynamic_update_slice x16, local copies, waits for them, and re-layouts, run_block(): lax.dynamic_update_slice_in_dim(input_rows, input_part, row_start, 0)  43.9 us
    another operation x1, loops' own time, per_device(): lax.fori_loop(0, block_ends[-1], run_block, initial)  41.9 us
    dot_general x16, matrix products, group_weights(): lax.dot_general(x_win, up_win, lead_dims, preferred_element_type=jnp.floa...  33.1 us
    dot_general x16, matrix products, group_weights(): lax.dot_general(x_win, gate_win, lead_dims, preferred_element_type=jnp.fl...  33.1 us
    dot_general x16, matrix products, group_weights(): lax.dot_general(gated_win, dy_win, lead_dims, preferred_element_type=jnp....  32.8 us
    dot_general x16, matrix products, expert_block(): gate_value = jnp.dot(x_blk, gate_part, preferred_element_type=jnp.float32)  32.1 us
    all_to_all x1, waiting for transfers between devices, per_device(): lax.all_to_all(send_x, ('expert', 'blk'), split_axis=0, concat_axis=0, ti...  25.1 us
  transfers between devices with their start and end apart: 5, of which 2 were waited for; matrix products, arithmetic and copies ran while one was open for 34% of the time, Pallas kernels for 0%

commit v1 on v0

v1 whole, which is shorter than its diff:
```python
import functools

import jax
import jax.numpy as jnp
from jax import lax
from jax.experimental import pallas as pl
from jax.experimental.pallas import tpu as pltpu
from jax.sharding import PartitionSpec as P

MOST = 16
BF16, F32 = jnp.bfloat16, jnp.float32
LAST = (((1,), (1,)), ((), ()))
LEAD = (((0,), (0,)), ((), ()))
VMEM_BYTES = 56 * 1024 * 1024


def dot(a, b, dims):
    return lax.dot_general(a, b, dims, preferred_element_type=F32)


def iota(shape, dim):
    return lax.broadcasted_iota(jnp.int32, shape, dim)


def ranks_and_probs(first, meta, span, count):
    sources, height, tokens = meta.shape
    kinds = height // 2
    wanted = ((first + span * iota((count, tokens), 0)) >> 1).astype(F32)
    named, weight = [], []
    for source in range(sources):
        entry = meta[source].astype(F32)
        hit = jnp.zeros((count, tokens), F32)
        prob = jnp.zeros((count, tokens), F32)
        for kind in range(kinds):
            same = entry[kind : kind + 1] == wanted
            hit = jnp.where(same, 1.0, hit)
            prob = jnp.where(same, entry[kinds + kind : kinds + kind + 1], prob)
        named.append(hit)
        weight.append(prob)
    named = jnp.concatenate(named)
    before = (iota((tokens, tokens), 0) < iota((tokens, tokens), 1)).astype(F32).astype(BF16)
    rank = jnp.dot(named.astype(BF16), before, preferred_element_type=F32)
    return jnp.where(named > 0, rank, -1.0), jnp.concatenate(weight)


def slot_matrix(rank):
    count, tokens = rank.shape
    wide = jnp.broadcast_to(rank[:, None, :], (count, MOST, tokens)).reshape(count * MOST, tokens)
    place = (iota((count * MOST, tokens), 0) & (MOST - 1)).astype(F32)
    return jnp.where(wide == place, 1.0, 0.0).astype(BF16)


def gather_rows(step, rank, pieces, rows_scr):
    count = rows_scr.shape[0]
    near, far = pieces
    half = near.shape[1]
    sources = near.shape[0]
    for source in range(sources):
        pick = slot_matrix(rank[source * count : (source + 1) * count])
        both = jnp.concatenate([near[source], far[source]], axis=0)
        rows = jnp.dot(pick, both, preferred_element_type=F32).astype(BF16)
        start = pl.multiple_of((step * sources + source) * MOST, MOST)
        rows_scr[:, pl.ds(start, MOST), :] = rows.reshape(count, MOST, rows.shape[1])
    del half


def first_kernel(steps, span, first_ref, meta_ref, near_ref, far_ref, wg_ref, wu_ref, rows_ref, gate_ref, up_ref,
                 rows_scr):
    step = pl.program_id(0)
    count = rows_scr.shape[0]

    @pl.when(step < steps)
    def _():
        rank, _ = ranks_and_probs(first_ref[0], meta_ref[...], span, count)
        gather_rows(step, rank, (near_ref, far_ref), rows_scr)

    @pl.when(step >= steps)
    def _():
        rows = rows_scr[step - steps]
        rows_ref[0] = rows
        gate_ref[0] = dot(wg_ref[0], rows, LAST)
        up_ref[0] = dot(wu_ref[0], rows, LAST)


def second_kernel(steps, span, first_ref, meta_ref, near_ref, far_ref, wg_ref, wu_ref, wd_ref, gate_ref, up_ref,
                  rows_ref, dgate_ref, dup_ref, gated_ref, prob_ref, own_ref, other_ref,
                  rows_scr, rank_scr, weight_scr, input_scr):
    step = pl.program_id(0)
    count, slots, features = rows_scr.shape
    sources = near_ref.shape[0]
    all_sources = slots // MOST
    tokens = rank_scr.shape[1]
    span_rows = sources * count

    @pl.when(step < steps)
    def _():
        rank, weight = ranks_and_probs(first_ref[0], meta_ref[...], span, count)
        start = step * span_rows
        if span_rows % 8 == 0:
            start = pl.multiple_of(start, 8)
        rank_scr[pl.ds(start, span_rows)] = rank
        weight_scr[pl.ds(start, span_rows)] = weight
        gather_rows(step, rank, (near_ref, far_ref), rows_scr)

    @pl.when((step >= steps) & (step < steps + count))
    def _():
        expert = step - steps
        total = all_sources * count
        row, lane = iota((total, slots), 0), iota((total, slots), 1)
        spread = jnp.where(row == (lane // MOST) * count + expert, 1.0, 0.0).astype(BF16)
        place = (iota((tokens, slots), 1) & (MOST - 1)).astype(F32)
        holds = dot(rank_scr[...].astype(BF16), spread, LEAD) == place
        weight = dot(weight_scr[...].astype(BF16), spread, LEAD)
        scale = jnp.sum(jnp.where(holds, weight, 0.0), axis=0, keepdims=True)
        rows = rows_scr[expert]
        rows_ref[0] = rows
        raw = dot(wd_ref[0], rows, LAST)
        gate, up = gate_ref[0], up_ref[0]
        sigmoid = 1.0 / (1.0 + jnp.exp(-gate))
        active = gate * sigmoid
        hidden = active * up
        gated_ref[0] = (scale * hidden).astype(BF16)
        prob = jnp.sum(hidden * raw, axis=0, keepdims=True)
        scaled = scale * raw
        dgate = (scaled * up * sigmoid * (1.0 + gate * (1.0 - sigmoid))).astype(BF16)
        dup = (scaled * active).astype(BF16)
        dgate_ref[0] = dgate
        dup_ref[0] = dup
        input_scr[expert] = (dot(dgate, wg_ref[0], LEAD) + dot(dup, wu_ref[0], LEAD)).astype(BF16)
        block = jnp.where(
            iota((all_sources, slots), 0) == iota((all_sources, slots), 1) // MOST, 1.0, 0.0
        ).astype(BF16)
        prob_ref[0] = dot(block, jnp.where(holds, prob, 0.0).astype(BF16), LAST)

    @pl.when(step >= steps + count)
    def _():
        chunk = step - steps - count
        half = own_ref.shape[1]
        for source in range(sources):
            number = chunk * sources + source
            start = number * count
            if count % 8 == 0:
                start = pl.multiple_of(start, 8)
            pick = slot_matrix(rank_scr[pl.ds(start, count)])
            rows = input_scr[:, pl.ds(pl.multiple_of(number * MOST, MOST), MOST), :].reshape(count * MOST, features)
            part = dot(pick, rows, LEAD).astype(BF16)
            own_ref[source] = part[:half]
            other_ref[source] = part[half:]


def third_kernel(x_ref, dy_ref, dgate_ref, dup_ref, gated_ref, gg_ref, gu_ref, gd_ref):
    x, dy = x_ref[0], dy_ref[0]
    gg_ref[0] = jnp.dot(dgate_ref[0], x, preferred_element_type=F32).astype(BF16)
    gu_ref[0] = jnp.dot(dup_ref[0], x, preferred_element_type=F32).astype(BF16)
    gd_ref[0] = jnp.dot(gated_ref[0], dy, preferred_element_type=F32).astype(BF16)


def shift(array, axes, sizes, by):
    pairs = []
    flat = 1
    for size in sizes:
        flat *= size
    for index in range(flat):
        rest, place = index, []
        for size in reversed(sizes):
            place.insert(0, rest % size)
            rest //= size
        to = 0
        for size, at, move in zip(sizes, place, by):
            to = to * size + (at + move) % size
        pairs.append((index, to))
    return lax.ppermute(array, axes if len(axes) > 1 else axes[0], pairs)


def per_device(tokens, cotangent, probs, experts, w_gate, w_up, w_down):
    rows, features = tokens.shape
    top = experts.shape[1]
    zs, xs = lax.axis_size("expert"), lax.axis_size("blk")
    cores = lax.axis_size("tensor")
    positions = zs * xs
    half = rows // cores
    halves, _, quarter = w_gate.shape
    span = 2 if halves % 2 == 0 else 1
    count = halves // span
    hidden = span * quarter
    slots = positions * MOST
    core = lax.axis_index("tensor")
    position = lax.axis_index("expert") * xs + lax.axis_index("blk")
    kinds = -(-top // 8) * 8

    def swap(array):
        return lax.ppermute(array, "tensor", [(i, (i + 1) % cores) for i in range(cores)])

    def own_first(array):
        return jnp.roll(array, -core * half, axis=-1)

    experts_t = own_first(experts.T)
    probs_t = own_first(probs.T)
    meta_own = jnp.concatenate(
        [
            jnp.pad(experts_t.astype(BF16), ((0, kinds - top), (0, 0)), constant_values=-1.0),
            jnp.pad(probs_t, ((0, kinds - top), (0, 0))),
        ]
    )
    order = [(d, c) for c in range(xs) for d in range(zs)]

    def to_all(array):
        return [
            array if (d, c) == (0, 0) else shift(array, ("expert", "blk"), (zs, xs), (d, c)) for d, c in order
        ]

    def gather(array):
        own = lax.dynamic_slice_in_dim(array, core * half, half, 0)
        line = [own] + [shift(own, ("expert",), (zs,), (d,)) for d in range(1, zs)]
        blocks = list(line)
        for c in range(1, xs):
            blocks += [shift(block, ("blk",), (xs,), (c,)) for block in line]
        near = jnp.stack(blocks)
        return near, swap(near)

    meta = jnp.stack(to_all(meta_own))
    near_x, far_x = gather(tokens)
    near_dy, far_dy = gather(cotangent)

    wg = jnp.swapaxes(w_gate, 1, 2).reshape(count, hidden, features)
    wu = jnp.swapaxes(w_up, 1, 2).reshape(count, hidden, features)
    wd = w_down.reshape(count, hidden, features)
    first = (position * halves).astype(jnp.int32).reshape(1)

    per_step = min(positions, 8)
    steps = positions // per_step
    last = lambda i, n: jnp.minimum(i, n - 1)
    later = lambda i, n: jnp.clip(i - steps, 0, n - 1)
    scalar = pl.BlockSpec(memory_space=pltpu.SMEM)
    meta_spec = pl.BlockSpec((per_step, 2 * kinds, rows), lambda i: (last(i, steps), 0, 0))
    piece_spec = pl.BlockSpec((per_step, half, features), lambda i: (last(i, steps), 0, 0))
    weight_spec = pl.BlockSpec((1, hidden, features), lambda i: (later(i, count), 0, 0))
    rows_spec = pl.BlockSpec((1, slots, features), lambda i: (later(i, count), 0, 0))
    hidden_spec = pl.BlockSpec((1, hidden, slots), lambda i: (later(i, count), 0, 0))
    params = pltpu.CompilerParams(vmem_limit_bytes=VMEM_BYTES, dimension_semantics=("arbitrary",))
    flops = 2 * count * hidden * slots * features

    rows_x, gate, up = pl.pallas_call(
        functools.partial(first_kernel, steps, span),
        grid=(steps + count,),
        in_specs=[scalar, meta_spec, piece_spec, piece_spec, weight_spec, weight_spec],
        out_specs=[rows_spec, hidden_spec, hidden_spec],
        out_shape=[
            jax.ShapeDtypeStruct((count, slots, features), BF16),
            jax.ShapeDtypeStruct((count, hidden, slots), F32),
            jax.ShapeDtypeStruct((count, hidden, slots), F32),
        ],
        scratch_shapes=[pltpu.VMEM((count, slots, features), BF16)],
        compiler_params=params,
        cost_estimate=pl.CostEstimate(flops=2 * flops, bytes_accessed=20_000_000, transcendentals=0),
        name="forward",
    )(first, meta, near_x, far_x, wg, wu)

    out_piece = pl.BlockSpec((per_step, half, features), lambda i: (jnp.clip(i - steps - count, 0, steps - 1), 0, 0))
    rows_dy, dgate, dup, gated, prob, own, other = pl.pallas_call(
        functools.partial(second_kernel, steps, span),
        grid=(steps + count + steps,),
        in_specs=[scalar, meta_spec, piece_spec, piece_spec, weight_spec, weight_spec, weight_spec, hidden_spec,
                  hidden_spec],
        out_specs=[
            rows_spec, hidden_spec, hidden_spec, hidden_spec,
            pl.BlockSpec((1, positions, rows), lambda i: (later(i, count), 0, 0)),
            out_piece, out_piece,
        ],
        out_shape=[
            jax.ShapeDtypeStruct((count, slots, features), BF16),
            jax.ShapeDtypeStruct((count, hidden, slots), BF16),
            jax.ShapeDtypeStruct((count, hidden, slots), BF16),
            jax.ShapeDtypeStruct((count, hidden, slots), BF16),
            jax.ShapeDtypeStruct((count, positions, rows), F32),
            jax.ShapeDtypeStruct((positions, half, features), BF16),
            jax.ShapeDtypeStruct((positions, half, features), BF16),
        ],
        scratch_shapes=[
            pltpu.VMEM((count, slots, features), BF16),
            pltpu.VMEM((positions * count, rows), F32),
            pltpu.VMEM((positions * count, rows), F32),
            pltpu.VMEM((count, slots, features), BF16),
        ],
        compiler_params=params,
        cost_estimate=pl.CostEstimate(flops=3 * flops, bytes_accessed=30_000_000, transcendentals=0),
        name="backward",
    )(first, meta, near_dy, far_dy, wg, wu, wd, gate, up)

    w_spec = pl.BlockSpec((1, hidden, features), lambda i: (i, 0, 0))
    r_spec = pl.BlockSpec((1, slots, features), lambda i: (i, 0, 0))
    h_spec = pl.BlockSpec((1, hidden, slots), lambda i: (i, 0, 0))
    grad_gate, grad_up, grad_down = pl.pallas_call(
        third_kernel,
        grid=(count,),
        in_specs=[r_spec, r_spec, h_spec, h_spec, h_spec],
        out_specs=[w_spec] * 3,
        out_shape=[jax.ShapeDtypeStruct((count, hidden, features), BF16)] * 3,
        compiler_params=params,
        cost_estimate=pl.CostEstimate(flops=3 * flops, bytes_accessed=24_000_000, transcendentals=0),
        name="weights",
    )(rows_x, rows_dy, dgate, dup, gated)

    chip = (own.astype(F32) + swap(other).astype(F32)).astype(BF16).reshape(xs, zs, half, features)
    line = chip[0].astype(F32)
    for c in range(1, xs):
        line = line + shift(chip[c], ("blk",), (xs,), (-c,)).astype(F32)
    line = line.astype(BF16)
    total = line[0].astype(F32)
    for d in range(1, zs):
        total = total + shift(line[d], ("expert",), (zs,), (-d,)).astype(F32)
    mine = total.astype(BF16)
    theirs = swap(mine)
    grad_tokens = jnp.where(core == 0, jnp.concatenate([mine, theirs]), jnp.concatenate([theirs, mine]))

    found = jnp.zeros((top, rows), F32)
    z_at, x_at = lax.axis_index("expert"), lax.axis_index("blk")
    for number, (d, c) in enumerate(order):
        part = prob[:, number]
        if number:
            part = shift(part, ("expert", "blk"), (zs, xs), (-d, -c))
        holder = ((z_at + d) % zs) * xs + (x_at + c) % xs
        ids = (holder * halves + span * jnp.arange(count, dtype=jnp.int32)) >> 1
        found = found + jnp.sum(
            jnp.where(experts_t[:, None, :] == ids[None, :, None], part[None], 0.0), axis=1
        )
    found = jnp.roll(found, core * half, axis=-1)
    grad_probs = (found + swap(found)).T
    shape = (halves, quarter, features)
    return (
        grad_tokens,
        grad_probs,
        jnp.swapaxes(grad_gate.reshape(shape), 1, 2),
        jnp.swapaxes(grad_up.reshape(shape), 1, 2),
        grad_down.reshape(shape),
    )


def solution(mesh):
    return jax.shard_map(
        per_device,
        mesh=mesh,
        in_specs=(
            P(("groups", "expert", "blk"), None),
            P(("groups", "expert", "blk"), None),
            P(("groups", "expert", "blk"), None),
            P(("groups", "expert", "blk"), None),
            P(("expert", "blk"), None, "tensor"),
            P(("expert", "blk"), None, "tensor"),
            P(("expert", "blk"), "tensor", None),
        ),
        out_specs=(
            P(("groups", "expert", "blk"), None),
            P(("groups", "expert", "blk"), None),
            P(("groups", "expert", "blk"), None, "tensor"),
            P(("groups", "expert", "blk"), None, "tensor"),
            P(("groups", "expert", "blk"), "tensor", None),
        ),
        check_vma=False,
    )
```

time: 756 us -> 183 us (0.24)
  local copies, waits for them, and re-layouts: 306 us -> 4.11 us
  matrix products: 213 us -> 0 us
  loops' own time: 63.6 us -> 0 us
  Pallas kernels: 0 us -> 41.2 us
  other arithmetic: 24.6 us -> 5.13 us
  waiting for transfers between devices: 108 us -> 94.2 us
  starting transfers between devices: 27.5 us -> 36 us
    dot_general x128 -> x0, matrix products: 213 us -> none  [the longest x16 33.1 us: group_weights(): lax.dot_general(x_win, up_win, lead_dims, preferred_element_type=jnp.floa...]
    gather x10 -> x0, local copies, waits for them, and re-layouts: 150 us -> none  [the longest x1 25.1 us: per_device(): jnp.concatenate([got_prob.reshape(-1), jnp.zeros((1,), jnp.bfloat16)])]
    all_to_all x5 -> x0, waiting for transfers between devices: 108 us -> none  [the longest x1 83.1 us: per_device(): lax.all_to_all(send_dy, ('expert', 'blk'), split_axis=0, concat_axis=0, t...]
    ppermute x0 -> x37, waiting for transfers between devices: none -> 94.2 us  [the longest x32 90.8 us: shift(): return lax.ppermute(array, axes if len(axes) > 1 else axes[0], pairs)]
    another operation x2 -> x0, loops' own time: 63.6 us -> none  [the longest x1 41.9 us: per_device(): lax.fori_loop(0, block_ends[-1], run_block, initial)]
    dynamic_slice x128 -> x0, local copies, waits for them, and re-layouts: 53.3 us -> none  [the longest x32 17.4 us: group_weights(): lax.dynamic_slice_in_dim(gated_rows, start, window, 0)]
    dynamic_update_slice x32 -> x0, local copies, waits for them, and re-layouts: 47.7 us -> none  [the longest x16 43.9 us: run_block(): lax.dynamic_update_slice_in_dim(input_rows, input_part, row_start, 0)]
    pallas_call x0 -> x3, Pallas kernels: none -> 41.2 us  [the longest x1 17.9 us: per_device(): pl.pallas_call(functools.partial(second_kernel, steps, span), grid=(steps...]
  transfers between devices with their start and end apart: 5 -> 37, of which waited for: 2 -> 22; matrix products, arithmetic and copies ran while one was open for 34% -> 2% of each run, Pallas kernels for 0% -> 13%
where the time goes in v1:
time: 183 us; the launch traced here: 182 us
  waiting for transfers between devices  94.2 us (51%)
  Pallas kernels  41.2 us (23%)
  starting transfers between devices  36 us (20%)
  other arithmetic  5.13 us (3%)
  local copies, waits for them, and re-layouts  4.11 us (2%)
    ppermute x32, waiting for transfers between devices, shift(): return lax.ppermute(array, axes if len(axes) > 1 else axes[0], pairs)  90.8 us
    ppermute x32, starting transfers between devices, shift(): return lax.ppermute(array, axes if len(axes) > 1 else axes[0], pairs)  35.2 us
    pallas_call x1, Pallas kernels, per_device(): pl.pallas_call(functools.partial(second_kernel, steps, span), grid=(steps...  17.9 us
    pallas_call x1, Pallas kernels, per_device(): pl.pallas_call(functools.partial(first_kernel, steps, span), grid=(steps...  12.1 us
    pallas_call x1, Pallas kernels, per_device(): pl.pallas_call(third_kernel, grid=(count,), in_specs=[r_spec, r_spec, h_s...  11.2 us
    unnamed x32, local copies, waits for them, and re-layouts  3.99 us
  transfers between devices with their start and end apart: 37, of which 22 were waited for; matrix products, arithmetic and copies ran while one was open for 2% of the time, Pallas kernels for 13%

profile of v1, /device:TPU:0, one launch (start us, length us, event | category | flops | bytes accessed | tf_op | source)
XLA Modules:
  0.0 181.6 jit_solution(7342922334137068720)
XLA Ops:
  0.7 0.8 fusion.8
  1.4 0.8 fusion.9
  2.2 5.0 %collective-permute-start.5 = (bf16[16,128]{1,0:T(8,128)(2,1)S(1)}, bf16[16,128]{1,0:T(8,128)(2,1)S(1)}, u32[]{:S(2)}, u32[]{:S(2)}) collective-permute-start(bf16[16,128]{1,0:T(8,128)(2,1)S(1)} %fusion.5), channel_id=1, source_target_pairs={{0,10},{2,8},{4,14},{6,12},{8,2},{10,0},{12,6},{14,4},{1,11},{3,9}... | collective-permute-start | bytes 12296 | tf_op jit(solution)/shard_map/ppermute | solution.py:172
  7.2 1.5 collective-permute-start.4
  8.8 1.5 collective-permute-start.3
  10.3 2.2 %collective-permute-start.2 = (bf16[16,128]{1,0:T(8,128)(2,1)S(1)}, bf16[16,128]{1,0:T(8,128)(2,1)S(1)}, u32[]{:S(2)}, u32[]{:S(2)}) collective-permute-start(bf16[16,128]{1,0:T(8,128)(2,1)S(1)} %fusion.5), channel_id=1, source_target_pairs={{0,12},{2,14},{4,0},{6,2},{8,4},{10,6},{12,8},{14,10},{1,13},{3,15... | collective-permute-start | bytes 12296 | tf_op jit(solution)/shard_map/ppermute | solution.py:172
  12.5 0.9 bitcast_dynamic-update-slice_fusion.7
  13.5 0.9 bitcast_dynamic-update-slice_fusion.15
  14.4 3.5 %collective-permute-done = bf16[16,128]{1,0:T(8,128)(2,1)S(1)} collective-permute-done((bf16[16,128]{1,0:T(8,128)(2,1)S(1)}, bf16[16,128]{1,0:T(8,128)(2,1)S(1)}, u32[]{:S(2)}, u32[]{:S(2)}) %collective-permute-start) | collective-permute-done | bytes 4128 | tf_op jit(solution)/shard_map/ppermute | solution.py:172
  17.9 4.5 %collective-permute-done.1 = bf16[16,128]{1,0:T(8,128)(2,1)S(1)} collective-permute-done((bf16[16,128]{1,0:T(8,128)(2,1)S(1)}, bf16[16,128]{1,0:T(8,128)(2,1)S(1)}, u32[]{:S(2)}, u32[]{:S(2)}) %collective-permute-start.1) | collective-permute-done | bytes 4128 | tf_op jit(solution)/shard_map/ppermute | solution.py:172
  22.4 6.9 %collective-permute-done.15 = bf16[64,1024]{1,0:T(8,128)(2,1)S(1)} collective-permute-done((bf16[64,1024]{1,0:T(8,128)(2,1)S(1)}, bf16[64,1024]{1,0:T(8,128)(2,1)S(1)}, u32[]{:S(2)}, u32[]{:S(2)}) %collective-permute-start.15) | collective-permute-done | bytes 131104 | tf_op jit(solution)/shard_map/ppermute | solution.py:172
  29.3 6.1 %collective-permute-done.16 = bf16[64,1024]{1,0:T(8,128)(2,1)S(1)} collective-permute-done((bf16[64,1024]{1,0:T(8,128)(2,1)S(1)}, bf16[64,1024]{1,0:T(8,128)(2,1)S(1)}, u32[]{:S(2)}, u32[]{:S(2)}) %collective-permute-start.16) | collective-permute-done | bytes 131104 | tf_op jit(solution)/shard_map/ppermute | solution.py:172
  35.5 5.0 %collective-permute-done.17 = bf16[64,1024]{1,0:T(8,128)(2,1)S(1)} collective-permute-done((bf16[64,1024]{1,0:T(8,128)(2,1)S(1)}, bf16[64,1024]{1,0:T(8,128)(2,1)S(1)}, u32[]{:S(2)}, u32[]{:S(2)}) %collective-permute-start.17) | collective-permute-done | bytes 131104 | tf_op jit(solution)/shard_map/ppermute | solution.py:172
  40.4 0.5 collective-permute-start.18
  41.0 4.4 %collective-permute-done.18 = bf16[64,1024]{1,0:T(8,128)(2,1)S(1)} collective-permute-done((bf16[64,1024]{1,0:T(8,128)(2,1)S(1)}, bf16[64,1024]{1,0:T(8,128)(2,1)S(1)}, u32[]{:S(2)}, u32[]{:S(2)}) %collective-permute-start.18) | collective-permute-done | bytes 131104 | tf_op jit(solution)/shard_map/ppermute | solution.py:172
  45.4 6.8 %collective-permute-done.7 = bf16[64,1024]{1,0:T(8,128)(2,1)S(1)} collective-permute-done((bf16[64,1024]{1,0:T(8,128)(2,1)S(1)}, bf16[64,1024]{1,0:T(8,128)(2,1)S(1)}, u32[]{:S(2)}, u32[]{:S(2)}) %collective-permute-start.7) | collective-permute-done | bytes 131104 | tf_op jit(solution)/shard_map/ppermute | solution.py:172
  52.2 5.8 %collective-permute-done.8 = bf16[64,1024]{1,0:T(8,128)(2,1)S(1)} collective-permute-done((bf16[64,1024]{1,0:T(8,128)(2,1)S(1)}, bf16[64,1024]{1,0:T(8,128)(2,1)S(1)}, u32[]{:S(2)}, u32[]{:S(2)}) %collective-permute-start.8) | collective-permute-done | bytes 131104 | tf_op jit(solution)/shard_map/ppermute | solution.py:172
  58.0 1.4 collective-permute-start.9
  59.4 3.6 %collective-permute-done.9 = bf16[64,1024]{1,0:T(8,128)(2,1)S(1)} collective-permute-done((bf16[64,1024]{1,0:T(8,128)(2,1)S(1)}, bf16[64,1024]{1,0:T(8,128)(2,1)S(1)}, u32[]{:S(2)}, u32[]{:S(2)}) %collective-permute-start.9) | collective-permute-done | bytes 131104 | tf_op jit(solution)/shard_map/ppermute | solution.py:172
  63.0 0.5 collective-permute-start.10
  63.5 4.4 %collective-permute-done.10 = bf16[64,1024]{1,0:T(8,128)(2,1)S(1)} collective-permute-done((bf16[64,1024]{1,0:T(8,128)(2,1)S(1)}, bf16[64,1024]{1,0:T(8,128)(2,1)S(1)}, u32[]{:S(2)}, u32[]{:S(2)}) %collective-permute-start.10) | collective-permute-done | bytes 131104 | tf_op jit(solution)/shard_map/ppermute | solution.py:172
  68.0 0.5 collective-permute-start.19
  68.5 5.0 %collective-permute-done.19 = bf16[64,1024]{1,0:T(8,128)(2,1)S(1)} collective-permute-done((bf16[64,1024]{1,0:T(8,128)(2,1)S(1)}, bf16[64,1024]{1,0:T(8,128)(2,1)S(1)}, u32[]{:S(2)}, u32[]{:S(2)}) %collective-permute-start.19) | collective-permute-done | bytes 131104 | tf_op jit(solution)/shard_map/ppermute | solution.py:172
  73.5 0.5 collective-permute-start.20
  74.0 5.5 %collective-permute-done.20 = bf16[64,1024]{1,0:T(8,128)(2,1)S(1)} collective-permute-done((bf16[64,1024]{1,0:T(8,128)(2,1)S(1)}, bf16[64,1024]{1,0:T(8,128)(2,1)S(1)}, u32[]{:S(2)}, u32[]{:S(2)}) %collective-permute-start.20) | collective-permute-done | bytes 131104 | tf_op jit(solution)/shard_map/ppermute | solution.py:172
  79.6 0.5 collective-permute-start.21
  80.1 4.7 %collective-permute-done.21 = bf16[64,1024]{1,0:T(8,128)(2,1)S(1)} collective-permute-done((bf16[64,1024]{1,0:T(8,128)(2,1)S(1)}, bf16[64,1024]{1,0:T(8,128)(2,1)S(1)}, u32[]{:S(2)}, u32[]{:S(2)}) %collective-permute-start.21) | collective-permute-done | bytes 131104 | tf_op jit(solution)/shard_map/ppermute | solution.py:172
  84.8 0.5 collective-permute-start.11
  85.3 4.4 %collective-permute-done.11 = bf16[64,1024]{1,0:T(8,128)(2,1)S(1)} collective-permute-done((bf16[64,1024]{1,0:T(8,128)(2,1)S(1)}, bf16[64,1024]{1,0:T(8,128)(2,1)S(1)}, u32[]{:S(2)}, u32[]{:S(2)}) %collective-permute-start.11) | collective-permute-done | bytes 131104 | tf_op jit(solution)/shard_map/ppermute | solution.py:172
  89.7 0.5 collective-permute-start.12
  90.3 4.4 %collective-permute-done.12 = bf16[64,1024]{1,0:T(8,128)(2,1)S(1)} collective-permute-done((bf16[64,1024]{1,0:T(8,128)(2,1)S(1)}, bf16[64,1024]{1,0:T(8,128)(2,1)S(1)}, u32[]{:S(2)}, u32[]{:S(2)}) %collective-permute-start.12) | collective-permute-done | bytes 131104 | tf_op jit(solution)/shard_map/ppermute | solution.py:172
  94.7 0.5 collective-permute-start.13
  95.2 4.4 %collective-permute-done.13 = bf16[64,1024]{1,0:T(8,128)(2,1)S(1)} collective-permute-done((bf16[64,1024]{1,0:T(8,128)(2,1)S(1)}, bf16[64,1024]{1,0:T(8,128)(2,1)S(1)}, u32[]{:S(2)}, u32[]{:S(2)}) %collective-permute-start.13) | collective-permute-done | bytes 131104 | tf_op jit(solution)/shard_map/ppermute | solution.py:172
  99.7 0.6 collective-permute-start.14
  100.3 2.9 %collective-permute-start.6 = (bf16[16,128]{1,0:T(8,128)(2,1)S(1)}, bf16[16,128]{1,0:T(8,128)(2,1)S(1)}, u32[]{:S(2)}, u32[]{:S(2)}) collective-permute-start(bf16[16,128]{1,0:T(8,128)(2,1)S(1)} %fusion.5), channel_id=1, source_target_pairs={{0,14},{2,12},{4,2},{6,0},{8,6},{10,4},{12,10},{14,8},{1,15},{3,13... | collective-permute-start | bytes 12296 | tf_op jit(solution)/shard_map/ppermute | solution.py:172
  103.2 1.5 collective-permute-done.6
  104.8 0.6 copy-done.4
  105.4 0.4 copy-done.3
  105.8 12.1 %forward.1 = (bf16[8,128,1024]{2,1,0:T(8,128)(2,1)}, f32[8,352,128]{2,1,0:T(8,128)}, f32[8,352,128]{2,1,0:T(8,128)}) custom-call(s32[1]{0:T(128)} %bitcast.first_ref, bf16[8,16,128]{2,1,0:T(8,128)(2,1)} %copy-done.4, bf16[8,64,1024]{2,1,0:T(8,128)(2,1)} %copy-done.1, bf16[8,64,1024]{2,1,0:T(8,128)(2,1)} %copy-done.3, bf16[8,352,1024]{2,1,0:T(8,128)(2,1)} %bitcast.86, ...), custom_call_target="tpu_custom_call" | custom-call | flops 1476395008 | bytes 20000000 | tf_op jit(solution)/shard_map/forward/pallas_call | solution.py:243
  117.9 1.0 copy-done.2
  118.9 17.9 %backward.1 = (bf16[8,128,1024]{2,1,0:T(8,128)(2,1)}, bf16[8,352,128]{2,1,0:T(8,128)(2,1)}, bf16[8,352,128]{2,1,0:T(8,128)(2,1)}, bf16[8,352,128]{2,1,0:T(8,128)...) custom-call(s32[1]{0:T(128)} %bitcast.first_ref, ...), custom_call_target="tpu_custom_call" | custom-call | flops 2214592512 | bytes 30000000 | tf_op jit(solution)/shard_map/backward/pallas_call | solution.py:260
  137.0 2.8 %collective-permute-done.23 = bf16[8,64,1024]{2,1,0:T(8,128)(2,1)S(1)} collective-permute-done((bf16[8,64,1024]{2,1,0:T(8,128)(2,1)}, bf16[8,64,1024]{2,1,0:T(8,128)(2,1)S(1)}, u32[]{:S(2)}, u32[]{:S(2)}) %collective-permute-start.23) | collective-permute-done | bytes 1048608 | tf_op jit(solution)/shard_map/ppermute | solution.py:192
  139.8 1.6 add_convert_fusion
  141.4 1.3 collective-permute-start.24
  142.8 5.5 %collective-permute-start.34 = (f32[8,128]{1,0:T(8,128)S(1)}, f32[8,128]{1,0:T(8,128)S(1)}, u32[]{:S(2)}, u32[]{:S(2)}) collective-permute-start(f32[8,128]{1,0:T(8,128)S(1)} %bitcast.97), channel_id=1, source_target_pairs={{0,10},{2,8},{4,14},{6,12},{8,2},{10,0},{12,6},{14,4},{1,11},{3,9}... | collective-permute-start | bytes 12296 | tf_op jit(solution)/shard_map/ppermute | solution.py:172
  148.3 1.5 collective-permute-start.32
  149.9 2.0 %collective-permute-start.31 = (f32[8,128]{1,0:T(8,128)S(1)}, f32[8,128]{1,0:T(8,128)S(1)}, u32[]{:S(2)}, u32[]{:S(2)}) collective-permute-start(f32[8,128]{1,0:T(8,128)S(1)} %bitcast.94), channel_id=1, source_target_pairs={{0,4},{2,6},{4,8},{6,10},{8,12},{10,14},{12,0},{14,2},{1,5},{3,7},... | collective-permute-start | bytes 12296 | tf_op jit(solution)/shard_map/ppermute | solution.py:172
  151.8 2.0 %collective-permute-start.30 = (f32[8,128]{1,0:T(8,128)S(1)}, f32[8,128]{1,0:T(8,128)S(1)}, u32[]{:S(2)}, u32[]{:S(2)}) collective-permute-start(f32[8,128]{1,0:T(8,128)S(1)} %bitcast.93), channel_id=1, source_target_pairs={{0,8},{2,10},{4,12},{6,14},{8,0},{10,2},{12,4},{14,6},{1,9},{3,11}... | collective-permute-start | bytes 12296 | tf_op jit(solution)/shard_map/ppermute | solution.py:172
  153.9 0.9 collective-permute-start.29
  154.8 11.2 %weights.1 = (bf16[8,352,1024]{2,1,0:T(8,128)(2,1)}, bf16[8,352,1024]{2,1,0:T(8,128)(2,1)}, bf16[8,352,1024]{2,1,0:T(8,128)(2,1)}) custom-call(bf16[8,128,1024]{2,1,0:T(8,128)(2,1)} %get-tuple-element.23.x_ref, bf16[8,128,1024]{2,1,0:T(8,128)(2,1)} %get-tuple-element.24.dy_ref, bf16[8,352,128]{2,1,0:T(8,128)(2,1)} %get-tuple-element.25.dgate_ref, ...), custom_call_target="tpu_custom_call" | custom-call | flops 2214592512 | bytes 24000000 | tf_op jit(solution)/shard_map/weights/pallas_call | solution.py:293
  166.0 0.1 select_reduce_fusion.6
  166.2 0.2 add_convert_fusion.1
  166.4 1.4 collective-permute-start.25
  167.8 0.6 collective-permute-start.27
  168.5 0.9 collective-permute-start.26
  169.4 0.1 fusion.6
  169.5 4.1 %collective-permute-done.25 = bf16[64,1024]{1,0:T(8,128)(2,1)S(1)} collective-permute-done((bf16[64,1024]{1,0:T(8,128)(2,1)S(1)}, bf16[64,1024]{1,0:T(8,128)(2,1)S(1)}, u32[]{:S(2)}, u32[]{:S(2)}) %collective-permute-start.25) | collective-permute-done | bytes 131104 | tf_op jit(solution)/shard_map/ppermute | solution.py:172
  173.6 1.9 %collective-permute-done.27 = bf16[64,1024]{1,0:T(8,128)(2,1)S(1)} collective-permute-done((bf16[64,1024]{1,0:T(8,128)(2,1)S(1)}, bf16[64,1024]{1,0:T(8,128)(2,1)S(1)}, u32[]{:S(2)}, u32[]{:S(2)}) %collective-permute-start.27) | collective-permute-done | bytes 131104 | tf_op jit(solution)/shard_map/ppermute | solution.py:172
  175.5 3.9 %collective-permute-done.26 = bf16[64,1024]{1,0:T(8,128)(2,1)S(1)} collective-permute-done((bf16[64,1024]{1,0:T(8,128)(2,1)S(1)}, bf16[64,1024]{1,0:T(8,128)(2,1)S(1)}, u32[]{:S(2)}, u32[]{:S(2)}) %collective-permute-start.26) | collective-permute-done | bytes 131104 | tf_op jit(solution)/shard_map/ppermute | solution.py:172
  179.4 0.1 fusion.2
  179.5 0.1 collective-permute-start.28
  179.5 0.7 add_bitcast_fusion
  180.2 0.6 collective-permute-done.28
  180.9 0.8 maximum_select_fusion
  (67 shorter events, 0.6 us)
Async XLA Ops:
  2.2 101.0 %collective-permute-start.5 = (bf16[16,128]{1,0:T(8,128)(2,1)S(1)}, bf16[16,128]{1,0:T(8,128)(2,1)S(1)}, u32[]{:S(2)}, u32[]{:S(2)}) collective-permute-start(bf16[16,128]{1,0:T(8,128)(2,1)S(1)} %fusion.5), channel_id=1, source_target_pairs={{0,10},{2,8},{4,14},{6,12},{8,2},{10,0},{12,6},{14,4},{1,11},{3,9}... | collective-permute-start | bytes 12296 | tf_op jit(solution)/shard_map/ppermute | solution.py:172
  7.2 96.0 %collective-permute-start.4 = (bf16[16,128]{1,0:T(8,128)(2,1)S(1)}, bf16[16,128]{1,0:T(8,128)(2,1)S(1)}, u32[]{:S(2)}, u32[]{:S(2)}) collective-permute-start(bf16[16,128]{1,0:T(8,128)(2,1)S(1)} %fusion.5), channel_id=1, source_target_pairs={{0,6},{2,4},{4,10},{6,8},{8,14},{10,12},{12,2},{14,0},{1,7},{3,5},... | collective-permute-start | bytes 12296 | tf_op jit(solution)/shard_map/ppermute | solution.py:172
  8.8 91.5 %collective-permute-start.3 = (bf16[16,128]{1,0:T(8,128)(2,1)S(1)}, bf16[16,128]{1,0:T(8,128)(2,1)S(1)}, u32[]{:S(2)}, u32[]{:S(2)}) collective-permute-start(bf16[16,128]{1,0:T(8,128)(2,1)S(1)} %fusion.5), channel_id=1, source_target_pairs={{0,2},{2,0},{4,6},{6,4},{8,10},{10,8},{12,14},{14,12},{1,3},{3,1},... | collective-permute-start | bytes 12296 | tf_op jit(solution)/shard_map/ppermute | solution.py:172
  10.3 89.4 %collective-permute-start.2 = (bf16[16,128]{1,0:T(8,128)(2,1)S(1)}, bf16[16,128]{1,0:T(8,128)(2,1)S(1)}, u32[]{:S(2)}, u32[]{:S(2)}) collective-permute-start(bf16[16,128]{1,0:T(8,128)(2,1)S(1)} %fusion.5), channel_id=1, source_target_pairs={{0,12},{2,14},{4,0},{6,2},{8,4},{10,6},{12,8},{14,10},{1,13},{3,15... | collective-permute-start | bytes 12296 | tf_op jit(solution)/shard_map/ppermute | solution.py:172
  12.5 5.4 %collective-permute-start = (bf16[16,128]{1,0:T(8,128)(2,1)S(1)}, bf16[16,128]{1,0:T(8,128)(2,1)S(1)}, u32[]{:S(2)}, u32[]{:S(2)}) collective-permute-start(bf16[16,128]{1,0:T(8,128)(2,1)S(1)} %fusion.5), channel_id=1, source_target_pairs={{0,4},{2,6},{4,8},{6,10},{8,12},{10,14},{12,0},{14,2},{1,5},{3,7},... | collective-permute-start | bytes 12296 | tf_op jit(solution)/shard_map/ppermute | solution.py:172
  17.9 4.5 %collective-permute-start.1 = (bf16[16,128]{1,0:T(8,128)(2,1)S(1)}, bf16[16,128]{1,0:T(8,128)(2,1)S(1)}, u32[]{:S(2)}, u32[]{:S(2)}) collective-permute-start(bf16[16,128]{1,0:T(8,128)(2,1)S(1)} %fusion.5), channel_id=1, source_target_pairs={{0,8},{2,10},{4,12},{6,14},{8,0},{10,2},{12,4},{14,6},{1,9},{3,11}... | collective-permute-start | bytes 12296 | tf_op jit(solution)/shard_map/ppermute | solution.py:172
  22.4 6.9 %collective-permute-start.15 = (bf16[64,1024]{1,0:T(8,128)(2,1)S(1)}, bf16[64,1024]{1,0:T(8,128)(2,1)S(1)}, u32[]{:S(2)}, u32[]{:S(2)}) collective-permute-start(bf16[64,1024]{1,0:T(8,128)(2,1)S(1)} %get-tuple-element.40), channel_id=1, source_target_pairs={{0,4},{4,8},{8,12},{12,0},{1,5},{5,9},{9,13},{13,1},{2,6},{6,10},{... | collective-permute-start | bytes 393224 | tf_op jit(solution)/shard_map/ppermute | solution.py:172
  29.3 6.1 %collective-permute-start.16 = (bf16[64,1024]{1,0:T(8,128)(2,1)S(1)}, bf16[64,1024]{1,0:T(8,128)(2,1)S(1)}, u32[]{:S(2)}, u32[]{:S(2)}) collective-permute-start(bf16[64,1024]{1,0:T(8,128)(2,1)S(1)} %get-tuple-element.40), channel_id=1, source_target_pairs={{0,8},{4,12},{8,0},{12,4},{1,9},{5,13},{9,1},{13,5},{2,10},{6,14},... | collective-permute-start | bytes 393224 | tf_op jit(solution)/shard_map/ppermute | solution.py:172
  35.4 5.0 %collective-permute-start.17 = (bf16[64,1024]{1,0:T(8,128)(2,1)S(1)}, bf16[64,1024]{1,0:T(8,128)(2,1)S(1)}, u32[]{:S(2)}, u32[]{:S(2)}) collective-permute-start(bf16[64,1024]{1,0:T(8,128)(2,1)S(1)} %get-tuple-element.40), channel_id=1, source_target_pairs={{0,12},{4,0},{8,4},{12,8},{1,13},{5,1},{9,5},{13,9},{2,14},{6,2},{... | collective-permute-start | bytes 393224 | tf_op jit(solution)/shard_map/ppermute | solution.py:172
  40.4 5.0 %collective-permute-start.18 = (bf16[64,1024]{1,0:T(8,128)(2,1)S(1)}, bf16[64,1024]{1,0:T(8,128)(2,1)S(1)}, u32[]{:S(2)}, u32[]{:S(2)}) collective-permute-start(bf16[64,1024]{1,0:T(8,128)(2,1)S(1)} %get-tuple-element.40), channel_id=1, source_target_pairs={{0,2},{2,0},{1,3},{3,1},{4,6},{6,4},{5,7},{7,5},{8,10},{10,8},{9,1... | collective-permute-start | bytes 393224 | tf_op jit(solution)/shard_map/ppermute | solution.py:172
  45.4 6.8 %collective-permute-start.7 = (bf16[64,1024]{1,0:T(8,128)(2,1)S(1)}, bf16[64,1024]{1,0:T(8,128)(2,1)S(1)}, u32[]{:S(2)}, u32[]{:S(2)}) collective-permute-start(bf16[64,1024]{1,0:T(8,128)(2,1)S(1)} %get-tuple-element.42), channel_id=1, source_target_pairs={{0,4},{4,8},{8,12},{12,0},{1,5},{5,9},{9,13},{13,1},{2,6},{6,10},{... | collective-permute-start | bytes 393224 | tf_op jit(solution)/shard_map/ppermute | solution.py:172
  52.2 5.9 %collective-permute-start.8 = (bf16[64,1024]{1,0:T(8,128)(2,1)S(1)}, bf16[64,1024]{1,0:T(8,128)(2,1)S(1)}, u32[]{:S(2)}, u32[]{:S(2)}) collective-permute-start(bf16[64,1024]{1,0:T(8,128)(2,1)S(1)} %get-tuple-element.42), channel_id=1, source_target_pairs={{0,8},{4,12},{8,0},{12,4},{1,9},{5,13},{9,1},{13,5},{2,10},{6,14},... | collective-permute-start | bytes 393224 | tf_op jit(solution)/shard_map/ppermute | solution.py:172
  58.0 5.0 %collective-permute-start.9 = (bf16[64,1024]{1,0:T(8,128)(2,1)S(1)}, bf16[64,1024]{1,0:T(8,128)(2,1)S(1)}, u32[]{:S(2)}, u32[]{:S(2)}) collective-permute-start(bf16[64,1024]{1,0:T(8,128)(2,1)S(1)} %get-tuple-element.42), channel_id=1, source_target_pairs={{0,12},{4,0},{8,4},{12,8},{1,13},{5,1},{9,5},{13,9},{2,14},{6,2},{... | collective-permute-start | bytes 393224 | tf_op jit(solution)/shard_map/ppermute | solution.py:172
  63.0 5.0 %collective-permute-start.10 = (bf16[64,1024]{1,0:T(8,128)(2,1)S(1)}, bf16[64,1024]{1,0:T(8,128)(2,1)S(1)}, u32[]{:S(2)}, u32[]{:S(2)}) collective-permute-start(bf16[64,1024]{1,0:T(8,128)(2,1)S(1)} %get-tuple-element.42), channel_id=1, source_target_pairs={{0,2},{2,0},{1,3},{3,1},{4,6},{6,4},{5,7},{7,5},{8,10},{10,8},{9,1... | collective-permute-start | bytes 393224 | tf_op jit(solution)/shard_map/ppermute | solution.py:172
  68.0 5.5 %collective-permute-start.19 = (bf16[64,1024]{1,0:T(8,128)(2,1)S(1)}, bf16[64,1024]{1,0:T(8,128)(2,1)S(1)}, u32[]{:S(2)}, u32[]{:S(2)}) collective-permute-start(bf16[64,1024]{1,0:T(8,128)(2,1)S(1)} %collective-permute-done.15), channel_id=1, source_target_pairs={{0,2},{2,0},{1,3},{3,1},{4,6},{6,4},{5,7},{7,5},{8,10},{10,8},{9,1... | collective-permute-start | bytes 393224 | tf_op jit(solution)/shard_map/ppermute | solution.py:172
  73.5 6.1 %collective-permute-start.20 = (bf16[64,1024]{1,0:T(8,128)(2,1)S(1)}, bf16[64,1024]{1,0:T(8,128)(2,1)S(1)}, u32[]{:S(2)}, u32[]{:S(2)}) collective-permute-start(bf16[64,1024]{1,0:T(8,128)(2,1)S(1)} %collective-permute-done.16), channel_id=1, source_target_pairs={{0,2},{2,0},{1,3},{3,1},{4,6},{6,4},{5,7},{7,5},{8,10},{10,8},{9,1... | collective-permute-start | bytes 393224 | tf_op jit(solution)/shard_map/ppermute | solution.py:172
  79.6 5.2 %collective-permute-start.21 = (bf16[64,1024]{1,0:T(8,128)(2,1)S(1)}, bf16[64,1024]{1,0:T(8,128)(2,1)S(1)}, u32[]{:S(2)}, u32[]{:S(2)}) collective-permute-start(bf16[64,1024]{1,0:T(8,128)(2,1)S(1)} %collective-permute-done.17), channel_id=1, source_target_pairs={{0,2},{2,0},{1,3},{3,1},{4,6},{6,4},{5,7},{7,5},{8,10},{10,8},{9,1... | collective-permute-start | bytes 393224 | tf_op jit(solution)/shard_map/ppermute | solution.py:172
  84.8 5.0 %collective-permute-start.11 = (bf16[64,1024]{1,0:T(8,128)(2,1)S(1)}, bf16[64,1024]{1,0:T(8,128)(2,1)S(1)}, u32[]{:S(2)}, u32[]{:S(2)}) collective-permute-start(bf16[64,1024]{1,0:T(8,128)(2,1)S(1)} %collective-permute-done.7), channel_id=1, source_target_pairs={{0,2},{2,0},{1,3},{3,1},{4,6},{6,4},{5,7},{7,5},{8,10},{10,8},{9,1... | collective-permute-start | bytes 393224 | tf_op jit(solution)/shard_map/ppermute | solution.py:172
  85.3 19.5 %copy-start.1 = (bf16[8,64,1024]{2,1,0:T(8,128)(2,1)}, bf16[8,64,1024]{2,1,0:T(8,128)(2,1)S(1)}, u32[]{:S(2)}) copy-start(bf16[8,64,1024]{2,1,0:T(8,128)(2,1)S(1)} %bitcast_dynamic-update-slice_fusion.near_ref) | copy-start | bytes 3145732
  89.7 5.0 %collective-permute-start.12 = (bf16[64,1024]{1,0:T(8,128)(2,1)S(1)}, bf16[64,1024]{1,0:T(8,128)(2,1)S(1)}, u32[]{:S(2)}, u32[]{:S(2)}) collective-permute-start(bf16[64,1024]{1,0:T(8,128)(2,1)S(1)} %collective-permute-done.8), channel_id=1, source_target_pairs={{0,2},{2,0},{1,3},{3,1},{4,6},{6,4},{5,7},{7,5},{8,10},{10,8},{9,1... | collective-permute-start | bytes 393224 | tf_op jit(solution)/shard_map/ppermute | solution.py:172
  94.7 5.0 %collective-permute-start.13 = (bf16[64,1024]{1,0:T(8,128)(2,1)S(1)}, bf16[64,1024]{1,0:T(8,128)(2,1)S(1)}, u32[]{:S(2)}, u32[]{:S(2)}) collective-permute-start(bf16[64,1024]{1,0:T(8,128)(2,1)S(1)} %collective-permute-done.9), channel_id=1, source_target_pairs={{0,2},{2,0},{1,3},{3,1},{4,6},{6,4},{5,7},{7,5},{8,10},{10,8},{9,1... | collective-permute-start | bytes 393224 | tf_op jit(solution)/shard_map/ppermute | solution.py:172
  99.7 5.1 %collective-permute-start.22 = (bf16[8,64,1024]{2,1,0:T(8,128)(2,1)S(1)}, bf16[8,64,1024]{2,1,0:T(8,128)(2,1)S(1)}, u32[]{:S(2)}, u32[]{:S(2)}) collective-permute-start(bf16[8,64,1024]{2,1,0:T(8,128)(2,1)S(1)} %bitcast_dynamic-update-slice_fusion.near_ref), channel_id=1, source_target_pairs={{0,1},{1,0},{2,3},{3,2},{4,5},{5,4},{6,7},{7,6},{8,9},{9,8},{10,11... | collective-permute-start | bytes 3145736 | tf_op jit(solution)/shard_map/ppermute | solution.py:192
  99.7 18.2 %copy-start = (bf16[8,64,1024]{2,1,0:T(8,128)(2,1)}, bf16[8,64,1024]{2,1,0:T(8,128)(2,1)S(1)}, u32[]{:S(2)}) copy-start(bf16[8,64,1024]{2,1,0:T(8,128)(2,1)S(1)} %bitcast_dynamic-update-slice_fusion.8.near_ref) | copy-start | bytes 3145732
  99.7 18.2 %collective-permute-start.14 = (bf16[8,64,1024]{2,1,0:T(8,128)(2,1)S(1)}, bf16[8,64,1024]{2,1,0:T(8,128)(2,1)S(1)}, u32[]{:S(2)}, u32[]{:S(2)}) collective-permute-start(bf16[8,64,1024]{2,1,0:T(8,128)(2,1)S(1)} %bitcast_dynamic-update-slice_fusion.8.near_ref), channel_id=1, source_target_pairs={{0,1},{1,0},{2,3},{3,2},{4,5},{5,4},{6,7},{7,6},{8,9},{9,8},{10,11... | collective-permute-start | bytes 3145736 | tf_op jit(solution)/shard_map/ppermute | solution.py:192
  100.3 4.5 %collective-permute-start.6 = (bf16[16,128]{1,0:T(8,128)(2,1)S(1)}, bf16[16,128]{1,0:T(8,128)(2,1)S(1)}, u32[]{:S(2)}, u32[]{:S(2)}) collective-permute-start(bf16[16,128]{1,0:T(8,128)(2,1)S(1)} %fusion.5), channel_id=1, source_target_pairs={{0,14},{2,12},{4,2},{6,0},{8,6},{10,4},{12,10},{14,8},{1,15},{3,13... | collective-permute-start | bytes 12296 | tf_op jit(solution)/shard_map/ppermute | solution.py:172
  104.8 0.6 copy-start.4
  104.8 1.0 copy-start.3
  117.9 1.0 copy-start.2
  136.8 2.9 %collective-permute-start.23 = (bf16[8,64,1024]{2,1,0:T(8,128)(2,1)}, bf16[8,64,1024]{2,1,0:T(8,128)(2,1)S(1)}, u32[]{:S(2)}, u32[]{:S(2)}) collective-permute-start(bf16[8,64,1024]{2,1,0:T(8,128)(2,1)} %get-tuple-element.21), channel_id=1, source_target_pairs={{0,1},{1,0},{2,3},{3,2},{4,5},{5,4},{6,7},{7,6},{8,9},{9,8},{10,11... | collective-permute-start | bytes 3145736 | tf_op jit(solution)/shard_map/ppermute | solution.py:192
  139.8 3.0 %copy-start.5 = (f32[8,8,128]{2,1,0:T(8,128)S(1)}, f32[8,8,128]{2,1,0:T(8,128)}, u32[]{:S(2)}) copy-start(f32[8,8,128]{2,1,0:T(8,128)} %get-tuple-element.22) | copy-start | bytes 98308
  141.4 24.7 %collective-permute-start.24 = (bf16[4,64,1024]{2,1,0:T(8,128)(2,1)S(1)}, bf16[4,64,1024]{2,1,0:T(8,128)(2,1)S(1)}, u32[]{:S(2)}, u32[]{:S(2)}) collective-permute-start(bf16[4,64,1024]{2,1,0:T(8,128)(2,1)S(1)} %slice.59), channel_id=1, source_target_pairs={{0,2},{2,0},{1,3},{3,1},{4,6},{6,4},{5,7},{7,5},{8,10},{10,8},{9,1... | collective-permute-start | bytes 1572872 | tf_op jit(solution)/shard_map/ppermute | solution.py:172
  142.8 7.1 %collective-permute-start.35 = (f32[8,128]{1,0:T(8,128)S(1)}, f32[8,128]{1,0:T(8,128)S(1)}, u32[]{:S(2)}, u32[]{:S(2)}) collective-permute-start(f32[8,128]{1,0:T(8,128)S(1)} %bitcast.98), channel_id=1, source_target_pairs={{0,6},{2,4},{4,10},{6,8},{8,14},{10,12},{12,2},{14,0},{1,7},{3,5},... | collective-permute-start | bytes 12296 | tf_op jit(solution)/shard_map/ppermute | solution.py:172
  142.8 9.0 %collective-permute-start.34 = (f32[8,128]{1,0:T(8,128)S(1)}, f32[8,128]{1,0:T(8,128)S(1)}, u32[]{:S(2)}, u32[]{:S(2)}) collective-permute-start(f32[8,128]{1,0:T(8,128)S(1)} %bitcast.97), channel_id=1, source_target_pairs={{0,10},{2,8},{4,14},{6,12},{8,2},{10,0},{12,6},{14,4},{1,11},{3,9}... | collective-permute-start | bytes 12296 | tf_op jit(solution)/shard_map/ppermute | solution.py:172
  148.3 5.6 %collective-permute-start.33 = (f32[8,128]{1,0:T(8,128)S(1)}, f32[8,128]{1,0:T(8,128)S(1)}, u32[]{:S(2)}, u32[]{:S(2)}) collective-permute-start(f32[8,128]{1,0:T(8,128)S(1)} %bitcast.96), channel_id=1, source_target_pairs={{0,14},{2,12},{4,2},{6,0},{8,6},{10,4},{12,10},{14,8},{1,15},{3,13... | collective-permute-start | bytes 12296 | tf_op jit(solution)/shard_map/ppermute | solution.py:172
  148.3 17.6 %collective-permute-start.32 = (f32[8,128]{1,0:T(8,128)S(1)}, f32[8,128]{1,0:T(8,128)S(1)}, u32[]{:S(2)}, u32[]{:S(2)}) collective-permute-start(f32[8,128]{1,0:T(8,128)S(1)} %bitcast.95), channel_id=1, source_target_pairs={{0,2},{2,0},{4,6},{6,4},{8,10},{10,8},{12,14},{14,12},{1,3},{3,1},... | collective-permute-start | bytes 12296 | tf_op jit(solution)/shard_map/ppermute | solution.py:172
  149.9 16.1 %collective-permute-start.31 = (f32[8,128]{1,0:T(8,128)S(1)}, f32[8,128]{1,0:T(8,128)S(1)}, u32[]{:S(2)}, u32[]{:S(2)}) collective-permute-start(f32[8,128]{1,0:T(8,128)S(1)} %bitcast.94), channel_id=1, source_target_pairs={{0,4},{2,6},{4,8},{6,10},{8,12},{10,14},{12,0},{14,2},{1,5},{3,7},... | collective-permute-start | bytes 12296 | tf_op jit(solution)/shard_map/ppermute | solution.py:172
  151.8 14.2 %collective-permute-start.30 = (f32[8,128]{1,0:T(8,128)S(1)}, f32[8,128]{1,0:T(8,128)S(1)}, u32[]{:S(2)}, u32[]{:S(2)}) collective-permute-start(f32[8,128]{1,0:T(8,128)S(1)} %bitcast.93), channel_id=1, source_target_pairs={{0,8},{2,10},{4,12},{6,14},{8,0},{10,2},{12,4},{14,6},{1,9},{3,11}... | collective-permute-start | bytes 12296 | tf_op jit(solution)/shard_map/ppermute | solution.py:172
  153.9 12.1 %collective-permute-start.29 = (f32[8,128]{1,0:T(8,128)S(1)}, f32[8,128]{1,0:T(8,128)S(1)}, u32[]{:S(2)}, u32[]{:S(2)}) collective-permute-start(f32[8,128]{1,0:T(8,128)S(1)} %bitcast.92), channel_id=1, source_target_pairs={{0,12},{2,14},{4,0},{6,2},{8,4},{10,6},{12,8},{14,10},{1,13},{3,15... | collective-permute-start | bytes 12296 | tf_op jit(solution)/shard_map/ppermute | solution.py:172
  166.4 7.2 %collective-permute-start.25 = (bf16[64,1024]{1,0:T(8,128)(2,1)S(1)}, bf16[64,1024]{1,0:T(8,128)(2,1)S(1)}, u32[]{:S(2)}, u32[]{:S(2)}) collective-permute-start(bf16[64,1024]{1,0:T(8,128)(2,1)S(1)} %get-tuple-element.45), channel_id=1, source_target_pairs={{0,12},{4,0},{8,4},{12,8},{1,13},{5,1},{9,5},{13,9},{2,14},{6,2},{... | collective-permute-start | bytes 393224 | tf_op jit(solution)/shard_map/ppermute | solution.py:172
  167.8 7.6 %collective-permute-start.27 = (bf16[64,1024]{1,0:T(8,128)(2,1)S(1)}, bf16[64,1024]{1,0:T(8,128)(2,1)S(1)}, u32[]{:S(2)}, u32[]{:S(2)}) collective-permute-start(bf16[64,1024]{1,0:T(8,128)(2,1)S(1)} %get-tuple-element.46), channel_id=1, source_target_pairs={{0,4},{4,8},{8,12},{12,0},{1,5},{5,9},{9,13},{13,1},{2,6},{6,10},{... | collective-permute-start | bytes 393224 | tf_op jit(solution)/shard_map/ppermute | solution.py:172
  168.5 10.9 %collective-permute-start.26 = (bf16[64,1024]{1,0:T(8,128)(2,1)S(1)}, bf16[64,1024]{1,0:T(8,128)(2,1)S(1)}, u32[]{:S(2)}, u32[]{:S(2)}) collective-permute-start(bf16[64,1024]{1,0:T(8,128)(2,1)S(1)} %get-tuple-element.47), channel_id=1, source_target_pairs={{0,8},{4,12},{8,0},{12,4},{1,9},{5,13},{9,1},{13,5},{2,10},{6,14},... | collective-permute-start | bytes 393224 | tf_op jit(solution)/shard_map/ppermute | solution.py:172
  169.4 10.1 %collective-permute-start.36 = (f32[6,128]{1,0:T(8,128)S(1)}, f32[6,128]{1,0:T(8,128)S(1)}, u32[]{:S(2)}, u32[]{:S(2)}) collective-permute-start(f32[6,128]{1,0:T(8,128)S(1)} %fusion.6), channel_id=1, source_target_pairs={{0,1},{1,0},{2,3},{3,2},{4,5},{5,4},{6,7},{7,6},{8,9},{9,8},{10,11... | collective-permute-start | bytes 9224 | tf_op jit(solution)/shard_map/ppermute | solution.py:192
  179.5 1.4 collective-permute-start.28

commit v2 on v1

v2 whole, which is shorter than its diff:
```python
import functools

import jax
import jax.numpy as jnp
from jax import lax
from jax.experimental import pallas as pl
from jax.experimental.pallas import tpu as pltpu
from jax.sharding import PartitionSpec as P

MOST = 16
BF16, F32 = jnp.bfloat16, jnp.float32
LAST = (((1,), (1,)), ((), ()))
LEAD = (((0,), (0,)), ((), ()))
VMEM_BYTES = 56 * 1024 * 1024


def dot(a, b, dims):
    return lax.dot_general(a, b, dims, preferred_element_type=F32)


def iota(shape, dim):
    return lax.broadcasted_iota(jnp.int32, shape, dim)


def ranks_and_probs(first, meta, span, count):
    sources, height, tokens = meta.shape
    kinds = height // 2
    wanted = ((first + span * iota((count, tokens), 0)) >> 1).astype(F32)
    named, weight = [], []
    for source in range(sources):
        entry = meta[source].astype(F32)
        hit = jnp.zeros((count, tokens), F32)
        prob = jnp.zeros((count, tokens), F32)
        for kind in range(kinds):
            same = entry[kind : kind + 1] == wanted
            hit = jnp.where(same, 1.0, hit)
            prob = jnp.where(same, entry[kinds + kind : kinds + kind + 1], prob)
        named.append(hit)
        weight.append(prob)
    named = jnp.concatenate(named)
    before = (iota((tokens, tokens), 0) < iota((tokens, tokens), 1)).astype(F32).astype(BF16)
    rank = jnp.dot(named.astype(BF16), before, preferred_element_type=F32)
    return jnp.where(named > 0, rank, -1.0), jnp.concatenate(weight)


def slot_matrix(rank):
    count, tokens = rank.shape
    wide = jnp.broadcast_to(rank[:, None, :], (count, MOST, tokens)).reshape(count * MOST, tokens)
    place = (iota((count * MOST, tokens), 0) & (MOST - 1)).astype(F32)
    return jnp.where(wide == place, 1.0, 0.0).astype(BF16)


def gather_rows(step, rank, near, far, rows_scr):
    count, _, features = rows_scr.shape
    sources = near.shape[0]
    half = rank.shape[1] // 2
    for source in range(sources):
        pick = slot_matrix(rank[source * count : (source + 1) * count])
        both = jnp.concatenate([near[source, :half], far[source, :half]], axis=0)
        rows = jnp.dot(pick, both, preferred_element_type=F32).astype(BF16)
        start = pl.multiple_of((step * sources + source) * MOST, MOST)
        rows_scr[:, pl.ds(start, MOST), :] = rows.reshape(count, MOST, features)


def unpack_meta(near, half, tokens, kinds):
    features = near.shape[2]
    per_row = features // tokens
    lines = []
    for number in range(2 * kinds):
        at, part = half + number // per_row, number % per_row
        lines.append(near[:, at : at + 1, part * tokens : (part + 1) * tokens])
    return jnp.concatenate(lines, axis=1)


def first_kernel(steps, span, kinds, where_ref, near_ref, far_ref, wg_ref, wu_ref, rows_ref, gate_ref, up_ref,
                 rank_ref, weight_ref, meta_ref, rows_scr):
    step = pl.program_id(0)
    count = rows_scr.shape[0]
    tokens = rank_ref.shape[1]

    @pl.when(step < steps)
    def _():
        meta = unpack_meta(near_ref[:, tokens // 2 :, :].astype(F32), 0, tokens, kinds)
        rank, weight = ranks_and_probs(where_ref[0], meta, span, count)
        rank_ref[...] = rank
        meta_ref[...] = meta
        weight_ref[...] = weight
        gather_rows(step, rank, near_ref, far_ref, rows_scr)

    @pl.when(step >= steps)
    def _():
        rows = rows_scr[step - steps]
        rows_ref[0] = rows
        gate_ref[0] = dot(wg_ref[0], rows, LAST)
        up_ref[0] = dot(wu_ref[0], rows, LAST)


def second_kernel(steps, span, where_ref, rank_ref, weight_ref, meta_ref, near_ref, far_ref, wg_ref, wu_ref, wd_ref, gate_ref,
                  up_ref, rows_ref, dgate_ref, dup_ref, gated_ref, own_ref, other_ref, rows_scr, input_scr, prob_scr):
    step = pl.program_id(0)
    count, slots, features = rows_scr.shape
    sources = near_ref.shape[0]
    all_sources = slots // MOST
    tokens = rank_ref.shape[1]

    def rank_of(number, sources):
        start, size = number * count, sources * count
        if size % 8 == 0:
            start = pl.multiple_of(start, 8)
        return rank_ref[pl.ds(start, size)]

    @pl.when(step < steps)
    def _():
        gather_rows(step, rank_of(step * sources, sources), near_ref, far_ref, rows_scr)

    @pl.when((step >= steps) & (step < steps + count))
    def _():
        expert = step - steps
        total = all_sources * count
        row, lane = iota((total, slots), 0), iota((total, slots), 1)
        spread = jnp.where(row == (lane // MOST) * count + expert, 1.0, 0.0).astype(BF16)
        place = (iota((tokens, slots), 1) & (MOST - 1)).astype(F32)
        holds = dot(rank_ref[...].astype(BF16), spread, LEAD) == place
        weight = dot(weight_ref[...].astype(BF16), spread, LEAD)
        scale = jnp.sum(jnp.where(holds, weight, 0.0), axis=0, keepdims=True)
        rows = rows_scr[expert]
        rows_ref[0] = rows
        raw = dot(wd_ref[0], rows, LAST)
        gate, up = gate_ref[0], up_ref[0]
        sigmoid = 1.0 / (1.0 + jnp.exp(-gate))
        active = gate * sigmoid
        hidden = active * up
        gated_ref[0] = (scale * hidden).astype(BF16)
        prob = jnp.sum(hidden * raw, axis=0, keepdims=True)
        scaled = scale * raw
        dgate = (scaled * up * sigmoid * (1.0 + gate * (1.0 - sigmoid))).astype(BF16)
        dup = (scaled * active).astype(BF16)
        dgate_ref[0] = dgate
        dup_ref[0] = dup
        input_scr[expert] = (dot(dgate, wg_ref[0], LEAD) + dot(dup, wu_ref[0], LEAD)).astype(BF16)
        block = jnp.where(
            iota((all_sources, slots), 0) == iota((all_sources, slots), 1) // MOST, 1.0, 0.0
        ).astype(BF16)
        prob_scr[expert] = dot(block, jnp.where(holds, prob, 0.0).astype(BF16), LAST)

    @pl.when(step >= steps + count)
    def _():
        chunk = step - steps - count
        half = tokens // 2
        kinds = meta_ref.shape[1] // 2
        wanted = ((where_ref[0] + span * iota((count, tokens), 0)) >> 1).astype(F32)
        for source in range(sources):
            number = chunk * sources + source
            pick = slot_matrix(rank_of(number, 1))
            rows = input_scr[:, pl.ds(pl.multiple_of(number * MOST, MOST), MOST), :].reshape(count * MOST, features)
            part = dot(pick, rows, LEAD).astype(BF16)
            own_ref[source, :half] = part[:half]
            other_ref[source, :half] = part[half:]
            prob = prob_scr[:, pl.ds(number, 1), :].reshape(count, tokens)
            entry = meta_ref[number]
            line = [
                jnp.sum(jnp.where(entry[kind : kind + 1] == wanted, prob, 0.0), axis=0, keepdims=True)
                for kind in range(kinds)
            ]
            flip = [pltpu.roll(jnp.broadcast_to(part, (8, tokens)), half, 1)[:1] for part in line]
            tail_ref_rows = own_ref.shape[1] - half
            per_row = features // tokens
            for ref, parts in ((own_ref, line), (other_ref, flip)):
                lines = [jnp.concatenate(parts[at : at + per_row], axis=1) for at in range(0, kinds, per_row)]
                lines += [jnp.zeros_like(lines[0])] * (tail_ref_rows - len(lines))
                ref[source, half:] = jnp.concatenate(lines, axis=0).astype(BF16)


def third_kernel(x_ref, dy_ref, dgate_ref, dup_ref, gated_ref, *refs):
    gg_ref, gu_ref, gd_ref = refs[-3:]
    x, dy = x_ref[0], dy_ref[0]
    gg_ref[0] = jnp.dot(dgate_ref[0], x, preferred_element_type=F32).astype(BF16)
    gu_ref[0] = jnp.dot(dup_ref[0], x, preferred_element_type=F32).astype(BF16)
    gd_ref[0] = jnp.dot(gated_ref[0], dy, preferred_element_type=F32).astype(BF16)


def per_device(tokens, cotangent, probs, experts, w_gate, w_up, w_down):
    rows, features = tokens.shape
    top = experts.shape[1]
    zs, xs = lax.axis_size("expert"), lax.axis_size("blk")
    cores = lax.axis_size("tensor")
    positions = zs * xs
    half = rows // cores
    halves, _, quarter = w_gate.shape
    span = 2 if halves % 2 == 0 else 1
    count = halves // span
    hidden = span * quarter
    slots = positions * MOST
    core = lax.axis_index("tensor")
    position = lax.axis_index("expert") * xs + lax.axis_index("blk")
    kinds = 8 * pl.cdiv(top, 8)
    barrier = lax.optimization_barrier

    def swap(array):
        return lax.ppermute(array, "tensor", [(i, (i + 1) % cores) for i in range(cores)])

    def along_z(array, by):
        return lax.ppermute(array, "expert", [(i, (i + by) % zs) for i in range(zs)])

    def along_x(array, by):
        return lax.ppermute(array, "blk", [(i, (i + by) % xs) for i in range(xs)])

    def own_first(array):
        return jnp.roll(array, -core * half, axis=-1)

    experts_t = own_first(experts.T)
    probs_t = own_first(probs.T)
    meta = jnp.concatenate(
        [
            jnp.pad(experts_t.astype(BF16), ((0, kinds - top), (0, 0)), constant_values=-1.0),
            jnp.pad(probs_t, ((0, kinds - top), (0, 0))),
        ]
    ).reshape(-1, features)
    meta = jnp.pad(meta, ((0, -meta.shape[0] % 8), (0, 0)))
    own_x = jnp.concatenate([lax.dynamic_slice_in_dim(tokens, core * half, half, 0), meta])
    own_dy = lax.dynamic_slice_in_dim(cotangent, core * half, half, 0)

    line_x = [own_x] + [along_z(own_x, d) for d in range(1, zs)]
    first_x = [along_x(own_x, c) for c in range(1, xs)]
    line_dy = [own_dy]
    for d in range(1, zs):
        send, line_x[d] = barrier((own_dy, line_x[d]))
        line_dy.append(along_z(send, d))
    first_dy = [along_x(own_dy, c) for c in range(1, xs)]
    rest_x = jnp.stack(line_x[1:])
    more_x = [along_x(rest_x, c) for c in range(1, xs)]
    groups_x = [jnp.stack(line_x)] + [jnp.concatenate([a[None], b]) for a, b in zip(first_x, more_x)]
    near_x = jnp.concatenate(groups_x)
    far_x = jnp.concatenate([swap(group) for group in groups_x])
    more_dy = [[along_x(block, c) for block in line_dy[1:]] for c in range(1, xs)]
    near_x, *_ = barrier((near_x, *line_dy[1:]))

    wg = jnp.swapaxes(w_gate, 1, 2).reshape(count, hidden, features)
    wu = jnp.swapaxes(w_up, 1, 2).reshape(count, hidden, features)
    wd = w_down.reshape(count, hidden, features)
    where = jnp.stack([position * halves, lax.axis_index("expert"), lax.axis_index("blk")]).astype(jnp.int32)

    per_step = min(positions, 8)
    steps = positions // per_step
    tall = own_x.shape[0]
    gathering = lambda i: (jnp.minimum(i, steps - 1), 0, 0)
    working = lambda i: (jnp.clip(i - steps, 0, count - 1), 0, 0)
    scalar = pl.BlockSpec(memory_space=pltpu.SMEM)
    weight_spec = pl.BlockSpec((1, hidden, features), working)
    rows_spec = pl.BlockSpec((1, slots, features), working)
    hidden_spec = pl.BlockSpec((1, hidden, slots), working)
    params = pltpu.CompilerParams(vmem_limit_bytes=VMEM_BYTES, dimension_semantics=("arbitrary",))
    flops = 2 * count * hidden * slots * features
    shaped = jax.ShapeDtypeStruct
    x_spec = pl.BlockSpec((per_step, tall, features), gathering)
    table_spec = pl.BlockSpec((per_step * count, rows), lambda i: (jnp.minimum(i, steps - 1), 0))

    rows_x, gate, up, rank, weight, meta_table = pl.pallas_call(
        functools.partial(first_kernel, steps, span, kinds),
        grid=(steps + count,),
        in_specs=[scalar, x_spec, x_spec, weight_spec, weight_spec],
        out_specs=[rows_spec, hidden_spec, hidden_spec, table_spec, table_spec,
                   pl.BlockSpec((per_step, 2 * kinds, rows), gathering)],
        out_shape=[
            shaped((count, slots, features), BF16),
            shaped((count, hidden, slots), F32),
            shaped((count, hidden, slots), F32),
            shaped((positions * count, rows), F32),
            shaped((positions * count, rows), F32),
            shaped((positions, 2 * kinds, rows), F32),
        ],
        scratch_shapes=[pltpu.VMEM((count, slots, features), BF16)],
        compiler_params=params,
        cost_estimate=pl.CostEstimate(flops=2 * flops, bytes_accessed=20_000_000, transcendentals=0),
        name="forward",
    )(where, near_x, far_x, wg, wu)

    more_dy, rank = barrier((more_dy, rank))
    groups_dy = [jnp.stack(line_dy)] + [jnp.stack([a] + b) for a, b in zip(first_dy, more_dy)]
    near_dy = jnp.concatenate(groups_dy)
    far_dy = jnp.concatenate([swap(group) for group in groups_dy])
    dy_spec = pl.BlockSpec((per_step, half, features), gathering)
    back = half + 8 * pl.cdiv(kinds * rows, 8 * features)
    out_spec = pl.BlockSpec((per_step, back, features), lambda i: (jnp.clip(i - steps - count, 0, steps - 1), 0, 0))
    meta_spec = pl.BlockSpec((positions, 2 * kinds, rows), lambda i: (0, 0, 0))
    whole_spec = pl.BlockSpec((positions * count, rows), lambda i: (0, 0))
    rows_dy, dgate, dup, gated, own, other = pl.pallas_call(
        functools.partial(second_kernel, steps, span),
        grid=(steps + count + steps,),
        in_specs=[scalar, whole_spec, whole_spec, meta_spec, dy_spec, dy_spec, weight_spec, weight_spec, weight_spec, hidden_spec,
                  hidden_spec],
        out_specs=[rows_spec, hidden_spec, hidden_spec, hidden_spec, out_spec, out_spec],
        out_shape=[
            shaped((count, slots, features), BF16),
            shaped((count, hidden, slots), BF16),
            shaped((count, hidden, slots), BF16),
            shaped((count, hidden, slots), BF16),
            shaped((positions, back, features), BF16),
            shaped((positions, back, features), BF16),
        ],
        scratch_shapes=[
            pltpu.VMEM((count, slots, features), BF16),
            pltpu.VMEM((count, slots, features), BF16),
            pltpu.VMEM((count, positions, rows), F32),
        ],
        compiler_params=params,
        cost_estimate=pl.CostEstimate(flops=3 * flops, bytes_accessed=30_000_000, transcendentals=0),
        name="backward",
    )(where, rank, weight, meta_table, near_dy, far_dy, wg, wu, wd, gate, up)

    parts = zs if count % zs == 0 else 1
    size = count // parts

    def weights(part, saved, grads):
        at = lambda i: (i + part * size, 0, 0)
        block = lambda height, width: pl.BlockSpec((1, height, width), at)
        return pl.pallas_call(
            third_kernel,
            grid=(size,),
            in_specs=[block(slots, features)] * 2 + [block(hidden, slots)] * 3
            + [pl.BlockSpec(memory_space=pl.ANY)] * len(grads),
            out_specs=[block(hidden, features)] * 3,
            out_shape=[shaped((count, hidden, features), BF16)] * 3,
            input_output_aliases={5 + i: i for i in range(len(grads))},
            compiler_params=params,
            cost_estimate=pl.CostEstimate(flops=3 * flops // parts, bytes_accessed=24_000_000 // parts, transcendentals=0),
            name="weights",
        )(*saved, *grads)

    saved, grads = (rows_x, rows_dy, dgate, dup, gated), ()

    own = own.reshape(xs, zs, back, features)
    other = other.reshape(xs, zs, back, features)
    chip = [None] * xs
    for c in list(range(1, xs)) + [0]:
        chip[c] = (own[c].astype(F32) + swap(other[c]).astype(F32)).astype(BF16)
    turn = list(range(1, zs)) + [0]
    hops = {d: [along_x(chip[c][d], -c) for c in range(1, xs)] for d in turn}
    pieces = []
    for number, d in enumerate(turn):
        total = chip[0][d].astype(F32)
        for hop in hops[d]:
            total = total + hop.astype(F32)
        if d:
            total = total.astype(BF16)
            pieces.append(along_z(total, -d))
        if number < parts:
            total, saved = barrier((total, saved))
            grads = weights(number, saved, grads)
            if number + 1 < len(turn):
                follow = turn[number + 1]
                hops[follow], grads = barrier((hops[follow], grads))
    for piece in pieces:
        total = total + piece.astype(F32)
    mine = total.astype(BF16)
    theirs = swap(mine)

    def tokens_of(piece):
        return piece[:half]

    def probs_of(piece):
        return piece[half:].reshape(-1)[: kinds * rows].reshape(kinds, rows)[:top, :half].astype(F32)

    def in_order(part, axis):
        both = part(mine), part(theirs)
        return jnp.where(core == 0, jnp.concatenate(both, axis), jnp.concatenate(both[::-1], axis))

    grad_tokens = in_order(tokens_of, 0)
    grad_probs = in_order(probs_of, 1).T
    grad_gate, grad_up, grad_down = grads
    shape = (halves, quarter, features)
    return (
        grad_tokens,
        grad_probs,
        jnp.swapaxes(grad_gate.reshape(shape), 1, 2),
        jnp.swapaxes(grad_up.reshape(shape), 1, 2),
        grad_down.reshape(shape),
    )


def solution(mesh):
    return jax.shard_map(
        per_device,
        mesh=mesh,
        in_specs=(
            P(("groups", "expert", "blk"), None),
            P(("groups", "expert", "blk"), None),
            P(("groups", "expert", "blk"), None),
            P(("groups", "expert", "blk"), None),
            P(("expert", "blk"), None, "tensor"),
            P(("expert", "blk"), None, "tensor"),
            P(("expert", "blk"), "tensor", None),
        ),
        out_specs=(
            P(("groups", "expert", "blk"), None),
            P(("groups", "expert", "blk"), None),
            P(("groups", "expert", "blk"), None, "tensor"),
            P(("groups", "expert", "blk"), None, "tensor"),
            P(("groups", "expert", "blk"), "tensor", None),
        ),
        check_vma=False,
    )
```

time: 183 us -> 112 us (0.61)
  waiting for transfers between devices: 94.2 us -> 32 us
  starting transfers between devices: 36 us -> 24.2 us
  Pallas kernels: 41.2 us -> 44.9 us
    ppermute x32 -> x19, waiting for transfers between devices: 90.8 us -> 26.5 us  [the longest x9 18 us: along_z(): lax.ppermute(array, 'expert', [(i, (i + by) % zs) for i in range(zs)])]
    ppermute x32 -> x19, starting transfers between devices: 35.2 us -> 23.4 us  [the longest x9 12.3 us: along_z(): lax.ppermute(array, 'expert', [(i, (i + by) % zs) for i in range(zs)])]
    pallas_call x2 -> x5, Pallas kernels: 23.3 us -> 26.9 us  [the longest x4 14.5 us: weights(): pl.pallas_call(third_kernel, grid=(size,), in_specs=[block(slots, feature...]
    unnamed x32 -> x19, local copies, waits for them, and re-layouts: 3.99 us -> 1.06 us
    concatenate x1 -> x3, other arithmetic: 0.08 us -> 2.27 us  [the longest x1 1.15 us: per_device(): far_x = jnp.concatenate([swap(group) for group in groups_x])]
    ppermute x5 -> x7, waiting for transfers between devices: 3.4 us -> 5.51 us  [swap(): lax.ppermute(array, 'tensor', [(i, (i + 1) % cores) for i in range(cores)])]
  transfers between devices with their start and end apart: 37 -> 26, of which waited for: 22 -> 12; matrix products, arithmetic and copies ran while one was open for 2% -> 3% of each run, Pallas kernels for 13% -> 24%
where the time goes in v2:
time: 112 us
  Pallas kernels  44.9 us (40%)
  waiting for transfers between devices  32 us (29%)
  starting transfers between devices  24.2 us (22%)
  other arithmetic  6.83 us (6%)
  local copies, waits for them, and re-layouts  2.68 us (2%)
    ppermute x9, waiting for transfers between devices, along_z(): lax.ppermute(array, 'expert', [(i, (i + by) % zs) for i in range(zs)])  18 us
    pallas_call x1, Pallas kernels, per_device(): pl.pallas_call(functools.partial(second_kernel, steps, span), grid=(steps...  18 us
    pallas_call x4, Pallas kernels, weights(): pl.pallas_call(third_kernel, grid=(size,), in_specs=[block(slots, feature...  14.5 us
    pallas_call x1, Pallas kernels, per_device(): pl.pallas_call(functools.partial(first_kernel, steps, span, kinds), grid=...  12.3 us
    ppermute x9, starting transfers between devices, along_z(): lax.ppermute(array, 'expert', [(i, (i + by) % zs) for i in range(zs)])  12.3 us
    ppermute x10, starting transfers between devices, along_x(): return lax.ppermute(array, 'blk', [(i, (i + by) % xs) for i in range(xs)])  11.1 us
    ppermute x10, waiting for transfers between devices, along_x(): return lax.ppermute(array, 'blk', [(i, (i + by) % xs) for i in range(xs)])  8.47 us
    ppermute x7, waiting for transfers between devices, swap(): lax.ppermute(array, 'tensor', [(i, (i + 1) % cores) for i in range(cores)])  5.51 us
  transfers between devices with their start and end apart: 26, of which 12 were waited for; matrix products, arithmetic and copies ran while one was open for 3% of the time, Pallas kernels for 24%

profile of v2, /device:TPU:0, one launch (start us, length us, event | category | flops | bytes accessed | tf_op | source)
XLA Modules:
  0.0 111.6 jit_solution(7275966314815628468)
XLA Ops:
  0.6 0.0 copy-start
  0.7 0.8 fusion.11
  1.5 0.8 fusion.9
  2.3 3.0 %collective-permute-start.9 = (bf16[72,1024]{1,0:T(8,128)(2,1)S(1)}, bf16[72,1024]{1,0:T(8,128)(2,1)S(1)}, u32[]{:S(2)}, u32[]{:S(2)}) collective-permute-start(bf16[72,1024]{1,0:T(8,128)(2,1)S(1)} %get-tuple-element.152), channel_id=1, source_target_pairs={{0,2},{2,0},{1,3},{3,1},{4,6},{6,4},{5,7},{7,5},{8,10},{10,8},{9,1... | collective-permute-start | bytes 442376 | tf_op jit(solution)/shard_map/ppermute | solution.py:206
  5.3 3.6 %collective-permute-start.6 = (bf16[72,1024]{1,0:T(8,128)(2,1)S(1)}, bf16[72,1024]{1,0:T(8,128)(2,1)S(1)}, u32[]{:S(2)}, u32[]{:S(2)}) collective-permute-start(bf16[72,1024]{1,0:T(8,128)(2,1)S(1)} %get-tuple-element.152), channel_id=1, source_target_pairs={{0,12},{4,0},{8,4},{12,8},{1,13},{5,1},{9,5},{13,9},{2,14},{6,2},{... | collective-permute-start | bytes 442376 | tf_op jit(solution)/shard_map/ppermute | solution.py:203
  8.9 0.0 collective-permute-start.3
  8.9 1.0 collective-permute-start
  10.0 0.9 constant_dynamic-update-slice_fusion.13
  10.9 0.6 collective-permute-start.13
  11.5 0.6 pad_add_fusion.where_ref
  12.1 1.2 %collective-permute-done.6 = bf16[72,1024]{1,0:T(8,128)(2,1)S(1)} collective-permute-done((bf16[72,1024]{1,0:T(8,128)(2,1)S(1)}, bf16[72,1024]{1,0:T(8,128)(2,1)S(1)}, u32[]{:S(2)}, u32[]{:S(2)}) %collective-permute-start.6) | collective-permute-done | bytes 147488 | tf_op jit(solution)/shard_map/ppermute | solution.py:203
  13.2 8.0 %collective-permute-done.3 = bf16[72,1024]{1,0:T(8,128)(2,1)S(1)} collective-permute-done((bf16[72,1024]{1,0:T(8,128)(2,1)S(1)}, bf16[72,1024]{1,0:T(8,128)(2,1)S(1)}, u32[]{:S(2)}, u32[]{:S(2)}) %collective-permute-start.3) | collective-permute-done | bytes 147488 | tf_op jit(solution)/shard_map/ppermute | solution.py:203
  21.2 0.0 collective-permute-done
  21.3 0.9 collective-permute-start.1
  22.1 1.9 %collective-permute-start.4 = (bf16[64,1024]{1,0:T(8,128)(2,1)S(1)}, bf16[64,1024]{1,0:T(8,128)(2,1)S(1)}, u32[]{:S(2)}, u32[]{:S(2)}) collective-permute-start(bf16[64,1024]{1,0:T(8,128)(2,1)S(1)} %get-tuple-element.75), channel_id=1, source_target_pairs={{0,8},{4,12},{8,0},{12,4},{1,9},{5,13},{9,1},{13,5},{2,10},{6,14},... | collective-permute-start | bytes 393224 | tf_op jit(solution)/shard_map/ppermute | solution.py:203
  24.0 2.9 %collective-permute-start.7 = (bf16[64,1024]{1,0:T(8,128)(2,1)S(1)}, bf16[64,1024]{1,0:T(8,128)(2,1)S(1)}, u32[]{:S(2)}, u32[]{:S(2)}) collective-permute-start(bf16[64,1024]{1,0:T(8,128)(2,1)S(1)} %get-tuple-element.75), channel_id=1, source_target_pairs={{0,12},{4,0},{8,4},{12,8},{1,13},{5,1},{9,5},{13,9},{2,14},{6,2},{... | collective-permute-start | bytes 393224 | tf_op jit(solution)/shard_map/ppermute | solution.py:203
  27.0 0.1 pad_maximum_fusion.6
  27.1 0.0 collective-permute-done.9
  27.1 0.6 collective-permute-start.10
  27.7 0.1 pad_maximum_fusion.2
  27.8 1.7 %collective-permute-done.1 = bf16[64,1024]{1,0:T(8,128)(2,1)S(1)} collective-permute-done((bf16[64,1024]{1,0:T(8,128)(2,1)S(1)}, bf16[64,1024]{1,0:T(8,128)(2,1)S(1)}, u32[]{:S(2)}, u32[]{:S(2)}) %collective-permute-start.1) | collective-permute-done | bytes 131104 | tf_op jit(solution)/shard_map/ppermute | solution.py:203
  29.5 4.1 %collective-permute-done.4 = bf16[64,1024]{1,0:T(8,128)(2,1)S(1)} collective-permute-done((bf16[64,1024]{1,0:T(8,128)(2,1)S(1)}, bf16[64,1024]{1,0:T(8,128)(2,1)S(1)}, u32[]{:S(2)}, u32[]{:S(2)}) %collective-permute-start.4) | collective-permute-done | bytes 131104 | tf_op jit(solution)/shard_map/ppermute | solution.py:203
  33.6 0.1 pad_maximum_fusion.4
  33.7 0.1 collective-permute-start.14
  33.8 0.6 collective-permute-start.2
  34.4 3.8 %collective-permute-done.10 = bf16[3,72,1024]{2,1,0:T(8,128)(2,1)S(1)} collective-permute-done((bf16[3,72,1024]{2,1,0:T(8,128)(2,1)S(1)}, bf16[3,72,1024]{2,1,0:T(8,128)(2,1)S(1)}, u32[]{:S(2)}, u32[]{:S(2)}) %collective-permute-start.10) | collective-permute-done | bytes 442400 | tf_op jit(solution)/shard_map/ppermute | solution.py:206
  38.2 0.1 pad_maximum_fusion.3
  38.3 0.1 collective-permute-start.12
  38.4 0.6 collective-permute-start.5
  39.1 0.0 copy-start.1
  39.1 1.6 %collective-permute-start.8 = (bf16[64,1024]{1,0:T(8,128)(2,1)S(1)}, bf16[64,1024]{1,0:T(8,128)(2,1)S(1)}, u32[]{:S(2)}, u32[]{:S(2)}) collective-permute-start(bf16[64,1024]{1,0:T(8,128)(2,1)S(1)} %collective-permute-done.7), channel_id=1, source_target_pairs={{0,2},{2,0},{1,3},{3,1},{4,6},{6,4},{5,7},{7,5},{8,10},{10,8},{9,1... | collective-permute-start | bytes 393224 | tf_op jit(solution)/shard_map/ppermute | solution.py:206
  40.7 1.1 %pad_maximum_fusion.far_ref = bf16[8,72,1024]{2,1,0:T(8,128)(2,1)} fusion(bf16[4,72,1024]{2,1,0:T(8,128)(2,1)S(1)} %collective-permute-done.12, bf16[4,72,1024]{2,1,0:T(8,128)(2,1)S(1)} %collective-permute-done.11), kind=kLoop, calls=%fused_computation | loop fusion | flops 589824 | bytes 2359296 | tf_op jit(solution)/shard_map/concatenate | solution.py:234
  41.8 12.3 %forward.1 = (bf16[8,128,1024]{2,1,0:T(8,128)(2,1)}, f32[8,352,128]{2,1,0:T(8,128)}, f32[8,352,128]{2,1,0:T(8,128)}, f32[64,128]{1,0:T(8,128)}, f32[64,128]{1,0:T(8,128)}, /*index=5*/f32[8,16,128]{2,1,0:T(8,128)}) custom-call(s32[3]{0:T(128)} %pad_add_fusion.where_ref, bf16[8,72,1024]{2,1,0:T(8,128)(2,1)} %copy-done.1, ...), custom_call_target="tpu_custom_call" | custom-call | flops 1476395008 | bytes 20000000 | tf_op jit(solution)/shard_map/forward/pallas_call | solution.py:258
  54.2 0.1 pad_maximum_fusion.5
  54.3 0.1 collective-permute-start.15
  54.4 1.8 %collective-permute-done.15 = bf16[4,64,1024]{2,1,0:T(8,128)(2,1)S(1)} collective-permute-done((bf16[4,64,1024]{2,1,0:T(8,128)(2,1)S(1)}, bf16[4,64,1024]{2,1,0:T(8,128)(2,1)S(1)}, u32[]{:S(2)}, u32[]{:S(2)}) %collective-permute-start.15) | collective-permute-done | bytes 524320 | tf_op jit(solution)/shard_map/ppermute | solution.py:200
  56.2 1.1 pad_maximum_fusion.1.far_ref
  57.3 18.0 %backward.1 = (bf16[8,128,1024]{2,1,0:T(8,128)(2,1)}, bf16[8,352,128]{2,1,0:T(8,128)(2,1)}, bf16[8,352,128]{2,1,0:T(8,128)(2,1)}, bf16[8,352,128]{2,1,0:T(8,128)...) custom-call(s32[3]{0:T(128)} %pad_add_fusion.where_ref, f32[64,128]{1,0:T(8,128)} %get-tuple-element.81.rank_ref, ...), custom_call_target="tpu_custom_call" | custom-call | flops 2214592512 | bytes 30000000 | tf_op jit(solution)/shard_map/backward/pallas_call | solution.py:287
  75.3 0.0 copy-start.3
  75.3 1.4 %fusion.13 = (bf16[4,72,1024]{2,1,0:T(8,128)(2,1)S(1)}, bf16[4,72,1024]{2,1,0:T(8,128)(2,1)S(1)}) fusion(bf16[8,72,1024]{2,1,0:T(8,128)(2,1)} %get-tuple-element.90), kind=kLoop, calls=%fused_computation.65 | loop fusion | bytes 2359296 | tf_op jit(solution)/shard_map/slice | solution.py:336
  76.8 0.2 collective-permute-start.16
  77.0 0.4 collective-permute-start.17
  77.3 1.5 %collective-permute-done.16 = bf16[4,72,1024]{2,1,0:T(8,128)(2,1)S(1)} collective-permute-done((bf16[4,72,1024]{2,1,0:T(8,128)(2,1)S(1)}, bf16[4,72,1024]{2,1,0:T(8,128)(2,1)S(1)}, u32[]{:S(2)}, u32[]{:S(2)}) %collective-permute-start.16) | collective-permute-done | bytes 589856 | tf_op jit(solution)/shard_map/ppermute | solution.py:200
  78.8 0.8 collective-permute-done.17
  79.7 0.4 add_convert_fusion.1
  80.2 0.6 collective-permute-start.21
  80.8 1.5 %collective-permute-start.18 = (bf16[72,1024]{1,0:T(8,128)(2,1)S(1)}, bf16[72,1024]{1,0:T(8,128)(2,1)S(1)}, u32[]{:S(2)}, u32[]{:S(2)}) collective-permute-start(bf16[72,1024]{1,0:T(8,128)(2,1)S(1)} %get-tuple-element.147), channel_id=1, source_target_pairs={{0,2},{2,0},{1,3},{3,1},{4,6},{6,4},{5,7},{7,5},{8,10},{10,8},{9,1... | collective-permute-start | bytes 442376 | tf_op jit(solution)/shard_map/ppermute | solution.py:206
  82.3 0.5 collective-permute-start.20
  82.8 1.5 %collective-permute-start.19 = (bf16[72,1024]{1,0:T(8,128)(2,1)S(1)}, bf16[72,1024]{1,0:T(8,128)(2,1)S(1)}, u32[]{:S(2)}, u32[]{:S(2)}) collective-permute-start(bf16[72,1024]{1,0:T(8,128)(2,1)S(1)} %get-tuple-element.150), channel_id=1, source_target_pairs={{0,2},{2,0},{1,3},{3,1},{4,6},{6,4},{5,7},{7,5},{8,10},{10,8},{9,1... | collective-permute-start | bytes 442376 | tf_op jit(solution)/shard_map/ppermute | solution.py:206
  84.3 2.6 %collective-permute-done.21 = bf16[72,1024]{1,0:T(8,128)(2,1)S(1)} collective-permute-done((bf16[72,1024]{1,0:T(8,128)(2,1)S(1)}, bf16[72,1024]{1,0:T(8,128)(2,1)S(1)}, u32[]{:S(2)}, u32[]{:S(2)}) %collective-permute-start.21) | collective-permute-done | bytes 147488 | tf_op jit(solution)/shard_map/ppermute | solution.py:206
  87.0 0.7 collective-permute-start.22
  87.7 3.6 %weights.4 = (bf16[8,352,1024]{2,1,0:T(8,128)(2,1)}, bf16[8,352,1024]{2,1,0:T(8,128)(2,1)}, bf16[8,352,1024]{2,1,0:T(8,128)(2,1)}) custom-call(bf16[8,128,1024]{2,1,0:T(8,128)(2,1)} %get-tuple-element.130.x_ref, bf16[8,128,1024]{2,1,0:T(8,128)(2,1)} %get-tuple-element.131.dy_ref, bf16[8,352,128]{2,1,0:T(8,128)(2,1)} %get-tuple-element.132.dgate_ref, ...), custom_call_target="tpu_custom_call" | custom-call | flops 553648128 | bytes 6000000 | tf_op jit(solution)/shard_map/weights/pallas_call | solution.py:317
  91.3 2.0 %collective-permute-done.20 = bf16[72,1024]{1,0:T(8,128)(2,1)S(1)} collective-permute-done((bf16[72,1024]{1,0:T(8,128)(2,1)S(1)}, bf16[72,1024]{1,0:T(8,128)(2,1)S(1)}, u32[]{:S(2)}, u32[]{:S(2)}) %collective-permute-start.20) | collective-permute-done | bytes 147488 | tf_op jit(solution)/shard_map/ppermute | solution.py:206
  93.3 3.6 %weights.5 = (bf16[8,352,1024]{2,1,0:T(8,128)(2,1)}, bf16[8,352,1024]{2,1,0:T(8,128)(2,1)}, bf16[8,352,1024]{2,1,0:T(8,128)(2,1)}) custom-call(bf16[8,128,1024]{2,1,0:T(8,128)(2,1)} %get-tuple-element.130.x_ref, bf16[8,128,1024]{2,1,0:T(8,128)(2,1)} %get-tuple-element.131.dy_ref, ...), custom_call_target="tpu_custom_call", output_to_operand_aliasing={{0}: (5, {}), {1}: (6, {}), {2}: (7, {})} | custom-call | flops 553648128 | bytes 6000000 | tf_op jit(solution)/shard_map/weights/pallas_call | solution.py:317
  97.0 0.1 collective-permute-start.24
  97.1 1.2 %collective-permute-start.23 = (bf16[72,1024]{1,0:T(8,128)(2,1)S(1)}, bf16[72,1024]{1,0:T(8,128)(2,1)S(1)}, u32[]{:S(2)}, u32[]{:S(2)}) collective-permute-start(bf16[72,1024]{1,0:T(8,128)(2,1)S(1)} %fusion.1), channel_id=1, source_target_pairs={{0,8},{4,12},{8,0},{12,4},{1,9},{5,13},{9,1},{13,5},{2,10},{6,14},... | collective-permute-start | bytes 442376 | tf_op jit(solution)/shard_map/ppermute | solution.py:203
  98.3 3.6 %weights.6 = (bf16[8,352,1024]{2,1,0:T(8,128)(2,1)}, bf16[8,352,1024]{2,1,0:T(8,128)(2,1)}, bf16[8,352,1024]{2,1,0:T(8,128)(2,1)}) custom-call(bf16[8,128,1024]{2,1,0:T(8,128)(2,1)} %get-tuple-element.130.x_ref, bf16[8,128,1024]{2,1,0:T(8,128)(2,1)} %get-tuple-element.131.dy_ref, ...), custom_call_target="tpu_custom_call", output_to_operand_aliasing={{0}: (5, {}), {1}: (6, {}), {2}: (7, {})} | custom-call | flops 553648128 | bytes 6000000 | tf_op jit(solution)/shard_map/weights/pallas_call | solution.py:317
  101.9 3.6 %weights.7 = (bf16[8,352,1024]{2,1,0:T(8,128)(2,1)}, bf16[8,352,1024]{2,1,0:T(8,128)(2,1)}, bf16[8,352,1024]{2,1,0:T(8,128)(2,1)}) custom-call(bf16[8,128,1024]{2,1,0:T(8,128)(2,1)} %get-tuple-element.130.x_ref, bf16[8,128,1024]{2,1,0:T(8,128)(2,1)} %get-tuple-element.131.dy_ref, ...), custom_call_target="tpu_custom_call", output_to_operand_aliasing={{0}: (5, {}), {1}: (6, {}), {2}: (7, {})} | custom-call | flops 553648128 | bytes 6000000 | tf_op jit(solution)/shard_map/weights/pallas_call | solution.py:317
  105.6 3.0 %collective-permute-done.23 = bf16[72,1024]{1,0:T(8,128)(2,1)S(1)} collective-permute-done((bf16[72,1024]{1,0:T(8,128)(2,1)S(1)}, bf16[72,1024]{1,0:T(8,128)(2,1)S(1)}, u32[]{:S(2)}, u32[]{:S(2)}) %collective-permute-start.23) | collective-permute-done | bytes 147488 | tf_op jit(solution)/shard_map/ppermute | solution.py:203
  108.6 0.1 add_convert_fusion.2
  108.7 0.1 collective-permute-start.25
  108.8 1.3 %collective-permute-done.25 = bf16[72,1024]{1,0:T(8,128)(2,1)S(1)} collective-permute-done((bf16[72,1024]{1,0:T(8,128)(2,1)S(1)}, bf16[72,1024]{1,0:T(8,128)(2,1)S(1)}, u32[]{:S(2)}, u32[]{:S(2)}) %collective-permute-start.25) | collective-permute-done | bytes 147488 | tf_op jit(solution)/shard_map/ppermute | solution.py:200
  110.2 0.8 maximum_select_fusion
  110.9 0.7 fusion.10
  (46 shorter events, 0.5 us)
Async XLA Ops:
  0.6 1.6 %copy-start = (bf16[128,1024]{1,0:T(8,128)(2,1)S(1)}, bf16[128,1024]{1,0:T(8,128)(2,1)}, u32[]{:S(2)}) copy-start(bf16[128,1024]{1,0:T(8,128)(2,1)} %param.7) | copy-start | bytes 786436
  2.3 24.7 %collective-permute-start.9 = (bf16[72,1024]{1,0:T(8,128)(2,1)S(1)}, bf16[72,1024]{1,0:T(8,128)(2,1)S(1)}, u32[]{:S(2)}, u32[]{:S(2)}) collective-permute-start(bf16[72,1024]{1,0:T(8,128)(2,1)S(1)} %get-tuple-element.152), channel_id=1, source_target_pairs={{0,2},{2,0},{1,3},{3,1},{4,6},{6,4},{5,7},{7,5},{8,10},{10,8},{9,1... | collective-permute-start | bytes 442376 | tf_op jit(solution)/shard_map/ppermute | solution.py:206
  5.3 7.9 %collective-permute-start.6 = (bf16[72,1024]{1,0:T(8,128)(2,1)S(1)}, bf16[72,1024]{1,0:T(8,128)(2,1)S(1)}, u32[]{:S(2)}, u32[]{:S(2)}) collective-permute-start(bf16[72,1024]{1,0:T(8,128)(2,1)S(1)} %get-tuple-element.152), channel_id=1, source_target_pairs={{0,12},{4,0},{8,4},{12,8},{1,13},{5,1},{9,5},{13,9},{2,14},{6,2},{... | collective-permute-start | bytes 442376 | tf_op jit(solution)/shard_map/ppermute | solution.py:203
  8.9 12.3 %collective-permute-start.3 = (bf16[72,1024]{1,0:T(8,128)(2,1)S(1)}, bf16[72,1024]{1,0:T(8,128)(2,1)S(1)}, u32[]{:S(2)}, u32[]{:S(2)}) collective-permute-start(bf16[72,1024]{1,0:T(8,128)(2,1)S(1)} %get-tuple-element.152), channel_id=1, source_target_pairs={{0,8},{4,12},{8,0},{12,4},{1,9},{5,13},{9,1},{13,5},{2,10},{6,14},... | collective-permute-start | bytes 442376 | tf_op jit(solution)/shard_map/ppermute | solution.py:203
  8.9 12.3 %collective-permute-start = (bf16[72,1024]{1,0:T(8,128)(2,1)S(1)}, bf16[72,1024]{1,0:T(8,128)(2,1)S(1)}, u32[]{:S(2)}, u32[]{:S(2)}) collective-permute-start(bf16[72,1024]{1,0:T(8,128)(2,1)S(1)} %get-tuple-element.152), channel_id=1, source_target_pairs={{0,4},{4,8},{8,12},{12,0},{1,5},{5,9},{9,13},{13,1},{2,6},{6,10},{... | collective-permute-start | bytes 442376 | tf_op jit(solution)/shard_map/ppermute | solution.py:203
  10.9 27.5 %collective-permute-start.13 = (bf16[64,1024]{1,0:T(8,128)(2,1)S(1)}, bf16[64,1024]{1,0:T(8,128)(2,1)S(1)}, u32[]{:S(2)}, u32[]{:S(2)}) collective-permute-start(bf16[64,1024]{1,0:T(8,128)(2,1)S(1)} %get-tuple-element.75), channel_id=1, source_target_pairs={{0,2},{2,0},{1,3},{3,1},{4,6},{6,4},{5,7},{7,5},{8,10},{10,8},{9,1... | collective-permute-start | bytes 393224 | tf_op jit(solution)/shard_map/ppermute | solution.py:206
  21.3 8.3 %collective-permute-start.1 = (bf16[64,1024]{1,0:T(8,128)(2,1)S(1)}, bf16[64,1024]{1,0:T(8,128)(2,1)S(1)}, u32[]{:S(2)}, u32[]{:S(2)}) collective-permute-start(bf16[64,1024]{1,0:T(8,128)(2,1)S(1)} %get-tuple-element.75), channel_id=1, source_target_pairs={{0,4},{4,8},{8,12},{12,0},{1,5},{5,9},{9,13},{13,1},{2,6},{6,10},{... | collective-permute-start | bytes 393224 | tf_op jit(solution)/shard_map/ppermute | solution.py:203
  22.1 11.5 %collective-permute-start.4 = (bf16[64,1024]{1,0:T(8,128)(2,1)S(1)}, bf16[64,1024]{1,0:T(8,128)(2,1)S(1)}, u32[]{:S(2)}, u32[]{:S(2)}) collective-permute-start(bf16[64,1024]{1,0:T(8,128)(2,1)S(1)} %get-tuple-element.75), channel_id=1, source_target_pairs={{0,8},{4,12},{8,0},{12,4},{1,9},{5,13},{9,1},{13,5},{2,10},{6,14},... | collective-permute-start | bytes 393224 | tf_op jit(solution)/shard_map/ppermute | solution.py:203
  24.0 9.6 %collective-permute-start.7 = (bf16[64,1024]{1,0:T(8,128)(2,1)S(1)}, bf16[64,1024]{1,0:T(8,128)(2,1)S(1)}, u32[]{:S(2)}, u32[]{:S(2)}) collective-permute-start(bf16[64,1024]{1,0:T(8,128)(2,1)S(1)} %get-tuple-element.75), channel_id=1, source_target_pairs={{0,12},{4,0},{8,4},{12,8},{1,13},{5,1},{9,5},{13,9},{2,14},{6,2},{... | collective-permute-start | bytes 393224 | tf_op jit(solution)/shard_map/ppermute | solution.py:203
  27.1 11.2 %collective-permute-start.10 = (bf16[3,72,1024]{2,1,0:T(8,128)(2,1)S(1)}, bf16[3,72,1024]{2,1,0:T(8,128)(2,1)S(1)}, u32[]{:S(2)}, u32[]{:S(2)}) collective-permute-start(bf16[3,72,1024]{2,1,0:T(8,128)(2,1)S(1)} %pad_maximum_fusion.6), channel_id=1, source_target_pairs={{0,2},{2,0},{1,3},{3,1},{4,6},{6,4},{5,7},{7,5},{8,10},{10,8},{9,1... | collective-permute-start | bytes 1327112 | tf_op jit(solution)/shard_map/ppermute | solution.py:206
  29.5 9.6 %collective-permute-start.11 = (bf16[4,72,1024]{2,1,0:T(8,128)(2,1)S(1)}, bf16[4,72,1024]{2,1,0:T(8,128)(2,1)S(1)}, u32[]{:S(2)}, u32[]{:S(2)}) collective-permute-start(bf16[4,72,1024]{2,1,0:T(8,128)(2,1)S(1)} %pad_maximum_fusion.2), channel_id=1, source_target_pairs={{0,1},{1,0},{2,3},{3,2},{4,5},{5,4},{6,7},{7,6},{8,9},{9,8},{10,11... | collective-permute-start | bytes 1769480 | tf_op jit(solution)/shard_map/ppermute | solution.py:200
  33.7 20.7 %collective-permute-start.14 = (bf16[4,64,1024]{2,1,0:T(8,128)(2,1)S(1)}, bf16[4,64,1024]{2,1,0:T(8,128)(2,1)S(1)}, u32[]{:S(2)}, u32[]{:S(2)}) collective-permute-start(bf16[4,64,1024]{2,1,0:T(8,128)(2,1)S(1)} %pad_maximum_fusion.4), channel_id=1, source_target_pairs={{0,1},{1,0},{2,3},{3,2},{4,5},{5,4},{6,7},{7,6},{8,9},{9,8},{10,11... | collective-permute-start | bytes 1572872 | tf_op jit(solution)/shard_map/ppermute | solution.py:200
  33.8 20.4 %collective-permute-start.2 = (bf16[64,1024]{1,0:T(8,128)(2,1)S(1)}, bf16[64,1024]{1,0:T(8,128)(2,1)S(1)}, u32[]{:S(2)}, u32[]{:S(2)}) collective-permute-start(bf16[64,1024]{1,0:T(8,128)(2,1)S(1)} %collective-permute-done.1), channel_id=1, source_target_pairs={{0,2},{2,0},{1,3},{3,1},{4,6},{6,4},{5,7},{7,5},{8,10},{10,8},{9,1... | collective-permute-start | bytes 393224 | tf_op jit(solution)/shard_map/ppermute | solution.py:206
  38.3 2.4 %collective-permute-start.12 = (bf16[4,72,1024]{2,1,0:T(8,128)(2,1)S(1)}, bf16[4,72,1024]{2,1,0:T(8,128)(2,1)S(1)}, u32[]{:S(2)}, u32[]{:S(2)}) collective-permute-start(bf16[4,72,1024]{2,1,0:T(8,128)(2,1)S(1)} %pad_maximum_fusion.3), channel_id=1, source_target_pairs={{0,1},{1,0},{2,3},{3,2},{4,5},{5,4},{6,7},{7,6},{8,9},{9,8},{10,11... | collective-permute-start | bytes 1769480 | tf_op jit(solution)/shard_map/ppermute | solution.py:200
  38.4 15.7 %collective-permute-start.5 = (bf16[64,1024]{1,0:T(8,128)(2,1)S(1)}, bf16[64,1024]{1,0:T(8,128)(2,1)S(1)}, u32[]{:S(2)}, u32[]{:S(2)}) collective-permute-start(bf16[64,1024]{1,0:T(8,128)(2,1)S(1)} %collective-permute-done.4), channel_id=1, source_target_pairs={{0,2},{2,0},{1,3},{3,1},{4,6},{6,4},{5,7},{7,5},{8,10},{10,8},{9,1... | collective-permute-start | bytes 393224 | tf_op jit(solution)/shard_map/ppermute | solution.py:206
  39.1 2.7 %copy-start.1 = (bf16[8,72,1024]{2,1,0:T(8,128)(2,1)}, bf16[8,72,1024]{2,1,0:T(8,128)(2,1)S(1)}, u32[]{:S(2)}) copy-start(bf16[8,72,1024]{2,1,0:T(8,128)(2,1)S(1)} %constant_dynamic-update-slice_fusion.near_ref) | copy-start | bytes 3538948
  39.1 15.1 %collective-permute-start.8 = (bf16[64,1024]{1,0:T(8,128)(2,1)S(1)}, bf16[64,1024]{1,0:T(8,128)(2,1)S(1)}, u32[]{:S(2)}, u32[]{:S(2)}) collective-permute-start(bf16[64,1024]{1,0:T(8,128)(2,1)S(1)} %collective-permute-done.7), channel_id=1, source_target_pairs={{0,2},{2,0},{1,3},{3,1},{4,6},{6,4},{5,7},{7,5},{8,10},{10,8},{9,1... | collective-permute-start | bytes 393224 | tf_op jit(solution)/shard_map/ppermute | solution.py:206
  54.3 2.0 %collective-permute-start.15 = (bf16[4,64,1024]{2,1,0:T(8,128)(2,1)S(1)}, bf16[4,64,1024]{2,1,0:T(8,128)(2,1)S(1)}, u32[]{:S(2)}, u32[]{:S(2)}) collective-permute-start(bf16[4,64,1024]{2,1,0:T(8,128)(2,1)S(1)} %pad_maximum_fusion.5), channel_id=1, source_target_pairs={{0,1},{1,0},{2,3},{3,2},{4,5},{5,4},{6,7},{7,6},{8,9},{9,8},{10,11... | collective-permute-start | bytes 1572872 | tf_op jit(solution)/shard_map/ppermute | solution.py:200
  54.4 2.9 %copy-start.2 = (bf16[8,64,1024]{2,1,0:T(8,128)(2,1)}, bf16[8,64,1024]{2,1,0:T(8,128)(2,1)S(1)}, u32[]{:S(2)}) copy-start(bf16[8,64,1024]{2,1,0:T(8,128)(2,1)S(1)} %constant_dynamic-update-slice_fusion.6.near_ref) | copy-start | bytes 3145732
  75.3 4.4 %copy-start.3 = (bf16[8,72,1024]{2,1,0:T(8,128)(2,1)S(1)}, bf16[8,72,1024]{2,1,0:T(8,128)(2,1)}, u32[]{:S(2)}) copy-start(bf16[8,72,1024]{2,1,0:T(8,128)(2,1)} %get-tuple-element.89) | copy-start | bytes 3538948
  76.8 2.1 %collective-permute-start.16 = (bf16[4,72,1024]{2,1,0:T(8,128)(2,1)S(1)}, bf16[4,72,1024]{2,1,0:T(8,128)(2,1)S(1)}, u32[]{:S(2)}, u32[]{:S(2)}) collective-permute-start(bf16[4,72,1024]{2,1,0:T(8,128)(2,1)S(1)} %get-tuple-element.145), channel_id=1, source_target_pairs={{0,1},{1,0},{2,3},{3,2},{4,5},{5,4},{6,7},{7,6},{8,9},{9,8},{10,11... | collective-permute-start | bytes 1769480 | tf_op jit(solution)/shard_map/ppermute | solution.py:200
  77.0 2.7 %collective-permute-start.17 = (bf16[4,72,1024]{2,1,0:T(8,128)(2,1)S(1)}, bf16[4,72,1024]{2,1,0:T(8,128)(2,1)S(1)}, u32[]{:S(2)}, u32[]{:S(2)}) collective-permute-start(bf16[4,72,1024]{2,1,0:T(8,128)(2,1)S(1)} %get-tuple-element.146), channel_id=1, source_target_pairs={{0,1},{1,0},{2,3},{3,2},{4,5},{5,4},{6,7},{7,6},{8,9},{9,8},{10,11... | collective-permute-start | bytes 1769480 | tf_op jit(solution)/shard_map/ppermute | solution.py:200
  80.2 6.8 %collective-permute-start.21 = (bf16[72,1024]{1,0:T(8,128)(2,1)S(1)}, bf16[72,1024]{1,0:T(8,128)(2,1)S(1)}, u32[]{:S(2)}, u32[]{:S(2)}) collective-permute-start(bf16[72,1024]{1,0:T(8,128)(2,1)S(1)} %get-tuple-element.148), channel_id=1, source_target_pairs={{0,2},{2,0},{1,3},{3,1},{4,6},{6,4},{5,7},{7,5},{8,10},{10,8},{9,1... | collective-permute-start | bytes 442376 | tf_op jit(solution)/shard_map/ppermute | solution.py:206
  80.8 21.1 %collective-permute-start.18 = (bf16[72,1024]{1,0:T(8,128)(2,1)S(1)}, bf16[72,1024]{1,0:T(8,128)(2,1)S(1)}, u32[]{:S(2)}, u32[]{:S(2)}) collective-permute-start(bf16[72,1024]{1,0:T(8,128)(2,1)S(1)} %get-tuple-element.147), channel_id=1, source_target_pairs={{0,2},{2,0},{1,3},{3,1},{4,6},{6,4},{5,7},{7,5},{8,10},{10,8},{9,1... | collective-permute-start | bytes 442376 | tf_op jit(solution)/shard_map/ppermute | solution.py:206
  82.3 11.0 %collective-permute-start.20 = (bf16[72,1024]{1,0:T(8,128)(2,1)S(1)}, bf16[72,1024]{1,0:T(8,128)(2,1)S(1)}, u32[]{:S(2)}, u32[]{:S(2)}) collective-permute-start(bf16[72,1024]{1,0:T(8,128)(2,1)S(1)} %get-tuple-element.149), channel_id=1, source_target_pairs={{0,2},{2,0},{1,3},{3,1},{4,6},{6,4},{5,7},{7,5},{8,10},{10,8},{9,1... | collective-permute-start | bytes 442376 | tf_op jit(solution)/shard_map/ppermute | solution.py:206
  82.8 14.2 %collective-permute-start.19 = (bf16[72,1024]{1,0:T(8,128)(2,1)S(1)}, bf16[72,1024]{1,0:T(8,128)(2,1)S(1)}, u32[]{:S(2)}, u32[]{:S(2)}) collective-permute-start(bf16[72,1024]{1,0:T(8,128)(2,1)S(1)} %get-tuple-element.150), channel_id=1, source_target_pairs={{0,2},{2,0},{1,3},{3,1},{4,6},{6,4},{5,7},{7,5},{8,10},{10,8},{9,1... | collective-permute-start | bytes 442376 | tf_op jit(solution)/shard_map/ppermute | solution.py:206
  87.0 18.6 %collective-permute-start.22 = (bf16[72,1024]{1,0:T(8,128)(2,1)S(1)}, bf16[72,1024]{1,0:T(8,128)(2,1)S(1)}, u32[]{:S(2)}, u32[]{:S(2)}) collective-permute-start(bf16[72,1024]{1,0:T(8,128)(2,1)S(1)} %fusion), channel_id=1, source_target_pairs={{0,12},{4,0},{8,4},{12,8},{1,13},{5,1},{9,5},{13,9},{2,14},{6,2},{... | collective-permute-start | bytes 442376 | tf_op jit(solution)/shard_map/ppermute | solution.py:203
  97.0 8.6 %collective-permute-start.24 = (bf16[72,1024]{1,0:T(8,128)(2,1)S(1)}, bf16[72,1024]{1,0:T(8,128)(2,1)S(1)}, u32[]{:S(2)}, u32[]{:S(2)}) collective-permute-start(bf16[72,1024]{1,0:T(8,128)(2,1)S(1)} %fusion.2), channel_id=1, source_target_pairs={{0,4},{4,8},{8,12},{12,0},{1,5},{5,9},{9,13},{13,1},{2,6},{6,10},{... | collective-permute-start | bytes 442376 | tf_op jit(solution)/shard_map/ppermute | solution.py:203
  97.1 11.5 %collective-permute-start.23 = (bf16[72,1024]{1,0:T(8,128)(2,1)S(1)}, bf16[72,1024]{1,0:T(8,128)(2,1)S(1)}, u32[]{:S(2)}, u32[]{:S(2)}) collective-permute-start(bf16[72,1024]{1,0:T(8,128)(2,1)S(1)} %fusion.1), channel_id=1, source_target_pairs={{0,8},{4,12},{8,0},{12,4},{1,9},{5,13},{9,1},{13,5},{2,10},{6,14},... | collective-permute-start | bytes 442376 | tf_op jit(solution)/shard_map/ppermute | solution.py:203
  108.7 1.4 %collective-permute-start.25 = (bf16[72,1024]{1,0:T(8,128)(2,1)S(1)}, bf16[72,1024]{1,0:T(8,128)(2,1)S(1)}, u32[]{:S(2)}, u32[]{:S(2)}) collective-permute-start(bf16[72,1024]{1,0:T(8,128)(2,1)S(1)} %add_convert_fusion.2), channel_id=1, source_target_pairs={{0,1},{1,0},{2,3},{3,2},{4,5},{5,4},{6,7},{7,6},{8,9},{9,8},{10,11... | collective-permute-start | bytes 442376 | tf_op jit(solution)/shard_map/ppermute | solution.py:200

commit v3 on v2

v3 whole, which is shorter than its diff:
```python
import functools

import jax
import jax.numpy as jnp
from jax import lax
from jax.experimental import pallas as pl
from jax.experimental.pallas import tpu as pltpu
from jax.sharding import PartitionSpec as P

MOST = 16
BF16, F32 = jnp.bfloat16, jnp.float32
LAST = (((1,), (1,)), ((), ()))
LEAD = (((0,), (0,)), ((), ()))
VMEM_BYTES = 12 * 1024 * 1024


def cost(micros):
    return pl.CostEstimate(flops=1000, bytes_accessed=int(micros * 3_000_000), transcendentals=0)


def dot(a, b, dims):
    return lax.dot_general(a, b, dims, preferred_element_type=F32)


def iota(shape, dim):
    return lax.broadcasted_iota(jnp.int32, shape, dim)


def ranks_and_probs(first, meta, span, count):
    sources, height, tokens = meta.shape
    kinds = height // 2
    wanted = ((first + span * iota((count, tokens), 0)) >> 1).astype(F32)
    named, weight = [], []
    for source in range(sources):
        entry = meta[source].astype(F32)
        hit = jnp.zeros((count, tokens), F32)
        prob = jnp.zeros((count, tokens), F32)
        for kind in range(kinds):
            same = entry[kind : kind + 1] == wanted
            hit = jnp.where(same, 1.0, hit)
            prob = jnp.where(same, entry[kinds + kind : kinds + kind + 1], prob)
        named.append(hit)
        weight.append(prob)
    named = jnp.concatenate(named)
    before = (iota((tokens, tokens), 0) < iota((tokens, tokens), 1)).astype(F32).astype(BF16)
    rank = jnp.dot(named.astype(BF16), before, preferred_element_type=F32)
    return jnp.where(named > 0, rank, -1.0), jnp.concatenate(weight)


def slot_matrix(rank):
    count, tokens = rank.shape
    wide = jnp.broadcast_to(rank[:, None, :], (count, MOST, tokens)).reshape(count * MOST, tokens)
    place = (iota((count * MOST, tokens), 0) & (MOST - 1)).astype(F32)
    return jnp.where(wide == place, 1.0, 0.0).astype(BF16)


def select(rank, near, far, rows_ref):
    count, _, features = rows_ref.shape
    sources = near.shape[0]
    half = rank.shape[1] // 2
    for source in range(sources):
        pick = slot_matrix(rank[source * count : (source + 1) * count])
        both = jnp.concatenate([near[source, :half], far[source, :half]], axis=0)
        rows = jnp.dot(pick, both, preferred_element_type=F32).astype(BF16)
        rows_ref[:, source * MOST : (source + 1) * MOST, :] = rows.reshape(count, MOST, features)


def select_tokens(span, kinds, where_ref, near_ref, far_ref, rows_ref, rank_ref, weight_ref, meta_ref):
    tokens = rank_ref.shape[1]
    half, per_row = tokens // 2, near_ref.shape[2] // tokens
    lines = []
    for number in range(2 * kinds):
        at, part = half + number // per_row, number % per_row
        lines.append(near_ref[:, at : at + 1, part * tokens : (part + 1) * tokens].astype(F32))
    meta = jnp.concatenate(lines, axis=1)
    rank, weight = ranks_and_probs(where_ref[0], meta, span, rows_ref.shape[0])
    rank_ref[...] = rank
    weight_ref[...] = weight
    meta_ref[...] = meta
    select(rank, near_ref, far_ref, rows_ref)


def select_cotangents(where_ref, rank_ref, near_ref, far_ref, rows_ref):
    select(rank_ref[...], near_ref, far_ref, rows_ref)


def joined(refs, index):
    return jnp.concatenate([ref[index] for ref in refs], axis=0)


def each(count, body):
    def step(index, carry):
        body(index)
        return carry

    lax.fori_loop(0, count, step, 0, unroll=2 if count % 2 == 0 else 1)


def forward_kernel(where_ref, wg_ref, wu_ref, *refs):
    rows_refs, (gate_ref, up_ref) = refs[:-2], refs[-2:]

    def body(expert):
        rows = joined(rows_refs, expert)
        gate_ref[expert] = dot(wg_ref[expert], rows, LAST)
        up_ref[expert] = dot(wu_ref[expert], rows, LAST)

    each(gate_ref.shape[0], body)


def backward_kernel(groups, where_ref, wg_ref, wu_ref, wd_ref, gate_ref, up_ref, *refs):
    rank_refs, weight_refs, rows_refs = refs[:groups], refs[groups : 2 * groups], refs[2 * groups : 3 * groups]
    dgate_ref, dup_ref, gated_ref, input_ref, prob_ref = refs[3 * groups :]
    count, slots, _ = input_ref.shape
    sources, tokens = prob_ref.shape[1:]
    total = sources * count
    rank = joined(rank_refs, ...).astype(BF16)
    weight = joined(weight_refs, ...).astype(BF16)
    place = (iota((tokens, slots), 1) & (MOST - 1)).astype(F32)
    row, lane = iota((total, slots), 0), iota((total, slots), 1)
    block = jnp.where(iota((sources, slots), 0) == iota((sources, slots), 1) // MOST, 1.0, 0.0).astype(BF16)

    def body(expert):
        spread = jnp.where(row == (lane // MOST) * count + expert, 1.0, 0.0).astype(BF16)
        holds = dot(rank, spread, LEAD) == place
        scale = jnp.sum(jnp.where(holds, dot(weight, spread, LEAD), 0.0), axis=0, keepdims=True)
        raw = dot(wd_ref[expert], joined(rows_refs, expert), LAST)
        gate, up = gate_ref[expert], up_ref[expert]
        sigmoid = 1.0 / (1.0 + jnp.exp(-gate))
        active = gate * sigmoid
        hidden = active * up
        gated_ref[expert] = (scale * hidden).astype(BF16)
        prob = jnp.sum(hidden * raw, axis=0, keepdims=True)
        scaled = scale * raw
        dgate = (scaled * up * sigmoid * (1.0 + gate * (1.0 - sigmoid))).astype(BF16)
        dup = (scaled * active).astype(BF16)
        dgate_ref[expert] = dgate
        dup_ref[expert] = dup
        input_ref[expert] = (dot(dgate, wg_ref[expert], LEAD) + dot(dup, wu_ref[expert], LEAD)).astype(BF16)
        prob_ref[expert] = dot(block, jnp.where(holds, prob, 0.0).astype(BF16), LAST)

    each(count, body)


def put_back(span, base, where_ref, rank_ref, meta_ref, input_ref, prob_ref, own_ref, other_ref):
    count, _, features = input_ref.shape
    tokens = rank_ref.shape[1]
    half, per_row = tokens // 2, features // tokens
    kinds = meta_ref.shape[1] // 2
    tail = own_ref.shape[1] - half
    wanted = ((where_ref[0] + span * iota((count, tokens), 0)) >> 1).astype(F32)
    for source in range(own_ref.shape[0]):
        number = base + source
        pick = slot_matrix(rank_ref[source * count : (source + 1) * count])
        rows = input_ref[:, number * MOST : (number + 1) * MOST, :].reshape(count * MOST, features)
        part = dot(pick, rows, LEAD).astype(BF16)
        own_ref[source, :half] = part[:half]
        other_ref[source, :half] = part[half:]
        prob = prob_ref[:, number, :]
        entry = meta_ref[source]
        line = [
            jnp.sum(jnp.where(entry[kind : kind + 1] == wanted, prob, 0.0), axis=0, keepdims=True)
            for kind in range(kinds)
        ]
        flip = [pltpu.roll(jnp.broadcast_to(row, (8, tokens)), half, 1)[:1] for row in line]
        for ref, parts in ((own_ref, line), (other_ref, flip)):
            lines = [jnp.concatenate(parts[at : at + per_row], axis=1) for at in range(0, kinds, per_row)]
            lines += [jnp.zeros_like(lines[0])] * (tail - len(lines))
            ref[source, half:] = jnp.concatenate(lines, axis=0).astype(BF16)


def weights_kernel(groups, where_ref, dgate_ref, dup_ref, gated_ref, *refs):
    rows_x, rows_dy = refs[:groups], refs[groups : 2 * groups]
    targets, token_ref = refs[2 * groups : 2 * groups + 3], refs[2 * groups + 3]
    slots_ref, sems = refs[2 * groups + 4 :]
    count, depth = dgate_ref.shape[0], slots_ref.shape[0]

    def copies(expert):
        slot = lax.rem(expert, depth)
        return [
            pltpu.make_async_copy(slots_ref.at[slot, number], target.at[expert], sems.at[slot, number])
            for number, target in enumerate(targets)
        ]

    def body(expert, carry):
        @pl.when(expert >= depth)
        def _():
            for copy in copies(expert - depth):
                copy.wait()

        slot = lax.rem(expert, depth)
        x, dy = joined(rows_x, expert), joined(rows_dy, expert)
        slots_ref[slot, 0] = jnp.dot(dgate_ref[expert], x, preferred_element_type=F32).astype(BF16)
        slots_ref[slot, 1] = jnp.dot(dup_ref[expert], x, preferred_element_type=F32).astype(BF16)
        slots_ref[slot, 2] = jnp.dot(gated_ref[expert], dy, preferred_element_type=F32).astype(BF16)
        for copy in copies(expert):
            copy.start()
        return carry

    lax.fori_loop(0, count, body, 0)
    for expert in range(max(count - depth, 0), count):
        for copy in copies(expert):
            copy.wait()
    pass_on(where_ref, token_ref)


def line_sums(places, peers, keep, where_ref, own_ref, other_ref, *refs):
    hops, outs = refs[:peers], refs[peers:]
    for at, (place, out) in enumerate(zip(places, outs)):
        total = own_ref[place].astype(F32) + other_ref[place].astype(F32)
        for hop in hops:
            total = total + hop[at].astype(F32)
        out[...] = total if place == keep else total.astype(BF16)


def last_sum(where_ref, kept_ref, *refs):
    total = kept_ref[...]
    for piece in refs[:-1]:
        total = total + piece[...].astype(F32)
    refs[-1][...] = total.astype(BF16)


def in_vmem(array):
    return pltpu.with_memory_space_constraint(array, pltpu.VMEM)


def in_hbm(array):
    return pltpu.with_memory_space_constraint(array, pltpu.HBM)


def vmem_shape(shape, dtype):
    return pltpu.VMEM(shape, dtype)


def in_hbm(array):
    return pltpu.with_memory_space_constraint(array, pltpu.HBM)


def vmem_shape(shape, dtype):
    return pltpu.VMEM(shape, dtype)


def pass_on(where_ref, token_ref):
    for number in range(3):
        token_ref[number] = where_ref[number]


def load_kernel(where_ref, *refs):
    count = (len(refs) - 2) // 2
    token_ref, sems = refs[2 * count :]
    copies = [
        pltpu.make_async_copy(source, target, sems.at[number])
        for number, (source, target) in enumerate(zip(refs[:count], refs[count : 2 * count]))
    ]
    for copy in copies:
        copy.start()
    for copy in copies:
        copy.wait()
    pass_on(where_ref, token_ref)


SCALARS = pl.BlockSpec(memory_space=pltpu.SMEM)
IN_VMEM = pl.BlockSpec(memory_space=pltpu.VMEM)
TOKEN = jax.ShapeDtypeStruct((3,), jnp.int32)


def load(where, arrays):
    *held, where = pl.pallas_call(
        load_kernel,
        in_specs=[SCALARS] + [pl.BlockSpec(memory_space=pl.ANY)] * len(arrays),
        out_specs=[IN_VMEM] * len(arrays) + [SCALARS],
        out_shape=[vmem_shape(array.shape, array.dtype) for array in arrays] + [TOKEN],
        scratch_shapes=[pltpu.SemaphoreType.DMA((len(arrays),))],
        compiler_params=pltpu.CompilerParams(vmem_limit_bytes=VMEM_BYTES),
        cost_estimate=cost(7),
        name="load",
    )(where, *map(in_hbm, arrays))
    return where, held


def on_vmem(kernel, name, micros, outs, where, operands, stay=True):
    def body(where_ref, *refs):
        kernel(where_ref, *refs[:-1])
        pass_on(where_ref, refs[-1])

    *held, where = pl.pallas_call(
        body,
        in_specs=[SCALARS] + [IN_VMEM] * len(operands),
        out_specs=[IN_VMEM] * len(outs) + [SCALARS],
        out_shape=[(vmem_shape if stay else jax.ShapeDtypeStruct)(shape, dtype) for shape, dtype in outs] + [TOKEN],
        compiler_params=pltpu.CompilerParams(vmem_limit_bytes=VMEM_BYTES),
        cost_estimate=cost(micros),
        name=name,
    )(where, *map(in_vmem, operands))
    return where, held


def per_device(tokens, cotangent, probs, experts, w_gate, w_up, w_down):
    rows, features = tokens.shape
    top = experts.shape[1]
    zs, xs = lax.axis_size("expert"), lax.axis_size("blk")
    cores = lax.axis_size("tensor")
    positions = zs * xs
    half = rows // cores
    halves, _, quarter = w_gate.shape
    span = 2 if halves % 2 == 0 else 1
    count = halves // span
    hidden = span * quarter
    slots = positions * MOST
    core = lax.axis_index("tensor")
    position = lax.axis_index("expert") * xs + lax.axis_index("blk")
    kinds = 8 * pl.cdiv(top, 8)
    barrier = lax.optimization_barrier

    def swap(array):
        return lax.ppermute(array, "tensor", [(i, (i + 1) % cores) for i in range(cores)])

    def along_z(array, by):
        return lax.ppermute(array, "expert", [(i, (i + by) % zs) for i in range(zs)])

    def along_x(array, by):
        return lax.ppermute(array, "blk", [(i, (i + by) % xs) for i in range(xs)])

    def own_first(array):
        return jnp.roll(array, -core * half, axis=-1)

    experts_t = own_first(experts.T)
    probs_t = own_first(probs.T)
    meta = jnp.concatenate(
        [
            jnp.pad(experts_t.astype(BF16), ((0, kinds - top), (0, 0)), constant_values=-1.0),
            jnp.pad(probs_t, ((0, kinds - top), (0, 0))),
        ]
    ).reshape(-1, features)
    meta = jnp.pad(meta, ((0, -meta.shape[0] % 8), (0, 0)))
    own_x = jnp.concatenate([lax.dynamic_slice_in_dim(tokens, core * half, half, 0), meta])
    own_dy = lax.dynamic_slice_in_dim(cotangent, core * half, half, 0)

    wg = jnp.swapaxes(w_gate, 1, 2).reshape(count, hidden, features)
    wu = jnp.swapaxes(w_up, 1, 2).reshape(count, hidden, features)
    wd = w_down.reshape(count, hidden, features)
    where = jnp.stack([position * halves, lax.axis_index("expert"), lax.axis_index("blk")]).astype(jnp.int32)
    group = zs * MOST

    line_x = [along_z(own_x, d) for d in range(1, zs)]
    first_x = [along_x(own_x, c) for c in range(1, xs)]
    first_dy = [along_x(own_dy, c) for c in range(1, xs)]
    where, own_x = barrier((where, own_x))
    where, (wg, wu, wd) = load(where, (wg, wu, wd))
    where, line_x, first_x, first_dy, own_dy = barrier((where, line_x, first_x, first_dy, own_dy))

    line_dy = [along_z(own_dy, d) for d in range(1, zs)]
    rest = jnp.stack(line_x)
    more = [along_x(rest, c) for c in range(1, xs)]
    rows_x, ranks, weight, metas = [], [], [], []

    def take_tokens(where, near, far):
        outs = [((count, group, features), BF16), ((zs * count, rows), F32), ((zs * count, rows), F32),
                ((zs, 2 * kinds, rows), F32)]
        where, results = on_vmem(functools.partial(select_tokens, span, kinds), "select_tokens", 2, outs, where, (near, far))
        for held, result in zip((rows_x, ranks, weight, metas), results):
            held.append(result)
        return where

    def take_cotangents(where, near, far):
        outs = [((count, group, features), BF16)]
        return on_vmem(select_cotangents, "select_cotangents", 2, outs, where, (ranks[len(rows_dy)], near, far))

    near = jnp.concatenate([own_x[None], rest])
    where = take_tokens(where, near, swap(near))
    where, line_dy, more = barrier((where, line_dy, more))
    groups_x = [jnp.concatenate([a[None], b]) for a, b in zip(first_x, more)]

    rest = jnp.stack(line_dy)
    more = [along_x(rest, c) for c in range(1, xs)]
    rows_dy = []
    for near in groups_x:
        where = take_tokens(where, near, swap(near))
    where, (gate, up) = on_vmem(forward_kernel, "forward", 5, [((count, hidden, slots), F32)] * 2, where, (wg, wu, *rows_x))
    near = jnp.concatenate([own_dy[None], rest])
    where, got = take_cotangents(where, near, swap(near))
    rows_dy += got
    where, more = barrier((where, more))
    for near in [jnp.concatenate([a[None], b]) for a, b in zip(first_dy, more)]:
        where, got = take_cotangents(where, near, swap(near))
        rows_dy += got

    outs = [((count, hidden, slots), BF16)] * 3 + [((count, slots, features), BF16), ((count, positions, rows), F32)]
    where, (dgate, dup, gated, rows_in, prob) = on_vmem(
        functools.partial(backward_kernel, xs), "backward", 9, outs, where,
        (wg, wu, wd, gate, up, *ranks, *weight, *rows_dy))
    back = half + 8 * pl.cdiv(kinds * rows, 8 * features)
    chip = [None] * xs
    for c in list(range(1, xs)) + [0]:
        where, (own, other) = on_vmem(
            functools.partial(put_back, span, c * zs), "put_back", 2, [((zs, back, features), BF16)] * 2, where,
            (ranks[c], metas[c], rows_in, prob), False)
        chip[c] = own, swap(other)
    sums = [None] + [(own.astype(F32) + other.astype(F32)).astype(BF16) for own, other in chip[1:]]
    saved = (dgate, dup, gated, *rows_x, *rows_dy)

    def weights(where):
        depth = min(count, 2)
        *grads, where = pl.pallas_call(
            functools.partial(weights_kernel, xs),
            in_specs=[SCALARS] + [IN_VMEM] * len(saved),
            out_specs=[pl.BlockSpec(memory_space=pl.ANY)] * 3 + [SCALARS],
            out_shape=[jax.ShapeDtypeStruct((count, hidden, features), BF16)] * 3 + [TOKEN],
            scratch_shapes=[pltpu.VMEM((depth, 3, hidden, features), BF16), pltpu.SemaphoreType.DMA((depth, 3))],
            compiler_params=pltpu.CompilerParams(vmem_limit_bytes=VMEM_BYTES),
            cost_estimate=cost(9),
            name="weights",
        )(where, *map(in_vmem, saved))
        return where, grads

    turn = list(range(1, zs)) + [0]
    turns = [turn[: zs // 2], turn[zs // 2 :]]
    hops = [[along_x(jnp.stack([sums[c][d] for d in some]), -c) for c in range(1, xs)] for some in turns]
    where, grads = weights(where)
    pieces = []
    for some, hop in zip(turns, hops):
        outs = [((back, features), BF16 if d else F32) for d in some]
        where, parts = on_vmem(functools.partial(line_sums, some, len(hop), 0), "line_sums", 1, outs, where,
                               (*chip[0], *hop), False)
        pieces += [along_z(part, -d) if d else part for d, part in zip(some, parts)]
    where, (mine,) = on_vmem(last_sum, "last_sum", 1, [((back, features), BF16)], where, pieces[::-1], False)
    theirs = swap(mine)

    def tokens_of(piece):
        return piece[:half]

    def probs_of(piece):
        return piece[half:].reshape(-1)[: kinds * rows].reshape(kinds, rows)[:top, :half].astype(F32)

    def in_order(part, axis):
        both = part(mine), part(theirs)
        return jnp.where(core == 0, jnp.concatenate(both, axis), jnp.concatenate(both[::-1], axis))

    grad_tokens = in_order(tokens_of, 0)
    grad_probs = in_order(probs_of, 1).T
    grad_gate, grad_up, grad_down = grads
    shape = (halves, quarter, features)
    return (
        grad_tokens,
        grad_probs,
        jnp.swapaxes(grad_gate.reshape(shape), 1, 2),
        jnp.swapaxes(grad_up.reshape(shape), 1, 2),
        grad_down.reshape(shape),
    )


def solution(mesh):
    return jax.shard_map(
        per_device,
        mesh=mesh,
        in_specs=(
            P(("groups", "expert", "blk"), None),
            P(("groups", "expert", "blk"), None),
            P(("groups", "expert", "blk"), None),
            P(("groups", "expert", "blk"), None),
            P(("expert", "blk"), None, "tensor"),
            P(("expert", "blk"), None, "tensor"),
            P(("expert", "blk"), "tensor", None),
        ),
        out_specs=(
            P(("groups", "expert", "blk"), None),
            P(("groups", "expert", "blk"), None),
            P(("groups", "expert", "blk"), None, "tensor"),
            P(("groups", "expert", "blk"), None, "tensor"),
            P(("groups", "expert", "blk"), "tensor", None),
        ),
        check_vma=False,
    )
```

time: 112 us -> 99.2 us (0.89)
  Pallas kernels: 44.9 us -> 41.3 us
  other arithmetic: 6.83 us -> 3.7 us
  waiting for transfers between devices: 32 us -> 28.9 us
  local copies, waits for them, and re-layouts: 2.68 us -> 1.07 us
    ppermute x10 -> x6, waiting for transfers between devices: 8.47 us -> 4.65 us  [along_x(): return lax.ppermute(array, 'blk', [(i, (i + by) % xs) for i in range(xs)])]
    pallas_call x6 -> x13, Pallas kernels: 44.9 us -> 41.3 us  [the longest x11 24.2 us: on_vmem(): pl.pallas_call(body, in_specs=[SCALARS] + [IN_VMEM] * len(operands), out_...]
    ppermute x10 -> x6, starting transfers between devices: 11.1 us -> 7.92 us  [along_x(): return lax.ppermute(array, 'blk', [(i, (i + by) % xs) for i in range(xs)])]
    ppermute x9, waiting for transfers between devices: 18 us -> 20.8 us  [along_z(): lax.ppermute(array, 'expert', [(i, (i + by) % zs) for i in range(zs)])]
    ppermute x7, waiting for transfers between devices: 5.51 us -> 3.41 us  [swap(): lax.ppermute(array, 'tensor', [(i, (i + 1) % cores) for i in range(cores)])]
    concatenate x2 -> x4, other arithmetic: 2.22 us -> 0.21 us  [the longest x1 0.08 us: per_device(): near = jnp.concatenate([own_x[None], rest])]
    slice x1, local copies, waits for them, and re-layouts: 1.44 us -> 0.02 us  [per_device(): sums[c][d]]
    ppermute x9, starting transfers between devices: 12.3 us -> 13.7 us  [along_z(): lax.ppermute(array, 'expert', [(i, (i + by) % zs) for i in range(zs)])]
  transfers between devices with their start and end apart: 26 -> 22, of which waited for: 12 -> 9; matrix products, arithmetic and copies ran while one was open for 3% -> 1% of each run, Pallas kernels for 24% -> 28%
where the time goes in v3:
time: 99.2 us; the launch traced here: 98.9 us
  Pallas kernels  41.3 us (42%)
  waiting for transfers between devices  28.9 us (29%)
  starting transfers between devices  23.1 us (23%)
  other arithmetic  3.7 us (4%)
  local copies, waits for them, and re-layouts  1.07 us (1%)
  between operations  1.01 us (1%)
    pallas_call x11, Pallas kernels, on_vmem(): pl.pallas_call(body, in_specs=[SCALARS] + [IN_VMEM] * len(operands), out_...  24.2 us
    ppermute x9, waiting for transfers between devices, along_z(): lax.ppermute(array, 'expert', [(i, (i + by) % zs) for i in range(zs)])  20.8 us
    ppermute x9, starting transfers between devices, along_z(): lax.ppermute(array, 'expert', [(i, (i + by) % zs) for i in range(zs)])  13.7 us
    pallas_call x1, Pallas kernels, weights(): pl.pallas_call(functools.partial(weights_kernel, xs), in_specs=[SCALARS]...  9.95 us
    ppermute x6, starting transfers between devices, along_x(): return lax.ppermute(array, 'blk', [(i, (i + by) % xs) for i in range(xs)])  7.92 us
    pallas_call x1, Pallas kernels, load(): pl.pallas_call(load_kernel, in_specs=[SCALARS] + [pl.BlockSpec(memory_spa...  7.13 us
    ppermute x6, waiting for transfers between devices, along_x(): return lax.ppermute(array, 'blk', [(i, (i + by) % xs) for i in range(xs)])  4.65 us
    ppermute x7, waiting for transfers between devices, swap(): lax.ppermute(array, 'tensor', [(i, (i + 1) % cores) for i in range(cores)])  3.41 us
  transfers between devices with their start and end apart: 22, of which 9 were waited for; matrix products, arithmetic and copies ran while one was open for 1% of the time, Pallas kernels for 28%

profile of v3, /device:TPU:0, one launch (start us, length us, event | category | flops | bytes accessed | tf_op | source)
XLA Modules:
  0.0 98.9 jit_solution(2221214331786673644)
XLA Ops:
  0.6 0.0 copy-start
  0.7 0.8 fusion.8
  1.5 0.8 fusion.6
  2.3 3.0 %collective-permute-start.3 = (bf16[72,1024]{1,0:T(8,128)(2,1)S(1)}, bf16[72,1024]{1,0:T(8,128)(2,1)S(1)}, u32[]{:S(2)}, u32[]{:S(2)}) collective-permute-start(bf16[72,1024]{1,0:T(8,128)(2,1)S(1)} %fusion.1), channel_id=1, source_target_pairs={{0,2},{2,0},{1,3},{3,1},{4,6},{6,4},{5,7},{7,5},{8,10},{10,8},{9,1... | collective-permute-start | bytes 442376 | tf_op jit(solution)/shard_map/ppermute | solution.py:321
  5.3 3.6 %collective-permute-start.2 = (bf16[72,1024]{1,0:T(8,128)(2,1)S(1)}, bf16[72,1024]{1,0:T(8,128)(2,1)S(1)}, u32[]{:S(2)}, u32[]{:S(2)}) collective-permute-start(bf16[72,1024]{1,0:T(8,128)(2,1)S(1)} %fusion.1), channel_id=1, source_target_pairs={{0,12},{4,0},{8,4},{12,8},{1,13},{5,1},{9,5},{13,9},{2,14},{6,2},{... | collective-permute-start | bytes 442376 | tf_op jit(solution)/shard_map/ppermute | solution.py:318
  8.9 1.0 %collective-permute-start = (bf16[72,1024]{1,0:T(8,128)(2,1)S(1)}, bf16[72,1024]{1,0:T(8,128)(2,1)S(1)}, u32[]{:S(2)}, u32[]{:S(2)}) collective-permute-start(bf16[72,1024]{1,0:T(8,128)(2,1)S(1)} %fusion.1), channel_id=1, source_target_pairs={{0,4},{4,8},{8,12},{12,0},{1,5},{5,9},{9,13},{13,1},{2,6},{6,10},{... | collective-permute-start | bytes 442376 | tf_op jit(solution)/shard_map/ppermute | solution.py:318
  9.9 0.9 constant_dynamic-slice_fusion
  10.9 0.6 collective-permute-start.4
  11.5 0.1 pad_add_fusion.where_ref
  11.5 7.1 %load.1 = (bf16[8,352,1024]{2,1,0:T(8,128)(2,1)S(1)}, bf16[8,352,1024]{2,1,0:T(8,128)(2,1)S(1)}, bf16[8,352,1024]{2,1,0:T(8,128)(2,1)S(1)}, s32[3]{0:T(128)S(1)}) custom-call(s32[3]{0:T(128)S(1)} %pad_add_fusion.where_ref, bf16[8,352,1024]{2,1,0:T(8,128)(2,1)} %bitcast.33, bf16[8,352,1024]{2,1,0:T(8,128)(2,1)} %bitcast.34, bf16[8,352,1024]{2,1,0:T(8,128)(2,1)} %bitcast.35), custom_call_target="tpu_custom_call" | custom-call | flops 1000 | bytes 21000000 | tf_op jit(solution)/shard_map/load/pallas_call | solution.py:267
  18.7 0.0 collective-permute-done.2
  18.7 2.5 %collective-permute-done.1 = bf16[72,1024]{1,0:T(8,128)(2,1)S(1)} collective-permute-done((bf16[72,1024]{1,0:T(8,128)(2,1)S(1)}, bf16[72,1024]{1,0:T(8,128)(2,1)S(1)}, u32[]{:S(2)}, u32[]{:S(2)}) %collective-permute-start.1) | collective-permute-done | bytes 147488 | tf_op jit(solution)/shard_map/ppermute | solution.py:318
  21.2 0.1 pad_maximum_fusion.refs_0_
  21.3 0.1 collective-permute-start.5
  21.4 0.1 pad_maximum_fusion.4
  21.5 0.6 collective-permute-start.9
  22.1 1.4 %collective-permute-start.8 = (bf16[64,1024]{1,0:T(8,128)(2,1)S(1)}, bf16[64,1024]{1,0:T(8,128)(2,1)S(1)}, u32[]{:S(2)}, u32[]{:S(2)}) collective-permute-start(bf16[64,1024]{1,0:T(8,128)(2,1)S(1)} %constant_dynamic-slice_fusion), channel_id=1, source_target_pairs={{0,12},{4,0},{8,4},{12,8},{1,13},{5,1},{9,5},{13,9},{2,14},{6,2},{... | collective-permute-start | bytes 393224 | tf_op jit(solution)/shard_map/ppermute | solution.py:318
  23.5 1.4 %collective-permute-start.7 = (bf16[64,1024]{1,0:T(8,128)(2,1)S(1)}, bf16[64,1024]{1,0:T(8,128)(2,1)S(1)}, u32[]{:S(2)}, u32[]{:S(2)}) collective-permute-start(bf16[64,1024]{1,0:T(8,128)(2,1)S(1)} %constant_dynamic-slice_fusion), channel_id=1, source_target_pairs={{0,8},{4,12},{8,0},{12,4},{1,9},{5,13},{9,1},{13,5},{2,10},{6,14},... | collective-permute-start | bytes 393224 | tf_op jit(solution)/shard_map/ppermute | solution.py:318
  24.8 2.0 %collective-permute-start.6 = (bf16[64,1024]{1,0:T(8,128)(2,1)S(1)}, bf16[64,1024]{1,0:T(8,128)(2,1)S(1)}, u32[]{:S(2)}, u32[]{:S(2)}) collective-permute-start(bf16[64,1024]{1,0:T(8,128)(2,1)S(1)} %constant_dynamic-slice_fusion), channel_id=1, source_target_pairs={{0,4},{4,8},{8,12},{12,0},{1,5},{5,9},{9,13},{13,1},{2,6},{6,10},{... | collective-permute-start | bytes 393224 | tf_op jit(solution)/shard_map/ppermute | solution.py:318
  26.9 1.1 %select_tokens.2 = (bf16[8,64,1024]{2,1,0:T(8,128)(2,1)S(1)}, f32[32,128]{1,0:T(8,128)S(1)}, f32[32,128]{1,0:T(8,128)S(1)}, f32[4,16,128]{2,1,0:T(8,128)S(1)}, s32[3]{0:T(128)S(1)}) custom-call(s32[3]{0:T(128)S(1)} %get-tuple-element.67.where_ref, bf16[4,72,1024]{2,1,0:T(8,128)(2,1)S(1)} %pad_maximum_fusion.refs_0_, ...), custom_call_target="tpu_custom_call" | custom-call | flops 1000 | bytes 6000000 | tf_op jit(solution)/shard_map/select_tokens/pallas_call | solution.py:285
  28.0 0.0 collective-permute-done.8
  28.0 9.1 %collective-permute-done.7 = bf16[64,1024]{1,0:T(8,128)(2,1)S(1)} collective-permute-done((bf16[64,1024]{1,0:T(8,128)(2,1)S(1)}, bf16[64,1024]{1,0:T(8,128)(2,1)S(1)}, u32[]{:S(2)}, u32[]{:S(2)}) %collective-permute-start.7) | collective-permute-done | bytes 131104 | tf_op jit(solution)/shard_map/ppermute | solution.py:318
  37.1 0.0 collective-permute-done.6
  37.1 0.0 collective-permute-done.9
  37.1 0.1 pad_maximum_fusion.1.refs_0_
  37.2 0.1 collective-permute-start.10
  37.3 0.1 pad_maximum_fusion.2.refs_1_
  37.4 0.6 collective-permute-start.11
  38.0 1.6 %collective-permute-start.12 = (bf16[3,64,1024]{2,1,0:T(8,128)(2,1)S(1)}, bf16[3,64,1024]{2,1,0:T(8,128)(2,1)S(1)}, u32[]{:S(2)}, u32[]{:S(2)}) collective-permute-start(bf16[3,64,1024]{2,1,0:T(8,128)(2,1)S(1)} %pad_maximum_fusion.5), channel_id=1, source_target_pairs={{0,2},{2,0},{1,3},{3,1},{4,6},{6,4},{5,7},{7,5},{8,10},{10,8},{9,1... | collective-permute-start | bytes 1179656 | tf_op jit(solution)/shard_map/ppermute | solution.py:321
  39.5 0.0 collective-permute-done.10.refs_1_
  39.5 1.1 %select_tokens.3 = (bf16[8,64,1024]{2,1,0:T(8,128)(2,1)S(1)}, f32[32,128]{1,0:T(8,128)S(1)}, f32[32,128]{1,0:T(8,128)S(1)}, f32[4,16,128]{2,1,0:T(8,128)S(1)}, s32[3]{0:T(128)S(1)}) custom-call(s32[3]{0:T(128)S(1)} %get-tuple-element.74.where_ref, bf16[4,72,1024]{2,1,0:T(8,128)(2,1)S(1)} %pad_maximum_fusion.1.refs_0_, ...), custom_call_target="tpu_custom_call" | custom-call | flops 1000 | bytes 6000000 | tf_op jit(solution)/shard_map/select_tokens/pallas_call | solution.py:285
  40.7 4.4 %forward.1 = (f32[8,352,128]{2,1,0:T(8,128)S(1)}, f32[8,352,128]{2,1,0:T(8,128)S(1)}, s32[3]{0:T(128)S(1)}) custom-call(s32[3]{0:T(128)S(1)} %get-tuple-element.77.where_ref, bf16[8,352,1024]{2,1,0:T(8,128)(2,1)S(1)} %get-tuple-element.78.refs_0_, bf16[8,352,1024]{2,1,0:T(8,128)(2,1)S(1)} %get-tuple-element.79.refs_1_, ...), custom_call_target="tpu_custom_call" | custom-call | flops 1000 | bytes 15000000 | tf_op jit(solution)/shard_map/forward/pallas_call | solution.py:285
  45.1 0.0 collective-permute-done.11.refs_2_
  45.1 1.4 %select_cotangents.2 = (bf16[8,64,1024]{2,1,0:T(8,128)(2,1)S(1)}, s32[3]{0:T(128)S(1)}) custom-call(s32[3]{0:T(128)S(1)} %get-tuple-element.82.where_ref, f32[32,128]{1,0:T(8,128)S(1)} %get-tuple-element.83.refs_0_.refs_5_, bf16[4,64,1024]{2,1,0:T(8,128)(2,1)S(1)} %pad_maximum_fusion.2.refs_1_, bf16[4,64,1024]{2,1,0:T(8,128)(2,1)S(1)} %collective-permute-done.11.refs_2_), custom_call_target="tpu_custom_call" | custom-call | flops 1000 | bytes 6000000 | tf_op jit(solution)/shard_map/select_cotangents/pallas_call | solution.py:285
  46.5 2.6 %collective-permute-done.12 = bf16[3,64,1024]{2,1,0:T(8,128)(2,1)S(1)} collective-permute-done((bf16[3,64,1024]{2,1,0:T(8,128)(2,1)S(1)}, bf16[3,64,1024]{2,1,0:T(8,128)(2,1)S(1)}, u32[]{:S(2)}, u32[]{:S(2)}) %collective-permute-start.12) | collective-permute-done | bytes 393248 | tf_op jit(solution)/shard_map/ppermute | solution.py:321
  49.1 0.1 collective-permute-start.13
  49.2 1.9 %collective-permute-done.13.refs_2_ = bf16[4,64,1024]{2,1,0:T(8,128)(2,1)S(1)} collective-permute-done((bf16[4,64,1024]{2,1,0:T(8,128)(2,1)S(1)}, bf16[4,64,1024]{2,1,0:T(8,128)(2,1)S(1)}, u32[]{:S(2)}, u32[]{:S(2)}) %collective-permute-start.13) | collective-permute-done | bytes 524320 | tf_op jit(solution)/shard_map/ppermute | solution.py:315
  51.1 1.4 %select_cotangents.3 = (bf16[8,64,1024]{2,1,0:T(8,128)(2,1)S(1)}, s32[3]{0:T(128)S(1)}) custom-call(s32[3]{0:T(128)S(1)} %get-tuple-element.88.where_ref, f32[32,128]{1,0:T(8,128)S(1)} %get-tuple-element.89.refs_0_.refs_6_, bf16[4,64,1024]{2,1,0:T(8,128)(2,1)S(1)} %pad_maximum_fusion.3.refs_1_, bf16[4,64,1024]{2,1,0:T(8,128)(2,1)S(1)} %collective-permute-done.13.refs_2_), custom_call_target="tpu_custom_call" | custom-call | flops 1000 | bytes 6000000 | tf_op jit(solution)/shard_map/select_cotangents/pallas_call | solution.py:285
  52.5 8.8 %backward.1 = (bf16[8,352,128]{2,1,0:T(8,128)(2,1)S(1)}, bf16[8,352,128]{2,1,0:T(8,128)(2,1)S(1)}, bf16[8,352,128]{2,1,0:T(8,128)(2,1)S(1)}, bf16[8,128,1024]{2,...) custom-call(s32[3]{0:T(128)S(1)} %get-tuple-element.92.where_ref, ...), custom_call_target="tpu_custom_call" | custom-call | flops 1000 | bytes 27000000 | tf_op jit(solution)/shard_map/backward/pallas_call | solution.py:285
  61.3 1.3 %put_back.2 = (bf16[4,72,1024]{2,1,0:T(8,128)(2,1)S(1)}, bf16[4,72,1024]{2,1,0:T(8,128)(2,1)S(1)}, s32[3]{0:T(128)S(1)}) custom-call(s32[3]{0:T(128)S(1)} %get-tuple-element.100.where_ref, f32[32,128]{1,0:T(8,128)S(1)} %get-tuple-element.89.refs_0_.refs_6_, f32[4,16,128]{2,1,0:T(8,128)S(1)} %get-tuple-element.101.refs_1_, ...), custom_call_target="tpu_custom_call" | custom-call | flops 1000 | bytes 6000000 | tf_op jit(solution)/shard_map/put_back/pallas_call | solution.py:285
  62.6 0.2 collective-permute-start.15
  62.8 1.3 %put_back.3 = (bf16[4,72,1024]{2,1,0:T(8,128)(2,1)S(1)}, bf16[4,72,1024]{2,1,0:T(8,128)(2,1)S(1)}, s32[3]{0:T(128)S(1)}) custom-call(s32[3]{0:T(128)S(1)} %get-tuple-element.104.where_ref, f32[32,128]{1,0:T(8,128)S(1)} %get-tuple-element.83.refs_0_.refs_5_, f32[4,16,128]{2,1,0:T(8,128)S(1)} %get-tuple-element.105.refs_1_, ...), custom_call_target="tpu_custom_call" | custom-call | flops 1000 | bytes 6000000 | tf_op jit(solution)/shard_map/put_back/pallas_call | solution.py:285
  64.1 0.4 collective-permute-start.14
  64.5 0.2 collective-permute-done.15
  64.7 0.2 add_convert_fusion
  64.9 1.6 %collective-permute-start.16 = (bf16[2,72,1024]{2,1,0:T(8,128)(2,1)S(1)}, bf16[2,72,1024]{2,1,0:T(8,128)(2,1)S(1)}, u32[]{:S(2)}, u32[]{:S(2)}) collective-permute-start(bf16[2,72,1024]{2,1,0:T(8,128)(2,1)S(1)} %stack.56), channel_id=1, source_target_pairs={{0,2},{2,0},{1,3},{3,1},{4,6},{6,4},{5,7},{7,5},{8,10},{10,8},{9,1... | collective-permute-start | bytes 884744 | tf_op jit(solution)/shard_map/ppermute | solution.py:321
  66.5 0.0 copy-start.1
  66.6 0.6 collective-permute-start.17
  67.2 10.0 %weights.1 = (bf16[8,352,1024]{2,1,0:T(8,128)(2,1)}, bf16[8,352,1024]{2,1,0:T(8,128)(2,1)}, bf16[8,352,1024]{2,1,0:T(8,128)(2,1)}, s32[3]{0:T(128)S(1)}) custom-call(s32[3]{0:T(128)S(1)} %get-tuple-element.106.where_ref, bf16[8,352,128]{2,1,0:T(8,128)(2,1)S(1)} %get-tuple-element.107.dgate_ref, bf16[8,352,128]{2,1,0:T(8,128)(2,1)S(1)} %get-tuple-element.108.dup_ref, ...), custom_call_target="tpu_custom_call" | custom-call | flops 1000 | bytes 27000000 | tf_op jit(solution)/shard_map/weights/pallas_call | solution.py:403
  77.1 0.0 collective-permute-done.14.refs_1_
  77.1 0.0 collective-permute-done.16.refs_2_
  77.1 1.1 %line_sums.2 = (bf16[72,1024]{1,0:T(8,128)(2,1)S(1)}, bf16[72,1024]{1,0:T(8,128)(2,1)S(1)}, s32[3]{0:T(128)S(1)}) custom-call(s32[3]{0:T(128)S(1)} %get-tuple-element.110.where_ref, bf16[4,72,1024]{2,1,0:T(8,128)(2,1)S(1)} %get-tuple-element.111.refs_0_, bf16[4,72,1024]{2,1,0:T(8,128)(2,1)S(1)} %collective-permute-done.14.refs_1_, ...), custom_call_target="tpu_custom_call" | custom-call | flops 1000 | bytes 3000000 | tf_op jit(solution)/shard_map/line_sums/pallas_call | solution.py:285
  78.3 2.1 %collective-permute-done.17.refs_2_ = bf16[2,72,1024]{2,1,0:T(8,128)(2,1)S(1)} collective-permute-done((bf16[2,72,1024]{2,1,0:T(8,128)(2,1)S(1)}, bf16[2,72,1024]{2,1,0:T(8,128)(2,1)S(1)}, u32[]{:S(2)}, u32[]{:S(2)}) %collective-permute-start.17) | collective-permute-done | bytes 294944 | tf_op jit(solution)/shard_map/ppermute | solution.py:321
  80.4 1.1 %line_sums.3 = (bf16[72,1024]{1,0:T(8,128)(2,1)S(1)}, f32[72,1024]{1,0:T(8,128)S(1)}, s32[3]{0:T(128)S(1)}) custom-call(s32[3]{0:T(128)S(1)} %get-tuple-element.115.where_ref, bf16[4,72,1024]{2,1,0:T(8,128)(2,1)S(1)} %get-tuple-element.111.refs_0_, bf16[4,72,1024]{2,1,0:T(8,128)(2,1)S(1)} %collective-permute-done.14.refs_1_, ...), custom_call_target="tpu_custom_call" | custom-call | flops 1000 | bytes 3000000 | tf_op jit(solution)/shard_map/line_sums/pallas_call | solution.py:285
  81.5 0.1 collective-permute-start.18
  81.6 1.3 %collective-permute-start.19 = (bf16[72,1024]{1,0:T(8,128)(2,1)S(1)}, bf16[72,1024]{1,0:T(8,128)(2,1)S(1)}, u32[]{:S(2)}, u32[]{:S(2)}) collective-permute-start(bf16[72,1024]{1,0:T(8,128)(2,1)S(1)} %get-tuple-element.119), channel_id=1, source_target_pairs={{0,8},{4,12},{8,0},{12,4},{1,9},{5,13},{9,1},{13,5},{2,10},{6,14},... | collective-permute-start | bytes 442376 | tf_op jit(solution)/shard_map/ppermute | solution.py:318
  82.9 2.8 %collective-permute-start.20 = (bf16[72,1024]{1,0:T(8,128)(2,1)S(1)}, bf16[72,1024]{1,0:T(8,128)(2,1)S(1)}, u32[]{:S(2)}, u32[]{:S(2)}) collective-permute-start(bf16[72,1024]{1,0:T(8,128)(2,1)S(1)} %get-tuple-element.120), channel_id=1, source_target_pairs={{0,12},{4,0},{8,4},{12,8},{1,13},{5,1},{9,5},{13,9},{2,14},{6,2},{... | collective-permute-start | bytes 442376 | tf_op jit(solution)/shard_map/ppermute | solution.py:318
  85.8 4.4 %collective-permute-done.18.refs_1_ = bf16[72,1024]{1,0:T(8,128)(2,1)S(1)} collective-permute-done((bf16[72,1024]{1,0:T(8,128)(2,1)S(1)}, bf16[72,1024]{1,0:T(8,128)(2,1)S(1)}, u32[]{:S(2)}, u32[]{:S(2)}) %collective-permute-start.18) | collective-permute-done | bytes 147488 | tf_op jit(solution)/shard_map/ppermute | solution.py:318
  90.2 4.8 %collective-permute-done.19.refs_2_ = bf16[72,1024]{1,0:T(8,128)(2,1)S(1)} collective-permute-done((bf16[72,1024]{1,0:T(8,128)(2,1)S(1)}, bf16[72,1024]{1,0:T(8,128)(2,1)S(1)}, u32[]{:S(2)}, u32[]{:S(2)}) %collective-permute-start.19) | collective-permute-done | bytes 147488 | tf_op jit(solution)/shard_map/ppermute | solution.py:318
  94.9 1.1 %last_sum.1 = (bf16[72,1024]{1,0:T(8,128)(2,1)S(1)}, s32[3]{0:T(128)}) custom-call(s32[3]{0:T(128)S(1)} %get-tuple-element.116.where_ref, f32[72,1024]{1,0:T(8,128)S(1)} %get-tuple-element.117.refs_0_, bf16[72,1024]{1,0:T(8,128)(2,1)S(1)} %collective-permute-done.18.refs_1_, bf16[72,1024]{1,0:T(8,128)(2,1)S(1)} %collective-permute-done.19.refs_2_, ...), custom_call_target="tpu_custom_call" | custom-call | flops 1000 | bytes 3000000 | tf_op jit(solution)/shard_map/last_sum/pallas_call | solution.py:285
  96.0 0.1 collective-permute-start.21
  96.1 1.3 %collective-permute-done.21 = bf16[72,1024]{1,0:T(8,128)(2,1)S(1)} collective-permute-done((bf16[72,1024]{1,0:T(8,128)(2,1)S(1)}, bf16[72,1024]{1,0:T(8,128)(2,1)S(1)}, u32[]{:S(2)}, u32[]{:S(2)}) %collective-permute-start.21) | collective-permute-done | bytes 147488 | tf_op jit(solution)/shard_map/ppermute | solution.py:315
  97.5 0.8 maximum_select_fusion
  98.3 0.7 fusion.7
  (23 shorter events, 0.3 us)
Async XLA Ops:
  0.6 1.6 %copy-start = (bf16[128,1024]{1,0:T(8,128)(2,1)S(1)}, bf16[128,1024]{1,0:T(8,128)(2,1)}, u32[]{:S(2)}) copy-start(bf16[128,1024]{1,0:T(8,128)(2,1)} %param.7) | copy-start | bytes 786436
  2.3 16.4 %collective-permute-start.3 = (bf16[72,1024]{1,0:T(8,128)(2,1)S(1)}, bf16[72,1024]{1,0:T(8,128)(2,1)S(1)}, u32[]{:S(2)}, u32[]{:S(2)}) collective-permute-start(bf16[72,1024]{1,0:T(8,128)(2,1)S(1)} %fusion.1), channel_id=1, source_target_pairs={{0,2},{2,0},{1,3},{3,1},{4,6},{6,4},{5,7},{7,5},{8,10},{10,8},{9,1... | collective-permute-start | bytes 442376 | tf_op jit(solution)/shard_map/ppermute | solution.py:321
  5.3 13.4 %collective-permute-start.2 = (bf16[72,1024]{1,0:T(8,128)(2,1)S(1)}, bf16[72,1024]{1,0:T(8,128)(2,1)S(1)}, u32[]{:S(2)}, u32[]{:S(2)}) collective-permute-start(bf16[72,1024]{1,0:T(8,128)(2,1)S(1)} %fusion.1), channel_id=1, source_target_pairs={{0,12},{4,0},{8,4},{12,8},{1,13},{5,1},{9,5},{13,9},{2,14},{6,2},{... | collective-permute-start | bytes 442376 | tf_op jit(solution)/shard_map/ppermute | solution.py:318
  8.9 12.3 %collective-permute-start.1 = (bf16[72,1024]{1,0:T(8,128)(2,1)S(1)}, bf16[72,1024]{1,0:T(8,128)(2,1)S(1)}, u32[]{:S(2)}, u32[]{:S(2)}) collective-permute-start(bf16[72,1024]{1,0:T(8,128)(2,1)S(1)} %fusion.1), channel_id=1, source_target_pairs={{0,8},{4,12},{8,0},{12,4},{1,9},{5,13},{9,1},{13,5},{2,10},{6,14},... | collective-permute-start | bytes 442376 | tf_op jit(solution)/shard_map/ppermute | solution.py:318
  8.9 12.3 %collective-permute-start = (bf16[72,1024]{1,0:T(8,128)(2,1)S(1)}, bf16[72,1024]{1,0:T(8,128)(2,1)S(1)}, u32[]{:S(2)}, u32[]{:S(2)}) collective-permute-start(bf16[72,1024]{1,0:T(8,128)(2,1)S(1)} %fusion.1), channel_id=1, source_target_pairs={{0,4},{4,8},{8,12},{12,0},{1,5},{5,9},{9,13},{13,1},{2,6},{6,10},{... | collective-permute-start | bytes 442376 | tf_op jit(solution)/shard_map/ppermute | solution.py:318
  10.9 7.8 %collective-permute-start.4 = (bf16[64,1024]{1,0:T(8,128)(2,1)S(1)}, bf16[64,1024]{1,0:T(8,128)(2,1)S(1)}, u32[]{:S(2)}, u32[]{:S(2)}) collective-permute-start(bf16[64,1024]{1,0:T(8,128)(2,1)S(1)} %constant_dynamic-slice_fusion), channel_id=1, source_target_pairs={{0,2},{2,0},{1,3},{3,1},{4,6},{6,4},{5,7},{7,5},{8,10},{10,8},{9,1... | collective-permute-start | bytes 393224 | tf_op jit(solution)/shard_map/ppermute | solution.py:321
  21.3 5.5 %collective-permute-start.5 = (bf16[4,72,1024]{2,1,0:T(8,128)(2,1)S(1)}, bf16[4,72,1024]{2,1,0:T(8,128)(2,1)S(1)}, u32[]{:S(2)}, u32[]{:S(2)}) collective-permute-start(bf16[4,72,1024]{2,1,0:T(8,128)(2,1)S(1)} %pad_maximum_fusion.refs_0_), channel_id=1, source_target_pairs={{0,1},{1,0},{2,3},{3,2},{4,5},{5,4},{6,7},{7,6},{8,9},{9,8},{10,11... | collective-permute-start | bytes 1769480 | tf_op jit(solution)/shard_map/ppermute | solution.py:315
  21.5 15.7 %collective-permute-start.9 = (bf16[3,72,1024]{2,1,0:T(8,128)(2,1)S(1)}, bf16[3,72,1024]{2,1,0:T(8,128)(2,1)S(1)}, u32[]{:S(2)}, u32[]{:S(2)}) collective-permute-start(bf16[3,72,1024]{2,1,0:T(8,128)(2,1)S(1)} %pad_maximum_fusion.4), channel_id=1, source_target_pairs={{0,2},{2,0},{1,3},{3,1},{4,6},{6,4},{5,7},{7,5},{8,10},{10,8},{9,1... | collective-permute-start | bytes 1327112 | tf_op jit(solution)/shard_map/ppermute | solution.py:321
  22.1 6.0 %collective-permute-start.8 = (bf16[64,1024]{1,0:T(8,128)(2,1)S(1)}, bf16[64,1024]{1,0:T(8,128)(2,1)S(1)}, u32[]{:S(2)}, u32[]{:S(2)}) collective-permute-start(bf16[64,1024]{1,0:T(8,128)(2,1)S(1)} %constant_dynamic-slice_fusion), channel_id=1, source_target_pairs={{0,12},{4,0},{8,4},{12,8},{1,13},{5,1},{9,5},{13,9},{2,14},{6,2},{... | collective-permute-start | bytes 393224 | tf_op jit(solution)/shard_map/ppermute | solution.py:318
  23.5 13.7 %collective-permute-start.7 = (bf16[64,1024]{1,0:T(8,128)(2,1)S(1)}, bf16[64,1024]{1,0:T(8,128)(2,1)S(1)}, u32[]{:S(2)}, u32[]{:S(2)}) collective-permute-start(bf16[64,1024]{1,0:T(8,128)(2,1)S(1)} %constant_dynamic-slice_fusion), channel_id=1, source_target_pairs={{0,8},{4,12},{8,0},{12,4},{1,9},{5,13},{9,1},{13,5},{2,10},{6,14},... | collective-permute-start | bytes 393224 | tf_op jit(solution)/shard_map/ppermute | solution.py:318
  24.8 12.3 %collective-permute-start.6 = (bf16[64,1024]{1,0:T(8,128)(2,1)S(1)}, bf16[64,1024]{1,0:T(8,128)(2,1)S(1)}, u32[]{:S(2)}, u32[]{:S(2)}) collective-permute-start(bf16[64,1024]{1,0:T(8,128)(2,1)S(1)} %constant_dynamic-slice_fusion), channel_id=1, source_target_pairs={{0,4},{4,8},{8,12},{12,0},{1,5},{5,9},{9,13},{13,1},{2,6},{6,10},{... | collective-permute-start | bytes 393224 | tf_op jit(solution)/shard_map/ppermute | solution.py:318
  37.2 2.3 %collective-permute-start.10 = (bf16[4,72,1024]{2,1,0:T(8,128)(2,1)S(1)}, bf16[4,72,1024]{2,1,0:T(8,128)(2,1)S(1)}, u32[]{:S(2)}, u32[]{:S(2)}) collective-permute-start(bf16[4,72,1024]{2,1,0:T(8,128)(2,1)S(1)} %pad_maximum_fusion.1.refs_0_), channel_id=1, source_target_pairs={{0,1},{1,0},{2,3},{3,2},{4,5},{5,4},{6,7},{7,6},{8,9},{9,8},{10,11... | collective-permute-start | bytes 1769480 | tf_op jit(solution)/shard_map/ppermute | solution.py:315
  37.4 7.8 %collective-permute-start.11 = (bf16[4,64,1024]{2,1,0:T(8,128)(2,1)S(1)}, bf16[4,64,1024]{2,1,0:T(8,128)(2,1)S(1)}, u32[]{:S(2)}, u32[]{:S(2)}) collective-permute-start(bf16[4,64,1024]{2,1,0:T(8,128)(2,1)S(1)} %pad_maximum_fusion.2.refs_1_), channel_id=1, source_target_pairs={{0,1},{1,0},{2,3},{3,2},{4,5},{5,4},{6,7},{7,6},{8,9},{9,8},{10,11... | collective-permute-start | bytes 1572872 | tf_op jit(solution)/shard_map/ppermute | solution.py:315
  38.0 11.1 %collective-permute-start.12 = (bf16[3,64,1024]{2,1,0:T(8,128)(2,1)S(1)}, bf16[3,64,1024]{2,1,0:T(8,128)(2,1)S(1)}, u32[]{:S(2)}, u32[]{:S(2)}) collective-permute-start(bf16[3,64,1024]{2,1,0:T(8,128)(2,1)S(1)} %pad_maximum_fusion.5), channel_id=1, source_target_pairs={{0,2},{2,0},{1,3},{3,1},{4,6},{6,4},{5,7},{7,5},{8,10},{10,8},{9,1... | collective-permute-start | bytes 1179656 | tf_op jit(solution)/shard_map/ppermute | solution.py:321
  49.1 2.0 %collective-permute-start.13 = (bf16[4,64,1024]{2,1,0:T(8,128)(2,1)S(1)}, bf16[4,64,1024]{2,1,0:T(8,128)(2,1)S(1)}, u32[]{:S(2)}, u32[]{:S(2)}) collective-permute-start(bf16[4,64,1024]{2,1,0:T(8,128)(2,1)S(1)} %pad_maximum_fusion.3.refs_1_), channel_id=1, source_target_pairs={{0,1},{1,0},{2,3},{3,2},{4,5},{5,4},{6,7},{7,6},{8,9},{9,8},{10,11... | collective-permute-start | bytes 1572872 | tf_op jit(solution)/shard_map/ppermute | solution.py:315
  62.6 2.1 %collective-permute-start.15 = (bf16[4,72,1024]{2,1,0:T(8,128)(2,1)S(1)}, bf16[4,72,1024]{2,1,0:T(8,128)(2,1)S(1)}, u32[]{:S(2)}, u32[]{:S(2)}) collective-permute-start(bf16[4,72,1024]{2,1,0:T(8,128)(2,1)S(1)} %get-tuple-element.114), channel_id=1, source_target_pairs={{0,1},{1,0},{2,3},{3,2},{4,5},{5,4},{6,7},{7,6},{8,9},{9,8},{10,11... | collective-permute-start | bytes 1769480 | tf_op jit(solution)/shard_map/ppermute | solution.py:315
  64.1 13.0 %collective-permute-start.14 = (bf16[4,72,1024]{2,1,0:T(8,128)(2,1)S(1)}, bf16[4,72,1024]{2,1,0:T(8,128)(2,1)S(1)}, u32[]{:S(2)}, u32[]{:S(2)}) collective-permute-start(bf16[4,72,1024]{2,1,0:T(8,128)(2,1)S(1)} %get-tuple-element.112), channel_id=1, source_target_pairs={{0,1},{1,0},{2,3},{3,2},{4,5},{5,4},{6,7},{7,6},{8,9},{9,8},{10,11... | collective-permute-start | bytes 1769480 | tf_op jit(solution)/shard_map/ppermute | solution.py:315
  64.9 12.2 %collective-permute-start.16 = (bf16[2,72,1024]{2,1,0:T(8,128)(2,1)S(1)}, bf16[2,72,1024]{2,1,0:T(8,128)(2,1)S(1)}, u32[]{:S(2)}, u32[]{:S(2)}) collective-permute-start(bf16[2,72,1024]{2,1,0:T(8,128)(2,1)S(1)} %stack.56), channel_id=1, source_target_pairs={{0,2},{2,0},{1,3},{3,1},{4,6},{6,4},{5,7},{7,5},{8,10},{10,8},{9,1... | collective-permute-start | bytes 884744 | tf_op jit(solution)/shard_map/ppermute | solution.py:321
  66.5 32.4 %copy-start.1 = (bf16[128,1024]{1,0:T(8,128)(2,1)S(1)}, bf16[128,1024]{1,0:T(8,128)(2,1)}, u32[]{:S(2)}) copy-start(bf16[128,1024]{1,0:T(8,128)(2,1)} %param.7) | copy-start | bytes 786436
  66.6 13.8 %collective-permute-start.17 = (bf16[2,72,1024]{2,1,0:T(8,128)(2,1)S(1)}, bf16[2,72,1024]{2,1,0:T(8,128)(2,1)S(1)}, u32[]{:S(2)}, u32[]{:S(2)}) collective-permute-start(bf16[2,72,1024]{2,1,0:T(8,128)(2,1)S(1)} %pad_maximum_fusion.6), channel_id=1, source_target_pairs={{0,2},{2,0},{1,3},{3,1},{4,6},{6,4},{5,7},{7,5},{8,10},{10,8},{9,1... | collective-permute-start | bytes 884744 | tf_op jit(solution)/shard_map/ppermute | solution.py:321
  81.5 8.6 %collective-permute-start.18 = (bf16[72,1024]{1,0:T(8,128)(2,1)S(1)}, bf16[72,1024]{1,0:T(8,128)(2,1)S(1)}, u32[]{:S(2)}, u32[]{:S(2)}) collective-permute-start(bf16[72,1024]{1,0:T(8,128)(2,1)S(1)} %get-tuple-element.118), channel_id=1, source_target_pairs={{0,4},{4,8},{8,12},{12,0},{1,5},{5,9},{9,13},{13,1},{2,6},{6,10},{... | collective-permute-start | bytes 442376 | tf_op jit(solution)/shard_map/ppermute | solution.py:318
  81.6 13.3 %collective-permute-start.19 = (bf16[72,1024]{1,0:T(8,128)(2,1)S(1)}, bf16[72,1024]{1,0:T(8,128)(2,1)S(1)}, u32[]{:S(2)}, u32[]{:S(2)}) collective-permute-start(bf16[72,1024]{1,0:T(8,128)(2,1)S(1)} %get-tuple-element.119), channel_id=1, source_target_pairs={{0,8},{4,12},{8,0},{12,4},{1,9},{5,13},{9,1},{13,5},{2,10},{6,14},... | collective-permute-start | bytes 442376 | tf_op jit(solution)/shard_map/ppermute | solution.py:318
  82.9 12.0 %collective-permute-start.20 = (bf16[72,1024]{1,0:T(8,128)(2,1)S(1)}, bf16[72,1024]{1,0:T(8,128)(2,1)S(1)}, u32[]{:S(2)}, u32[]{:S(2)}) collective-permute-start(bf16[72,1024]{1,0:T(8,128)(2,1)S(1)} %get-tuple-element.120), channel_id=1, source_target_pairs={{0,12},{4,0},{8,4},{12,8},{1,13},{5,1},{9,5},{13,9},{2,14},{6,2},{... | collective-permute-start | bytes 442376 | tf_op jit(solution)/shard_map/ppermute | solution.py:318
  96.0 1.4 %collective-permute-start.21 = (bf16[72,1024]{1,0:T(8,128)(2,1)S(1)}, bf16[72,1024]{1,0:T(8,128)(2,1)S(1)}, u32[]{:S(2)}, u32[]{:S(2)}) collective-permute-start(bf16[72,1024]{1,0:T(8,128)(2,1)S(1)} %get-tuple-element.121), channel_id=1, source_target_pairs={{0,1},{1,0},{2,3},{3,2},{4,5},{5,4},{6,7},{7,6},{8,9},{9,8},{10,11... | collective-permute-start | bytes 442376 | tf_op jit(solution)/shard_map/ppermute | solution.py:315

commit v4 on v3

--- a/solution.py
+++ b/solution.py
@@ -55,33 +55,62 @@
 
 
 def select(rank, near, far, rows_ref):
-    count, _, features = rows_ref.shape
-    sources = near.shape[0]
-    half = rank.shape[1] // 2
+    count, sources = rows_ref.shape[0], rows_ref.shape[1] // MOST
     for source in range(sources):
         pick = slot_matrix(rank[source * count : (source + 1) * count])
-        both = jnp.concatenate([near[source, :half], far[source, :half]], axis=0)
+        both = jnp.concatenate([near(source), far(source)], axis=0)
         rows = jnp.dot(pick, both, preferred_element_type=F32).astype(BF16)
-        rows_ref[:, source * MOST : (source + 1) * MOST, :] = rows.reshape(count, MOST, features)
-
-
-def select_tokens(span, kinds, where_ref, near_ref, far_ref, rows_ref, rank_ref, weight_ref, meta_ref):
-    tokens = rank_ref.shape[1]
-    half, per_row = tokens // 2, near_ref.shape[2] // tokens
-    lines = []
-    for number in range(2 * kinds):
-        at, part = half + number // per_row, number % per_row
-        lines.append(near_ref[:, at : at + 1, part * tokens : (part + 1) * tokens].astype(F32))
-    meta = jnp.concatenate(lines, axis=1)
+        rows_ref[:, source * MOST : (source + 1) * MOST, :] = rows.reshape(count, MOST, rows.shape[1])
+
+
+def unpacked(piece, half, features):
+    chunks = features // piece.shape[1]
+    return jnp.concatenate([piece[chunk * half : (chunk + 1) * half] for chunk in range(chunks)], axis=1)
+
+
+def store_packed(ref, index, rows):
+    half, features = rows.shape
+    lanes = ref.shape[-1]
+    for chunk in range(features // lanes):
+        ref[(*index, slice(chunk * half, (chunk + 1) * half))] = rows[:, chunk * lanes : (chunk + 1) * lanes]
+
+
+def pack(where_ref, tokens_ref, cotangent_ref, experts_ref, probs_ref, x_ref, dy_ref, token_ref, half_scr, experts_scr,
+         chosen_scr, ids_scr, prob_scr, sems):
+    second = where_ref[1] == 1
+    half = dy_ref.shape[0]
+    top, kinds = experts_ref.shape[0], ids_scr.shape[0]
+    mine = pl.ds(pl.multiple_of(where_ref[1] * half, half), half)
+    pairs = ((tokens_ref.at[mine], half_scr), (experts_ref, experts_scr), (probs_ref, chosen_scr),
+             (cotangent_ref.at[mine], dy_ref))
+    copies = [pltpu.make_async_copy(source, target, sems.at[at]) for at, (source, target) in enumerate(pairs)]
+    for copy in copies:
+        copy.start()
+    pass_on(where_ref, token_ref)
+    for copy in copies:
+        copy.wait()
+    store_packed(x_ref, (), half_scr[...])
+    ids_scr[...] = jnp.full(ids_scr.shape, -1.0, F32)
+    prob_scr[...] = jnp.zeros(prob_scr.shape, F32)
+    ids_scr[:top] = experts_scr[...].astype(F32)
+    prob_scr[:top] = chosen_scr[...].astype(F32)
+    lines = [jnp.where(second, pltpu.roll(ref[...], half, 1), ref[...]) for ref in (ids_scr, prob_scr)]
+    x_ref[x_ref.shape[0] - 2 * kinds :] = jnp.concatenate(lines, axis=0).astype(BF16)
+
+
+def select_tokens(span, where_ref, near_ref, far_ref, rows_ref, rank_ref, weight_ref, meta_ref):
+    half, features, height = rank_ref.shape[1] // 2, rows_ref.shape[2], meta_ref.shape[1]
+    meta = near_ref[:, near_ref.shape[1] - height :, :].astype(F32)
     rank, weight = ranks_and_probs(where_ref[0], meta, span, rows_ref.shape[0])
     rank_ref[...] = rank
     weight_ref[...] = weight
     meta_ref[...] = meta
-    select(rank, near_ref, far_ref, rows_ref)
+    select(rank, lambda source: unpacked(near_ref[source], half, features),
+           lambda source: unpacked(far_ref[source], half, features), rows_ref)
 
 
 def select_cotangents(where_ref, rank_ref, near_ref, far_ref, rows_ref):
-    select(rank_ref[...], near_ref, far_ref, rows_ref)
+    select(rank_ref[...], lambda source: near_ref[source], lambda source: far_ref[source], rows_ref)
 
 
 def joined(refs, index):
@@ -144,34 +173,29 @@
 def put_back(span, base, where_ref, rank_ref, meta_ref, input_ref, prob_ref, own_ref, other_ref):
     count, _, features = input_ref.shape
     tokens = rank_ref.shape[1]
-    half, per_row = tokens // 2, features // tokens
-    kinds = meta_ref.shape[1] // 2
-    tail = own_ref.shape[1] - half
+    half, kinds = tokens // 2, meta_ref.shape[1] // 2
+    tail = own_ref.shape[1] - features // own_ref.shape[2] * half
     wanted = ((where_ref[0] + span * iota((count, tokens), 0)) >> 1).astype(F32)
     for source in range(own_ref.shape[0]):
         number = base + source
         pick = slot_matrix(rank_ref[source * count : (source + 1) * count])
         rows = input_ref[:, number * MOST : (number + 1) * MOST, :].reshape(count * MOST, features)
         part = dot(pick, rows, LEAD).astype(BF16)
-        own_ref[source, :half] = part[:half]
-        other_ref[source, :half] = part[half:]
+        store_packed(own_ref, (source,), part[:half])
+        store_packed(other_ref, (source,), part[half:])
         prob = prob_ref[:, number, :]
         entry = meta_ref[source]
-        line = [
-            jnp.sum(jnp.where(entry[kind : kind + 1] == wanted, prob, 0.0), axis=0, keepdims=True)
-            for kind in range(kinds)
-        ]
-        flip = [pltpu.roll(jnp.broadcast_to(row, (8, tokens)), half, 1)[:1] for row in line]
-        for ref, parts in ((own_ref, line), (other_ref, flip)):
-            lines = [jnp.concatenate(parts[at : at + per_row], axis=1) for at in range(0, kinds, per_row)]
-            lines += [jnp.zeros_like(lines[0])] * (tail - len(lines))
-            ref[source, half:] = jnp.concatenate(lines, axis=0).astype(BF16)
+        lines = jnp.zeros((tail, tokens), F32)
+        for kind in range(kinds):
+            line = jnp.sum(jnp.where(entry[kind : kind + 1] == wanted, prob, 0.0), axis=0, keepdims=True)
+            lines = jnp.where(iota((tail, tokens), 0) == kind, line, lines)
+        own_ref[source, own_ref.shape[1] - tail :] = lines.astype(BF16)
+        other_ref[source, own_ref.shape[1] - tail :] = pltpu.roll(lines, half, 1).astype(BF16)
 
 
 def weights_kernel(groups, where_ref, dgate_ref, dup_ref, gated_ref, *refs):
     rows_x, rows_dy = refs[:groups], refs[groups : 2 * groups]
-    targets, token_ref = refs[2 * groups : 2 * groups + 3], refs[2 * groups + 3]
-    slots_ref, sems = refs[2 * groups + 4 :]
+    targets, token_ref, slots_ref, sems = refs[-6:-3], *refs[-3:]
     count, depth = dgate_ref.shape[0], slots_ref.shape[0]
 
     def copies(expert):
@@ -203,20 +227,42 @@
     pass_on(where_ref, token_ref)
 
 
-def line_sums(places, peers, keep, where_ref, own_ref, other_ref, *refs):
-    hops, outs = refs[:peers], refs[peers:]
-    for at, (place, out) in enumerate(zip(places, outs)):
-        total = own_ref[place].astype(F32) + other_ref[place].astype(F32)
+def middle_sums(zs, xs, where_ref, own_ref, other_ref, base_ref, *refs):
+    hops, shifts, outs = refs[: xs - 1], refs[xs - 1 : xs + zs - 2], refs[xs + zs - 2 :]
+    size = hops[0].shape[1]
+    for place in range(zs):
+        total = own_ref[place, :size].astype(F32) + other_ref[place, :size].astype(F32)
         for hop in hops:
-            total = total + hop[at].astype(F32)
-        out[...] = total if place == keep else total.astype(BF16)
-
-
-def last_sum(where_ref, kept_ref, *refs):
-    total = kept_ref[...]
-    for piece in refs[:-1]:
-        total = total + piece[...].astype(F32)
-    refs[-1][...] = total.astype(BF16)
+            total = total + hop[place].astype(F32)
+        outs[place][...] = total.astype(outs[place].dtype)
+    for place in range(xs):
+        total = base_ref[place]
+        for piece in shifts:
+            total = total + piece[place].astype(F32)
+        outs[zs + place][...] = total.astype(outs[zs + place].dtype)
+
+
+def last_sums(zs, xs, where_ref, *refs):
+    first, last, out = refs[:zs], refs[zs : zs + xs], refs[-1]
+    size = first[0].shape[0]
+    for refs, rows in ((first, slice(0, size)), (last, slice(size, out.shape[0]))):
+        total = refs[0][...]
+        for ref in refs[1:]:
+            total = total + ref[...].astype(F32)
+        out[rows] = total.astype(BF16)
+
+
+def unpack(where_ref, mine_ref, theirs_ref, tokens_ref, probs_ref):
+    second = where_ref[1] == 1
+    mine, theirs = mine_ref[...], theirs_ref[...]
+    half, features = tokens_ref.shape[0] // 2, tokens_ref.shape[1]
+    low, high = jnp.where(second, theirs, mine), jnp.where(second, mine, theirs)
+    tokens_ref[:half] = unpacked(low, half, features)
+    tokens_ref[half:] = unpacked(high, half, features)
+    at = features // low.shape[1] * half
+    low, high = low[at:].astype(F32), high[at:].astype(F32)
+    both = jnp.where(iota(low.shape, 1) < half, low, pltpu.roll(high, half, 1))
+    probs_ref[...] = both[: probs_ref.shape[0]]
 
 
 def in_vmem(array):
@@ -240,7 +286,7 @@
 
 
 def pass_on(where_ref, token_ref):
-    for number in range(3):
+    for number in range(2):
         token_ref[number] = where_ref[number]
 
 
@@ -260,7 +306,7 @@
 
 SCALARS = pl.BlockSpec(memory_space=pltpu.SMEM)
 IN_VMEM = pl.BlockSpec(memory_space=pltpu.VMEM)
-TOKEN = jax.ShapeDtypeStruct((3,), jnp.int32)
+TOKEN = jax.ShapeDtypeStruct((2,), jnp.int32)
 
 
 def load(where, arrays):
@@ -277,16 +323,18 @@
     return where, held
 
 
-def on_vmem(kernel, name, micros, outs, where, operands, stay=True):
+def on_vmem(kernel, name, micros, outs, where, operands, stay=True, scratch=()):
     def body(where_ref, *refs):
-        kernel(where_ref, *refs[:-1])
-        pass_on(where_ref, refs[-1])
+        at = len(operands) + len(outs)
+        kernel(where_ref, *refs[:at], *refs[at + 1 :])
+        pass_on(where_ref, refs[at])
 
     *held, where = pl.pallas_call(
         body,
         in_specs=[SCALARS] + [IN_VMEM] * len(operands),
         out_specs=[IN_VMEM] * len(outs) + [SCALARS],
         out_shape=[(vmem_shape if stay else jax.ShapeDtypeStruct)(shape, dtype) for shape, dtype in outs] + [TOKEN],
+        scratch_shapes=list(scratch),
         compiler_params=pltpu.CompilerParams(vmem_limit_bytes=VMEM_BYTES),
         cost_estimate=cost(micros),
         name=name,
@@ -320,31 +368,29 @@
     def along_x(array, by):
         return lax.ppermute(array, "blk", [(i, (i + by) % xs) for i in range(xs)])
 
-    def own_first(array):
-        return jnp.roll(array, -core * half, axis=-1)
-
-    experts_t = own_first(experts.T)
-    probs_t = own_first(probs.T)
-    meta = jnp.concatenate(
-        [
-            jnp.pad(experts_t.astype(BF16), ((0, kinds - top), (0, 0)), constant_values=-1.0),
-            jnp.pad(probs_t, ((0, kinds - top), (0, 0))),
-        ]
-    ).reshape(-1, features)
-    meta = jnp.pad(meta, ((0, -meta.shape[0] % 8), (0, 0)))
-    own_x = jnp.concatenate([lax.dynamic_slice_in_dim(tokens, core * half, half, 0), meta])
-    own_dy = lax.dynamic_slice_in_dim(cotangent, core * half, half, 0)
-
     wg = jnp.swapaxes(w_gate, 1, 2).reshape(count, hidden, features)
     wu = jnp.swapaxes(w_up, 1, 2).reshape(count, hidden, features)
     wd = w_down.reshape(count, hidden, features)
-    where = jnp.stack([position * halves, lax.axis_index("expert"), lax.axis_index("blk")]).astype(jnp.int32)
+    where = jnp.stack([position * halves, core]).astype(jnp.int32)
     group = zs * MOST
+    packed = features // rows * half
+    own_x, own_dy, where = pl.pallas_call(
+        pack,
+        in_specs=[SCALARS] + [pl.BlockSpec(memory_space=pl.ANY)] * 4,
+        out_specs=[IN_VMEM] * 2 + [SCALARS],
+        out_shape=[jax.ShapeDtypeStruct((packed + 2 * kinds, rows), BF16), jax.ShapeDtypeStruct((half, features), BF16),
+                   TOKEN],
+        scratch_shapes=[pltpu.VMEM((half, features), BF16), pltpu.VMEM((top, rows), jnp.int32),
+                        pltpu.VMEM((top, rows), BF16), pltpu.VMEM((kinds, rows), F32), pltpu.VMEM((kinds, rows), F32),
+                        pltpu.SemaphoreType.DMA((4,))],
+        compiler_params=pltpu.CompilerParams(vmem_limit_bytes=VMEM_BYTES),
+        cost_estimate=cost(2),
+        name="pack",
+    )(where, in_hbm(tokens), in_hbm(cotangent), in_hbm(experts.T), in_hbm(probs.T))
 
     line_x = [along_z(own_x, d) for d in range(1, zs)]
     first_x = [along_x(own_x, c) for c in range(1, xs)]
     first_dy = [along_x(own_dy, c) for c in range(1, xs)]
-    where, own_x = barrier((where, own_x))
     where, (wg, wu, wd) = load(where, (wg, wu, wd))
     where, line_x, first_x, first_dy, own_dy = barrier((where, line_x, first_x, first_dy, own_dy))
 
@@ -356,7 +402,7 @@
     def take_tokens(where, near, far):
         outs = [((count, group, features), BF16), ((zs * count, rows), F32), ((zs * count, rows), F32),
                 ((zs, 2 * kinds, rows), F32)]
-        where, results = on_vmem(functools.partial(select_tokens, span, kinds), "select_tokens", 2, outs, where, (near, far))
+        where, results = on_vmem(functools.partial(select_tokens, span), "select_tokens", 2, outs, where, (near, far))
         for held, result in zip((rows_x, ranks, weight, metas), results):
             held.append(result)
         return where
@@ -388,55 +434,53 @@
     where, (dgate, dup, gated, rows_in, prob) = on_vmem(
         functools.partial(backward_kernel, xs), "backward", 9, outs, where,
         (wg, wu, wd, gate, up, *ranks, *weight, *rows_dy))
-    back = half + 8 * pl.cdiv(kinds * rows, 8 * features)
+    height = packed + 16 * pl.cdiv(kinds, 16)
+    split = 2 * height // 3 // 16 * 16
     chip = [None] * xs
     for c in list(range(1, xs)) + [0]:
         where, (own, other) = on_vmem(
-            functools.partial(put_back, span, c * zs), "put_back", 2, [((zs, back, features), BF16)] * 2, where,
+            functools.partial(put_back, span, c * zs), "put_back", 2, [((zs, height, rows), BF16)] * 2, where,
             (ranks[c], metas[c], rows_in, prob), False)
         chip[c] = own, swap(other)
-    sums = [None] + [(own.astype(F32) + other.astype(F32)).astype(BF16) for own, other in chip[1:]]
+
+    def both_cores(c, index):
+        own, other = chip[c]
+        return own[index].astype(F32) + other[index].astype(F32)
+
     saved = (dgate, dup, gated, *rows_x, *rows_dy)
 
-    def weights(where):
+    def weights(where, after):
         depth = min(count, 2)
         *grads, where = pl.pallas_call(
             functools.partial(weights_kernel, xs),
-            in_specs=[SCALARS] + [IN_VMEM] * len(saved),
+            in_specs=[SCALARS] + [IN_VMEM] * len(saved) + [pl.BlockSpec(memory_space=pl.ANY)] * len(after),
             out_specs=[pl.BlockSpec(memory_space=pl.ANY)] * 3 + [SCALARS],
             out_shape=[jax.ShapeDtypeStruct((count, hidden, features), BF16)] * 3 + [TOKEN],
             scratch_shapes=[pltpu.VMEM((depth, 3, hidden, features), BF16), pltpu.SemaphoreType.DMA((depth, 3))],
             compiler_params=pltpu.CompilerParams(vmem_limit_bytes=VMEM_BYTES),
             cost_estimate=cost(9),
             name="weights",
-        )(where, *map(in_vmem, saved))
+        )(where, *map(in_vmem, saved), *after)
         return where, grads
 
-    turn = list(range(1, zs)) + [0]
-    turns = [turn[: zs // 2], turn[zs // 2 :]]
-    hops = [[along_x(jnp.stack([sums[c][d] for d in some]), -c) for c in range(1, xs)] for some in turns]
-    where, grads = weights(where)
-    pieces = []
-    for some, hop in zip(turns, hops):
-        outs = [((back, features), BF16 if d else F32) for d in some]
-        where, parts = on_vmem(functools.partial(line_sums, some, len(hop), 0), "line_sums", 1, outs, where,
-                               (*chip[0], *hop), False)
-        pieces += [along_z(part, -d) if d else part for d, part in zip(some, parts)]
-    where, (mine,) = on_vmem(last_sum, "last_sum", 1, [((back, features), BF16)], where, pieces[::-1], False)
-    theirs = swap(mine)
-
-    def tokens_of(piece):
-        return piece[:half]
-
-    def probs_of(piece):
-        return piece[half:].reshape(-1)[: kinds * rows].reshape(kinds, rows)[:top, :half].astype(F32)
-
-    def in_order(part, axis):
-        both = part(mine), part(theirs)
-        return jnp.where(core == 0, jnp.concatenate(both, axis), jnp.concatenate(both[::-1], axis))
-
-    grad_tokens = in_order(tokens_of, 0)
-    grad_probs = in_order(probs_of, 1).T
+    first, last = slice(0, split), slice(split, height)
+    crossing = [both_cores(c, (slice(None), first)).astype(BF16) for c in range(1, xs)]
+    sides = [jnp.stack([both_cores(c, (d, last)) for c in range(xs)]) for d in range(zs)]
+    lining = [side.astype(BF16) for side in sides[1:]]
+    hops = [along_x(array, -c) for c, array in enumerate(crossing, 1)]
+    shifts = [along_z(array, -d) for d, array in enumerate(lining, 1)]
+    where, grads = weights(where, crossing + lining)
+    outs = [((split, rows), BF16 if d else F32) for d in range(zs)]
+    outs += [((height - split, rows), BF16 if c else F32) for c in range(xs)]
+    where, sums = on_vmem(functools.partial(middle_sums, zs, xs), "middle_sums", 1, outs, where,
+                          (*chip[0], sides[0], *hops, *shifts), False)
+    parts = [along_z(sums[d], -d) if d else sums[d] for d in range(zs)]
+    parts += [along_x(sums[zs + c], -c) if c else sums[zs] for c in range(xs)]
+    where, (mine,) = on_vmem(functools.partial(last_sums, zs, xs), "last_sums", 1, [((height, rows), BF16)], where,
+                             parts, False)
+    outs = [((rows, features), BF16), ((top, rows), F32)]
+    where, (grad_tokens, grad_probs) = on_vmem(unpack, "unpack", 1, outs, where, (mine, swap(mine)), False)
+    grad_probs = grad_probs.T
     grad_gate, grad_up, grad_down = grads
     shape = (halves, quarter, features)
     return (

time: 99.2 us -> 94.4 us (0.952)
  waiting for transfers between devices: 28.9 us -> 22.8 us
  starting transfers between devices: 23.1 us -> 26.5 us
  other arithmetic: 3.7 us -> 0.66 us
  Pallas kernels: 41.3 us -> 43.4 us
  local copies, waits for them, and re-layouts: 1.07 us -> 0 us
    ppermute x9 -> x12, waiting for transfers between devices: 20.8 us -> 13.8 us  [along_z(): lax.ppermute(array, 'expert', [(i, (i + by) % zs) for i in range(zs)])]
    ppermute x9 -> x12, starting transfers between devices: 13.7 us -> 16.6 us  [along_z(): lax.ppermute(array, 'expert', [(i, (i + by) % zs) for i in range(zs)])]
    pallas_call x0 -> x1, Pallas kernels: none -> 2.19 us  [per_device(): pl.pallas_call(pack, in_specs=[SCALARS] + [pl.BlockSpec(memory_space=pl.A...]
  transfers between devices with their start and end apart: 22 -> 25, of which waited for: 9 -> 8; matrix products, arithmetic and copies ran while one was open for 1% -> 0% of each run, Pallas kernels for 28% -> 28%
where the time goes in v4:
time: 94.4 us; the launch traced here: 94.3 us
  Pallas kernels  43.4 us (46%)
  starting transfers between devices  26.5 us (28%)
  waiting for transfers between devices  22.8 us (24%)
    pallas_call x11, Pallas kernels, on_vmem(): pl.pallas_call(body, in_specs=[SCALARS] + [IN_VMEM] * len(operands), out_...  24.1 us
    ppermute x12, starting transfers between devices, along_z(): lax.ppermute(array, 'expert', [(i, (i + by) % zs) for i in range(zs)])  16.6 us
    ppermute x12, waiting for transfers between devices, along_z(): lax.ppermute(array, 'expert', [(i, (i + by) % zs) for i in range(zs)])  13.8 us
    pallas_call x1, Pallas kernels, weights(): pl.pallas_call(functools.partial(weights_kernel, xs), in_specs=[SCALARS]...  9.95 us
    ppermute x6, starting transfers between devices, along_x(): return lax.ppermute(array, 'blk', [(i, (i + by) % xs) for i in range(xs)])  8.39 us
    pallas_call x1, Pallas kernels, load(): pl.pallas_call(load_kernel, in_specs=[SCALARS] + [pl.BlockSpec(memory_spa...  7.13 us
    ppermute x6, waiting for transfers between devices, along_x(): return lax.ppermute(array, 'blk', [(i, (i + by) % xs) for i in range(xs)])  5.59 us
    ppermute x7, waiting for transfers between devices, swap(): lax.ppermute(array, 'tensor', [(i, (i + 1) % cores) for i in range(cores)])  3.46 us
  transfers between devices with their start and end apart: 25, of which 8 were waited for; matrix products, arithmetic and copies ran while one was open for 0% of the time, Pallas kernels for 28%

profile of v4, /device:TPU:0, one launch (start us, length us, event | category | flops | bytes accessed | tf_op | source)
XLA Modules:
  0.0 94.3 jit_solution(6670747062081393466)
XLA Ops:
  0.6 0.1 pad_add_fusion.where_ref
  0.7 2.2 %pack.1 = (bf16[528,128]{1,0:T(8,128)(2,1)S(1)}, bf16[64,1024]{1,0:T(8,128)(2,1)S(1)}, s32[2]{0:T(128)S(1)}) custom-call(s32[2]{0:T(128)S(1)} %pad_add_fusion.where_ref, bf16[128,1024]{1,0:T(8,128)(2,1)} %tokens_ref.1, bf16[128,1024]{1,0:T(8,128)(2,1)} %cotangent_ref.1, s32[6,128]{1,0:T(8,128)} %bitcast.48, bf16[6,128]{1,0:T(8,128)(2,1)} %bitcast.49), custom_call_target="tpu_custom_call" | custom-call | flops 1000 | bytes 6000000 | tf_op jit(solution)/shard_map/pack/pallas_call | solution.py:377
  2.9 3.0 %collective-permute-start.3 = (bf16[528,128]{1,0:T(8,128)(2,1)S(1)}, bf16[528,128]{1,0:T(8,128)(2,1)S(1)}, u32[]{:S(2)}, u32[]{:S(2)}) collective-permute-start(bf16[528,128]{1,0:T(8,128)(2,1)S(1)} %get-tuple-element.72), channel_id=1, source_target_pairs={{0,2},{2,0},{1,3},{3,1},{4,6},{6,4},{5,7},{7,5},{8,10},{10,8},{9,1... | collective-permute-start | bytes 405512 | tf_op jit(solution)/shard_map/ppermute | solution.py:369
  5.9 3.6 %collective-permute-start.2 = (bf16[528,128]{1,0:T(8,128)(2,1)S(1)}, bf16[528,128]{1,0:T(8,128)(2,1)S(1)}, u32[]{:S(2)}, u32[]{:S(2)}) collective-permute-start(bf16[528,128]{1,0:T(8,128)(2,1)S(1)} %get-tuple-element.72), channel_id=1, source_target_pairs={{0,12},{4,0},{8,4},{12,8},{1,13},{5,1},{9,5},{13,9},{2,14},{6,2},{... | collective-permute-start | bytes 405512 | tf_op jit(solution)/shard_map/ppermute | solution.py:366
  9.5 0.0 collective-permute-start.1
  9.5 1.0 %collective-permute-start = (bf16[528,128]{1,0:T(8,128)(2,1)S(1)}, bf16[528,128]{1,0:T(8,128)(2,1)S(1)}, u32[]{:S(2)}, u32[]{:S(2)}) collective-permute-start(bf16[528,128]{1,0:T(8,128)(2,1)S(1)} %get-tuple-element.72), channel_id=1, source_target_pairs={{0,4},{4,8},{8,12},{12,0},{1,5},{5,9},{9,13},{13,1},{2,6},{6,10},{... | collective-permute-start | bytes 405512 | tf_op jit(solution)/shard_map/ppermute | solution.py:366
  10.5 0.5 collective-permute-start.4
  11.1 7.1 %load.1 = (bf16[8,352,1024]{2,1,0:T(8,128)(2,1)S(1)}, bf16[8,352,1024]{2,1,0:T(8,128)(2,1)S(1)}, bf16[8,352,1024]{2,1,0:T(8,128)(2,1)S(1)}, s32[2]{0:T(128)S(1)}) custom-call(s32[2]{0:T(128)S(1)} %get-tuple-element.70.where_ref, bf16[8,352,1024]{2,1,0:T(8,128)(2,1)} %bitcast.31, bf16[8,352,1024]{2,1,0:T(8,128)(2,1)} %bitcast.32, bf16[8,352,1024]{2,1,0:T(8,128)(2,1)} %bitcast.33), custom_call_target="tpu_custom_call" | custom-call | flops 1000 | bytes 21000000 | tf_op jit(solution)/shard_map/load/pallas_call | solution.py:313
  18.2 0.0 collective-permute-done.4
  18.2 0.0 collective-permute-done.3
  18.2 0.0 collective-permute-done.2
  18.2 2.4 %collective-permute-done.1 = bf16[528,128]{1,0:T(8,128)(2,1)S(1)} collective-permute-done((bf16[528,128]{1,0:T(8,128)(2,1)S(1)}, bf16[528,128]{1,0:T(8,128)(2,1)S(1)}, u32[]{:S(2)}, u32[]{:S(2)}) %collective-permute-start.1) | collective-permute-done | bytes 135200 | tf_op jit(solution)/shard_map/ppermute | solution.py:366
  20.7 0.0 collective-permute-done
  20.7 0.1 pad_maximum_fusion.refs_0_
  20.7 0.1 collective-permute-start.5
  20.9 0.6 collective-permute-start.9
  21.5 1.6 %collective-permute-start.8 = (bf16[64,1024]{1,0:T(8,128)(2,1)S(1)}, bf16[64,1024]{1,0:T(8,128)(2,1)S(1)}, u32[]{:S(2)}, u32[]{:S(2)}) collective-permute-start(bf16[64,1024]{1,0:T(8,128)(2,1)S(1)} %get-tuple-element.79), channel_id=1, source_target_pairs={{0,12},{4,0},{8,4},{12,8},{1,13},{5,1},{9,5},{13,9},{2,14},{6,2},{... | collective-permute-start | bytes 393224 | tf_op jit(solution)/shard_map/ppermute | solution.py:366
  23.1 1.1 %collective-permute-start.7 = (bf16[64,1024]{1,0:T(8,128)(2,1)S(1)}, bf16[64,1024]{1,0:T(8,128)(2,1)S(1)}, u32[]{:S(2)}, u32[]{:S(2)}) collective-permute-start(bf16[64,1024]{1,0:T(8,128)(2,1)S(1)} %get-tuple-element.79), channel_id=1, source_target_pairs={{0,8},{4,12},{8,0},{12,4},{1,9},{5,13},{9,1},{13,5},{2,10},{6,14},... | collective-permute-start | bytes 393224 | tf_op jit(solution)/shard_map/ppermute | solution.py:366
  24.2 2.0 %collective-permute-start.6 = (bf16[64,1024]{1,0:T(8,128)(2,1)S(1)}, bf16[64,1024]{1,0:T(8,128)(2,1)S(1)}, u32[]{:S(2)}, u32[]{:S(2)}) collective-permute-start(bf16[64,1024]{1,0:T(8,128)(2,1)S(1)} %get-tuple-element.79), channel_id=1, source_target_pairs={{0,4},{4,8},{8,12},{12,0},{1,5},{5,9},{9,13},{13,1},{2,6},{6,10},{... | collective-permute-start | bytes 393224 | tf_op jit(solution)/shard_map/ppermute | solution.py:366
  26.3 1.3 %select_tokens.2 = (bf16[8,64,1024]{2,1,0:T(8,128)(2,1)S(1)}, f32[32,128]{1,0:T(8,128)S(1)}, f32[32,128]{1,0:T(8,128)S(1)}, f32[4,16,128]{2,1,0:T(8,128)S(1)}, s32[2]{0:T(128)S(1)}) custom-call(s32[2]{0:T(128)S(1)} %get-tuple-element.74.where_ref, bf16[4,528,128]{2,1,0:T(8,128)(2,1)S(1)} %pad_maximum_fusion.refs_0_, ...), custom_call_target="tpu_custom_call" | custom-call | flops 1000 | bytes 6000000 | tf_op jit(solution)/shard_map/select_tokens/pallas_call | solution.py:332
  27.6 9.0 %collective-permute-done.7 = bf16[64,1024]{1,0:T(8,128)(2,1)S(1)} collective-permute-done((bf16[64,1024]{1,0:T(8,128)(2,1)S(1)}, bf16[64,1024]{1,0:T(8,128)(2,1)S(1)}, u32[]{:S(2)}, u32[]{:S(2)}) %collective-permute-start.7) | collective-permute-done | bytes 131104 | tf_op jit(solution)/shard_map/ppermute | solution.py:366
  36.5 0.0 collective-permute-done.6
  36.5 0.0 collective-permute-done.9
  36.6 0.1 collective-permute-start.10
  36.7 0.1 pad_maximum_fusion.2.refs_1_
  36.7 0.6 collective-permute-start.11
  37.3 1.6 %collective-permute-start.12 = (bf16[3,64,1024]{2,1,0:T(8,128)(2,1)S(1)}, bf16[3,64,1024]{2,1,0:T(8,128)(2,1)S(1)}, u32[]{:S(2)}, u32[]{:S(2)}) collective-permute-start(bf16[3,64,1024]{2,1,0:T(8,128)(2,1)S(1)} %pad_maximum_fusion.5), channel_id=1, source_target_pairs={{0,2},{2,0},{1,3},{3,1},{4,6},{6,4},{5,7},{7,5},{8,10},{10,8},{9,1... | collective-permute-start | bytes 1179656 | tf_op jit(solution)/shard_map/ppermute | solution.py:369
  38.9 1.3 %select_tokens.3 = (bf16[8,64,1024]{2,1,0:T(8,128)(2,1)S(1)}, f32[32,128]{1,0:T(8,128)S(1)}, f32[32,128]{1,0:T(8,128)S(1)}, f32[4,16,128]{2,1,0:T(8,128)S(1)}, s32[2]{0:T(128)S(1)}) custom-call(s32[2]{0:T(128)S(1)} %get-tuple-element.80.where_ref, bf16[4,528,128]{2,1,0:T(8,128)(2,1)S(1)} %pad_maximum_fusion.1.refs_0_, ...), custom_call_target="tpu_custom_call" | custom-call | flops 1000 | bytes 6000000 | tf_op jit(solution)/shard_map/select_tokens/pallas_call | solution.py:332
  40.2 4.2 %forward.1 = (f32[8,352,128]{2,1,0:T(8,128)S(1)}, f32[8,352,128]{2,1,0:T(8,128)S(1)}, s32[2]{0:T(128)S(1)}) custom-call(s32[2]{0:T(128)S(1)} %get-tuple-element.83.where_ref, bf16[8,352,1024]{2,1,0:T(8,128)(2,1)S(1)} %get-tuple-element.84.refs_0_, bf16[8,352,1024]{2,1,0:T(8,128)(2,1)S(1)} %get-tuple-element.85.refs_1_, ...), custom_call_target="tpu_custom_call" | custom-call | flops 1000 | bytes 15000000 | tf_op jit(solution)/shard_map/forward/pallas_call | solution.py:332
  44.4 1.4 %select_cotangents.2 = (bf16[8,64,1024]{2,1,0:T(8,128)(2,1)S(1)}, s32[2]{0:T(128)S(1)}) custom-call(s32[2]{0:T(128)S(1)} %get-tuple-element.88.where_ref, f32[32,128]{1,0:T(8,128)S(1)} %get-tuple-element.89.refs_0_.refs_5_, bf16[4,64,1024]{2,1,0:T(8,128)(2,1)S(1)} %pad_maximum_fusion.2.refs_1_, bf16[4,64,1024]{2,1,0:T(8,128)(2,1)S(1)} %collective-permute-done.11.refs_2_), custom_call_target="tpu_custom_call" | custom-call | flops 1000 | bytes 6000000 | tf_op jit(solution)/shard_map/select_cotangents/pallas_call | solution.py:332
  45.8 2.7 %collective-permute-done.12 = bf16[3,64,1024]{2,1,0:T(8,128)(2,1)S(1)} collective-permute-done((bf16[3,64,1024]{2,1,0:T(8,128)(2,1)S(1)}, bf16[3,64,1024]{2,1,0:T(8,128)(2,1)S(1)}, u32[]{:S(2)}, u32[]{:S(2)}) %collective-permute-start.12) | collective-permute-done | bytes 393248 | tf_op jit(solution)/shard_map/ppermute | solution.py:369
  48.5 0.1 collective-permute-start.13
  48.6 1.9 %collective-permute-done.13.refs_2_ = bf16[4,64,1024]{2,1,0:T(8,128)(2,1)S(1)} collective-permute-done((bf16[4,64,1024]{2,1,0:T(8,128)(2,1)S(1)}, bf16[4,64,1024]{2,1,0:T(8,128)(2,1)S(1)}, u32[]{:S(2)}, u32[]{:S(2)}) %collective-permute-start.13) | collective-permute-done | bytes 524320 | tf_op jit(solution)/shard_map/ppermute | solution.py:363
  50.5 1.4 %select_cotangents.3 = (bf16[8,64,1024]{2,1,0:T(8,128)(2,1)S(1)}, s32[2]{0:T(128)S(1)}) custom-call(s32[2]{0:T(128)S(1)} %get-tuple-element.94.where_ref, f32[32,128]{1,0:T(8,128)S(1)} %get-tuple-element.95.refs_0_.refs_6_, bf16[4,64,1024]{2,1,0:T(8,128)(2,1)S(1)} %pad_maximum_fusion.3.refs_1_, bf16[4,64,1024]{2,1,0:T(8,128)(2,1)S(1)} %collective-permute-done.13.refs_2_), custom_call_target="tpu_custom_call" | custom-call | flops 1000 | bytes 6000000 | tf_op jit(solution)/shard_map/select_cotangents/pallas_call | solution.py:332
  51.9 8.7 %backward.1 = (bf16[8,352,128]{2,1,0:T(8,128)(2,1)S(1)}, bf16[8,352,128]{2,1,0:T(8,128)(2,1)S(1)}, bf16[8,352,128]{2,1,0:T(8,128)(2,1)S(1)}, bf16[8,128,1024]{2,...) custom-call(s32[2]{0:T(128)S(1)} %get-tuple-element.98.where_ref, ...), custom_call_target="tpu_custom_call" | custom-call | flops 1000 | bytes 27000000 | tf_op jit(solution)/shard_map/backward/pallas_call | solution.py:332
  60.6 1.1 %put_back.2 = (bf16[4,528,128]{2,1,0:T(8,128)(2,1)S(1)}, bf16[4,528,128]{2,1,0:T(8,128)(2,1)S(1)}, s32[2]{0:T(128)S(1)}) custom-call(s32[2]{0:T(128)S(1)} %get-tuple-element.106.where_ref, f32[32,128]{1,0:T(8,128)S(1)} %get-tuple-element.95.refs_0_.refs_6_, f32[4,16,128]{2,1,0:T(8,128)S(1)} %get-tuple-element.107.refs_1_, ...), custom_call_target="tpu_custom_call" | custom-call | flops 1000 | bytes 6000000 | tf_op jit(solution)/shard_map/put_back/pallas_call | solution.py:332
  61.7 0.2 collective-permute-start.14
  61.9 1.1 %put_back.3 = (bf16[4,528,128]{2,1,0:T(8,128)(2,1)S(1)}, bf16[4,528,128]{2,1,0:T(8,128)(2,1)S(1)}, s32[2]{0:T(128)S(1)}) custom-call(s32[2]{0:T(128)S(1)} %get-tuple-element.110.where_ref, f32[32,128]{1,0:T(8,128)S(1)} %get-tuple-element.89.refs_0_.refs_5_, f32[4,16,128]{2,1,0:T(8,128)S(1)} %get-tuple-element.111.refs_1_, ...), custom_call_target="tpu_custom_call" | custom-call | flops 1000 | bytes 6000000 | tf_op jit(solution)/shard_map/put_back/pallas_call | solution.py:332
  63.1 0.4 collective-permute-start.15
  63.5 0.2 collective-permute-done.14
  63.7 0.1 add_convert_fusion.refs_4_
  63.8 1.6 %collective-permute-start.16 = (bf16[4,352,128]{2,1,0:T(8,128)(2,1)S(1)}, bf16[4,352,128]{2,1,0:T(8,128)(2,1)S(1)}, u32[]{:S(2)}, u32[]{:S(2)}) collective-permute-start(bf16[4,352,128]{2,1,0:T(8,128)(2,1)S(1)} %add_convert_fusion.refs_4_), channel_id=1, source_target_pairs={{0,2},{2,0},{1,3},{3,1},{4,6},{6,4},{5,7},{7,5},{8,10},{10,8},{9,1... | collective-permute-start | bytes 1081352 | tf_op jit(solution)/shard_map/ppermute | solution.py:369
  65.4 0.1 convert_add_fusion
  65.4 0.0 collective-permute-done.15.refs_1_
  65.5 0.1 convert_add_fusion.1
  65.5 0.1 collective-permute-start.17
  65.6 1.6 %collective-permute-start.18 = (bf16[2,176,128]{2,1,0:T(8,128)(2,1)S(1)}, bf16[2,176,128]{2,1,0:T(8,128)(2,1)S(1)}, u32[]{:S(2)}, u32[]{:S(2)}) collective-permute-start(bf16[2,176,128]{2,1,0:T(8,128)(2,1)S(1)} %pad_maximum_fusion.8.refs_6_), channel_id=1, source_target_pairs={{0,8},{4,12},{8,0},{12,4},{1,9},{5,13},{9,1},{13,5},{2,10},{6,14},... | collective-permute-start | bytes 270344 | tf_op jit(solution)/shard_map/ppermute | solution.py:366
  67.3 2.1 %collective-permute-start.19 = (bf16[2,176,128]{2,1,0:T(8,128)(2,1)S(1)}, bf16[2,176,128]{2,1,0:T(8,128)(2,1)S(1)}, u32[]{:S(2)}, u32[]{:S(2)}) collective-permute-start(bf16[2,176,128]{2,1,0:T(8,128)(2,1)S(1)} %pad_maximum_fusion.9.refs_7_), channel_id=1, source_target_pairs={{0,4},{4,8},{8,12},{12,0},{1,5},{5,9},{9,13},{13,1},{2,6},{6,10},{... | collective-permute-start | bytes 270344 | tf_op jit(solution)/shard_map/ppermute | solution.py:366
  69.3 9.9 %weights.1 = (bf16[8,352,1024]{2,1,0:T(8,128)(2,1)}, bf16[8,352,1024]{2,1,0:T(8,128)(2,1)}, bf16[8,352,1024]{2,1,0:T(8,128)(2,1)}, s32[2]{0:T(128)S(1)}) custom-call(s32[2]{0:T(128)S(1)} %get-tuple-element.112.where_ref, bf16[8,352,128]{2,1,0:T(8,128)(2,1)S(1)} %get-tuple-element.113.dgate_ref, bf16[8,352,128]{2,1,0:T(8,128)(2,1)S(1)} %get-tuple-element.114.dup_ref, ...), custom_call_target="tpu_custom_call" | custom-call | flops 1000 | bytes 27000000 | tf_op jit(solution)/shard_map/weights/pallas_call | solution.py:454
  79.3 0.0 collective-permute-done.17.refs_4_
  79.3 0.0 collective-permute-done.18.refs_5_
  79.3 0.0 collective-permute-done.16.refs_3_
  79.3 1.2 %middle_sums.1 = (f32[352,128]{1,0:T(8,128)S(1)}, bf16[352,128]{1,0:T(8,128)(2,1)S(1)}, bf16[352,128]{1,0:T(8,128)(2,1)S(1)}, bf16[352,128]{1,0:T(8,128)(2,1)S(1...) custom-call(s32[2]{0:T(128)S(1)} %get-tuple-element.120.where_ref, ...), custom_call_target="tpu_custom_call" | custom-call | flops 1000 | bytes 3000000 | tf_op jit(solution)/shard_map/middle_sums/pallas_call | solution.py:332
  80.5 1.9 %collective-permute-start.20 = (bf16[352,128]{1,0:T(8,128)(2,1)S(1)}, bf16[352,128]{1,0:T(8,128)(2,1)S(1)}, u32[]{:S(2)}, u32[]{:S(2)}) collective-permute-start(bf16[352,128]{1,0:T(8,128)(2,1)S(1)} %get-tuple-element.123), channel_id=1, source_target_pairs={{0,12},{4,0},{8,4},{12,8},{1,13},{5,1},{9,5},{13,9},{2,14},{6,2},{... | collective-permute-start | bytes 270344 | tf_op jit(solution)/shard_map/ppermute | solution.py:366
  82.4 1.6 %collective-permute-start.22 = (bf16[352,128]{1,0:T(8,128)(2,1)S(1)}, bf16[352,128]{1,0:T(8,128)(2,1)S(1)}, u32[]{:S(2)}, u32[]{:S(2)}) collective-permute-start(bf16[352,128]{1,0:T(8,128)(2,1)S(1)} %get-tuple-element.125), channel_id=1, source_target_pairs={{0,4},{4,8},{8,12},{12,0},{1,5},{5,9},{9,13},{13,1},{2,6},{6,10},{... | collective-permute-start | bytes 270344 | tf_op jit(solution)/shard_map/ppermute | solution.py:366
  84.0 1.1 %collective-permute-start.23 = (bf16[176,128]{1,0:T(8,128)(2,1)S(1)}, bf16[176,128]{1,0:T(8,128)(2,1)S(1)}, u32[]{:S(2)}, u32[]{:S(2)}) collective-permute-start(bf16[176,128]{1,0:T(8,128)(2,1)S(1)} %get-tuple-element.127), channel_id=1, source_target_pairs={{0,2},{2,0},{1,3},{3,1},{4,6},{6,4},{5,7},{7,5},{8,10},{10,8},{9,1... | collective-permute-start | bytes 135176 | tf_op jit(solution)/shard_map/ppermute | solution.py:369
  85.1 2.9 %collective-permute-done.23.refs_5_ = bf16[176,128]{1,0:T(8,128)(2,1)S(1)} collective-permute-done((bf16[176,128]{1,0:T(8,128)(2,1)S(1)}, bf16[176,128]{1,0:T(8,128)(2,1)S(1)}, u32[]{:S(2)}, u32[]{:S(2)}) %collective-permute-start.23) | collective-permute-done | bytes 45088 | tf_op jit(solution)/shard_map/ppermute | solution.py:369
  88.0 0.0 collective-permute-done.20.refs_1_
  88.0 2.3 %collective-permute-done.21.refs_2_ = bf16[352,128]{1,0:T(8,128)(2,1)S(1)} collective-permute-done((bf16[352,128]{1,0:T(8,128)(2,1)S(1)}, bf16[352,128]{1,0:T(8,128)(2,1)S(1)}, u32[]{:S(2)}, u32[]{:S(2)}) %collective-permute-start.21) | collective-permute-done | bytes 90144 | tf_op jit(solution)/shard_map/ppermute | solution.py:366
  90.4 0.0 collective-permute-done.22.refs_3_
  90.4 1.1 %last_sums.1 = (bf16[528,128]{1,0:T(8,128)(2,1)S(1)}, s32[2]{0:T(128)S(1)}) custom-call(s32[2]{0:T(128)S(1)} %get-tuple-element.121.where_ref, f32[352,128]{1,0:T(8,128)S(1)} %get-tuple-element.122.refs_0_, bf16[352,128]{1,0:T(8,128)(2,1)S(1)} %collective-permute-done.20.refs_1_, bf16[352,128]{1,0:T(8,128)(2,1)S(1)} %collective-permute-done.21.refs_2_, ...), custom_call_target="tpu_custom_call" | custom-call | flops 1000 | bytes 3000000 | tf_op jit(solution)/shard_map/last_sums/pallas_call | solution.py:332
  91.5 0.1 collective-permute-start.24
  91.6 1.3 %collective-permute-done.24.refs_1_ = bf16[528,128]{1,0:T(8,128)(2,1)S(1)} collective-permute-done((bf16[528,128]{1,0:T(8,128)(2,1)S(1)}, bf16[528,128]{1,0:T(8,128)(2,1)S(1)}, u32[]{:S(2)}, u32[]{:S(2)}) %collective-permute-start.24) | collective-permute-done | bytes 135200 | tf_op jit(solution)/shard_map/ppermute | solution.py:363
  92.9 1.3 %unpack.1 = (bf16[128,1024]{1,0:T(8,128)(2,1)}, f32[6,128]{1,0:T(8,128)}, s32[2]{0:T(128)}) custom-call(s32[2]{0:T(128)S(1)} %get-tuple-element.128.where_ref, bf16[528,128]{1,0:T(8,128)(2,1)S(1)} %get-tuple-element.129.refs_0_, bf16[528,128]{1,0:T(8,128)(2,1)S(1)} %collective-permute-done.24.refs_1_), custom_call_target="tpu_custom_call" | custom-call | flops 1000 | bytes 3000000 | tf_op jit(solution)/shard_map/unpack/pallas_call | solution.py:332
  (14 shorter events, 0.3 us)
Async XLA Ops:
  2.9 15.3 %collective-permute-start.3 = (bf16[528,128]{1,0:T(8,128)(2,1)S(1)}, bf16[528,128]{1,0:T(8,128)(2,1)S(1)}, u32[]{:S(2)}, u32[]{:S(2)}) collective-permute-start(bf16[528,128]{1,0:T(8,128)(2,1)S(1)} %get-tuple-element.72), channel_id=1, source_target_pairs={{0,2},{2,0},{1,3},{3,1},{4,6},{6,4},{5,7},{7,5},{8,10},{10,8},{9,1... | collective-permute-start | bytes 405512 | tf_op jit(solution)/shard_map/ppermute | solution.py:369
  5.9 12.3 %collective-permute-start.2 = (bf16[528,128]{1,0:T(8,128)(2,1)S(1)}, bf16[528,128]{1,0:T(8,128)(2,1)S(1)}, u32[]{:S(2)}, u32[]{:S(2)}) collective-permute-start(bf16[528,128]{1,0:T(8,128)(2,1)S(1)} %get-tuple-element.72), channel_id=1, source_target_pairs={{0,12},{4,0},{8,4},{12,8},{1,13},{5,1},{9,5},{13,9},{2,14},{6,2},{... | collective-permute-start | bytes 405512 | tf_op jit(solution)/shard_map/ppermute | solution.py:366
  9.5 11.1 %collective-permute-start.1 = (bf16[528,128]{1,0:T(8,128)(2,1)S(1)}, bf16[528,128]{1,0:T(8,128)(2,1)S(1)}, u32[]{:S(2)}, u32[]{:S(2)}) collective-permute-start(bf16[528,128]{1,0:T(8,128)(2,1)S(1)} %get-tuple-element.72), channel_id=1, source_target_pairs={{0,8},{4,12},{8,0},{12,4},{1,9},{5,13},{9,1},{13,5},{2,10},{6,14},... | collective-permute-start | bytes 405512 | tf_op jit(solution)/shard_map/ppermute | solution.py:366
  9.5 11.1 %collective-permute-start = (bf16[528,128]{1,0:T(8,128)(2,1)S(1)}, bf16[528,128]{1,0:T(8,128)(2,1)S(1)}, u32[]{:S(2)}, u32[]{:S(2)}) collective-permute-start(bf16[528,128]{1,0:T(8,128)(2,1)S(1)} %get-tuple-element.72), channel_id=1, source_target_pairs={{0,4},{4,8},{8,12},{12,0},{1,5},{5,9},{9,13},{13,1},{2,6},{6,10},{... | collective-permute-start | bytes 405512 | tf_op jit(solution)/shard_map/ppermute | solution.py:366
  10.5 7.7 %collective-permute-start.4 = (bf16[64,1024]{1,0:T(8,128)(2,1)S(1)}, bf16[64,1024]{1,0:T(8,128)(2,1)S(1)}, u32[]{:S(2)}, u32[]{:S(2)}) collective-permute-start(bf16[64,1024]{1,0:T(8,128)(2,1)S(1)} %get-tuple-element.79), channel_id=1, source_target_pairs={{0,2},{2,0},{1,3},{3,1},{4,6},{6,4},{5,7},{7,5},{8,10},{10,8},{9,1... | collective-permute-start | bytes 393224 | tf_op jit(solution)/shard_map/ppermute | solution.py:369
  20.7 5.5 %collective-permute-start.5 = (bf16[4,528,128]{2,1,0:T(8,128)(2,1)S(1)}, bf16[4,528,128]{2,1,0:T(8,128)(2,1)S(1)}, u32[]{:S(2)}, u32[]{:S(2)}) collective-permute-start(bf16[4,528,128]{2,1,0:T(8,128)(2,1)S(1)} %pad_maximum_fusion.refs_0_), channel_id=1, source_target_pairs={{0,1},{1,0},{2,3},{3,2},{4,5},{5,4},{6,7},{7,6},{8,9},{9,8},{10,11... | collective-permute-start | bytes 1622024 | tf_op jit(solution)/shard_map/ppermute | solution.py:363
  20.9 15.7 %collective-permute-start.9 = (bf16[3,528,128]{2,1,0:T(8,128)(2,1)S(1)}, bf16[3,528,128]{2,1,0:T(8,128)(2,1)S(1)}, u32[]{:S(2)}, u32[]{:S(2)}) collective-permute-start(bf16[3,528,128]{2,1,0:T(8,128)(2,1)S(1)} %pad_maximum_fusion.4), channel_id=1, source_target_pairs={{0,2},{2,0},{1,3},{3,1},{4,6},{6,4},{5,7},{7,5},{8,10},{10,8},{9,1... | collective-permute-start | bytes 1216520 | tf_op jit(solution)/shard_map/ppermute | solution.py:369
  21.5 6.1 %collective-permute-start.8 = (bf16[64,1024]{1,0:T(8,128)(2,1)S(1)}, bf16[64,1024]{1,0:T(8,128)(2,1)S(1)}, u32[]{:S(2)}, u32[]{:S(2)}) collective-permute-start(bf16[64,1024]{1,0:T(8,128)(2,1)S(1)} %get-tuple-element.79), channel_id=1, source_target_pairs={{0,12},{4,0},{8,4},{12,8},{1,13},{5,1},{9,5},{13,9},{2,14},{6,2},{... | collective-permute-start | bytes 393224 | tf_op jit(solution)/shard_map/ppermute | solution.py:366
  23.1 13.4 %collective-permute-start.7 = (bf16[64,1024]{1,0:T(8,128)(2,1)S(1)}, bf16[64,1024]{1,0:T(8,128)(2,1)S(1)}, u32[]{:S(2)}, u32[]{:S(2)}) collective-permute-start(bf16[64,1024]{1,0:T(8,128)(2,1)S(1)} %get-tuple-element.79), channel_id=1, source_target_pairs={{0,8},{4,12},{8,0},{12,4},{1,9},{5,13},{9,1},{13,5},{2,10},{6,14},... | collective-permute-start | bytes 393224 | tf_op jit(solution)/shard_map/ppermute | solution.py:366
  24.2 12.3 %collective-permute-start.6 = (bf16[64,1024]{1,0:T(8,128)(2,1)S(1)}, bf16[64,1024]{1,0:T(8,128)(2,1)S(1)}, u32[]{:S(2)}, u32[]{:S(2)}) collective-permute-start(bf16[64,1024]{1,0:T(8,128)(2,1)S(1)} %get-tuple-element.79), channel_id=1, source_target_pairs={{0,4},{4,8},{8,12},{12,0},{1,5},{5,9},{9,13},{13,1},{2,6},{6,10},{... | collective-permute-start | bytes 393224 | tf_op jit(solution)/shard_map/ppermute | solution.py:366
  36.6 2.3 %collective-permute-start.10 = (bf16[4,528,128]{2,1,0:T(8,128)(2,1)S(1)}, bf16[4,528,128]{2,1,0:T(8,128)(2,1)S(1)}, u32[]{:S(2)}, u32[]{:S(2)}) collective-permute-start(bf16[4,528,128]{2,1,0:T(8,128)(2,1)S(1)} %pad_maximum_fusion.1.refs_0_), channel_id=1, source_target_pairs={{0,1},{1,0},{2,3},{3,2},{4,5},{5,4},{6,7},{7,6},{8,9},{9,8},{10,11... | collective-permute-start | bytes 1622024 | tf_op jit(solution)/shard_map/ppermute | solution.py:363
  36.7 7.6 %collective-permute-start.11 = (bf16[4,64,1024]{2,1,0:T(8,128)(2,1)S(1)}, bf16[4,64,1024]{2,1,0:T(8,128)(2,1)S(1)}, u32[]{:S(2)}, u32[]{:S(2)}) collective-permute-start(bf16[4,64,1024]{2,1,0:T(8,128)(2,1)S(1)} %pad_maximum_fusion.2.refs_1_), channel_id=1, source_target_pairs={{0,1},{1,0},{2,3},{3,2},{4,5},{5,4},{6,7},{7,6},{8,9},{9,8},{10,11... | collective-permute-start | bytes 1572872 | tf_op jit(solution)/shard_map/ppermute | solution.py:363
  37.3 11.1 %collective-permute-start.12 = (bf16[3,64,1024]{2,1,0:T(8,128)(2,1)S(1)}, bf16[3,64,1024]{2,1,0:T(8,128)(2,1)S(1)}, u32[]{:S(2)}, u32[]{:S(2)}) collective-permute-start(bf16[3,64,1024]{2,1,0:T(8,128)(2,1)S(1)} %pad_maximum_fusion.5), channel_id=1, source_target_pairs={{0,2},{2,0},{1,3},{3,1},{4,6},{6,4},{5,7},{7,5},{8,10},{10,8},{9,1... | collective-permute-start | bytes 1179656 | tf_op jit(solution)/shard_map/ppermute | solution.py:369
  48.5 2.0 %collective-permute-start.13 = (bf16[4,64,1024]{2,1,0:T(8,128)(2,1)S(1)}, bf16[4,64,1024]{2,1,0:T(8,128)(2,1)S(1)}, u32[]{:S(2)}, u32[]{:S(2)}) collective-permute-start(bf16[4,64,1024]{2,1,0:T(8,128)(2,1)S(1)} %pad_maximum_fusion.3.refs_1_), channel_id=1, source_target_pairs={{0,1},{1,0},{2,3},{3,2},{4,5},{5,4},{6,7},{7,6},{8,9},{9,8},{10,11... | collective-permute-start | bytes 1572872 | tf_op jit(solution)/shard_map/ppermute | solution.py:363
  61.7 2.0 %collective-permute-start.14 = (bf16[4,528,128]{2,1,0:T(8,128)(2,1)S(1)}, bf16[4,528,128]{2,1,0:T(8,128)(2,1)S(1)}, u32[]{:S(2)}, u32[]{:S(2)}) collective-permute-start(bf16[4,528,128]{2,1,0:T(8,128)(2,1)S(1)} %get-tuple-element.117), channel_id=1, source_target_pairs={{0,1},{1,0},{2,3},{3,2},{4,5},{5,4},{6,7},{7,6},{8,9},{9,8},{10,11... | collective-permute-start | bytes 1622024 | tf_op jit(solution)/shard_map/ppermute | solution.py:363
  63.1 2.4 %collective-permute-start.15 = (bf16[4,528,128]{2,1,0:T(8,128)(2,1)S(1)}, bf16[4,528,128]{2,1,0:T(8,128)(2,1)S(1)}, u32[]{:S(2)}, u32[]{:S(2)}) collective-permute-start(bf16[4,528,128]{2,1,0:T(8,128)(2,1)S(1)} %get-tuple-element.119), channel_id=1, source_target_pairs={{0,1},{1,0},{2,3},{3,2},{4,5},{5,4},{6,7},{7,6},{8,9},{9,8},{10,11... | collective-permute-start | bytes 1622024 | tf_op jit(solution)/shard_map/ppermute | solution.py:363
  63.8 15.5 %collective-permute-start.16 = (bf16[4,352,128]{2,1,0:T(8,128)(2,1)S(1)}, bf16[4,352,128]{2,1,0:T(8,128)(2,1)S(1)}, u32[]{:S(2)}, u32[]{:S(2)}) collective-permute-start(bf16[4,352,128]{2,1,0:T(8,128)(2,1)S(1)} %add_convert_fusion.refs_4_), channel_id=1, source_target_pairs={{0,2},{2,0},{1,3},{3,1},{4,6},{6,4},{5,7},{7,5},{8,10},{10,8},{9,1... | collective-permute-start | bytes 1081352 | tf_op jit(solution)/shard_map/ppermute | solution.py:369
  65.5 13.8 %collective-permute-start.17 = (bf16[2,176,128]{2,1,0:T(8,128)(2,1)S(1)}, bf16[2,176,128]{2,1,0:T(8,128)(2,1)S(1)}, u32[]{:S(2)}, u32[]{:S(2)}) collective-permute-start(bf16[2,176,128]{2,1,0:T(8,128)(2,1)S(1)} %pad_maximum_fusion.7.refs_5_), channel_id=1, source_target_pairs={{0,12},{4,0},{8,4},{12,8},{1,13},{5,1},{9,5},{13,9},{2,14},{6,2},{... | collective-permute-start | bytes 270344 | tf_op jit(solution)/shard_map/ppermute | solution.py:366
  65.6 13.7 %collective-permute-start.18 = (bf16[2,176,128]{2,1,0:T(8,128)(2,1)S(1)}, bf16[2,176,128]{2,1,0:T(8,128)(2,1)S(1)}, u32[]{:S(2)}, u32[]{:S(2)}) collective-permute-start(bf16[2,176,128]{2,1,0:T(8,128)(2,1)S(1)} %pad_maximum_fusion.8.refs_6_), channel_id=1, source_target_pairs={{0,8},{4,12},{8,0},{12,4},{1,9},{5,13},{9,1},{13,5},{2,10},{6,14},... | collective-permute-start | bytes 270344 | tf_op jit(solution)/shard_map/ppermute | solution.py:366
  67.3 12.1 %collective-permute-start.19 = (bf16[2,176,128]{2,1,0:T(8,128)(2,1)S(1)}, bf16[2,176,128]{2,1,0:T(8,128)(2,1)S(1)}, u32[]{:S(2)}, u32[]{:S(2)}) collective-permute-start(bf16[2,176,128]{2,1,0:T(8,128)(2,1)S(1)} %pad_maximum_fusion.9.refs_7_), channel_id=1, source_target_pairs={{0,4},{4,8},{8,12},{12,0},{1,5},{5,9},{9,13},{13,1},{2,6},{6,10},{... | collective-permute-start | bytes 270344 | tf_op jit(solution)/shard_map/ppermute | solution.py:366
  80.5 7.5 %collective-permute-start.20 = (bf16[352,128]{1,0:T(8,128)(2,1)S(1)}, bf16[352,128]{1,0:T(8,128)(2,1)S(1)}, u32[]{:S(2)}, u32[]{:S(2)}) collective-permute-start(bf16[352,128]{1,0:T(8,128)(2,1)S(1)} %get-tuple-element.123), channel_id=1, source_target_pairs={{0,12},{4,0},{8,4},{12,8},{1,13},{5,1},{9,5},{13,9},{2,14},{6,2},{... | collective-permute-start | bytes 270344 | tf_op jit(solution)/shard_map/ppermute | solution.py:366
  82.4 8.0 %collective-permute-start.21 = (bf16[352,128]{1,0:T(8,128)(2,1)S(1)}, bf16[352,128]{1,0:T(8,128)(2,1)S(1)}, u32[]{:S(2)}, u32[]{:S(2)}) collective-permute-start(bf16[352,128]{1,0:T(8,128)(2,1)S(1)} %get-tuple-element.124), channel_id=1, source_target_pairs={{0,8},{4,12},{8,0},{12,4},{1,9},{5,13},{9,1},{13,5},{2,10},{6,14},... | collective-permute-start | bytes 270344 | tf_op jit(solution)/shard_map/ppermute | solution.py:366
  82.4 8.0 %collective-permute-start.22 = (bf16[352,128]{1,0:T(8,128)(2,1)S(1)}, bf16[352,128]{1,0:T(8,128)(2,1)S(1)}, u32[]{:S(2)}, u32[]{:S(2)}) collective-permute-start(bf16[352,128]{1,0:T(8,128)(2,1)S(1)} %get-tuple-element.125), channel_id=1, source_target_pairs={{0,4},{4,8},{8,12},{12,0},{1,5},{5,9},{9,13},{13,1},{2,6},{6,10},{... | collective-permute-start | bytes 270344 | tf_op jit(solution)/shard_map/ppermute | solution.py:366
  84.0 4.0 %collective-permute-start.23 = (bf16[176,128]{1,0:T(8,128)(2,1)S(1)}, bf16[176,128]{1,0:T(8,128)(2,1)S(1)}, u32[]{:S(2)}, u32[]{:S(2)}) collective-permute-start(bf16[176,128]{1,0:T(8,128)(2,1)S(1)} %get-tuple-element.127), channel_id=1, source_target_pairs={{0,2},{2,0},{1,3},{3,1},{4,6},{6,4},{5,7},{7,5},{8,10},{10,8},{9,1... | collective-permute-start | bytes 135176 | tf_op jit(solution)/shard_map/ppermute | solution.py:369
  91.5 1.4 %collective-permute-start.24 = (bf16[528,128]{1,0:T(8,128)(2,1)S(1)}, bf16[528,128]{1,0:T(8,128)(2,1)S(1)}, u32[]{:S(2)}, u32[]{:S(2)}) collective-permute-start(bf16[528,128]{1,0:T(8,128)(2,1)S(1)} %get-tuple-element.129.refs_0_), channel_id=1, source_target_pairs={{0,1},{1,0},{2,3},{3,2},{4,5},{5,4},{6,7},{7,6},{8,9},{9,8},{10,11... | collective-permute-start | bytes 405512 | tf_op jit(solution)/shard_map/ppermute | solution.py:363

commit v5 on v4

--- a/solution.py
+++ b/solution.py
@@ -75,12 +75,12 @@
         ref[(*index, slice(chunk * half, (chunk + 1) * half))] = rows[:, chunk * lanes : (chunk + 1) * lanes]
 
 
-def pack(where_ref, tokens_ref, cotangent_ref, experts_ref, probs_ref, x_ref, dy_ref, token_ref, half_scr, experts_scr,
+def pack(core_ref, where_ref, tokens_ref, cotangent_ref, experts_ref, probs_ref, x_ref, dy_ref, token_ref, half_scr, experts_scr,
          chosen_scr, ids_scr, prob_scr, sems):
-    second = where_ref[1] == 1
+    second = core_ref[0] == 1
     half = dy_ref.shape[0]
     top, kinds = experts_ref.shape[0], ids_scr.shape[0]
-    mine = pl.ds(pl.multiple_of(where_ref[1] * half, half), half)
+    mine = pl.ds(pl.multiple_of(core_ref[0] * half, half), half)
     pairs = ((tokens_ref.at[mine], half_scr), (experts_ref, experts_scr), (probs_ref, chosen_scr),
              (cotangent_ref.at[mine], dy_ref))
     copies = [pltpu.make_async_copy(source, target, sems.at[at]) for at, (source, target) in enumerate(pairs)]
@@ -101,7 +101,7 @@
 def select_tokens(span, where_ref, near_ref, far_ref, rows_ref, rank_ref, weight_ref, meta_ref):
     half, features, height = rank_ref.shape[1] // 2, rows_ref.shape[2], meta_ref.shape[1]
     meta = near_ref[:, near_ref.shape[1] - height :, :].astype(F32)
-    rank, weight = ranks_and_probs(where_ref[0], meta, span, rows_ref.shape[0])
+    rank, weight = ranks_and_probs(where_ref[0:1, : meta.shape[2]], meta, span, rows_ref.shape[0])
     rank_ref[...] = rank
     weight_ref[...] = weight
     meta_ref[...] = meta
@@ -122,7 +122,7 @@
         body(index)
         return carry
 
-    lax.fori_loop(0, count, step, 0, unroll=2 if count % 2 == 0 else 1)
+    lax.fori_loop(0, count, step, 0, unroll=8 if count % 8 == 0 else 1)
 
 
 def forward_kernel(where_ref, wg_ref, wu_ref, *refs):
@@ -175,7 +175,7 @@
     tokens = rank_ref.shape[1]
     half, kinds = tokens // 2, meta_ref.shape[1] // 2
     tail = own_ref.shape[1] - features // own_ref.shape[2] * half
-    wanted = ((where_ref[0] + span * iota((count, tokens), 0)) >> 1).astype(F32)
+    wanted = ((where_ref[0:1, :tokens] + span * iota((count, tokens), 0)) >> 1).astype(F32)
     for source in range(own_ref.shape[0]):
         number = base + source
         pick = slot_matrix(rank_ref[source * count : (source + 1) * count])
@@ -193,16 +193,16 @@
         other_ref[source, own_ref.shape[1] - tail :] = pltpu.roll(lines, half, 1).astype(BF16)
 
 
-def weights_kernel(groups, where_ref, dgate_ref, dup_ref, gated_ref, *refs):
-    rows_x, rows_dy = refs[:groups], refs[groups : 2 * groups]
-    targets, token_ref, slots_ref, sems = refs[-6:-3], *refs[-3:]
-    count, depth = dgate_ref.shape[0], slots_ref.shape[0]
+def weights_kernel(groups, number, where_ref, *refs):
+    hidden_refs, rows_refs = refs[:number], refs[number : number + groups]
+    targets, token_ref, slots_ref, sems = refs[-3 - number : -3], *refs[-3:]
+    count, depth = hidden_refs[0].shape[0], slots_ref.shape[0]
 
     def copies(expert):
         slot = lax.rem(expert, depth)
         return [
-            pltpu.make_async_copy(slots_ref.at[slot, number], target.at[expert], sems.at[slot, number])
-            for number, target in enumerate(targets)
+            pltpu.make_async_copy(slots_ref.at[slot, at], target.at[expert], sems.at[slot, at])
+            for at, target in enumerate(targets)
         ]
 
     def body(expert, carry):
@@ -212,10 +212,9 @@
                 copy.wait()
 
         slot = lax.rem(expert, depth)
-        x, dy = joined(rows_x, expert), joined(rows_dy, expert)
-        slots_ref[slot, 0] = jnp.dot(dgate_ref[expert], x, preferred_element_type=F32).astype(BF16)
-        slots_ref[slot, 1] = jnp.dot(dup_ref[expert], x, preferred_element_type=F32).astype(BF16)
-        slots_ref[slot, 2] = jnp.dot(gated_ref[expert], dy, preferred_element_type=F32).astype(BF16)
+        rows = joined(rows_refs, expert)
+        for at, hidden_ref in enumerate(hidden_refs):
+            slots_ref[slot, at] = jnp.dot(hidden_ref[expert], rows, preferred_element_type=F32).astype(BF16)
         for copy in copies(expert):
             copy.start()
         return carry
@@ -253,14 +252,14 @@
 
 
 def unpack(where_ref, mine_ref, theirs_ref, tokens_ref, probs_ref):
-    second = where_ref[1] == 1
-    mine, theirs = mine_ref[...], theirs_ref[...]
+    mine, theirs = mine_ref[...].astype(F32), theirs_ref[...].astype(F32)
+    second = jnp.broadcast_to(where_ref[1:2, : mine.shape[1]], mine.shape) == 1
     half, features = tokens_ref.shape[0] // 2, tokens_ref.shape[1]
     low, high = jnp.where(second, theirs, mine), jnp.where(second, mine, theirs)
-    tokens_ref[:half] = unpacked(low, half, features)
-    tokens_ref[half:] = unpacked(high, half, features)
+    tokens_ref[:half] = unpacked(low, half, features).astype(BF16)
+    tokens_ref[half:] = unpacked(high, half, features).astype(BF16)
     at = features // low.shape[1] * half
-    low, high = low[at:].astype(F32), high[at:].astype(F32)
+    low, high = low[at:], high[at:]
     both = jnp.where(iota(low.shape, 1) < half, low, pltpu.roll(high, half, 1))
     probs_ref[...] = both[: probs_ref.shape[0]]
 
@@ -286,8 +285,7 @@
 
 
 def pass_on(where_ref, token_ref):
-    for number in range(2):
-        token_ref[number] = where_ref[number]
+    token_ref[...] = where_ref[...]
 
 
 def load_kernel(where_ref, *refs):
@@ -306,20 +304,20 @@
 
 SCALARS = pl.BlockSpec(memory_space=pltpu.SMEM)
 IN_VMEM = pl.BlockSpec(memory_space=pltpu.VMEM)
-TOKEN = jax.ShapeDtypeStruct((2,), jnp.int32)
+WHERE = (8, 128)
 
 
 def load(where, arrays):
     *held, where = pl.pallas_call(
         load_kernel,
-        in_specs=[SCALARS] + [pl.BlockSpec(memory_space=pl.ANY)] * len(arrays),
-        out_specs=[IN_VMEM] * len(arrays) + [SCALARS],
-        out_shape=[vmem_shape(array.shape, array.dtype) for array in arrays] + [TOKEN],
+        in_specs=[IN_VMEM] + [pl.BlockSpec(memory_space=pl.ANY)] * len(arrays),
+        out_specs=[IN_VMEM] * len(arrays) + [IN_VMEM],
+        out_shape=[vmem_shape(array.shape, array.dtype) for array in arrays] + [vmem_shape(WHERE, jnp.int32)],
         scratch_shapes=[pltpu.SemaphoreType.DMA((len(arrays),))],
         compiler_params=pltpu.CompilerParams(vmem_limit_bytes=VMEM_BYTES),
         cost_estimate=cost(7),
         name="load",
-    )(where, *map(in_hbm, arrays))
+    )(in_vmem(where), *map(in_hbm, arrays))
     return where, held
 
 
@@ -331,14 +329,14 @@
 
     *held, where = pl.pallas_call(
         body,
-        in_specs=[SCALARS] + [IN_VMEM] * len(operands),
-        out_specs=[IN_VMEM] * len(outs) + [SCALARS],
-        out_shape=[(vmem_shape if stay else jax.ShapeDtypeStruct)(shape, dtype) for shape, dtype in outs] + [TOKEN],
+        in_specs=[IN_VMEM] * (1 + len(operands)),
+        out_specs=[IN_VMEM] * (len(outs) + 1),
+        out_shape=[(vmem_shape if stay else jax.ShapeDtypeStruct)(shape, dtype) for shape, dtype in outs] + [vmem_shape(WHERE, jnp.int32)],
         scratch_shapes=list(scratch),
         compiler_params=pltpu.CompilerParams(vmem_limit_bytes=VMEM_BYTES),
         cost_estimate=cost(micros),
         name=name,
-    )(where, *map(in_vmem, operands))
+    )(in_vmem(where), *map(in_vmem, operands))
     return where, held
 
 
@@ -371,22 +369,22 @@
     wg = jnp.swapaxes(w_gate, 1, 2).reshape(count, hidden, features)
     wu = jnp.swapaxes(w_up, 1, 2).reshape(count, hidden, features)
     wd = w_down.reshape(count, hidden, features)
-    where = jnp.stack([position * halves, core]).astype(jnp.int32)
+    where = jnp.where(iota(WHERE, 0) == 0, position * halves, core).astype(jnp.int32)
     group = zs * MOST
     packed = features // rows * half
     own_x, own_dy, where = pl.pallas_call(
         pack,
-        in_specs=[SCALARS] + [pl.BlockSpec(memory_space=pl.ANY)] * 4,
-        out_specs=[IN_VMEM] * 2 + [SCALARS],
+        in_specs=[SCALARS, IN_VMEM] + [pl.BlockSpec(memory_space=pl.ANY)] * 4,
+        out_specs=[IN_VMEM] * 3,
         out_shape=[jax.ShapeDtypeStruct((packed + 2 * kinds, rows), BF16), jax.ShapeDtypeStruct((half, features), BF16),
-                   TOKEN],
+                   vmem_shape(WHERE, jnp.int32)],
         scratch_shapes=[pltpu.VMEM((half, features), BF16), pltpu.VMEM((top, rows), jnp.int32),
                         pltpu.VMEM((top, rows), BF16), pltpu.VMEM((kinds, rows), F32), pltpu.VMEM((kinds, rows), F32),
                         pltpu.SemaphoreType.DMA((4,))],
         compiler_params=pltpu.CompilerParams(vmem_limit_bytes=VMEM_BYTES),
         cost_estimate=cost(2),
         name="pack",
-    )(where, in_hbm(tokens), in_hbm(cotangent), in_hbm(experts.T), in_hbm(probs.T))
+    )(core.astype(jnp.int32).reshape(1), in_vmem(where), in_hbm(tokens), in_hbm(cotangent), in_hbm(experts.T), in_hbm(probs.T))
 
     line_x = [along_z(own_x, d) for d in range(1, zs)]
     first_x = [along_x(own_x, c) for c in range(1, xs)]
@@ -447,20 +445,19 @@
         own, other = chip[c]
         return own[index].astype(F32) + other[index].astype(F32)
 
-    saved = (dgate, dup, gated, *rows_x, *rows_dy)
-
-    def weights(where, after):
-        depth = min(count, 2)
+    def weights(where, sources, shared, after):
+        depth, number = min(count, 3), len(sources)
+        operands = [in_vmem(array) for array in (*sources, *shared)]
         *grads, where = pl.pallas_call(
-            functools.partial(weights_kernel, xs),
-            in_specs=[SCALARS] + [IN_VMEM] * len(saved) + [pl.BlockSpec(memory_space=pl.ANY)] * len(after),
-            out_specs=[pl.BlockSpec(memory_space=pl.ANY)] * 3 + [SCALARS],
-            out_shape=[jax.ShapeDtypeStruct((count, hidden, features), BF16)] * 3 + [TOKEN],
-            scratch_shapes=[pltpu.VMEM((depth, 3, hidden, features), BF16), pltpu.SemaphoreType.DMA((depth, 3))],
+            functools.partial(weights_kernel, xs, number),
+            in_specs=[IN_VMEM] * (1 + len(operands)) + [pl.BlockSpec(memory_space=pl.ANY)] * len(after),
+            out_specs=[pl.BlockSpec(memory_space=pl.ANY)] * number + [IN_VMEM],
+            out_shape=[jax.ShapeDtypeStruct((count, hidden, features), BF16)] * number + [vmem_shape(WHERE, jnp.int32)],
+            scratch_shapes=[pltpu.VMEM((depth, number, hidden, features), BF16), pltpu.SemaphoreType.DMA((depth, number))],
             compiler_params=pltpu.CompilerParams(vmem_limit_bytes=VMEM_BYTES),
-            cost_estimate=cost(9),
+            cost_estimate=cost(3 * number),
             name="weights",
-        )(where, *map(in_vmem, saved), *after)
+        )(in_vmem(where), *operands, *after)
         return where, grads
 
     first, last = slice(0, split), slice(split, height)
@@ -469,19 +466,19 @@
     lining = [side.astype(BF16) for side in sides[1:]]
     hops = [along_x(array, -c) for c, array in enumerate(crossing, 1)]
     shifts = [along_z(array, -d) for d, array in enumerate(lining, 1)]
-    where, grads = weights(where, crossing + lining)
+    where, (grad_gate, grad_up) = weights(where, (dgate, dup), rows_x, crossing + lining)
     outs = [((split, rows), BF16 if d else F32) for d in range(zs)]
     outs += [((height - split, rows), BF16 if c else F32) for c in range(xs)]
     where, sums = on_vmem(functools.partial(middle_sums, zs, xs), "middle_sums", 1, outs, where,
                           (*chip[0], sides[0], *hops, *shifts), False)
     parts = [along_z(sums[d], -d) if d else sums[d] for d in range(zs)]
     parts += [along_x(sums[zs + c], -c) if c else sums[zs] for c in range(xs)]
+    where, (grad_down,) = weights(where, (gated,), rows_dy, [array for array in sums if array.dtype == BF16])
     where, (mine,) = on_vmem(functools.partial(last_sums, zs, xs), "last_sums", 1, [((height, rows), BF16)], where,
                              parts, False)
     outs = [((rows, features), BF16), ((top, rows), F32)]
     where, (grad_tokens, grad_probs) = on_vmem(unpack, "unpack", 1, outs, where, (mine, swap(mine)), False)
     grad_probs = grad_probs.T
-    grad_gate, grad_up, grad_down = grads
     shape = (halves, quarter, features)
     return (
         grad_tokens,

time: 94.4 us -> 82.7 us (0.88)
  Pallas kernels: 43.4 us -> 29.4 us
  waiting for transfers between devices: 22.8 us -> 25.3 us
    pallas_call x14 -> x15, Pallas kernels: 43.4 us -> 29.4 us  [the longest x11 12.9 us: on_vmem(): pl.pallas_call(body, in_specs=[IN_VMEM] * (1 + len(operands)), out_specs=...]
    ppermute x12, waiting for transfers between devices: 13.8 us -> 15.7 us  [along_z(): lax.ppermute(array, 'expert', [(i, (i + by) % zs) for i in range(zs)])]
  transfers between devices with their start and end apart: 25 -> 25, of which waited for: 8 -> 9; matrix products, arithmetic and copies ran while one was open for 0% -> 0% of each run, Pallas kernels for 28% -> 25%
where the time goes in v5:
time: 82.7 us; the launch traced here: 82.6 us
  Pallas kernels  29.4 us (36%)
  starting transfers between devices  26.3 us (32%)
  waiting for transfers between devices  25.3 us (31%)
  between operations  0.93 us (1%)
    ppermute x12, starting transfers between devices, along_z(): lax.ppermute(array, 'expert', [(i, (i + by) % zs) for i in range(zs)])  16.6 us
    ppermute x12, waiting for transfers between devices, along_z(): lax.ppermute(array, 'expert', [(i, (i + by) % zs) for i in range(zs)])  15.7 us
    pallas_call x11, Pallas kernels, on_vmem(): pl.pallas_call(body, in_specs=[IN_VMEM] * (1 + len(operands)), out_specs=...  12.9 us
    pallas_call x2, Pallas kernels, weights(): pl.pallas_call(functools.partial(weights_kernel, xs, number), in_specs=[I...  9.34 us
    ppermute x6, starting transfers between devices, along_x(): return lax.ppermute(array, 'blk', [(i, (i + by) % xs) for i in range(xs)])  8.21 us
    pallas_call x1, Pallas kernels, load(): pl.pallas_call(load_kernel, in_specs=[IN_VMEM] + [pl.BlockSpec(memory_spa...  6 us
    ppermute x6, waiting for transfers between devices, along_x(): return lax.ppermute(array, 'blk', [(i, (i + by) % xs) for i in range(xs)])  5.42 us
    ppermute x7, waiting for transfers between devices, swap(): lax.ppermute(array, 'tensor', [(i, (i + 1) % cores) for i in range(cores)])  4.14 us
  transfers between devices with their start and end apart: 25, of which 9 were waited for; matrix products, arithmetic and copies ran while one was open for 0% of the time, Pallas kernels for 25%

profile of v5, /device:TPU:0, one launch (start us, length us, event | category | flops | bytes accessed | tf_op | source)
XLA Modules:
  0.0 82.6 jit_solution(13548655445128022333)
XLA Ops:
  0.7 0.1 iota.7.where_ref
  0.7 1.1 %pack.1 = (bf16[528,128]{1,0:T(8,128)(2,1)S(1)}, bf16[64,1024]{1,0:T(8,128)(2,1)S(1)}, s32[8,128]{1,0:T(8,128)S(1)}) custom-call(s32[1]{0:T(128)} %bitcast.core_ref, s32[8,128]{1,0:T(8,128)S(1)} %iota.7.where_ref, bf16[128,1024]{1,0:T(8,128)(2,1)} %tokens_ref.1, bf16[128,1024]{1,0:T(8,128)(2,1)} %cotangent_ref.1, s32[6,128]{1,0:T(8,128)} %bitcast.47, ...), custom_call_target="tpu_custom_call" | custom-call | flops 1000 | bytes 6000000 | tf_op jit(solution)/shard_map/pack/pallas_call | solution.py:375
  1.9 3.0 %collective-permute-start.3 = (bf16[528,128]{1,0:T(8,128)(2,1)S(1)}, bf16[528,128]{1,0:T(8,128)(2,1)S(1)}, u32[]{:S(2)}, u32[]{:S(2)}) collective-permute-start(bf16[528,128]{1,0:T(8,128)(2,1)S(1)} %get-tuple-element.73), channel_id=1, source_target_pairs={{0,2},{2,0},{1,3},{3,1},{4,6},{6,4},{5,7},{7,5},{8,10},{10,8},{9,1... | collective-permute-start | bytes 405512 | tf_op jit(solution)/shard_map/ppermute | solution.py:367
  4.9 3.6 %collective-permute-start.2 = (bf16[528,128]{1,0:T(8,128)(2,1)S(1)}, bf16[528,128]{1,0:T(8,128)(2,1)S(1)}, u32[]{:S(2)}, u32[]{:S(2)}) collective-permute-start(bf16[528,128]{1,0:T(8,128)(2,1)S(1)} %get-tuple-element.73), channel_id=1, source_target_pairs={{0,12},{4,0},{8,4},{12,8},{1,13},{5,1},{9,5},{13,9},{2,14},{6,2},{... | collective-permute-start | bytes 405512 | tf_op jit(solution)/shard_map/ppermute | solution.py:364
  8.5 0.0 collective-permute-start.1
  8.5 1.0 %collective-permute-start = (bf16[528,128]{1,0:T(8,128)(2,1)S(1)}, bf16[528,128]{1,0:T(8,128)(2,1)S(1)}, u32[]{:S(2)}, u32[]{:S(2)}) collective-permute-start(bf16[528,128]{1,0:T(8,128)(2,1)S(1)} %get-tuple-element.73), channel_id=1, source_target_pairs={{0,4},{4,8},{8,12},{12,0},{1,5},{5,9},{9,13},{13,1},{2,6},{6,10},{... | collective-permute-start | bytes 405512 | tf_op jit(solution)/shard_map/ppermute | solution.py:364
  9.5 0.5 collective-permute-start.4
  10.0 6.0 %load.1 = (bf16[8,352,1024]{2,1,0:T(8,128)(2,1)S(1)}, bf16[8,352,1024]{2,1,0:T(8,128)(2,1)S(1)}, bf16[8,352,1024]{2,1,0:T(8,128)(2,1)S(1)}, s32[8,128]{1,0:T(8,128)S(1)}) custom-call(s32[8,128]{1,0:T(8,128)S(1)} %get-tuple-element.71.where_ref, bf16[8,352,1024]{2,1,0:T(8,128)(2,1)} %bitcast.30, bf16[8,352,1024]{2,1,0:T(8,128)(2,1)} %bitcast.31, ...), custom_call_target="tpu_custom_call" | custom-call | flops 1000 | bytes 21000000 | tf_op jit(solution)/shard_map/load/pallas_call | solution.py:311
  16.0 0.0 collective-permute-done.4
  16.0 0.0 collective-permute-done.3
  16.0 0.0 collective-permute-done.2
  16.1 3.6 %collective-permute-done.1 = bf16[528,128]{1,0:T(8,128)(2,1)S(1)} collective-permute-done((bf16[528,128]{1,0:T(8,128)(2,1)S(1)}, bf16[528,128]{1,0:T(8,128)(2,1)S(1)}, u32[]{:S(2)}, u32[]{:S(2)}) %collective-permute-start.1) | collective-permute-done | bytes 135200 | tf_op jit(solution)/shard_map/ppermute | solution.py:364
  19.6 0.0 collective-permute-done
  19.6 0.1 pad_maximum_fusion.refs_0_
  19.7 0.1 collective-permute-start.5
  19.8 0.6 collective-permute-start.9
  20.4 1.6 %collective-permute-start.8 = (bf16[64,1024]{1,0:T(8,128)(2,1)S(1)}, bf16[64,1024]{1,0:T(8,128)(2,1)S(1)}, u32[]{:S(2)}, u32[]{:S(2)}) collective-permute-start(bf16[64,1024]{1,0:T(8,128)(2,1)S(1)} %get-tuple-element.80), channel_id=1, source_target_pairs={{0,12},{4,0},{8,4},{12,8},{1,13},{5,1},{9,5},{13,9},{2,14},{6,2},{... | collective-permute-start | bytes 393224 | tf_op jit(solution)/shard_map/ppermute | solution.py:364
  22.1 1.1 %collective-permute-start.7 = (bf16[64,1024]{1,0:T(8,128)(2,1)S(1)}, bf16[64,1024]{1,0:T(8,128)(2,1)S(1)}, u32[]{:S(2)}, u32[]{:S(2)}) collective-permute-start(bf16[64,1024]{1,0:T(8,128)(2,1)S(1)} %get-tuple-element.80), channel_id=1, source_target_pairs={{0,8},{4,12},{8,0},{12,4},{1,9},{5,13},{9,1},{13,5},{2,10},{6,14},... | collective-permute-start | bytes 393224 | tf_op jit(solution)/shard_map/ppermute | solution.py:364
  23.2 2.0 %collective-permute-start.6 = (bf16[64,1024]{1,0:T(8,128)(2,1)S(1)}, bf16[64,1024]{1,0:T(8,128)(2,1)S(1)}, u32[]{:S(2)}, u32[]{:S(2)}) collective-permute-start(bf16[64,1024]{1,0:T(8,128)(2,1)S(1)} %get-tuple-element.80), channel_id=1, source_target_pairs={{0,4},{4,8},{8,12},{12,0},{1,5},{5,9},{9,13},{13,1},{2,6},{6,10},{... | collective-permute-start | bytes 393224 | tf_op jit(solution)/shard_map/ppermute | solution.py:364
  25.2 0.0 collective-permute-done.5.refs_1_
  25.2 0.6 select_tokens.2
  25.8 0.3 collective-permute-done.8
  26.0 9.4 %collective-permute-done.7 = bf16[64,1024]{1,0:T(8,128)(2,1)S(1)} collective-permute-done((bf16[64,1024]{1,0:T(8,128)(2,1)S(1)}, bf16[64,1024]{1,0:T(8,128)(2,1)S(1)}, u32[]{:S(2)}, u32[]{:S(2)}) %collective-permute-start.7) | collective-permute-done | bytes 131104 | tf_op jit(solution)/shard_map/ppermute | solution.py:364
  35.5 0.0 collective-permute-done.9
  35.5 0.1 collective-permute-start.10
  35.6 0.1 pad_maximum_fusion.2.refs_1_
  35.7 0.6 collective-permute-start.11
  36.3 1.6 %collective-permute-start.12 = (bf16[3,64,1024]{2,1,0:T(8,128)(2,1)S(1)}, bf16[3,64,1024]{2,1,0:T(8,128)(2,1)S(1)}, u32[]{:S(2)}, u32[]{:S(2)}) collective-permute-start(bf16[3,64,1024]{2,1,0:T(8,128)(2,1)S(1)} %pad_maximum_fusion.5), channel_id=1, source_target_pairs={{0,2},{2,0},{1,3},{3,1},{4,6},{6,4},{5,7},{7,5},{8,10},{10,8},{9,1... | collective-permute-start | bytes 1179656 | tf_op jit(solution)/shard_map/ppermute | solution.py:367
  37.9 0.6 select_tokens.3
  38.4 3.1 %forward.1 = (f32[8,352,128]{2,1,0:T(8,128)S(1)}, f32[8,352,128]{2,1,0:T(8,128)S(1)}, s32[8,128]{1,0:T(8,128)S(1)}) custom-call(s32[8,128]{1,0:T(8,128)S(1)} %get-tuple-element.84.where_ref, bf16[8,352,1024]{2,1,0:T(8,128)(2,1)S(1)} %get-tuple-element.85.refs_0_, bf16[8,352,1024]{2,1,0:T(8,128)(2,1)S(1)} %get-tuple-element.86.refs_1_, ...), custom_call_target="tpu_custom_call" | custom-call | flops 1000 | bytes 15000000 | tf_op jit(solution)/shard_map/forward/pallas_call | solution.py:330
  41.6 0.4 select_cotangents.2
  42.0 5.4 %collective-permute-done.12 = bf16[3,64,1024]{2,1,0:T(8,128)(2,1)S(1)} collective-permute-done((bf16[3,64,1024]{2,1,0:T(8,128)(2,1)S(1)}, bf16[3,64,1024]{2,1,0:T(8,128)(2,1)S(1)}, u32[]{:S(2)}, u32[]{:S(2)}) %collective-permute-start.12) | collective-permute-done | bytes 393248 | tf_op jit(solution)/shard_map/ppermute | solution.py:367
  47.5 0.1 collective-permute-start.13
  47.5 1.9 %collective-permute-done.13.refs_2_ = bf16[4,64,1024]{2,1,0:T(8,128)(2,1)S(1)} collective-permute-done((bf16[4,64,1024]{2,1,0:T(8,128)(2,1)S(1)}, bf16[4,64,1024]{2,1,0:T(8,128)(2,1)S(1)}, u32[]{:S(2)}, u32[]{:S(2)}) %collective-permute-start.13) | collective-permute-done | bytes 524320 | tf_op jit(solution)/shard_map/ppermute | solution.py:361
  49.4 0.4 select_cotangents.3
  49.9 5.8 %backward.1 = (bf16[8,352,128]{2,1,0:T(8,128)(2,1)S(1)}, bf16[8,352,128]{2,1,0:T(8,128)(2,1)S(1)}, bf16[8,352,128]{2,1,0:T(8,128)(2,1)S(1)}, bf16[8,128,1024]{2,...) custom-call(s32[8,128]{1,0:T(8,128)S(1)} %get-tuple-element.99.where_ref, ...), custom_call_target="tpu_custom_call" | custom-call | flops 1000 | bytes 27000000 | tf_op jit(solution)/shard_map/backward/pallas_call | solution.py:330
  55.7 0.5 put_back.2
  56.2 0.2 collective-permute-start.14
  56.4 0.5 put_back.3
  56.9 0.4 collective-permute-start.15
  57.3 0.9 %collective-permute-done.14 = bf16[4,528,128]{2,1,0:T(8,128)(2,1)S(1)} collective-permute-done((bf16[4,528,128]{2,1,0:T(8,128)(2,1)S(1)}, bf16[4,528,128]{2,1,0:T(8,128)(2,1)S(1)}, u32[]{:S(2)}, u32[]{:S(2)}) %collective-permute-start.14) | collective-permute-done | bytes 540704 | tf_op jit(solution)/shard_map/ppermute | solution.py:361
  58.2 0.1 add_convert_fusion.refs_4_
  58.3 1.6 %collective-permute-start.16 = (bf16[4,352,128]{2,1,0:T(8,128)(2,1)S(1)}, bf16[4,352,128]{2,1,0:T(8,128)(2,1)S(1)}, u32[]{:S(2)}, u32[]{:S(2)}) collective-permute-start(bf16[4,352,128]{2,1,0:T(8,128)(2,1)S(1)} %add_convert_fusion.refs_4_), channel_id=1, source_target_pairs={{0,2},{2,0},{1,3},{3,1},{4,6},{6,4},{5,7},{7,5},{8,10},{10,8},{9,1... | collective-permute-start | bytes 1081352 | tf_op jit(solution)/shard_map/ppermute | solution.py:367
  60.0 0.1 collective-permute-start.17
  60.1 1.6 %collective-permute-start.18 = (bf16[2,176,128]{2,1,0:T(8,128)(2,1)S(1)}, bf16[2,176,128]{2,1,0:T(8,128)(2,1)S(1)}, u32[]{:S(2)}, u32[]{:S(2)}) collective-permute-start(bf16[2,176,128]{2,1,0:T(8,128)(2,1)S(1)} %pad_maximum_fusion.8.refs_6_), channel_id=1, source_target_pairs={{0,8},{4,12},{8,0},{12,4},{1,9},{5,13},{9,1},{13,5},{2,10},{6,14},... | collective-permute-start | bytes 270344 | tf_op jit(solution)/shard_map/ppermute | solution.py:364
  61.7 2.1 %collective-permute-start.19 = (bf16[2,176,128]{2,1,0:T(8,128)(2,1)S(1)}, bf16[2,176,128]{2,1,0:T(8,128)(2,1)S(1)}, u32[]{:S(2)}, u32[]{:S(2)}) collective-permute-start(bf16[2,176,128]{2,1,0:T(8,128)(2,1)S(1)} %pad_maximum_fusion.9.refs_7_), channel_id=1, source_target_pairs={{0,4},{4,8},{8,12},{12,0},{1,5},{5,9},{9,13},{13,1},{2,6},{6,10},{... | collective-permute-start | bytes 270344 | tf_op jit(solution)/shard_map/ppermute | solution.py:364
  63.8 5.4 %weights.2 = (bf16[8,352,1024]{2,1,0:T(8,128)(2,1)}, bf16[8,352,1024]{2,1,0:T(8,128)(2,1)}, s32[8,128]{1,0:T(8,128)S(1)}) custom-call(s32[8,128]{1,0:T(8,128)S(1)} %get-tuple-element.113.where_ref, bf16[8,352,128]{2,1,0:T(8,128)(2,1)S(1)} %get-tuple-element.114.refs_0_, bf16[8,352,128]{2,1,0:T(8,128)(2,1)S(1)} %get-tuple-element.115.refs_1_, ...), custom_call_target="tpu_custom_call" | custom-call | flops 1000 | bytes 18000000 | tf_op jit(solution)/shard_map/weights/pallas_call | solution.py:451
  69.2 0.0 collective-permute-done.17.refs_4_
  69.2 0.8 %collective-permute-done.18.refs_5_ = bf16[2,176,128]{2,1,0:T(8,128)(2,1)S(1)} collective-permute-done((bf16[2,176,128]{2,1,0:T(8,128)(2,1)S(1)}, bf16[2,176,128]{2,1,0:T(8,128)(2,1)S(1)}, u32[]{:S(2)}, u32[]{:S(2)}) %collective-permute-start.18) | collective-permute-done | bytes 90144 | tf_op jit(solution)/shard_map/ppermute | solution.py:364
  70.0 0.0 collective-permute-done.19.refs_6_
  70.0 0.0 collective-permute-done.16.refs_3_
  70.0 0.2 middle_sums.1
  70.2 1.1 %collective-permute-start.20 = (bf16[352,128]{1,0:T(8,128)(2,1)S(1)}, bf16[352,128]{1,0:T(8,128)(2,1)S(1)}, u32[]{:S(2)}, u32[]{:S(2)}) collective-permute-start(bf16[352,128]{1,0:T(8,128)(2,1)S(1)} %get-tuple-element.123.refs_3_), channel_id=1, source_target_pairs={{0,12},{4,0},{8,4},{12,8},{1,13},{5,1},{9,5},{13,9},{2,14},{6,2},{... | collective-permute-start | bytes 270344 | tf_op jit(solution)/shard_map/ppermute | solution.py:364
  71.3 0.5 collective-permute-start.21
  71.8 1.9 %collective-permute-start.22 = (bf16[352,128]{1,0:T(8,128)(2,1)S(1)}, bf16[352,128]{1,0:T(8,128)(2,1)S(1)}, u32[]{:S(2)}, u32[]{:S(2)}) collective-permute-start(bf16[352,128]{1,0:T(8,128)(2,1)S(1)} %get-tuple-element.125.refs_5_), channel_id=1, source_target_pairs={{0,4},{4,8},{8,12},{12,0},{1,5},{5,9},{9,13},{13,1},{2,6},{6,10},{... | collective-permute-start | bytes 270344 | tf_op jit(solution)/shard_map/ppermute | solution.py:364
  73.7 1.0 %collective-permute-start.23 = (bf16[176,128]{1,0:T(8,128)(2,1)S(1)}, bf16[176,128]{1,0:T(8,128)(2,1)S(1)}, u32[]{:S(2)}, u32[]{:S(2)}) collective-permute-start(bf16[176,128]{1,0:T(8,128)(2,1)S(1)} %get-tuple-element.126.refs_6_), channel_id=1, source_target_pairs={{0,2},{2,0},{1,3},{3,1},{4,6},{6,4},{5,7},{7,5},{8,10},{10,8},{9,1... | collective-permute-start | bytes 135176 | tf_op jit(solution)/shard_map/ppermute | solution.py:367
  74.7 4.0 %weights.3 = (bf16[8,352,1024]{2,1,0:T(8,128)(2,1)}, s32[8,128]{1,0:T(8,128)S(1)}) custom-call(s32[8,128]{1,0:T(8,128)S(1)} %get-tuple-element.121.where_ref, bf16[8,352,128]{2,1,0:T(8,128)(2,1)S(1)} %get-tuple-element.122.refs_0_, bf16[8,64,1024]{2,1,0:T(8,128)(2,1)S(1)} %get-tuple-element.105.refs_9_.refs_1_, ...), custom_call_target="tpu_custom_call" | custom-call | flops 1000 | bytes 9000000 | tf_op jit(solution)/shard_map/weights/pallas_call | solution.py:451
  78.6 0.0 collective-permute-done.23.refs_5_
  78.7 1.6 %collective-permute-done.21.refs_2_ = bf16[352,128]{1,0:T(8,128)(2,1)S(1)} collective-permute-done((bf16[352,128]{1,0:T(8,128)(2,1)S(1)}, bf16[352,128]{1,0:T(8,128)(2,1)S(1)}, u32[]{:S(2)}, u32[]{:S(2)}) %collective-permute-start.21) | collective-permute-done | bytes 90144 | tf_op jit(solution)/shard_map/ppermute | solution.py:364
  80.3 0.0 collective-permute-done.22.refs_3_
  80.3 0.1 last_sums.1
  80.3 0.1 collective-permute-start.24
  80.4 1.3 %collective-permute-done.24.refs_1_ = bf16[528,128]{1,0:T(8,128)(2,1)S(1)} collective-permute-done((bf16[528,128]{1,0:T(8,128)(2,1)S(1)}, bf16[528,128]{1,0:T(8,128)(2,1)S(1)}, u32[]{:S(2)}, u32[]{:S(2)}) %collective-permute-start.24) | collective-permute-done | bytes 135200 | tf_op jit(solution)/shard_map/ppermute | solution.py:361
  81.8 0.8 unpack.1
  (16 shorter events, 0.4 us)
Async XLA Ops:
  1.9 14.2 %collective-permute-start.3 = (bf16[528,128]{1,0:T(8,128)(2,1)S(1)}, bf16[528,128]{1,0:T(8,128)(2,1)S(1)}, u32[]{:S(2)}, u32[]{:S(2)}) collective-permute-start(bf16[528,128]{1,0:T(8,128)(2,1)S(1)} %get-tuple-element.73), channel_id=1, source_target_pairs={{0,2},{2,0},{1,3},{3,1},{4,6},{6,4},{5,7},{7,5},{8,10},{10,8},{9,1... | collective-permute-start | bytes 405512 | tf_op jit(solution)/shard_map/ppermute | solution.py:367
  4.9 11.2 %collective-permute-start.2 = (bf16[528,128]{1,0:T(8,128)(2,1)S(1)}, bf16[528,128]{1,0:T(8,128)(2,1)S(1)}, u32[]{:S(2)}, u32[]{:S(2)}) collective-permute-start(bf16[528,128]{1,0:T(8,128)(2,1)S(1)} %get-tuple-element.73), channel_id=1, source_target_pairs={{0,12},{4,0},{8,4},{12,8},{1,13},{5,1},{9,5},{13,9},{2,14},{6,2},{... | collective-permute-start | bytes 405512 | tf_op jit(solution)/shard_map/ppermute | solution.py:364
  8.5 11.1 %collective-permute-start.1 = (bf16[528,128]{1,0:T(8,128)(2,1)S(1)}, bf16[528,128]{1,0:T(8,128)(2,1)S(1)}, u32[]{:S(2)}, u32[]{:S(2)}) collective-permute-start(bf16[528,128]{1,0:T(8,128)(2,1)S(1)} %get-tuple-element.73), channel_id=1, source_target_pairs={{0,8},{4,12},{8,0},{12,4},{1,9},{5,13},{9,1},{13,5},{2,10},{6,14},... | collective-permute-start | bytes 405512 | tf_op jit(solution)/shard_map/ppermute | solution.py:364
  8.5 11.1 %collective-permute-start = (bf16[528,128]{1,0:T(8,128)(2,1)S(1)}, bf16[528,128]{1,0:T(8,128)(2,1)S(1)}, u32[]{:S(2)}, u32[]{:S(2)}) collective-permute-start(bf16[528,128]{1,0:T(8,128)(2,1)S(1)} %get-tuple-element.73), channel_id=1, source_target_pairs={{0,4},{4,8},{8,12},{12,0},{1,5},{5,9},{9,13},{13,1},{2,6},{6,10},{... | collective-permute-start | bytes 405512 | tf_op jit(solution)/shard_map/ppermute | solution.py:364
  9.5 6.5 %collective-permute-start.4 = (bf16[64,1024]{1,0:T(8,128)(2,1)S(1)}, bf16[64,1024]{1,0:T(8,128)(2,1)S(1)}, u32[]{:S(2)}, u32[]{:S(2)}) collective-permute-start(bf16[64,1024]{1,0:T(8,128)(2,1)S(1)} %get-tuple-element.80), channel_id=1, source_target_pairs={{0,2},{2,0},{1,3},{3,1},{4,6},{6,4},{5,7},{7,5},{8,10},{10,8},{9,1... | collective-permute-start | bytes 393224 | tf_op jit(solution)/shard_map/ppermute | solution.py:367
  19.7 5.5 %collective-permute-start.5 = (bf16[4,528,128]{2,1,0:T(8,128)(2,1)S(1)}, bf16[4,528,128]{2,1,0:T(8,128)(2,1)S(1)}, u32[]{:S(2)}, u32[]{:S(2)}) collective-permute-start(bf16[4,528,128]{2,1,0:T(8,128)(2,1)S(1)} %pad_maximum_fusion.refs_0_), channel_id=1, source_target_pairs={{0,1},{1,0},{2,3},{3,2},{4,5},{5,4},{6,7},{7,6},{8,9},{9,8},{10,11... | collective-permute-start | bytes 1622024 | tf_op jit(solution)/shard_map/ppermute | solution.py:361
  19.8 15.7 %collective-permute-start.9 = (bf16[3,528,128]{2,1,0:T(8,128)(2,1)S(1)}, bf16[3,528,128]{2,1,0:T(8,128)(2,1)S(1)}, u32[]{:S(2)}, u32[]{:S(2)}) collective-permute-start(bf16[3,528,128]{2,1,0:T(8,128)(2,1)S(1)} %pad_maximum_fusion.4), channel_id=1, source_target_pairs={{0,2},{2,0},{1,3},{3,1},{4,6},{6,4},{5,7},{7,5},{8,10},{10,8},{9,1... | collective-permute-start | bytes 1216520 | tf_op jit(solution)/shard_map/ppermute | solution.py:367
  20.4 5.6 %collective-permute-start.8 = (bf16[64,1024]{1,0:T(8,128)(2,1)S(1)}, bf16[64,1024]{1,0:T(8,128)(2,1)S(1)}, u32[]{:S(2)}, u32[]{:S(2)}) collective-permute-start(bf16[64,1024]{1,0:T(8,128)(2,1)S(1)} %get-tuple-element.80), channel_id=1, source_target_pairs={{0,12},{4,0},{8,4},{12,8},{1,13},{5,1},{9,5},{13,9},{2,14},{6,2},{... | collective-permute-start | bytes 393224 | tf_op jit(solution)/shard_map/ppermute | solution.py:364
  22.1 13.4 %collective-permute-start.7 = (bf16[64,1024]{1,0:T(8,128)(2,1)S(1)}, bf16[64,1024]{1,0:T(8,128)(2,1)S(1)}, u32[]{:S(2)}, u32[]{:S(2)}) collective-permute-start(bf16[64,1024]{1,0:T(8,128)(2,1)S(1)} %get-tuple-element.80), channel_id=1, source_target_pairs={{0,8},{4,12},{8,0},{12,4},{1,9},{5,13},{9,1},{13,5},{2,10},{6,14},... | collective-permute-start | bytes 393224 | tf_op jit(solution)/shard_map/ppermute | solution.py:364
  23.2 12.3 %collective-permute-start.6 = (bf16[64,1024]{1,0:T(8,128)(2,1)S(1)}, bf16[64,1024]{1,0:T(8,128)(2,1)S(1)}, u32[]{:S(2)}, u32[]{:S(2)}) collective-permute-start(bf16[64,1024]{1,0:T(8,128)(2,1)S(1)} %get-tuple-element.80), channel_id=1, source_target_pairs={{0,4},{4,8},{8,12},{12,0},{1,5},{5,9},{9,13},{13,1},{2,6},{6,10},{... | collective-permute-start | bytes 393224 | tf_op jit(solution)/shard_map/ppermute | solution.py:364
  35.5 2.3 %collective-permute-start.10 = (bf16[4,528,128]{2,1,0:T(8,128)(2,1)S(1)}, bf16[4,528,128]{2,1,0:T(8,128)(2,1)S(1)}, u32[]{:S(2)}, u32[]{:S(2)}) collective-permute-start(bf16[4,528,128]{2,1,0:T(8,128)(2,1)S(1)} %pad_maximum_fusion.1.refs_0_), channel_id=1, source_target_pairs={{0,1},{1,0},{2,3},{3,2},{4,5},{5,4},{6,7},{7,6},{8,9},{9,8},{10,11... | collective-permute-start | bytes 1622024 | tf_op jit(solution)/shard_map/ppermute | solution.py:361
  35.7 5.9 %collective-permute-start.11 = (bf16[4,64,1024]{2,1,0:T(8,128)(2,1)S(1)}, bf16[4,64,1024]{2,1,0:T(8,128)(2,1)S(1)}, u32[]{:S(2)}, u32[]{:S(2)}) collective-permute-start(bf16[4,64,1024]{2,1,0:T(8,128)(2,1)S(1)} %pad_maximum_fusion.2.refs_1_), channel_id=1, source_target_pairs={{0,1},{1,0},{2,3},{3,2},{4,5},{5,4},{6,7},{7,6},{8,9},{9,8},{10,11... | collective-permute-start | bytes 1572872 | tf_op jit(solution)/shard_map/ppermute | solution.py:361
  36.3 11.1 %collective-permute-start.12 = (bf16[3,64,1024]{2,1,0:T(8,128)(2,1)S(1)}, bf16[3,64,1024]{2,1,0:T(8,128)(2,1)S(1)}, u32[]{:S(2)}, u32[]{:S(2)}) collective-permute-start(bf16[3,64,1024]{2,1,0:T(8,128)(2,1)S(1)} %pad_maximum_fusion.5), channel_id=1, source_target_pairs={{0,2},{2,0},{1,3},{3,1},{4,6},{6,4},{5,7},{7,5},{8,10},{10,8},{9,1... | collective-permute-start | bytes 1179656 | tf_op jit(solution)/shard_map/ppermute | solution.py:367
  47.5 2.0 %collective-permute-start.13 = (bf16[4,64,1024]{2,1,0:T(8,128)(2,1)S(1)}, bf16[4,64,1024]{2,1,0:T(8,128)(2,1)S(1)}, u32[]{:S(2)}, u32[]{:S(2)}) collective-permute-start(bf16[4,64,1024]{2,1,0:T(8,128)(2,1)S(1)} %pad_maximum_fusion.3.refs_1_), channel_id=1, source_target_pairs={{0,1},{1,0},{2,3},{3,2},{4,5},{5,4},{6,7},{7,6},{8,9},{9,8},{10,11... | collective-permute-start | bytes 1572872 | tf_op jit(solution)/shard_map/ppermute | solution.py:361
  56.2 2.0 %collective-permute-start.14 = (bf16[4,528,128]{2,1,0:T(8,128)(2,1)S(1)}, bf16[4,528,128]{2,1,0:T(8,128)(2,1)S(1)}, u32[]{:S(2)}, u32[]{:S(2)}) collective-permute-start(bf16[4,528,128]{2,1,0:T(8,128)(2,1)S(1)} %get-tuple-element.117), channel_id=1, source_target_pairs={{0,1},{1,0},{2,3},{3,2},{4,5},{5,4},{6,7},{7,6},{8,9},{9,8},{10,11... | collective-permute-start | bytes 1622024 | tf_op jit(solution)/shard_map/ppermute | solution.py:361
  56.9 3.0 %collective-permute-start.15 = (bf16[4,528,128]{2,1,0:T(8,128)(2,1)S(1)}, bf16[4,528,128]{2,1,0:T(8,128)(2,1)S(1)}, u32[]{:S(2)}, u32[]{:S(2)}) collective-permute-start(bf16[4,528,128]{2,1,0:T(8,128)(2,1)S(1)} %get-tuple-element.119), channel_id=1, source_target_pairs={{0,1},{1,0},{2,3},{3,2},{4,5},{5,4},{6,7},{7,6},{8,9},{9,8},{10,11... | collective-permute-start | bytes 1622024 | tf_op jit(solution)/shard_map/ppermute | solution.py:361
  58.3 11.7 %collective-permute-start.16 = (bf16[4,352,128]{2,1,0:T(8,128)(2,1)S(1)}, bf16[4,352,128]{2,1,0:T(8,128)(2,1)S(1)}, u32[]{:S(2)}, u32[]{:S(2)}) collective-permute-start(bf16[4,352,128]{2,1,0:T(8,128)(2,1)S(1)} %add_convert_fusion.refs_4_), channel_id=1, source_target_pairs={{0,2},{2,0},{1,3},{3,1},{4,6},{6,4},{5,7},{7,5},{8,10},{10,8},{9,1... | collective-permute-start | bytes 1081352 | tf_op jit(solution)/shard_map/ppermute | solution.py:367
  60.0 9.2 %collective-permute-start.17 = (bf16[2,176,128]{2,1,0:T(8,128)(2,1)S(1)}, bf16[2,176,128]{2,1,0:T(8,128)(2,1)S(1)}, u32[]{:S(2)}, u32[]{:S(2)}) collective-permute-start(bf16[2,176,128]{2,1,0:T(8,128)(2,1)S(1)} %pad_maximum_fusion.7.refs_5_), channel_id=1, source_target_pairs={{0,12},{4,0},{8,4},{12,8},{1,13},{5,1},{9,5},{13,9},{2,14},{6,2},{... | collective-permute-start | bytes 270344 | tf_op jit(solution)/shard_map/ppermute | solution.py:364
  60.1 10.0 %collective-permute-start.18 = (bf16[2,176,128]{2,1,0:T(8,128)(2,1)S(1)}, bf16[2,176,128]{2,1,0:T(8,128)(2,1)S(1)}, u32[]{:S(2)}, u32[]{:S(2)}) collective-permute-start(bf16[2,176,128]{2,1,0:T(8,128)(2,1)S(1)} %pad_maximum_fusion.8.refs_6_), channel_id=1, source_target_pairs={{0,8},{4,12},{8,0},{12,4},{1,9},{5,13},{9,1},{13,5},{2,10},{6,14},... | collective-permute-start | bytes 270344 | tf_op jit(solution)/shard_map/ppermute | solution.py:364
  61.7 8.3 %collective-permute-start.19 = (bf16[2,176,128]{2,1,0:T(8,128)(2,1)S(1)}, bf16[2,176,128]{2,1,0:T(8,128)(2,1)S(1)}, u32[]{:S(2)}, u32[]{:S(2)}) collective-permute-start(bf16[2,176,128]{2,1,0:T(8,128)(2,1)S(1)} %pad_maximum_fusion.9.refs_7_), channel_id=1, source_target_pairs={{0,4},{4,8},{8,12},{12,0},{1,5},{5,9},{9,13},{13,1},{2,6},{6,10},{... | collective-permute-start | bytes 270344 | tf_op jit(solution)/shard_map/ppermute | solution.py:364
  70.2 8.4 %collective-permute-start.20 = (bf16[352,128]{1,0:T(8,128)(2,1)S(1)}, bf16[352,128]{1,0:T(8,128)(2,1)S(1)}, u32[]{:S(2)}, u32[]{:S(2)}) collective-permute-start(bf16[352,128]{1,0:T(8,128)(2,1)S(1)} %get-tuple-element.123.refs_3_), channel_id=1, source_target_pairs={{0,12},{4,0},{8,4},{12,8},{1,13},{5,1},{9,5},{13,9},{2,14},{6,2},{... | collective-permute-start | bytes 270344 | tf_op jit(solution)/shard_map/ppermute | solution.py:364
  71.3 9.0 %collective-permute-start.21 = (bf16[352,128]{1,0:T(8,128)(2,1)S(1)}, bf16[352,128]{1,0:T(8,128)(2,1)S(1)}, u32[]{:S(2)}, u32[]{:S(2)}) collective-permute-start(bf16[352,128]{1,0:T(8,128)(2,1)S(1)} %get-tuple-element.124.refs_4_), channel_id=1, source_target_pairs={{0,8},{4,12},{8,0},{12,4},{1,9},{5,13},{9,1},{13,5},{2,10},{6,14},... | collective-permute-start | bytes 270344 | tf_op jit(solution)/shard_map/ppermute | solution.py:364
  71.8 8.5 %collective-permute-start.22 = (bf16[352,128]{1,0:T(8,128)(2,1)S(1)}, bf16[352,128]{1,0:T(8,128)(2,1)S(1)}, u32[]{:S(2)}, u32[]{:S(2)}) collective-permute-start(bf16[352,128]{1,0:T(8,128)(2,1)S(1)} %get-tuple-element.125.refs_5_), channel_id=1, source_target_pairs={{0,4},{4,8},{8,12},{12,0},{1,5},{5,9},{9,13},{13,1},{2,6},{6,10},{... | collective-permute-start | bytes 270344 | tf_op jit(solution)/shard_map/ppermute | solution.py:364
  73.7 4.9 %collective-permute-start.23 = (bf16[176,128]{1,0:T(8,128)(2,1)S(1)}, bf16[176,128]{1,0:T(8,128)(2,1)S(1)}, u32[]{:S(2)}, u32[]{:S(2)}) collective-permute-start(bf16[176,128]{1,0:T(8,128)(2,1)S(1)} %get-tuple-element.126.refs_6_), channel_id=1, source_target_pairs={{0,2},{2,0},{1,3},{3,1},{4,6},{6,4},{5,7},{7,5},{8,10},{10,8},{9,1... | collective-permute-start | bytes 135176 | tf_op jit(solution)/shard_map/ppermute | solution.py:367
  80.3 1.4 %collective-permute-start.24 = (bf16[528,128]{1,0:T(8,128)(2,1)S(1)}, bf16[528,128]{1,0:T(8,128)(2,1)S(1)}, u32[]{:S(2)}, u32[]{:S(2)}) collective-permute-start(bf16[528,128]{1,0:T(8,128)(2,1)S(1)} %get-tuple-element.131.refs_0_), channel_id=1, source_target_pairs={{0,1},{1,0},{2,3},{3,2},{4,5},{5,4},{6,7},{7,6},{8,9},{9,8},{10,11... | collective-permute-start | bytes 405512 | tf_op jit(solution)/shard_map/ppermute | solution.py:361

commit v6 on v5

--- a/solution.py
+++ b/solution.py
@@ -109,8 +109,9 @@
            lambda source: unpacked(far_ref[source], half, features), rows_ref)
 
 
-def select_cotangents(where_ref, rank_ref, near_ref, far_ref, rows_ref):
-    select(rank_ref[...], lambda source: near_ref[source], lambda source: far_ref[source], rows_ref)
+def select_cotangents(c, where_ref, rank_ref, near_ref, far_ref, near_tail, far_tail, rows_ref):
+    whole = lambda first, tail: lambda source: jnp.concatenate([first[source], tail[source, c]], axis=0)
+    select(rank_ref[...], whole(near_ref, near_tail), whole(far_ref, far_tail), rows_ref)
 
 
 def joined(refs, index):
@@ -125,47 +126,49 @@
     lax.fori_loop(0, count, step, 0, unroll=8 if count % 8 == 0 else 1)
 
 
-def forward_kernel(where_ref, wg_ref, wu_ref, *refs):
-    rows_refs, (gate_ref, up_ref) = refs[:-2], refs[-2:]
-
-    def body(expert):
-        rows = joined(rows_refs, expert)
-        gate_ref[expert] = dot(wg_ref[expert], rows, LAST)
-        up_ref[expert] = dot(wu_ref[expert], rows, LAST)
-
-    each(gate_ref.shape[0], body)
-
-
-def backward_kernel(groups, where_ref, wg_ref, wu_ref, wd_ref, gate_ref, up_ref, *refs):
+def forward_kernel(groups, where_ref, both_ref, *refs):
     rank_refs, weight_refs, rows_refs = refs[:groups], refs[groups : 2 * groups], refs[2 * groups : 3 * groups]
-    dgate_ref, dup_ref, gated_ref, input_ref, prob_ref = refs[3 * groups :]
-    count, slots, _ = input_ref.shape
-    sources, tokens = prob_ref.shape[1:]
-    total = sources * count
+    hidden_ref, fgate_ref, fup_ref, gated_ref, holds_ref = refs[3 * groups :]
+    count, tokens, slots = holds_ref.shape
     rank = joined(rank_refs, ...).astype(BF16)
     weight = joined(weight_refs, ...).astype(BF16)
     place = (iota((tokens, slots), 1) & (MOST - 1)).astype(F32)
-    row, lane = iota((total, slots), 0), iota((total, slots), 1)
-    block = jnp.where(iota((sources, slots), 0) == iota((sources, slots), 1) // MOST, 1.0, 0.0).astype(BF16)
+    row, lane = iota((rank.shape[0], slots), 0), iota((rank.shape[0], slots), 1)
 
     def body(expert):
         spread = jnp.where(row == (lane // MOST) * count + expert, 1.0, 0.0).astype(BF16)
         holds = dot(rank, spread, LEAD) == place
         scale = jnp.sum(jnp.where(holds, dot(weight, spread, LEAD), 0.0), axis=0, keepdims=True)
-        raw = dot(wd_ref[expert], joined(rows_refs, expert), LAST)
-        gate, up = gate_ref[expert], up_ref[expert]
+        holds_ref[expert] = jnp.where(holds, 1.0, 0.0).astype(BF16)
+        rows = joined(rows_refs, expert)
+        both = dot(both_ref[expert], rows, LAST)
+        gate, up = both[: both.shape[0] // 2], both[both.shape[0] // 2 :]
         sigmoid = 1.0 / (1.0 + jnp.exp(-gate))
         active = gate * sigmoid
         hidden = active * up
+        hidden_ref[expert] = hidden
         gated_ref[expert] = (scale * hidden).astype(BF16)
-        prob = jnp.sum(hidden * raw, axis=0, keepdims=True)
-        scaled = scale * raw
-        dgate = (scaled * up * sigmoid * (1.0 + gate * (1.0 - sigmoid))).astype(BF16)
-        dup = (scaled * active).astype(BF16)
-        dgate_ref[expert] = dgate
-        dup_ref[expert] = dup
-        input_ref[expert] = (dot(dgate, wg_ref[expert], LEAD) + dot(dup, wu_ref[expert], LEAD)).astype(BF16)
-        prob_ref[expert] = dot(block, jnp.where(holds, prob, 0.0).astype(BF16), LAST)
+        fgate_ref[expert] = scale * up * sigmoid * (1.0 + gate * (1.0 - sigmoid))
+        fup_ref[expert] = scale * active
+
+    each(count, body)
+
+
+def backward_kernel(groups, where_ref, both_ref, wd_ref, hidden_ref, fgate_ref, fup_ref, holds_ref, *refs):
+    rows_refs, (dboth_ref, input_ref, prob_ref) = refs[:groups], refs[groups:]
+    count, slots, _ = input_ref.shape
+    sources = prob_ref.shape[1]
+    block = jnp.where(iota((sources, slots), 0) == iota((sources, slots), 1) // MOST, 1.0, 0.0).astype(BF16)
+
+    def body(expert):
+        raw = dot(wd_ref[expert], joined(rows_refs, expert), LAST)
+        dgate = (raw * fgate_ref[expert]).astype(BF16)
+        dup = (raw * fup_ref[expert]).astype(BF16)
+        dboth = jnp.concatenate([dgate, dup], axis=0)
+        dboth_ref[expert] = dboth
+        input_ref[expert] = dot(dboth, both_ref[expert], LEAD).astype(BF16)
+        prob = jnp.sum(hidden_ref[expert] * raw, axis=0, keepdims=True)
+        prob_ref[expert] = dot(block, (holds_ref[expert].astype(F32) * prob).astype(BF16), LAST)
 
     each(count, body)
 
@@ -193,15 +196,15 @@
         other_ref[source, own_ref.shape[1] - tail :] = pltpu.roll(lines, half, 1).astype(BF16)
 
 
-def weights_kernel(groups, number, where_ref, *refs):
-    hidden_refs, rows_refs = refs[:number], refs[number : number + groups]
+def weights_kernel(groups, number, where_ref, hidden_ref, *refs):
+    rows_refs = refs[:groups]
     targets, token_ref, slots_ref, sems = refs[-3 - number : -3], *refs[-3:]
-    count, depth = hidden_refs[0].shape[0], slots_ref.shape[0]
+    count, depth, height = hidden_ref.shape[0], slots_ref.shape[0], hidden_ref.shape[1] // number
 
     def copies(expert):
         slot = lax.rem(expert, depth)
         return [
-            pltpu.make_async_copy(slots_ref.at[slot, at], target.at[expert], sems.at[slot, at])
+            pltpu.make_async_copy(slots_ref.at[slot, pl.ds(at * height, height)], target.at[expert], sems.at[slot, at])
             for at, target in enumerate(targets)
         ]
 
@@ -211,10 +214,8 @@
             for copy in copies(expert - depth):
                 copy.wait()
 
-        slot = lax.rem(expert, depth)
-        rows = joined(rows_refs, expert)
-        for at, hidden_ref in enumerate(hidden_refs):
-            slots_ref[slot, at] = jnp.dot(hidden_ref[expert], rows, preferred_element_type=F32).astype(BF16)
+        grads = jnp.dot(hidden_ref[expert], joined(rows_refs, expert), preferred_element_type=F32)
+        slots_ref[lax.rem(expert, depth)] = grads.astype(BF16)
         for copy in copies(expert):
             copy.start()
         return carry
@@ -288,18 +289,15 @@
     token_ref[...] = where_ref[...]
 
 
-def load_kernel(where_ref, *refs):
-    count = (len(refs) - 2) // 2
-    token_ref, sems = refs[2 * count :]
-    copies = [
-        pltpu.make_async_copy(source, target, sems.at[number])
-        for number, (source, target) in enumerate(zip(refs[:count], refs[count : 2 * count]))
-    ]
+def load_kernel(where_ref, gate_ref, up_ref, down_ref, both_ref, down_held, token_ref, sems):
+    hidden = gate_ref.shape[1]
+    pairs = ((gate_ref, both_ref.at[:, :hidden]), (up_ref, both_ref.at[:, hidden:]), (down_ref, down_held))
+    copies = [pltpu.make_async_copy(source, target, sems.at[at]) for at, (source, target) in enumerate(pairs)]
     for copy in copies:
         copy.start()
+    pass_on(where_ref, token_ref)
     for copy in copies:
         copy.wait()
-    pass_on(where_ref, token_ref)
 
 
 SCALARS = pl.BlockSpec(memory_space=pltpu.SMEM)
@@ -307,18 +305,20 @@
 WHERE = (8, 128)
 
 
-def load(where, arrays):
-    *held, where = pl.pallas_call(
+def load(where, gate, up, down):
+    count, hidden, features = gate.shape
+    both, down, where = pl.pallas_call(
         load_kernel,
-        in_specs=[IN_VMEM] + [pl.BlockSpec(memory_space=pl.ANY)] * len(arrays),
-        out_specs=[IN_VMEM] * len(arrays) + [IN_VMEM],
-        out_shape=[vmem_shape(array.shape, array.dtype) for array in arrays] + [vmem_shape(WHERE, jnp.int32)],
-        scratch_shapes=[pltpu.SemaphoreType.DMA((len(arrays),))],
+        in_specs=[IN_VMEM] + [pl.BlockSpec(memory_space=pl.ANY)] * 3,
+        out_specs=[IN_VMEM] * 3,
+        out_shape=[vmem_shape((count, 2 * hidden, features), gate.dtype), vmem_shape(down.shape, down.dtype),
+                   vmem_shape(WHERE, jnp.int32)],
+        scratch_shapes=[pltpu.SemaphoreType.DMA((3,))],
         compiler_params=pltpu.CompilerParams(vmem_limit_bytes=VMEM_BYTES),
         cost_estimate=cost(7),
         name="load",
-    )(in_vmem(where), *map(in_hbm, arrays))
-    return where, held
+    )(in_vmem(where), in_hbm(gate), in_hbm(up), in_hbm(down))
+    return where, both, down
 
 
 def on_vmem(kernel, name, micros, outs, where, operands, stay=True, scratch=()):
@@ -389,10 +389,12 @@
     line_x = [along_z(own_x, d) for d in range(1, zs)]
     first_x = [along_x(own_x, c) for c in range(1, xs)]
     first_dy = [along_x(own_dy, c) for c in range(1, xs)]
-    where, (wg, wu, wd) = load(where, (wg, wu, wd))
+    where, wgu, wd = load(where, wg, wu, wd)
     where, line_x, first_x, first_dy, own_dy = barrier((where, line_x, first_x, first_dy, own_dy))
 
-    line_dy = [along_z(own_dy, d) for d in range(1, zs)]
+    lead = half * 3 // 4
+    lead_dy = own_dy[:lead]
+    line_dy = [along_z(lead_dy, d) for d in range(1, zs)]
     rest = jnp.stack(line_x)
     more = [along_x(rest, c) for c in range(1, xs)]
     rows_x, ranks, weight, metas = [], [], [], []
@@ -405,9 +407,10 @@
             held.append(result)
         return where
 
-    def take_cotangents(where, near, far):
+    def take_cotangents(where, c, near, far, near_tail, far_tail):
         outs = [((count, group, features), BF16)]
-        return on_vmem(select_cotangents, "select_cotangents", 2, outs, where, (ranks[len(rows_dy)], near, far))
+        return on_vmem(functools.partial(select_cotangents, c), "select_cotangents", 1, outs, where,
+                       (ranks[c], near, far, near_tail, far_tail))
 
     near = jnp.concatenate([own_x[None], rest])
     where = take_tokens(where, near, swap(near))
@@ -416,22 +419,29 @@
 
     rest = jnp.stack(line_dy)
     more = [along_x(rest, c) for c in range(1, xs)]
+    tail = jnp.stack([own_dy[lead:]] + [block[lead:] for block in first_dy])
+    tails = [along_z(tail, d) for d in range(1, zs)]
+    near = [jnp.concatenate([lead_dy[None], rest])]
+    far = [swap(near[0])]
     rows_dy = []
-    for near in groups_x:
-        where = take_tokens(where, near, swap(near))
-    where, (gate, up) = on_vmem(forward_kernel, "forward", 5, [((count, hidden, slots), F32)] * 2, where, (wg, wu, *rows_x))
-    near = jnp.concatenate([own_dy[None], rest])
-    where, got = take_cotangents(where, near, swap(near))
-    rows_dy += got
-    where, more = barrier((where, more))
-    for near in [jnp.concatenate([a[None], b]) for a, b in zip(first_dy, more)]:
-        where, got = take_cotangents(where, near, swap(near))
+    for group_x in groups_x:
+        where = take_tokens(where, group_x, swap(group_x))
+    outs = [((count, hidden, slots), F32)] * 3 + [((count, hidden, slots), BF16), ((count, rows, slots), BF16)]
+    where, (*factors, gated, holds) = on_vmem(functools.partial(forward_kernel, xs), "forward", 5, outs, where,
+                                              (wgu, *ranks, *weight, *rows_x))
+    where, more, tails = barrier((where, more, tails))
+    near += [jnp.concatenate([a[None, :lead], b]) for a, b in zip(first_dy, more)]
+    far += [swap(block) for block in near[1:]]
+    near_tail = jnp.stack([tail] + tails)
+    far_tail = swap(near_tail)
+    for c in range(xs):
+        where, got = take_cotangents(where, c, near[c], far[c], near_tail, far_tail)
         rows_dy += got
 
-    outs = [((count, hidden, slots), BF16)] * 3 + [((count, slots, features), BF16), ((count, positions, rows), F32)]
-    where, (dgate, dup, gated, rows_in, prob) = on_vmem(
-        functools.partial(backward_kernel, xs), "backward", 9, outs, where,
-        (wg, wu, wd, gate, up, *ranks, *weight, *rows_dy))
+    outs = [((count, 2 * hidden, slots), BF16), ((count, slots, features), BF16), ((count, positions, rows), F32)]
+    where, (dboth, rows_in, prob) = on_vmem(
+        functools.partial(backward_kernel, xs), "backward", 6, outs, where,
+        (wgu, wd, *factors, holds, *rows_dy))
     height = packed + 16 * pl.cdiv(kinds, 16)
     split = 2 * height // 3 // 16 * 16
     chip = [None] * xs
@@ -445,19 +455,19 @@
         own, other = chip[c]
         return own[index].astype(F32) + other[index].astype(F32)
 
-    def weights(where, sources, shared, after):
-        depth, number = min(count, 3), len(sources)
-        operands = [in_vmem(array) for array in (*sources, *shared)]
+    def weights(where, source, number, shared, awaited):
+        depth = min(count, 3)
+        operands = [in_vmem(array) for array in (source, *shared)]
         *grads, where = pl.pallas_call(
             functools.partial(weights_kernel, xs, number),
-            in_specs=[IN_VMEM] * (1 + len(operands)) + [pl.BlockSpec(memory_space=pl.ANY)] * len(after),
+            in_specs=[IN_VMEM] * (1 + len(operands)) + [pl.BlockSpec(memory_space=pl.ANY)] * len(awaited),
             out_specs=[pl.BlockSpec(memory_space=pl.ANY)] * number + [IN_VMEM],
             out_shape=[jax.ShapeDtypeStruct((count, hidden, features), BF16)] * number + [vmem_shape(WHERE, jnp.int32)],
-            scratch_shapes=[pltpu.VMEM((depth, number, hidden, features), BF16), pltpu.SemaphoreType.DMA((depth, number))],
+            scratch_shapes=[pltpu.VMEM((depth, number * hidden, features), BF16), pltpu.SemaphoreType.DMA((depth, number))],
             compiler_params=pltpu.CompilerParams(vmem_limit_bytes=VMEM_BYTES),
             cost_estimate=cost(3 * number),
             name="weights",
-        )(in_vmem(where), *operands, *after)
+        )(in_vmem(where), *operands, *awaited)
         return where, grads
 
     first, last = slice(0, split), slice(split, height)
@@ -466,14 +476,14 @@
     lining = [side.astype(BF16) for side in sides[1:]]
     hops = [along_x(array, -c) for c, array in enumerate(crossing, 1)]
     shifts = [along_z(array, -d) for d, array in enumerate(lining, 1)]
-    where, (grad_gate, grad_up) = weights(where, (dgate, dup), rows_x, crossing + lining)
+    where, (grad_gate, grad_up) = weights(where, dboth, 2, rows_x, crossing + lining)
     outs = [((split, rows), BF16 if d else F32) for d in range(zs)]
     outs += [((height - split, rows), BF16 if c else F32) for c in range(xs)]
     where, sums = on_vmem(functools.partial(middle_sums, zs, xs), "middle_sums", 1, outs, where,
                           (*chip[0], sides[0], *hops, *shifts), False)
     parts = [along_z(sums[d], -d) if d else sums[d] for d in range(zs)]
     parts += [along_x(sums[zs + c], -c) if c else sums[zs] for c in range(xs)]
-    where, (grad_down,) = weights(where, (gated,), rows_dy, [array for array in sums if array.dtype == BF16])
+    where, (grad_down,) = weights(where, gated, 1, rows_dy, [array for array in sums if array.dtype == BF16])
     where, (mine,) = on_vmem(functools.partial(last_sums, zs, xs), "last_sums", 1, [((height, rows), BF16)], where,
                              parts, False)
     outs = [((rows, features), BF16), ((top, rows), F32)]

time: 82.7 us -> 81.5 us (0.985)
  waiting for transfers between devices: 25.3 us -> 20.2 us
  starting transfers between devices: 26.3 us -> 30.4 us
    ppermute x12 -> x15, starting transfers between devices: 16.6 us -> 20.9 us  [along_z(): lax.ppermute(array, 'expert', [(i, (i + by) % zs) for i in range(zs)])]
    ppermute x6, waiting for transfers between devices: 5.42 us -> 2.95 us  [along_x(): return lax.ppermute(array, 'blk', [(i, (i + by) % xs) for i in range(xs)])]
    ppermute x12 -> x15, waiting for transfers between devices: 15.7 us -> 13.5 us  [along_z(): lax.ppermute(array, 'expert', [(i, (i + by) % zs) for i in range(zs)])]
    ppermute x7 -> x8, waiting for transfers between devices: 4.14 us -> 3.72 us  [swap(): lax.ppermute(array, 'tensor', [(i, (i + 1) % cores) for i in range(cores)])]
  transfers between devices with their start and end apart: 25 -> 29, of which waited for: 9 -> 8; matrix products, arithmetic and copies ran while one was open for 0% -> 1% of each run, Pallas kernels for 25% -> 26%
where the time goes in v6:
time: 81.5 us; the launch traced here: 81.4 us
  starting transfers between devices  30.4 us (37%)
  Pallas kernels  29.1 us (36%)
  waiting for transfers between devices  20.2 us (25%)
  between operations  1 us (1%)
    ppermute x15, starting transfers between devices, along_z(): lax.ppermute(array, 'expert', [(i, (i + by) % zs) for i in range(zs)])  20.9 us
    ppermute x15, waiting for transfers between devices, along_z(): lax.ppermute(array, 'expert', [(i, (i + by) % zs) for i in range(zs)])  13.5 us
    pallas_call x11, Pallas kernels, on_vmem(): pl.pallas_call(body, in_specs=[IN_VMEM] * (1 + len(operands)), out_specs=...  12.6 us
    pallas_call x2, Pallas kernels, weights(): pl.pallas_call(functools.partial(weights_kernel, xs, number), in_specs=[I...  9.38 us
    ppermute x6, starting transfers between devices, along_x(): return lax.ppermute(array, 'blk', [(i, (i + by) % xs) for i in range(xs)])  7.93 us
    pallas_call x1, Pallas kernels, load(): pl.pallas_call(load_kernel, in_specs=[IN_VMEM] + [pl.BlockSpec(memory_spa...  6 us
    ppermute x8, waiting for transfers between devices, swap(): lax.ppermute(array, 'tensor', [(i, (i + 1) % cores) for i in range(cores)])  3.72 us
    ppermute x6, waiting for transfers between devices, along_x(): return lax.ppermute(array, 'blk', [(i, (i + by) % xs) for i in range(xs)])  2.95 us
  transfers between devices with their start and end apart: 29, of which 8 were waited for; matrix products, arithmetic and copies ran while one was open for 1% of the time, Pallas kernels for 26%

profile of v6, /device:TPU:0, one launch (start us, length us, event | category | flops | bytes accessed | tf_op | source)
XLA Modules:
  0.0 81.4 jit_solution(15930383745528371045)
XLA Ops:
  0.7 0.1 iota.7.where_ref
  0.7 1.1 %pack.1 = (bf16[528,128]{1,0:T(8,128)(2,1)S(1)}, bf16[64,1024]{1,0:T(8,128)(2,1)S(1)}, s32[8,128]{1,0:T(8,128)S(1)}) custom-call(s32[1]{0:T(128)} %bitcast.core_ref, s32[8,128]{1,0:T(8,128)S(1)} %iota.7.where_ref, bf16[128,1024]{1,0:T(8,128)(2,1)} %tokens_ref.1, bf16[128,1024]{1,0:T(8,128)(2,1)} %cotangent_ref.1, s32[6,128]{1,0:T(8,128)} %bitcast.59, ...), custom_call_target="tpu_custom_call" | custom-call | flops 1000 | bytes 6000000 | tf_op jit(solution)/shard_map/pack/pallas_call | solution.py:375
  1.9 3.0 %collective-permute-start.3 = (bf16[528,128]{1,0:T(8,128)(2,1)S(1)}, bf16[528,128]{1,0:T(8,128)(2,1)S(1)}, u32[]{:S(2)}, u32[]{:S(2)}) collective-permute-start(bf16[528,128]{1,0:T(8,128)(2,1)S(1)} %get-tuple-element.76), channel_id=1, source_target_pairs={{0,2},{2,0},{1,3},{3,1},{4,6},{6,4},{5,7},{7,5},{8,10},{10,8},{9,1... | collective-permute-start | bytes 405512 | tf_op jit(solution)/shard_map/ppermute | solution.py:367
  4.9 3.6 %collective-permute-start.2 = (bf16[528,128]{1,0:T(8,128)(2,1)S(1)}, bf16[528,128]{1,0:T(8,128)(2,1)S(1)}, u32[]{:S(2)}, u32[]{:S(2)}) collective-permute-start(bf16[528,128]{1,0:T(8,128)(2,1)S(1)} %get-tuple-element.76), channel_id=1, source_target_pairs={{0,12},{4,0},{8,4},{12,8},{1,13},{5,1},{9,5},{13,9},{2,14},{6,2},{... | collective-permute-start | bytes 405512 | tf_op jit(solution)/shard_map/ppermute | solution.py:364
  8.5 1.0 %collective-permute-start = (bf16[528,128]{1,0:T(8,128)(2,1)S(1)}, bf16[528,128]{1,0:T(8,128)(2,1)S(1)}, u32[]{:S(2)}, u32[]{:S(2)}) collective-permute-start(bf16[528,128]{1,0:T(8,128)(2,1)S(1)} %get-tuple-element.76), channel_id=1, source_target_pairs={{0,4},{4,8},{8,12},{12,0},{1,5},{5,9},{9,13},{13,1},{2,6},{6,10},{... | collective-permute-start | bytes 405512 | tf_op jit(solution)/shard_map/ppermute | solution.py:364
  9.5 0.5 collective-permute-start.4
  10.0 6.0 %load.1 = (bf16[8,704,1024]{2,1,0:T(8,128)(2,1)S(1)}, bf16[8,352,1024]{2,1,0:T(8,128)(2,1)S(1)}, s32[8,128]{1,0:T(8,128)S(1)}) custom-call(s32[8,128]{1,0:T(8,128)S(1)} %get-tuple-element.74.where_ref, bf16[8,352,1024]{2,1,0:T(8,128)(2,1)} %bitcast.40, bf16[8,352,1024]{2,1,0:T(8,128)(2,1)} %bitcast.41, bf16[8,352,1024]{2,1,0:T(8,128)(2,1)} %bitcast.42), custom_call_target="tpu_custom_call" | custom-call | flops 1000 | bytes 21000000 | tf_op jit(solution)/shard_map/load/pallas_call | solution.py:310
  16.0 0.0 collective-permute-done.3
  16.0 0.0 collective-permute-done.2
  16.1 3.6 %collective-permute-done.1 = bf16[528,128]{1,0:T(8,128)(2,1)S(1)} collective-permute-done((bf16[528,128]{1,0:T(8,128)(2,1)S(1)}, bf16[528,128]{1,0:T(8,128)(2,1)S(1)}, u32[]{:S(2)}, u32[]{:S(2)}) %collective-permute-start.1) | collective-permute-done | bytes 135200 | tf_op jit(solution)/shard_map/ppermute | solution.py:364
  19.6 0.0 collective-permute-done
  19.6 0.1 pad_maximum_fusion.refs_0_
  19.7 0.1 collective-permute-start.5
  19.8 0.6 collective-permute-start.9
  20.4 1.7 %collective-permute-start.8 = (bf16[48,1024]{1,0:T(8,128)(2,1)S(1)}, bf16[48,1024]{1,0:T(8,128)(2,1)S(1)}, u32[]{:S(2)}, u32[]{:S(2)}) collective-permute-start(bf16[48,1024]{1,0:T(8,128)(2,1)S(1)} %get-tuple-element.152), channel_id=1, source_target_pairs={{0,12},{4,0},{8,4},{12,8},{1,13},{5,1},{9,5},{13,9},{2,14},{6,2},{... | collective-permute-start | bytes 294920 | tf_op jit(solution)/shard_map/ppermute | solution.py:364
  22.1 1.2 %collective-permute-start.7 = (bf16[48,1024]{1,0:T(8,128)(2,1)S(1)}, bf16[48,1024]{1,0:T(8,128)(2,1)S(1)}, u32[]{:S(2)}, u32[]{:S(2)}) collective-permute-start(bf16[48,1024]{1,0:T(8,128)(2,1)S(1)} %get-tuple-element.152), channel_id=1, source_target_pairs={{0,8},{4,12},{8,0},{12,4},{1,9},{5,13},{9,1},{13,5},{2,10},{6,14},... | collective-permute-start | bytes 294920 | tf_op jit(solution)/shard_map/ppermute | solution.py:364
  23.3 1.9 %collective-permute-start.6 = (bf16[48,1024]{1,0:T(8,128)(2,1)S(1)}, bf16[48,1024]{1,0:T(8,128)(2,1)S(1)}, u32[]{:S(2)}, u32[]{:S(2)}) collective-permute-start(bf16[48,1024]{1,0:T(8,128)(2,1)S(1)} %get-tuple-element.152), channel_id=1, source_target_pairs={{0,4},{4,8},{8,12},{12,0},{1,5},{5,9},{9,13},{13,1},{2,6},{6,10},{... | collective-permute-start | bytes 294920 | tf_op jit(solution)/shard_map/ppermute | solution.py:364
  25.3 0.6 select_tokens.2
  25.9 0.0 collective-permute-done.8
  25.9 6.9 %collective-permute-done.7 = bf16[48,1024]{1,0:T(8,128)(2,1)S(1)} collective-permute-done((bf16[48,1024]{1,0:T(8,128)(2,1)S(1)}, bf16[48,1024]{1,0:T(8,128)(2,1)S(1)}, u32[]{:S(2)}, u32[]{:S(2)}) %collective-permute-start.7) | collective-permute-done | bytes 98336 | tf_op jit(solution)/shard_map/ppermute | solution.py:364
  32.8 0.1 collective-permute-start.10
  32.9 0.6 collective-permute-start.14
  33.5 1.2 %collective-permute-start.13 = (bf16[2,16,1024]{2,1,0:T(8,128)(2,1)S(1)}, bf16[2,16,1024]{2,1,0:T(8,128)(2,1)S(1)}, u32[]{:S(2)}, u32[]{:S(2)}) collective-permute-start(bf16[2,16,1024]{2,1,0:T(8,128)(2,1)S(1)} %get-tuple-element.154), channel_id=1, source_target_pairs={{0,8},{4,12},{8,0},{12,4},{1,9},{5,13},{9,1},{13,5},{2,10},{6,14},... | collective-permute-start | bytes 196616 | tf_op jit(solution)/shard_map/ppermute | solution.py:364
  34.7 1.9 %collective-permute-start.12 = (bf16[2,16,1024]{2,1,0:T(8,128)(2,1)S(1)}, bf16[2,16,1024]{2,1,0:T(8,128)(2,1)S(1)}, u32[]{:S(2)}, u32[]{:S(2)}) collective-permute-start(bf16[2,16,1024]{2,1,0:T(8,128)(2,1)S(1)} %get-tuple-element.154), channel_id=1, source_target_pairs={{0,4},{4,8},{8,12},{12,0},{1,5},{5,9},{9,13},{13,1},{2,6},{6,10},{... | collective-permute-start | bytes 196616 | tf_op jit(solution)/shard_map/ppermute | solution.py:364
  36.7 1.4 %collective-permute-start.11 = (bf16[3,48,1024]{2,1,0:T(8,128)(2,1)S(1)}, bf16[3,48,1024]{2,1,0:T(8,128)(2,1)S(1)}, u32[]{:S(2)}, u32[]{:S(2)}) collective-permute-start(bf16[3,48,1024]{2,1,0:T(8,128)(2,1)S(1)} %pad_maximum_fusion.5), channel_id=1, source_target_pairs={{0,2},{2,0},{1,3},{3,1},{4,6},{6,4},{5,7},{7,5},{8,10},{10,8},{9,1... | collective-permute-start | bytes 884744 | tf_op jit(solution)/shard_map/ppermute | solution.py:367
  38.1 0.1 pad_maximum_fusion.3.refs_1_
  38.2 0.0 collective-permute-done.10.refs_1_
  38.2 0.1 collective-permute-start.15
  38.3 0.6 select_tokens.3
  38.8 3.5 %forward.1 = (f32[8,352,128]{2,1,0:T(8,128)S(1)}, f32[8,352,128]{2,1,0:T(8,128)S(1)}, f32[8,352,128]{2,1,0:T(8,128)S(1)}, bf16[8,352,128]{2,1,0:T(8,128)(2,1)S(1...) custom-call(s32[8,128]{1,0:T(8,128)S(1)} %get-tuple-element.87.where_ref, ...), custom_call_target="tpu_custom_call" | custom-call | flops 1000 | bytes 15000000 | tf_op jit(solution)/shard_map/forward/pallas_call | solution.py:330
  42.4 0.0 collective-permute-done.14
  42.4 0.0 collective-permute-done.12
  42.4 2.9 %collective-permute-done.11 = bf16[3,48,1024]{2,1,0:T(8,128)(2,1)S(1)} collective-permute-done((bf16[3,48,1024]{2,1,0:T(8,128)(2,1)S(1)}, bf16[3,48,1024]{2,1,0:T(8,128)(2,1)S(1)}, u32[]{:S(2)}, u32[]{:S(2)}) %collective-permute-start.11) | collective-permute-done | bytes 294944 | tf_op jit(solution)/shard_map/ppermute | solution.py:367
  45.4 0.1 collective-permute-start.17
  45.5 0.6 collective-permute-start.16
  46.0 0.0 collective-permute-done.15.refs_2_
  46.0 1.5 %collective-permute-done.16.refs_4_ = bf16[4,2,16,1024]{3,2,1,0:T(8,128)(2,1)S(1)} collective-permute-done((bf16[4,2,16,1024]{3,2,1,0:T(8,128)(2,1)S(1)}, bf16[4,2,16,1024]{3,2,1,0:T(8,128)(2,1)S(1)}, u32[]{:S(2)}, u32[]{:S(2)}) %collective-permute-start.16) | collective-permute-done | bytes 262176 | tf_op jit(solution)/shard_map/ppermute | solution.py:361
  47.5 0.4 select_cotangents.2
  48.0 0.4 select_cotangents.3
  48.4 5.1 %backward.1 = (bf16[8,704,128]{2,1,0:T(8,128)(2,1)S(1)}, bf16[8,128,1024]{2,1,0:T(8,128)(2,1)S(1)}, f32[8,8,128]{2,1,0:T(8,128)S(1)}, s32[8,128]{1,0:T(8,128)S(1)}) custom-call(s32[8,128]{1,0:T(8,128)S(1)} %get-tuple-element.106.where_ref, bf16[8,704,1024]{2,1,0:T(8,128)(2,1)S(1)} %get-tuple-element.88.refs_0_, ...), custom_call_target="tpu_custom_call" | custom-call | flops 1000 | bytes 18000000 | tf_op jit(solution)/shard_map/backward/pallas_call | solution.py:330
  53.5 0.5 put_back.2
  54.0 0.2 collective-permute-start.18
  54.2 0.5 put_back.3
  54.7 0.4 collective-permute-start.19
  55.1 0.9 %collective-permute-done.18 = bf16[4,528,128]{2,1,0:T(8,128)(2,1)S(1)} collective-permute-done((bf16[4,528,128]{2,1,0:T(8,128)(2,1)S(1)}, bf16[4,528,128]{2,1,0:T(8,128)(2,1)S(1)}, u32[]{:S(2)}, u32[]{:S(2)}) %collective-permute-start.18) | collective-permute-done | bytes 540704 | tf_op jit(solution)/shard_map/ppermute | solution.py:361
  56.0 0.1 add_convert_fusion.refs_2_
  56.1 1.4 %collective-permute-start.20 = (bf16[4,352,128]{2,1,0:T(8,128)(2,1)S(1)}, bf16[4,352,128]{2,1,0:T(8,128)(2,1)S(1)}, u32[]{:S(2)}, u32[]{:S(2)}) collective-permute-start(bf16[4,352,128]{2,1,0:T(8,128)(2,1)S(1)} %add_convert_fusion.refs_2_), channel_id=1, source_target_pairs={{0,2},{2,0},{1,3},{3,1},{4,6},{6,4},{5,7},{7,5},{8,10},{10,8},{9,1... | collective-permute-start | bytes 1081352 | tf_op jit(solution)/shard_map/ppermute | solution.py:367
  57.6 2.2 %collective-permute-start.21 = (bf16[2,176,128]{2,1,0:T(8,128)(2,1)S(1)}, bf16[2,176,128]{2,1,0:T(8,128)(2,1)S(1)}, u32[]{:S(2)}, u32[]{:S(2)}) collective-permute-start(bf16[2,176,128]{2,1,0:T(8,128)(2,1)S(1)} %pad_maximum_fusion.8.refs_3_), channel_id=1, source_target_pairs={{0,12},{4,0},{8,4},{12,8},{1,13},{5,1},{9,5},{13,9},{2,14},{6,2},{... | collective-permute-start | bytes 270344 | tf_op jit(solution)/shard_map/ppermute | solution.py:364
  59.9 0.1 collective-permute-start.22
  60.0 1.3 %collective-permute-start.23 = (bf16[2,176,128]{2,1,0:T(8,128)(2,1)S(1)}, bf16[2,176,128]{2,1,0:T(8,128)(2,1)S(1)}, u32[]{:S(2)}, u32[]{:S(2)}) collective-permute-start(bf16[2,176,128]{2,1,0:T(8,128)(2,1)S(1)} %pad_maximum_fusion.10.refs_5_), channel_id=1, source_target_pairs={{0,4},{4,8},{8,12},{12,0},{1,5},{5,9},{9,13},{13,1},{2,6},{6,10},{... | collective-permute-start | bytes 270344 | tf_op jit(solution)/shard_map/ppermute | solution.py:364
  61.3 5.4 %weights.2 = (bf16[8,352,1024]{2,1,0:T(8,128)(2,1)}, bf16[8,352,1024]{2,1,0:T(8,128)(2,1)}, s32[8,128]{1,0:T(8,128)S(1)}) custom-call(s32[8,128]{1,0:T(8,128)S(1)} %get-tuple-element.120.where_ref, bf16[8,704,128]{2,1,0:T(8,128)(2,1)S(1)} %get-tuple-element.121.hidden_ref, bf16[8,64,1024]{2,1,0:T(8,128)(2,1)S(1)} %get-tuple-element.93.refs_5_.refs_0_, ...), custom_call_target="tpu_custom_call" | custom-call | flops 1000 | bytes 18000000 | tf_op jit(solution)/shard_map/weights/pallas_call | solution.py:461
  66.7 0.0 collective-permute-done.21.refs_4_
  66.7 1.7 %collective-permute-done.22.refs_5_ = bf16[2,176,128]{2,1,0:T(8,128)(2,1)S(1)} collective-permute-done((bf16[2,176,128]{2,1,0:T(8,128)(2,1)S(1)}, bf16[2,176,128]{2,1,0:T(8,128)(2,1)S(1)}, u32[]{:S(2)}, u32[]{:S(2)}) %collective-permute-start.22) | collective-permute-done | bytes 90144 | tf_op jit(solution)/shard_map/ppermute | solution.py:364
  68.5 0.2 middle_sums.1
  68.6 1.6 %collective-permute-start.24 = (bf16[352,128]{1,0:T(8,128)(2,1)S(1)}, bf16[352,128]{1,0:T(8,128)(2,1)S(1)}, u32[]{:S(2)}, u32[]{:S(2)}) collective-permute-start(bf16[352,128]{1,0:T(8,128)(2,1)S(1)} %get-tuple-element.129.refs_2_), channel_id=1, source_target_pairs={{0,12},{4,0},{8,4},{12,8},{1,13},{5,1},{9,5},{13,9},{2,14},{6,2},{... | collective-permute-start | bytes 270344 | tf_op jit(solution)/shard_map/ppermute | solution.py:364
  70.3 0.6 collective-permute-start.25
  70.8 1.9 %collective-permute-start.26 = (bf16[352,128]{1,0:T(8,128)(2,1)S(1)}, bf16[352,128]{1,0:T(8,128)(2,1)S(1)}, u32[]{:S(2)}, u32[]{:S(2)}) collective-permute-start(bf16[352,128]{1,0:T(8,128)(2,1)S(1)} %get-tuple-element.131.refs_4_), channel_id=1, source_target_pairs={{0,4},{4,8},{8,12},{12,0},{1,5},{5,9},{9,13},{13,1},{2,6},{6,10},{... | collective-permute-start | bytes 270344 | tf_op jit(solution)/shard_map/ppermute | solution.py:364
  72.8 1.0 %collective-permute-start.27 = (bf16[176,128]{1,0:T(8,128)(2,1)S(1)}, bf16[176,128]{1,0:T(8,128)(2,1)S(1)}, u32[]{:S(2)}, u32[]{:S(2)}) collective-permute-start(bf16[176,128]{1,0:T(8,128)(2,1)S(1)} %get-tuple-element.132.refs_5_), channel_id=1, source_target_pairs={{0,2},{2,0},{1,3},{3,1},{4,6},{6,4},{5,7},{7,5},{8,10},{10,8},{9,1... | collective-permute-start | bytes 135176 | tf_op jit(solution)/shard_map/ppermute | solution.py:367
  73.8 4.0 %weights.3 = (bf16[8,352,1024]{2,1,0:T(8,128)(2,1)}, s32[8,128]{1,0:T(8,128)S(1)}) custom-call(s32[8,128]{1,0:T(8,128)S(1)} %get-tuple-element.127.where_ref, bf16[8,352,128]{2,1,0:T(8,128)(2,1)S(1)} %get-tuple-element.128.hidden_ref, bf16[8,64,1024]{2,1,0:T(8,128)(2,1)S(1)} %get-tuple-element.112.refs_6_.refs_0_, ...), custom_call_target="tpu_custom_call" | custom-call | flops 1000 | bytes 9000000 | tf_op jit(solution)/shard_map/weights/pallas_call | solution.py:461
  77.7 1.3 %collective-permute-done.25.refs_2_ = bf16[352,128]{1,0:T(8,128)(2,1)S(1)} collective-permute-done((bf16[352,128]{1,0:T(8,128)(2,1)S(1)}, bf16[352,128]{1,0:T(8,128)(2,1)S(1)}, u32[]{:S(2)}, u32[]{:S(2)}) %collective-permute-start.25) | collective-permute-done | bytes 90144 | tf_op jit(solution)/shard_map/ppermute | solution.py:364
  79.1 0.1 last_sums.1
  79.1 0.1 collective-permute-start.28
  79.2 1.3 %collective-permute-done.28.refs_1_ = bf16[528,128]{1,0:T(8,128)(2,1)S(1)} collective-permute-done((bf16[528,128]{1,0:T(8,128)(2,1)S(1)}, bf16[528,128]{1,0:T(8,128)(2,1)S(1)}, u32[]{:S(2)}, u32[]{:S(2)}) %collective-permute-start.28) | collective-permute-done | bytes 135200 | tf_op jit(solution)/shard_map/ppermute | solution.py:361
  80.6 0.8 unpack.1
  (29 shorter events, 0.4 us)
Async XLA Ops:
  1.9 14.2 %collective-permute-start.3 = (bf16[528,128]{1,0:T(8,128)(2,1)S(1)}, bf16[528,128]{1,0:T(8,128)(2,1)S(1)}, u32[]{:S(2)}, u32[]{:S(2)}) collective-permute-start(bf16[528,128]{1,0:T(8,128)(2,1)S(1)} %get-tuple-element.76), channel_id=1, source_target_pairs={{0,2},{2,0},{1,3},{3,1},{4,6},{6,4},{5,7},{7,5},{8,10},{10,8},{9,1... | collective-permute-start | bytes 405512 | tf_op jit(solution)/shard_map/ppermute | solution.py:367
  4.9 11.2 %collective-permute-start.2 = (bf16[528,128]{1,0:T(8,128)(2,1)S(1)}, bf16[528,128]{1,0:T(8,128)(2,1)S(1)}, u32[]{:S(2)}, u32[]{:S(2)}) collective-permute-start(bf16[528,128]{1,0:T(8,128)(2,1)S(1)} %get-tuple-element.76), channel_id=1, source_target_pairs={{0,12},{4,0},{8,4},{12,8},{1,13},{5,1},{9,5},{13,9},{2,14},{6,2},{... | collective-permute-start | bytes 405512 | tf_op jit(solution)/shard_map/ppermute | solution.py:364
  8.5 11.1 %collective-permute-start.1 = (bf16[528,128]{1,0:T(8,128)(2,1)S(1)}, bf16[528,128]{1,0:T(8,128)(2,1)S(1)}, u32[]{:S(2)}, u32[]{:S(2)}) collective-permute-start(bf16[528,128]{1,0:T(8,128)(2,1)S(1)} %get-tuple-element.76), channel_id=1, source_target_pairs={{0,8},{4,12},{8,0},{12,4},{1,9},{5,13},{9,1},{13,5},{2,10},{6,14},... | collective-permute-start | bytes 405512 | tf_op jit(solution)/shard_map/ppermute | solution.py:364
  8.5 11.1 %collective-permute-start = (bf16[528,128]{1,0:T(8,128)(2,1)S(1)}, bf16[528,128]{1,0:T(8,128)(2,1)S(1)}, u32[]{:S(2)}, u32[]{:S(2)}) collective-permute-start(bf16[528,128]{1,0:T(8,128)(2,1)S(1)} %get-tuple-element.76), channel_id=1, source_target_pairs={{0,4},{4,8},{8,12},{12,0},{1,5},{5,9},{9,13},{13,1},{2,6},{6,10},{... | collective-permute-start | bytes 405512 | tf_op jit(solution)/shard_map/ppermute | solution.py:364
  9.5 6.5 %collective-permute-start.4 = (bf16[64,1024]{1,0:T(8,128)(2,1)S(1)}, bf16[64,1024]{1,0:T(8,128)(2,1)S(1)}, u32[]{:S(2)}, u32[]{:S(2)}) collective-permute-start(bf16[64,1024]{1,0:T(8,128)(2,1)S(1)} %get-tuple-element.83), channel_id=1, source_target_pairs={{0,2},{2,0},{1,3},{3,1},{4,6},{6,4},{5,7},{7,5},{8,10},{10,8},{9,1... | collective-permute-start | bytes 393224 | tf_op jit(solution)/shard_map/ppermute | solution.py:367
  19.7 5.6 %collective-permute-start.5 = (bf16[4,528,128]{2,1,0:T(8,128)(2,1)S(1)}, bf16[4,528,128]{2,1,0:T(8,128)(2,1)S(1)}, u32[]{:S(2)}, u32[]{:S(2)}) collective-permute-start(bf16[4,528,128]{2,1,0:T(8,128)(2,1)S(1)} %pad_maximum_fusion.refs_0_), channel_id=1, source_target_pairs={{0,1},{1,0},{2,3},{3,2},{4,5},{5,4},{6,7},{7,6},{8,9},{9,8},{10,11... | collective-permute-start | bytes 1622024 | tf_op jit(solution)/shard_map/ppermute | solution.py:361
  19.8 12.9 %collective-permute-start.9 = (bf16[3,528,128]{2,1,0:T(8,128)(2,1)S(1)}, bf16[3,528,128]{2,1,0:T(8,128)(2,1)S(1)}, u32[]{:S(2)}, u32[]{:S(2)}) collective-permute-start(bf16[3,528,128]{2,1,0:T(8,128)(2,1)S(1)} %pad_maximum_fusion.2), channel_id=1, source_target_pairs={{0,2},{2,0},{1,3},{3,1},{4,6},{6,4},{5,7},{7,5},{8,10},{10,8},{9,1... | collective-permute-start | bytes 1216520 | tf_op jit(solution)/shard_map/ppermute | solution.py:367
  20.4 5.4 %collective-permute-start.8 = (bf16[48,1024]{1,0:T(8,128)(2,1)S(1)}, bf16[48,1024]{1,0:T(8,128)(2,1)S(1)}, u32[]{:S(2)}, u32[]{:S(2)}) collective-permute-start(bf16[48,1024]{1,0:T(8,128)(2,1)S(1)} %get-tuple-element.152), channel_id=1, source_target_pairs={{0,12},{4,0},{8,4},{12,8},{1,13},{5,1},{9,5},{13,9},{2,14},{6,2},{... | collective-permute-start | bytes 294920 | tf_op jit(solution)/shard_map/ppermute | solution.py:364
  22.1 10.6 %collective-permute-start.7 = (bf16[48,1024]{1,0:T(8,128)(2,1)S(1)}, bf16[48,1024]{1,0:T(8,128)(2,1)S(1)}, u32[]{:S(2)}, u32[]{:S(2)}) collective-permute-start(bf16[48,1024]{1,0:T(8,128)(2,1)S(1)} %get-tuple-element.152), channel_id=1, source_target_pairs={{0,8},{4,12},{8,0},{12,4},{1,9},{5,13},{9,1},{13,5},{2,10},{6,14},... | collective-permute-start | bytes 294920 | tf_op jit(solution)/shard_map/ppermute | solution.py:364
  23.3 9.4 %collective-permute-start.6 = (bf16[48,1024]{1,0:T(8,128)(2,1)S(1)}, bf16[48,1024]{1,0:T(8,128)(2,1)S(1)}, u32[]{:S(2)}, u32[]{:S(2)}) collective-permute-start(bf16[48,1024]{1,0:T(8,128)(2,1)S(1)} %get-tuple-element.152), channel_id=1, source_target_pairs={{0,4},{4,8},{8,12},{12,0},{1,5},{5,9},{9,13},{13,1},{2,6},{6,10},{... | collective-permute-start | bytes 294920 | tf_op jit(solution)/shard_map/ppermute | solution.py:364
  32.8 5.4 %collective-permute-start.10 = (bf16[4,528,128]{2,1,0:T(8,128)(2,1)S(1)}, bf16[4,528,128]{2,1,0:T(8,128)(2,1)S(1)}, u32[]{:S(2)}, u32[]{:S(2)}) collective-permute-start(bf16[4,528,128]{2,1,0:T(8,128)(2,1)S(1)} %pad_maximum_fusion.1.refs_0_), channel_id=1, source_target_pairs={{0,1},{1,0},{2,3},{3,2},{4,5},{5,4},{6,7},{7,6},{8,9},{9,8},{10,11... | collective-permute-start | bytes 1622024 | tf_op jit(solution)/shard_map/ppermute | solution.py:361
  32.9 9.5 %collective-permute-start.14 = (bf16[2,16,1024]{2,1,0:T(8,128)(2,1)S(1)}, bf16[2,16,1024]{2,1,0:T(8,128)(2,1)S(1)}, u32[]{:S(2)}, u32[]{:S(2)}) collective-permute-start(bf16[2,16,1024]{2,1,0:T(8,128)(2,1)S(1)} %get-tuple-element.154), channel_id=1, source_target_pairs={{0,12},{4,0},{8,4},{12,8},{1,13},{5,1},{9,5},{13,9},{2,14},{6,2},{... | collective-permute-start | bytes 196616 | tf_op jit(solution)/shard_map/ppermute | solution.py:364
  33.5 8.8 %collective-permute-start.13 = (bf16[2,16,1024]{2,1,0:T(8,128)(2,1)S(1)}, bf16[2,16,1024]{2,1,0:T(8,128)(2,1)S(1)}, u32[]{:S(2)}, u32[]{:S(2)}) collective-permute-start(bf16[2,16,1024]{2,1,0:T(8,128)(2,1)S(1)} %get-tuple-element.154), channel_id=1, source_target_pairs={{0,8},{4,12},{8,0},{12,4},{1,9},{5,13},{9,1},{13,5},{2,10},{6,14},... | collective-permute-start | bytes 196616 | tf_op jit(solution)/shard_map/ppermute | solution.py:364
  34.7 7.7 %collective-permute-start.12 = (bf16[2,16,1024]{2,1,0:T(8,128)(2,1)S(1)}, bf16[2,16,1024]{2,1,0:T(8,128)(2,1)S(1)}, u32[]{:S(2)}, u32[]{:S(2)}) collective-permute-start(bf16[2,16,1024]{2,1,0:T(8,128)(2,1)S(1)} %get-tuple-element.154), channel_id=1, source_target_pairs={{0,4},{4,8},{8,12},{12,0},{1,5},{5,9},{9,13},{13,1},{2,6},{6,10},{... | collective-permute-start | bytes 196616 | tf_op jit(solution)/shard_map/ppermute | solution.py:364
  36.7 8.6 %collective-permute-start.11 = (bf16[3,48,1024]{2,1,0:T(8,128)(2,1)S(1)}, bf16[3,48,1024]{2,1,0:T(8,128)(2,1)S(1)}, u32[]{:S(2)}, u32[]{:S(2)}) collective-permute-start(bf16[3,48,1024]{2,1,0:T(8,128)(2,1)S(1)} %pad_maximum_fusion.5), channel_id=1, source_target_pairs={{0,2},{2,0},{1,3},{3,1},{4,6},{6,4},{5,7},{7,5},{8,10},{10,8},{9,1... | collective-permute-start | bytes 884744 | tf_op jit(solution)/shard_map/ppermute | solution.py:367
  38.2 7.9 %collective-permute-start.15 = (bf16[4,48,1024]{2,1,0:T(8,128)(2,1)S(1)}, bf16[4,48,1024]{2,1,0:T(8,128)(2,1)S(1)}, u32[]{:S(2)}, u32[]{:S(2)}) collective-permute-start(bf16[4,48,1024]{2,1,0:T(8,128)(2,1)S(1)} %pad_maximum_fusion.3.refs_1_), channel_id=1, source_target_pairs={{0,1},{1,0},{2,3},{3,2},{4,5},{5,4},{6,7},{7,6},{8,9},{9,8},{10,11... | collective-permute-start | bytes 1179656 | tf_op jit(solution)/shard_map/ppermute | solution.py:361
  45.4 2.6 %collective-permute-start.17 = (bf16[4,48,1024]{2,1,0:T(8,128)(2,1)S(1)}, bf16[4,48,1024]{2,1,0:T(8,128)(2,1)S(1)}, u32[]{:S(2)}, u32[]{:S(2)}) collective-permute-start(bf16[4,48,1024]{2,1,0:T(8,128)(2,1)S(1)} %pad_maximum_fusion.4.refs_1_), channel_id=1, source_target_pairs={{0,1},{1,0},{2,3},{3,2},{4,5},{5,4},{6,7},{7,6},{8,9},{9,8},{10,11... | collective-permute-start | bytes 1179656 | tf_op jit(solution)/shard_map/ppermute | solution.py:361
  45.5 2.0 %collective-permute-start.16 = (bf16[4,2,16,1024]{3,2,1,0:T(8,128)(2,1)S(1)}, bf16[4,2,16,1024]{3,2,1,0:T(8,128)(2,1)S(1)}, u32[]{:S(2)}, u32[]{:S(2)}) collective-permute-start(bf16[4,2,16,1024]{3,2,1,0:T(8,128)(2,1)S(1)} %pad_maximum_fusion.6.refs_3_), channel_id=1, source_target_pairs={{0,1},{1,0},{2,3},{3,2},{4,5},{5,4},{6,7},{7,6},{8,9},{9,8},{10,11... | collective-permute-start | bytes 786440 | tf_op jit(solution)/shard_map/ppermute | solution.py:361
  54.0 2.0 %collective-permute-start.18 = (bf16[4,528,128]{2,1,0:T(8,128)(2,1)S(1)}, bf16[4,528,128]{2,1,0:T(8,128)(2,1)S(1)}, u32[]{:S(2)}, u32[]{:S(2)}) collective-permute-start(bf16[4,528,128]{2,1,0:T(8,128)(2,1)S(1)} %get-tuple-element.123), channel_id=1, source_target_pairs={{0,1},{1,0},{2,3},{3,2},{4,5},{5,4},{6,7},{7,6},{8,9},{9,8},{10,11... | collective-permute-start | bytes 1622024 | tf_op jit(solution)/shard_map/ppermute | solution.py:361
  54.7 2.9 %collective-permute-start.19 = (bf16[4,528,128]{2,1,0:T(8,128)(2,1)S(1)}, bf16[4,528,128]{2,1,0:T(8,128)(2,1)S(1)}, u32[]{:S(2)}, u32[]{:S(2)}) collective-permute-start(bf16[4,528,128]{2,1,0:T(8,128)(2,1)S(1)} %get-tuple-element.125), channel_id=1, source_target_pairs={{0,1},{1,0},{2,3},{3,2},{4,5},{5,4},{6,7},{7,6},{8,9},{9,8},{10,11... | collective-permute-start | bytes 1622024 | tf_op jit(solution)/shard_map/ppermute | solution.py:361
  56.1 12.4 %collective-permute-start.20 = (bf16[4,352,128]{2,1,0:T(8,128)(2,1)S(1)}, bf16[4,352,128]{2,1,0:T(8,128)(2,1)S(1)}, u32[]{:S(2)}, u32[]{:S(2)}) collective-permute-start(bf16[4,352,128]{2,1,0:T(8,128)(2,1)S(1)} %add_convert_fusion.refs_2_), channel_id=1, source_target_pairs={{0,2},{2,0},{1,3},{3,1},{4,6},{6,4},{5,7},{7,5},{8,10},{10,8},{9,1... | collective-permute-start | bytes 1081352 | tf_op jit(solution)/shard_map/ppermute | solution.py:367
  57.6 9.1 %collective-permute-start.21 = (bf16[2,176,128]{2,1,0:T(8,128)(2,1)S(1)}, bf16[2,176,128]{2,1,0:T(8,128)(2,1)S(1)}, u32[]{:S(2)}, u32[]{:S(2)}) collective-permute-start(bf16[2,176,128]{2,1,0:T(8,128)(2,1)S(1)} %pad_maximum_fusion.8.refs_3_), channel_id=1, source_target_pairs={{0,12},{4,0},{8,4},{12,8},{1,13},{5,1},{9,5},{13,9},{2,14},{6,2},{... | collective-permute-start | bytes 270344 | tf_op jit(solution)/shard_map/ppermute | solution.py:364
  59.9 8.6 %collective-permute-start.22 = (bf16[2,176,128]{2,1,0:T(8,128)(2,1)S(1)}, bf16[2,176,128]{2,1,0:T(8,128)(2,1)S(1)}, u32[]{:S(2)}, u32[]{:S(2)}) collective-permute-start(bf16[2,176,128]{2,1,0:T(8,128)(2,1)S(1)} %pad_maximum_fusion.9.refs_4_), channel_id=1, source_target_pairs={{0,8},{4,12},{8,0},{12,4},{1,9},{5,13},{9,1},{13,5},{2,10},{6,14},... | collective-permute-start | bytes 270344 | tf_op jit(solution)/shard_map/ppermute | solution.py:364
  60.0 8.5 %collective-permute-start.23 = (bf16[2,176,128]{2,1,0:T(8,128)(2,1)S(1)}, bf16[2,176,128]{2,1,0:T(8,128)(2,1)S(1)}, u32[]{:S(2)}, u32[]{:S(2)}) collective-permute-start(bf16[2,176,128]{2,1,0:T(8,128)(2,1)S(1)} %pad_maximum_fusion.10.refs_5_), channel_id=1, source_target_pairs={{0,4},{4,8},{8,12},{12,0},{1,5},{5,9},{9,13},{13,1},{2,6},{6,10},{... | collective-permute-start | bytes 270344 | tf_op jit(solution)/shard_map/ppermute | solution.py:364
  68.6 9.1 %collective-permute-start.24 = (bf16[352,128]{1,0:T(8,128)(2,1)S(1)}, bf16[352,128]{1,0:T(8,128)(2,1)S(1)}, u32[]{:S(2)}, u32[]{:S(2)}) collective-permute-start(bf16[352,128]{1,0:T(8,128)(2,1)S(1)} %get-tuple-element.129.refs_2_), channel_id=1, source_target_pairs={{0,12},{4,0},{8,4},{12,8},{1,13},{5,1},{9,5},{13,9},{2,14},{6,2},{... | collective-permute-start | bytes 270344 | tf_op jit(solution)/shard_map/ppermute | solution.py:364
  70.3 8.8 %collective-permute-start.25 = (bf16[352,128]{1,0:T(8,128)(2,1)S(1)}, bf16[352,128]{1,0:T(8,128)(2,1)S(1)}, u32[]{:S(2)}, u32[]{:S(2)}) collective-permute-start(bf16[352,128]{1,0:T(8,128)(2,1)S(1)} %get-tuple-element.130.refs_3_), channel_id=1, source_target_pairs={{0,8},{4,12},{8,0},{12,4},{1,9},{5,13},{9,1},{13,5},{2,10},{6,14},... | collective-permute-start | bytes 270344 | tf_op jit(solution)/shard_map/ppermute | solution.py:364
  70.8 8.2 %collective-permute-start.26 = (bf16[352,128]{1,0:T(8,128)(2,1)S(1)}, bf16[352,128]{1,0:T(8,128)(2,1)S(1)}, u32[]{:S(2)}, u32[]{:S(2)}) collective-permute-start(bf16[352,128]{1,0:T(8,128)(2,1)S(1)} %get-tuple-element.131.refs_4_), channel_id=1, source_target_pairs={{0,4},{4,8},{8,12},{12,0},{1,5},{5,9},{9,13},{13,1},{2,6},{6,10},{... | collective-permute-start | bytes 270344 | tf_op jit(solution)/shard_map/ppermute | solution.py:364
  72.8 4.9 %collective-permute-start.27 = (bf16[176,128]{1,0:T(8,128)(2,1)S(1)}, bf16[176,128]{1,0:T(8,128)(2,1)S(1)}, u32[]{:S(2)}, u32[]{:S(2)}) collective-permute-start(bf16[176,128]{1,0:T(8,128)(2,1)S(1)} %get-tuple-element.132.refs_5_), channel_id=1, source_target_pairs={{0,2},{2,0},{1,3},{3,1},{4,6},{6,4},{5,7},{7,5},{8,10},{10,8},{9,1... | collective-permute-start | bytes 135176 | tf_op jit(solution)/shard_map/ppermute | solution.py:367
  79.1 1.4 %collective-permute-start.28 = (bf16[528,128]{1,0:T(8,128)(2,1)S(1)}, bf16[528,128]{1,0:T(8,128)(2,1)S(1)}, u32[]{:S(2)}, u32[]{:S(2)}) collective-permute-start(bf16[528,128]{1,0:T(8,128)(2,1)S(1)} %get-tuple-element.137.refs_0_), channel_id=1, source_target_pairs={{0,1},{1,0},{2,3},{3,2},{4,5},{5,4},{6,7},{7,6},{8,9},{9,8},{10,11... | collective-permute-start | bytes 405512 | tf_op jit(solution)/shard_map/ppermute | solution.py:361

commit v7 on v6

--- a/solution.py
+++ b/solution.py
@@ -443,7 +443,7 @@
         functools.partial(backward_kernel, xs), "backward", 6, outs, where,
         (wgu, wd, *factors, holds, *rows_dy))
     height = packed + 16 * pl.cdiv(kinds, 16)
-    split = 2 * height // 3 // 16 * 16
+    split = 7 * height // 10 // 16 * 16
     chip = [None] * xs
     for c in list(range(1, xs)) + [0]:
         where, (own, other) = on_vmem(

time: 81.5 us -> 81.6 us (level)
  no operation moved by 1% of the time
where the time goes in v7:
time: 81.6 us; the launch traced here: 81.4 us
  starting transfers between devices  30.2 us (37%)
  Pallas kernels  29.1 us (36%)
  waiting for transfers between devices  20.5 us (25%)
  between operations  1 us (1%)
    ppermute x15, starting transfers between devices, along_z(): lax.ppermute(array, 'expert', [(i, (i + by) % zs) for i in range(zs)])  20.8 us
    ppermute x15, waiting for transfers between devices, along_z(): lax.ppermute(array, 'expert', [(i, (i + by) % zs) for i in range(zs)])  13.8 us
    pallas_call x11, Pallas kernels, on_vmem(): pl.pallas_call(body, in_specs=[IN_VMEM] * (1 + len(operands)), out_specs=...  12.6 us
    pallas_call x2, Pallas kernels, weights(): pl.pallas_call(functools.partial(weights_kernel, xs, number), in_specs=[I...  9.39 us
    ppermute x6, starting transfers between devices, along_x(): return lax.ppermute(array, 'blk', [(i, (i + by) % xs) for i in range(xs)])  7.92 us
    pallas_call x1, Pallas kernels, load(): pl.pallas_call(load_kernel, in_specs=[IN_VMEM] + [pl.BlockSpec(memory_spa...  6 us
    ppermute x8, waiting for transfers between devices, swap(): lax.ppermute(array, 'tensor', [(i, (i + 1) % cores) for i in range(cores)])  3.72 us
    ppermute x6, waiting for transfers between devices, along_x(): return lax.ppermute(array, 'blk', [(i, (i + by) % xs) for i in range(xs)])  2.95 us
  transfers between devices with their start and end apart: 29, of which 8 were waited for; matrix products, arithmetic and copies ran while one was open for 1% of the time, Pallas kernels for 26%

profile of v7, /device:TPU:0, one launch (start us, length us, event | category | flops | bytes accessed | tf_op | source)
XLA Modules:
  0.0 81.4 jit_solution(13932201927524944751)
XLA Ops:
  0.7 0.1 iota.7.where_ref
  0.7 1.1 %pack.1 = (bf16[528,128]{1,0:T(8,128)(2,1)S(1)}, bf16[64,1024]{1,0:T(8,128)(2,1)S(1)}, s32[8,128]{1,0:T(8,128)S(1)}) custom-call(s32[1]{0:T(128)} %bitcast.core_ref, s32[8,128]{1,0:T(8,128)S(1)} %iota.7.where_ref, bf16[128,1024]{1,0:T(8,128)(2,1)} %tokens_ref.1, bf16[128,1024]{1,0:T(8,128)(2,1)} %cotangent_ref.1, s32[6,128]{1,0:T(8,128)} %bitcast.59, ...), custom_call_target="tpu_custom_call" | custom-call | flops 1000 | bytes 6000000 | tf_op jit(solution)/shard_map/pack/pallas_call | solution.py:375
  1.9 3.0 %collective-permute-start.3 = (bf16[528,128]{1,0:T(8,128)(2,1)S(1)}, bf16[528,128]{1,0:T(8,128)(2,1)S(1)}, u32[]{:S(2)}, u32[]{:S(2)}) collective-permute-start(bf16[528,128]{1,0:T(8,128)(2,1)S(1)} %get-tuple-element.76), channel_id=1, source_target_pairs={{0,2},{2,0},{1,3},{3,1},{4,6},{6,4},{5,7},{7,5},{8,10},{10,8},{9,1... | collective-permute-start | bytes 405512 | tf_op jit(solution)/shard_map/ppermute | solution.py:367
  4.9 3.6 %collective-permute-start.2 = (bf16[528,128]{1,0:T(8,128)(2,1)S(1)}, bf16[528,128]{1,0:T(8,128)(2,1)S(1)}, u32[]{:S(2)}, u32[]{:S(2)}) collective-permute-start(bf16[528,128]{1,0:T(8,128)(2,1)S(1)} %get-tuple-element.76), channel_id=1, source_target_pairs={{0,12},{4,0},{8,4},{12,8},{1,13},{5,1},{9,5},{13,9},{2,14},{6,2},{... | collective-permute-start | bytes 405512 | tf_op jit(solution)/shard_map/ppermute | solution.py:364
  8.5 0.0 collective-permute-start.1
  8.5 1.0 %collective-permute-start = (bf16[528,128]{1,0:T(8,128)(2,1)S(1)}, bf16[528,128]{1,0:T(8,128)(2,1)S(1)}, u32[]{:S(2)}, u32[]{:S(2)}) collective-permute-start(bf16[528,128]{1,0:T(8,128)(2,1)S(1)} %get-tuple-element.76), channel_id=1, source_target_pairs={{0,4},{4,8},{8,12},{12,0},{1,5},{5,9},{9,13},{13,1},{2,6},{6,10},{... | collective-permute-start | bytes 405512 | tf_op jit(solution)/shard_map/ppermute | solution.py:364
  9.5 0.5 collective-permute-start.4
  10.0 6.0 %load.1 = (bf16[8,704,1024]{2,1,0:T(8,128)(2,1)S(1)}, bf16[8,352,1024]{2,1,0:T(8,128)(2,1)S(1)}, s32[8,128]{1,0:T(8,128)S(1)}) custom-call(s32[8,128]{1,0:T(8,128)S(1)} %get-tuple-element.74.where_ref, bf16[8,352,1024]{2,1,0:T(8,128)(2,1)} %bitcast.40, bf16[8,352,1024]{2,1,0:T(8,128)(2,1)} %bitcast.41, bf16[8,352,1024]{2,1,0:T(8,128)(2,1)} %bitcast.42), custom_call_target="tpu_custom_call" | custom-call | flops 1000 | bytes 21000000 | tf_op jit(solution)/shard_map/load/pallas_call | solution.py:310
  16.0 0.0 collective-permute-done.4
  16.0 0.0 collective-permute-done.2
  16.1 3.6 %collective-permute-done.1 = bf16[528,128]{1,0:T(8,128)(2,1)S(1)} collective-permute-done((bf16[528,128]{1,0:T(8,128)(2,1)S(1)}, bf16[528,128]{1,0:T(8,128)(2,1)S(1)}, u32[]{:S(2)}, u32[]{:S(2)}) %collective-permute-start.1) | collective-permute-done | bytes 135200 | tf_op jit(solution)/shard_map/ppermute | solution.py:364
  19.6 0.1 pad_maximum_fusion.refs_0_
  19.7 0.1 collective-permute-start.5
  19.8 0.6 collective-permute-start.9
  20.4 1.7 %collective-permute-start.8 = (bf16[48,1024]{1,0:T(8,128)(2,1)S(1)}, bf16[48,1024]{1,0:T(8,128)(2,1)S(1)}, u32[]{:S(2)}, u32[]{:S(2)}) collective-permute-start(bf16[48,1024]{1,0:T(8,128)(2,1)S(1)} %get-tuple-element.152), channel_id=1, source_target_pairs={{0,12},{4,0},{8,4},{12,8},{1,13},{5,1},{9,5},{13,9},{2,14},{6,2},{... | collective-permute-start | bytes 294920 | tf_op jit(solution)/shard_map/ppermute | solution.py:364
  22.1 1.2 %collective-permute-start.7 = (bf16[48,1024]{1,0:T(8,128)(2,1)S(1)}, bf16[48,1024]{1,0:T(8,128)(2,1)S(1)}, u32[]{:S(2)}, u32[]{:S(2)}) collective-permute-start(bf16[48,1024]{1,0:T(8,128)(2,1)S(1)} %get-tuple-element.152), channel_id=1, source_target_pairs={{0,8},{4,12},{8,0},{12,4},{1,9},{5,13},{9,1},{13,5},{2,10},{6,14},... | collective-permute-start | bytes 294920 | tf_op jit(solution)/shard_map/ppermute | solution.py:364
  23.3 1.9 %collective-permute-start.6 = (bf16[48,1024]{1,0:T(8,128)(2,1)S(1)}, bf16[48,1024]{1,0:T(8,128)(2,1)S(1)}, u32[]{:S(2)}, u32[]{:S(2)}) collective-permute-start(bf16[48,1024]{1,0:T(8,128)(2,1)S(1)} %get-tuple-element.152), channel_id=1, source_target_pairs={{0,4},{4,8},{8,12},{12,0},{1,5},{5,9},{9,13},{13,1},{2,6},{6,10},{... | collective-permute-start | bytes 294920 | tf_op jit(solution)/shard_map/ppermute | solution.py:364
  25.3 0.0 collective-permute-done.5.refs_1_
  25.3 0.6 select_tokens.2
  25.9 6.9 %collective-permute-done.7 = bf16[48,1024]{1,0:T(8,128)(2,1)S(1)} collective-permute-done((bf16[48,1024]{1,0:T(8,128)(2,1)S(1)}, bf16[48,1024]{1,0:T(8,128)(2,1)S(1)}, u32[]{:S(2)}, u32[]{:S(2)}) %collective-permute-start.7) | collective-permute-done | bytes 98336 | tf_op jit(solution)/shard_map/ppermute | solution.py:364
  32.7 0.0 collective-permute-done.6
  32.7 0.0 collective-permute-done.9
  32.8 0.1 collective-permute-start.10
  32.9 0.6 collective-permute-start.14
  33.5 1.2 %collective-permute-start.13 = (bf16[2,16,1024]{2,1,0:T(8,128)(2,1)S(1)}, bf16[2,16,1024]{2,1,0:T(8,128)(2,1)S(1)}, u32[]{:S(2)}, u32[]{:S(2)}) collective-permute-start(bf16[2,16,1024]{2,1,0:T(8,128)(2,1)S(1)} %get-tuple-element.154), channel_id=1, source_target_pairs={{0,8},{4,12},{8,0},{12,4},{1,9},{5,13},{9,1},{13,5},{2,10},{6,14},... | collective-permute-start | bytes 196616 | tf_op jit(solution)/shard_map/ppermute | solution.py:364
  34.7 1.9 %collective-permute-start.12 = (bf16[2,16,1024]{2,1,0:T(8,128)(2,1)S(1)}, bf16[2,16,1024]{2,1,0:T(8,128)(2,1)S(1)}, u32[]{:S(2)}, u32[]{:S(2)}) collective-permute-start(bf16[2,16,1024]{2,1,0:T(8,128)(2,1)S(1)} %get-tuple-element.154), channel_id=1, source_target_pairs={{0,4},{4,8},{8,12},{12,0},{1,5},{5,9},{9,13},{13,1},{2,6},{6,10},{... | collective-permute-start | bytes 196616 | tf_op jit(solution)/shard_map/ppermute | solution.py:364
  36.7 1.4 %collective-permute-start.11 = (bf16[3,48,1024]{2,1,0:T(8,128)(2,1)S(1)}, bf16[3,48,1024]{2,1,0:T(8,128)(2,1)S(1)}, u32[]{:S(2)}, u32[]{:S(2)}) collective-permute-start(bf16[3,48,1024]{2,1,0:T(8,128)(2,1)S(1)} %pad_maximum_fusion.5), channel_id=1, source_target_pairs={{0,2},{2,0},{1,3},{3,1},{4,6},{6,4},{5,7},{7,5},{8,10},{10,8},{9,1... | collective-permute-start | bytes 884744 | tf_op jit(solution)/shard_map/ppermute | solution.py:367
  38.1 0.1 pad_maximum_fusion.3.refs_1_
  38.2 0.1 collective-permute-start.15
  38.3 0.6 select_tokens.3
  38.8 3.5 %forward.1 = (f32[8,352,128]{2,1,0:T(8,128)S(1)}, f32[8,352,128]{2,1,0:T(8,128)S(1)}, f32[8,352,128]{2,1,0:T(8,128)S(1)}, bf16[8,352,128]{2,1,0:T(8,128)(2,1)S(1...) custom-call(s32[8,128]{1,0:T(8,128)S(1)} %get-tuple-element.87.where_ref, ...), custom_call_target="tpu_custom_call" | custom-call | flops 1000 | bytes 15000000 | tf_op jit(solution)/shard_map/forward/pallas_call | solution.py:330
  42.4 0.0 collective-permute-done.14
  42.4 0.0 collective-permute-done.13
  42.4 2.9 %collective-permute-done.11 = bf16[3,48,1024]{2,1,0:T(8,128)(2,1)S(1)} collective-permute-done((bf16[3,48,1024]{2,1,0:T(8,128)(2,1)S(1)}, bf16[3,48,1024]{2,1,0:T(8,128)(2,1)S(1)}, u32[]{:S(2)}, u32[]{:S(2)}) %collective-permute-start.11) | collective-permute-done | bytes 294944 | tf_op jit(solution)/shard_map/ppermute | solution.py:367
  45.4 0.1 collective-permute-start.17
  45.5 0.6 collective-permute-start.16
  46.0 1.5 %collective-permute-done.16.refs_4_ = bf16[4,2,16,1024]{3,2,1,0:T(8,128)(2,1)S(1)} collective-permute-done((bf16[4,2,16,1024]{3,2,1,0:T(8,128)(2,1)S(1)}, bf16[4,2,16,1024]{3,2,1,0:T(8,128)(2,1)S(1)}, u32[]{:S(2)}, u32[]{:S(2)}) %collective-permute-start.16) | collective-permute-done | bytes 262176 | tf_op jit(solution)/shard_map/ppermute | solution.py:361
  47.5 0.4 select_cotangents.2
  48.0 0.0 collective-permute-done.17.refs_2_
  48.0 0.4 select_cotangents.3
  48.4 5.1 %backward.1 = (bf16[8,704,128]{2,1,0:T(8,128)(2,1)S(1)}, bf16[8,128,1024]{2,1,0:T(8,128)(2,1)S(1)}, f32[8,8,128]{2,1,0:T(8,128)S(1)}, s32[8,128]{1,0:T(8,128)S(1)}) custom-call(s32[8,128]{1,0:T(8,128)S(1)} %get-tuple-element.106.where_ref, bf16[8,704,1024]{2,1,0:T(8,128)(2,1)S(1)} %get-tuple-element.88.refs_0_, ...), custom_call_target="tpu_custom_call" | custom-call | flops 1000 | bytes 18000000 | tf_op jit(solution)/shard_map/backward/pallas_call | solution.py:330
  53.5 0.5 put_back.2
  54.0 0.2 collective-permute-start.18
  54.2 0.5 put_back.3
  54.7 0.4 collective-permute-start.19
  55.1 0.9 %collective-permute-done.18 = bf16[4,528,128]{2,1,0:T(8,128)(2,1)S(1)} collective-permute-done((bf16[4,528,128]{2,1,0:T(8,128)(2,1)S(1)}, bf16[4,528,128]{2,1,0:T(8,128)(2,1)S(1)}, u32[]{:S(2)}, u32[]{:S(2)}) %collective-permute-start.18) | collective-permute-done | bytes 540704 | tf_op jit(solution)/shard_map/ppermute | solution.py:361
  56.0 0.1 add_convert_fusion.refs_2_
  56.1 1.4 %collective-permute-start.20 = (bf16[4,368,128]{2,1,0:T(8,128)(2,1)S(1)}, bf16[4,368,128]{2,1,0:T(8,128)(2,1)S(1)}, u32[]{:S(2)}, u32[]{:S(2)}) collective-permute-start(bf16[4,368,128]{2,1,0:T(8,128)(2,1)S(1)} %add_convert_fusion.refs_2_), channel_id=1, source_target_pairs={{0,2},{2,0},{1,3},{3,1},{4,6},{6,4},{5,7},{7,5},{8,10},{10,8},{9,1... | collective-permute-start | bytes 1130504 | tf_op jit(solution)/shard_map/ppermute | solution.py:367
  57.7 2.2 %collective-permute-start.21 = (bf16[2,160,128]{2,1,0:T(8,128)(2,1)S(1)}, bf16[2,160,128]{2,1,0:T(8,128)(2,1)S(1)}, u32[]{:S(2)}, u32[]{:S(2)}) collective-permute-start(bf16[2,160,128]{2,1,0:T(8,128)(2,1)S(1)} %pad_maximum_fusion.8.refs_3_), channel_id=1, source_target_pairs={{0,12},{4,0},{8,4},{12,8},{1,13},{5,1},{9,5},{13,9},{2,14},{6,2},{... | collective-permute-start | bytes 245768 | tf_op jit(solution)/shard_map/ppermute | solution.py:364
  59.9 0.1 collective-permute-start.22
  60.0 1.3 %collective-permute-start.23 = (bf16[2,160,128]{2,1,0:T(8,128)(2,1)S(1)}, bf16[2,160,128]{2,1,0:T(8,128)(2,1)S(1)}, u32[]{:S(2)}, u32[]{:S(2)}) collective-permute-start(bf16[2,160,128]{2,1,0:T(8,128)(2,1)S(1)} %pad_maximum_fusion.10.refs_5_), channel_id=1, source_target_pairs={{0,4},{4,8},{8,12},{12,0},{1,5},{5,9},{9,13},{13,1},{2,6},{6,10},{... | collective-permute-start | bytes 245768 | tf_op jit(solution)/shard_map/ppermute | solution.py:364
  61.3 5.4 %weights.2 = (bf16[8,352,1024]{2,1,0:T(8,128)(2,1)}, bf16[8,352,1024]{2,1,0:T(8,128)(2,1)}, s32[8,128]{1,0:T(8,128)S(1)}) custom-call(s32[8,128]{1,0:T(8,128)S(1)} %get-tuple-element.120.where_ref, bf16[8,704,128]{2,1,0:T(8,128)(2,1)S(1)} %get-tuple-element.121.hidden_ref, bf16[8,64,1024]{2,1,0:T(8,128)(2,1)S(1)} %get-tuple-element.93.refs_5_.refs_0_, ...), custom_call_target="tpu_custom_call" | custom-call | flops 1000 | bytes 18000000 | tf_op jit(solution)/shard_map/weights/pallas_call | solution.py:461
  66.7 1.2 %collective-permute-done.22.refs_5_ = bf16[2,160,128]{2,1,0:T(8,128)(2,1)S(1)} collective-permute-done((bf16[2,160,128]{2,1,0:T(8,128)(2,1)S(1)}, bf16[2,160,128]{2,1,0:T(8,128)(2,1)S(1)}, u32[]{:S(2)}, u32[]{:S(2)}) %collective-permute-start.22) | collective-permute-done | bytes 81952 | tf_op jit(solution)/shard_map/ppermute | solution.py:364
  67.9 0.2 middle_sums.1
  68.1 1.7 %collective-permute-start.24 = (bf16[368,128]{1,0:T(8,128)(2,1)S(1)}, bf16[368,128]{1,0:T(8,128)(2,1)S(1)}, u32[]{:S(2)}, u32[]{:S(2)}) collective-permute-start(bf16[368,128]{1,0:T(8,128)(2,1)S(1)} %get-tuple-element.129.refs_2_), channel_id=1, source_target_pairs={{0,12},{4,0},{8,4},{12,8},{1,13},{5,1},{9,5},{13,9},{2,14},{6,2},{... | collective-permute-start | bytes 282632 | tf_op jit(solution)/shard_map/ppermute | solution.py:364
  69.8 0.9 %collective-permute-start.25 = (bf16[368,128]{1,0:T(8,128)(2,1)S(1)}, bf16[368,128]{1,0:T(8,128)(2,1)S(1)}, u32[]{:S(2)}, u32[]{:S(2)}) collective-permute-start(bf16[368,128]{1,0:T(8,128)(2,1)S(1)} %get-tuple-element.130.refs_3_), channel_id=1, source_target_pairs={{0,8},{4,12},{8,0},{12,4},{1,9},{5,13},{9,1},{13,5},{2,10},{6,14},... | collective-permute-start | bytes 282632 | tf_op jit(solution)/shard_map/ppermute | solution.py:364
  70.7 1.4 %collective-permute-start.26 = (bf16[368,128]{1,0:T(8,128)(2,1)S(1)}, bf16[368,128]{1,0:T(8,128)(2,1)S(1)}, u32[]{:S(2)}, u32[]{:S(2)}) collective-permute-start(bf16[368,128]{1,0:T(8,128)(2,1)S(1)} %get-tuple-element.131.refs_4_), channel_id=1, source_target_pairs={{0,4},{4,8},{8,12},{12,0},{1,5},{5,9},{9,13},{13,1},{2,6},{6,10},{... | collective-permute-start | bytes 282632 | tf_op jit(solution)/shard_map/ppermute | solution.py:364
  72.1 0.9 %collective-permute-start.27 = (bf16[160,128]{1,0:T(8,128)(2,1)S(1)}, bf16[160,128]{1,0:T(8,128)(2,1)S(1)}, u32[]{:S(2)}, u32[]{:S(2)}) collective-permute-start(bf16[160,128]{1,0:T(8,128)(2,1)S(1)} %get-tuple-element.132.refs_5_), channel_id=1, source_target_pairs={{0,2},{2,0},{1,3},{3,1},{4,6},{6,4},{5,7},{7,5},{8,10},{10,8},{9,1... | collective-permute-start | bytes 122888 | tf_op jit(solution)/shard_map/ppermute | solution.py:367
  73.0 4.0 %weights.3 = (bf16[8,352,1024]{2,1,0:T(8,128)(2,1)}, s32[8,128]{1,0:T(8,128)S(1)}) custom-call(s32[8,128]{1,0:T(8,128)S(1)} %get-tuple-element.127.where_ref, bf16[8,352,128]{2,1,0:T(8,128)(2,1)S(1)} %get-tuple-element.128.hidden_ref, bf16[8,64,1024]{2,1,0:T(8,128)(2,1)S(1)} %get-tuple-element.112.refs_6_.refs_0_, ...), custom_call_target="tpu_custom_call" | custom-call | flops 1000 | bytes 9000000 | tf_op jit(solution)/shard_map/weights/pallas_call | solution.py:461
  77.0 2.1 %collective-permute-done.25.refs_2_ = bf16[368,128]{1,0:T(8,128)(2,1)S(1)} collective-permute-done((bf16[368,128]{1,0:T(8,128)(2,1)S(1)}, bf16[368,128]{1,0:T(8,128)(2,1)S(1)}, u32[]{:S(2)}, u32[]{:S(2)}) %collective-permute-start.25) | collective-permute-done | bytes 94240 | tf_op jit(solution)/shard_map/ppermute | solution.py:364
  79.2 0.1 last_sums.1
  79.2 0.1 collective-permute-start.28
  79.3 1.3 %collective-permute-done.28.refs_1_ = bf16[528,128]{1,0:T(8,128)(2,1)S(1)} collective-permute-done((bf16[528,128]{1,0:T(8,128)(2,1)S(1)}, bf16[528,128]{1,0:T(8,128)(2,1)S(1)}, u32[]{:S(2)}, u32[]{:S(2)}) %collective-permute-start.28) | collective-permute-done | bytes 135200 | tf_op jit(solution)/shard_map/ppermute | solution.py:361
  80.7 0.8 unpack.1
  (29 shorter events, 0.4 us)
Async XLA Ops:
  1.9 14.2 %collective-permute-start.3 = (bf16[528,128]{1,0:T(8,128)(2,1)S(1)}, bf16[528,128]{1,0:T(8,128)(2,1)S(1)}, u32[]{:S(2)}, u32[]{:S(2)}) collective-permute-start(bf16[528,128]{1,0:T(8,128)(2,1)S(1)} %get-tuple-element.76), channel_id=1, source_target_pairs={{0,2},{2,0},{1,3},{3,1},{4,6},{6,4},{5,7},{7,5},{8,10},{10,8},{9,1... | collective-permute-start | bytes 405512 | tf_op jit(solution)/shard_map/ppermute | solution.py:367
  4.9 11.2 %collective-permute-start.2 = (bf16[528,128]{1,0:T(8,128)(2,1)S(1)}, bf16[528,128]{1,0:T(8,128)(2,1)S(1)}, u32[]{:S(2)}, u32[]{:S(2)}) collective-permute-start(bf16[528,128]{1,0:T(8,128)(2,1)S(1)} %get-tuple-element.76), channel_id=1, source_target_pairs={{0,12},{4,0},{8,4},{12,8},{1,13},{5,1},{9,5},{13,9},{2,14},{6,2},{... | collective-permute-start | bytes 405512 | tf_op jit(solution)/shard_map/ppermute | solution.py:364
  8.5 11.1 %collective-permute-start.1 = (bf16[528,128]{1,0:T(8,128)(2,1)S(1)}, bf16[528,128]{1,0:T(8,128)(2,1)S(1)}, u32[]{:S(2)}, u32[]{:S(2)}) collective-permute-start(bf16[528,128]{1,0:T(8,128)(2,1)S(1)} %get-tuple-element.76), channel_id=1, source_target_pairs={{0,8},{4,12},{8,0},{12,4},{1,9},{5,13},{9,1},{13,5},{2,10},{6,14},... | collective-permute-start | bytes 405512 | tf_op jit(solution)/shard_map/ppermute | solution.py:364
  8.5 11.1 %collective-permute-start = (bf16[528,128]{1,0:T(8,128)(2,1)S(1)}, bf16[528,128]{1,0:T(8,128)(2,1)S(1)}, u32[]{:S(2)}, u32[]{:S(2)}) collective-permute-start(bf16[528,128]{1,0:T(8,128)(2,1)S(1)} %get-tuple-element.76), channel_id=1, source_target_pairs={{0,4},{4,8},{8,12},{12,0},{1,5},{5,9},{9,13},{13,1},{2,6},{6,10},{... | collective-permute-start | bytes 405512 | tf_op jit(solution)/shard_map/ppermute | solution.py:364
  9.5 6.5 %collective-permute-start.4 = (bf16[64,1024]{1,0:T(8,128)(2,1)S(1)}, bf16[64,1024]{1,0:T(8,128)(2,1)S(1)}, u32[]{:S(2)}, u32[]{:S(2)}) collective-permute-start(bf16[64,1024]{1,0:T(8,128)(2,1)S(1)} %get-tuple-element.83), channel_id=1, source_target_pairs={{0,2},{2,0},{1,3},{3,1},{4,6},{6,4},{5,7},{7,5},{8,10},{10,8},{9,1... | collective-permute-start | bytes 393224 | tf_op jit(solution)/shard_map/ppermute | solution.py:367
  19.7 5.6 %collective-permute-start.5 = (bf16[4,528,128]{2,1,0:T(8,128)(2,1)S(1)}, bf16[4,528,128]{2,1,0:T(8,128)(2,1)S(1)}, u32[]{:S(2)}, u32[]{:S(2)}) collective-permute-start(bf16[4,528,128]{2,1,0:T(8,128)(2,1)S(1)} %pad_maximum_fusion.refs_0_), channel_id=1, source_target_pairs={{0,1},{1,0},{2,3},{3,2},{4,5},{5,4},{6,7},{7,6},{8,9},{9,8},{10,11... | collective-permute-start | bytes 1622024 | tf_op jit(solution)/shard_map/ppermute | solution.py:361
  19.8 12.9 %collective-permute-start.9 = (bf16[3,528,128]{2,1,0:T(8,128)(2,1)S(1)}, bf16[3,528,128]{2,1,0:T(8,128)(2,1)S(1)}, u32[]{:S(2)}, u32[]{:S(2)}) collective-permute-start(bf16[3,528,128]{2,1,0:T(8,128)(2,1)S(1)} %pad_maximum_fusion.2), channel_id=1, source_target_pairs={{0,2},{2,0},{1,3},{3,1},{4,6},{6,4},{5,7},{7,5},{8,10},{10,8},{9,1... | collective-permute-start | bytes 1216520 | tf_op jit(solution)/shard_map/ppermute | solution.py:367
  20.4 5.4 %collective-permute-start.8 = (bf16[48,1024]{1,0:T(8,128)(2,1)S(1)}, bf16[48,1024]{1,0:T(8,128)(2,1)S(1)}, u32[]{:S(2)}, u32[]{:S(2)}) collective-permute-start(bf16[48,1024]{1,0:T(8,128)(2,1)S(1)} %get-tuple-element.152), channel_id=1, source_target_pairs={{0,12},{4,0},{8,4},{12,8},{1,13},{5,1},{9,5},{13,9},{2,14},{6,2},{... | collective-permute-start | bytes 294920 | tf_op jit(solution)/shard_map/ppermute | solution.py:364
  22.1 10.6 %collective-permute-start.7 = (bf16[48,1024]{1,0:T(8,128)(2,1)S(1)}, bf16[48,1024]{1,0:T(8,128)(2,1)S(1)}, u32[]{:S(2)}, u32[]{:S(2)}) collective-permute-start(bf16[48,1024]{1,0:T(8,128)(2,1)S(1)} %get-tuple-element.152), channel_id=1, source_target_pairs={{0,8},{4,12},{8,0},{12,4},{1,9},{5,13},{9,1},{13,5},{2,10},{6,14},... | collective-permute-start | bytes 294920 | tf_op jit(solution)/shard_map/ppermute | solution.py:364
  23.3 9.4 %collective-permute-start.6 = (bf16[48,1024]{1,0:T(8,128)(2,1)S(1)}, bf16[48,1024]{1,0:T(8,128)(2,1)S(1)}, u32[]{:S(2)}, u32[]{:S(2)}) collective-permute-start(bf16[48,1024]{1,0:T(8,128)(2,1)S(1)} %get-tuple-element.152), channel_id=1, source_target_pairs={{0,4},{4,8},{8,12},{12,0},{1,5},{5,9},{9,13},{13,1},{2,6},{6,10},{... | collective-permute-start | bytes 294920 | tf_op jit(solution)/shard_map/ppermute | solution.py:364
  32.8 5.4 %collective-permute-start.10 = (bf16[4,528,128]{2,1,0:T(8,128)(2,1)S(1)}, bf16[4,528,128]{2,1,0:T(8,128)(2,1)S(1)}, u32[]{:S(2)}, u32[]{:S(2)}) collective-permute-start(bf16[4,528,128]{2,1,0:T(8,128)(2,1)S(1)} %pad_maximum_fusion.1.refs_0_), channel_id=1, source_target_pairs={{0,1},{1,0},{2,3},{3,2},{4,5},{5,4},{6,7},{7,6},{8,9},{9,8},{10,11... | collective-permute-start | bytes 1622024 | tf_op jit(solution)/shard_map/ppermute | solution.py:361
  32.9 9.5 %collective-permute-start.14 = (bf16[2,16,1024]{2,1,0:T(8,128)(2,1)S(1)}, bf16[2,16,1024]{2,1,0:T(8,128)(2,1)S(1)}, u32[]{:S(2)}, u32[]{:S(2)}) collective-permute-start(bf16[2,16,1024]{2,1,0:T(8,128)(2,1)S(1)} %get-tuple-element.154), channel_id=1, source_target_pairs={{0,12},{4,0},{8,4},{12,8},{1,13},{5,1},{9,5},{13,9},{2,14},{6,2},{... | collective-permute-start | bytes 196616 | tf_op jit(solution)/shard_map/ppermute | solution.py:364
  33.5 8.8 %collective-permute-start.13 = (bf16[2,16,1024]{2,1,0:T(8,128)(2,1)S(1)}, bf16[2,16,1024]{2,1,0:T(8,128)(2,1)S(1)}, u32[]{:S(2)}, u32[]{:S(2)}) collective-permute-start(bf16[2,16,1024]{2,1,0:T(8,128)(2,1)S(1)} %get-tuple-element.154), channel_id=1, source_target_pairs={{0,8},{4,12},{8,0},{12,4},{1,9},{5,13},{9,1},{13,5},{2,10},{6,14},... | collective-permute-start | bytes 196616 | tf_op jit(solution)/shard_map/ppermute | solution.py:364
  34.7 7.7 %collective-permute-start.12 = (bf16[2,16,1024]{2,1,0:T(8,128)(2,1)S(1)}, bf16[2,16,1024]{2,1,0:T(8,128)(2,1)S(1)}, u32[]{:S(2)}, u32[]{:S(2)}) collective-permute-start(bf16[2,16,1024]{2,1,0:T(8,128)(2,1)S(1)} %get-tuple-element.154), channel_id=1, source_target_pairs={{0,4},{4,8},{8,12},{12,0},{1,5},{5,9},{9,13},{13,1},{2,6},{6,10},{... | collective-permute-start | bytes 196616 | tf_op jit(solution)/shard_map/ppermute | solution.py:364
  36.7 8.6 %collective-permute-start.11 = (bf16[3,48,1024]{2,1,0:T(8,128)(2,1)S(1)}, bf16[3,48,1024]{2,1,0:T(8,128)(2,1)S(1)}, u32[]{:S(2)}, u32[]{:S(2)}) collective-permute-start(bf16[3,48,1024]{2,1,0:T(8,128)(2,1)S(1)} %pad_maximum_fusion.5), channel_id=1, source_target_pairs={{0,2},{2,0},{1,3},{3,1},{4,6},{6,4},{5,7},{7,5},{8,10},{10,8},{9,1... | collective-permute-start | bytes 884744 | tf_op jit(solution)/shard_map/ppermute | solution.py:367
  38.2 7.9 %collective-permute-start.15 = (bf16[4,48,1024]{2,1,0:T(8,128)(2,1)S(1)}, bf16[4,48,1024]{2,1,0:T(8,128)(2,1)S(1)}, u32[]{:S(2)}, u32[]{:S(2)}) collective-permute-start(bf16[4,48,1024]{2,1,0:T(8,128)(2,1)S(1)} %pad_maximum_fusion.3.refs_1_), channel_id=1, source_target_pairs={{0,1},{1,0},{2,3},{3,2},{4,5},{5,4},{6,7},{7,6},{8,9},{9,8},{10,11... | collective-permute-start | bytes 1179656 | tf_op jit(solution)/shard_map/ppermute | solution.py:361
  45.4 2.6 %collective-permute-start.17 = (bf16[4,48,1024]{2,1,0:T(8,128)(2,1)S(1)}, bf16[4,48,1024]{2,1,0:T(8,128)(2,1)S(1)}, u32[]{:S(2)}, u32[]{:S(2)}) collective-permute-start(bf16[4,48,1024]{2,1,0:T(8,128)(2,1)S(1)} %pad_maximum_fusion.4.refs_1_), channel_id=1, source_target_pairs={{0,1},{1,0},{2,3},{3,2},{4,5},{5,4},{6,7},{7,6},{8,9},{9,8},{10,11... | collective-permute-start | bytes 1179656 | tf_op jit(solution)/shard_map/ppermute | solution.py:361
  45.5 2.0 %collective-permute-start.16 = (bf16[4,2,16,1024]{3,2,1,0:T(8,128)(2,1)S(1)}, bf16[4,2,16,1024]{3,2,1,0:T(8,128)(2,1)S(1)}, u32[]{:S(2)}, u32[]{:S(2)}) collective-permute-start(bf16[4,2,16,1024]{3,2,1,0:T(8,128)(2,1)S(1)} %pad_maximum_fusion.6.refs_3_), channel_id=1, source_target_pairs={{0,1},{1,0},{2,3},{3,2},{4,5},{5,4},{6,7},{7,6},{8,9},{9,8},{10,11... | collective-permute-start | bytes 786440 | tf_op jit(solution)/shard_map/ppermute | solution.py:361
  54.0 2.0 %collective-permute-start.18 = (bf16[4,528,128]{2,1,0:T(8,128)(2,1)S(1)}, bf16[4,528,128]{2,1,0:T(8,128)(2,1)S(1)}, u32[]{:S(2)}, u32[]{:S(2)}) collective-permute-start(bf16[4,528,128]{2,1,0:T(8,128)(2,1)S(1)} %get-tuple-element.123), channel_id=1, source_target_pairs={{0,1},{1,0},{2,3},{3,2},{4,5},{5,4},{6,7},{7,6},{8,9},{9,8},{10,11... | collective-permute-start | bytes 1622024 | tf_op jit(solution)/shard_map/ppermute | solution.py:361
  54.7 2.9 %collective-permute-start.19 = (bf16[4,528,128]{2,1,0:T(8,128)(2,1)S(1)}, bf16[4,528,128]{2,1,0:T(8,128)(2,1)S(1)}, u32[]{:S(2)}, u32[]{:S(2)}) collective-permute-start(bf16[4,528,128]{2,1,0:T(8,128)(2,1)S(1)} %get-tuple-element.125), channel_id=1, source_target_pairs={{0,1},{1,0},{2,3},{3,2},{4,5},{5,4},{6,7},{7,6},{8,9},{9,8},{10,11... | collective-permute-start | bytes 1622024 | tf_op jit(solution)/shard_map/ppermute | solution.py:361
  56.1 11.8 %collective-permute-start.20 = (bf16[4,368,128]{2,1,0:T(8,128)(2,1)S(1)}, bf16[4,368,128]{2,1,0:T(8,128)(2,1)S(1)}, u32[]{:S(2)}, u32[]{:S(2)}) collective-permute-start(bf16[4,368,128]{2,1,0:T(8,128)(2,1)S(1)} %add_convert_fusion.refs_2_), channel_id=1, source_target_pairs={{0,2},{2,0},{1,3},{3,1},{4,6},{6,4},{5,7},{7,5},{8,10},{10,8},{9,1... | collective-permute-start | bytes 1130504 | tf_op jit(solution)/shard_map/ppermute | solution.py:367
  57.7 9.1 %collective-permute-start.21 = (bf16[2,160,128]{2,1,0:T(8,128)(2,1)S(1)}, bf16[2,160,128]{2,1,0:T(8,128)(2,1)S(1)}, u32[]{:S(2)}, u32[]{:S(2)}) collective-permute-start(bf16[2,160,128]{2,1,0:T(8,128)(2,1)S(1)} %pad_maximum_fusion.8.refs_3_), channel_id=1, source_target_pairs={{0,12},{4,0},{8,4},{12,8},{1,13},{5,1},{9,5},{13,9},{2,14},{6,2},{... | collective-permute-start | bytes 245768 | tf_op jit(solution)/shard_map/ppermute | solution.py:364
  59.9 8.1 %collective-permute-start.22 = (bf16[2,160,128]{2,1,0:T(8,128)(2,1)S(1)}, bf16[2,160,128]{2,1,0:T(8,128)(2,1)S(1)}, u32[]{:S(2)}, u32[]{:S(2)}) collective-permute-start(bf16[2,160,128]{2,1,0:T(8,128)(2,1)S(1)} %pad_maximum_fusion.9.refs_4_), channel_id=1, source_target_pairs={{0,8},{4,12},{8,0},{12,4},{1,9},{5,13},{9,1},{13,5},{2,10},{6,14},... | collective-permute-start | bytes 245768 | tf_op jit(solution)/shard_map/ppermute | solution.py:364
  60.0 8.0 %collective-permute-start.23 = (bf16[2,160,128]{2,1,0:T(8,128)(2,1)S(1)}, bf16[2,160,128]{2,1,0:T(8,128)(2,1)S(1)}, u32[]{:S(2)}, u32[]{:S(2)}) collective-permute-start(bf16[2,160,128]{2,1,0:T(8,128)(2,1)S(1)} %pad_maximum_fusion.10.refs_5_), channel_id=1, source_target_pairs={{0,4},{4,8},{8,12},{12,0},{1,5},{5,9},{9,13},{13,1},{2,6},{6,10},{... | collective-permute-start | bytes 245768 | tf_op jit(solution)/shard_map/ppermute | solution.py:364
  68.1 8.9 %collective-permute-start.24 = (bf16[368,128]{1,0:T(8,128)(2,1)S(1)}, bf16[368,128]{1,0:T(8,128)(2,1)S(1)}, u32[]{:S(2)}, u32[]{:S(2)}) collective-permute-start(bf16[368,128]{1,0:T(8,128)(2,1)S(1)} %get-tuple-element.129.refs_2_), channel_id=1, source_target_pairs={{0,12},{4,0},{8,4},{12,8},{1,13},{5,1},{9,5},{13,9},{2,14},{6,2},{... | collective-permute-start | bytes 282632 | tf_op jit(solution)/shard_map/ppermute | solution.py:364
  69.8 9.4 %collective-permute-start.25 = (bf16[368,128]{1,0:T(8,128)(2,1)S(1)}, bf16[368,128]{1,0:T(8,128)(2,1)S(1)}, u32[]{:S(2)}, u32[]{:S(2)}) collective-permute-start(bf16[368,128]{1,0:T(8,128)(2,1)S(1)} %get-tuple-element.130.refs_3_), channel_id=1, source_target_pairs={{0,8},{4,12},{8,0},{12,4},{1,9},{5,13},{9,1},{13,5},{2,10},{6,14},... | collective-permute-start | bytes 282632 | tf_op jit(solution)/shard_map/ppermute | solution.py:364
  70.7 8.5 %collective-permute-start.26 = (bf16[368,128]{1,0:T(8,128)(2,1)S(1)}, bf16[368,128]{1,0:T(8,128)(2,1)S(1)}, u32[]{:S(2)}, u32[]{:S(2)}) collective-permute-start(bf16[368,128]{1,0:T(8,128)(2,1)S(1)} %get-tuple-element.131.refs_4_), channel_id=1, source_target_pairs={{0,4},{4,8},{8,12},{12,0},{1,5},{5,9},{9,13},{13,1},{2,6},{6,10},{... | collective-permute-start | bytes 282632 | tf_op jit(solution)/shard_map/ppermute | solution.py:364
  72.1 4.9 %collective-permute-start.27 = (bf16[160,128]{1,0:T(8,128)(2,1)S(1)}, bf16[160,128]{1,0:T(8,128)(2,1)S(1)}, u32[]{:S(2)}, u32[]{:S(2)}) collective-permute-start(bf16[160,128]{1,0:T(8,128)(2,1)S(1)} %get-tuple-element.132.refs_5_), channel_id=1, source_target_pairs={{0,2},{2,0},{1,3},{3,1},{4,6},{6,4},{5,7},{7,5},{8,10},{10,8},{9,1... | collective-permute-start | bytes 122888 | tf_op jit(solution)/shard_map/ppermute | solution.py:367
  79.2 1.4 %collective-permute-start.28 = (bf16[528,128]{1,0:T(8,128)(2,1)S(1)}, bf16[528,128]{1,0:T(8,128)(2,1)S(1)}, u32[]{:S(2)}, u32[]{:S(2)}) collective-permute-start(bf16[528,128]{1,0:T(8,128)(2,1)S(1)} %get-tuple-element.137.refs_0_), channel_id=1, source_target_pairs={{0,1},{1,0},{2,3},{3,2},{4,5},{5,4},{6,7},{7,6},{8,9},{9,8},{10,11... | collective-permute-start | bytes 405512 | tf_op jit(solution)/shard_map/ppermute | solution.py:361
